TPU v7x, 32 devices: a whole 2x2x4 slice. The times are simulated.
32 devices in a mesh: seq: 4 (over z), fft: 8 (over y, x, core).
Axes of the slice: x: 2, y: 2, z: 4, core: 2. Of those that a mesh axis runs over, the one named last changes fastest.
Arguments:
- features: bfloat16 [256, 4096], P(None, ('seq', 'fft')), may hold values from -6 to 6
- sink_order: int32 [32, 128], P(('seq', 'fft')), may hold values from 0 to 127, each once within a row
- cotangent: bfloat16 [256, 4096], P(None, ('seq', 'fft')), may hold values from -6 to 6
- w_in: bfloat16 [768, 256], replicated, may hold values from -0.375 to 0.375
- short_taps: float32 [768, 3], replicated, may hold values from -1 to 1
- w_out: bfloat16 [256, 256], replicated, may hold values from -0.375 to 0.375
- filter_one: float32 [256, 4096], P(('seq', 'fft')), may hold values from -2 to 2
- filter_two: float32 [256, 4096], P(('seq', 'fft')), may hold values from -2 to 2
Outputs:
- grad_features: bfloat16 [256, 4096], P(None, ('seq', 'fft'))
- grad_w_in: float32 [768, 256], replicated
- grad_w_out: float32 [256, 256], replicated
- grad_short: float32 [768, 3], replicated
- grad_filter_one: float32 [256, 4096], P(('seq', 'fft'))
- grad_filter_two: float32 [256, 4096], P(('seq', 'fft'))
Inputs may be any that keep to these rules, and one draw needn't show every extreme that they name: Each row of sink_order names every position of a block of 128 sinks once.
All inputs are finite; a program needn't handle non-finite values.
Results may differ from a plain program's by a relative error of at most 0.0089.
Values may be sent and summed in bfloat16 or wider, within the bound.
No kernel may reach another device: no remote copies, remote signals or barrier semaphores. Data moves between devices by JAX's collectives and lax.ppermute only.
A program may use at most 64 MiB of HBM per device.

v0:
```python
import math

import jax
import jax.numpy as jnp
import numpy as np
from jax import lax
from jax.experimental import pallas as pl
from jax.experimental.pallas import tpu as pltpu
from jax.sharding import PartitionSpec as P

AXES = ("seq", "fft")
LANES = 128
bf16 = jnp.bfloat16
f32 = jnp.float32
PARAMS = pltpu.CompilerParams(vmem_limit_bytes=24 * 1024 * 1024)


def halves(table):
    high = table.astype(np.float32).astype(jnp.bfloat16)
    low = (table - high.astype(np.float64)).astype(np.float32).astype(jnp.bfloat16)
    return high, low


def make_tables(count, channels):
    length = count * LANES
    outer = np.arange(count, dtype=np.float64)
    inner = np.arange(LANES, dtype=np.float64)
    angle = 2.0 * np.pi * (outer[:, None] + 0.25) * outer[None, :] / count
    first = np.concatenate([np.cos(angle), -np.sin(angle)], axis=0)
    first = np.kron(first, np.eye(channels))
    turn = 2.0 * np.pi * (inner[:, None] * inner[None, :] % LANES) / LANES
    cos, sin = np.cos(turn), np.sin(turn)
    second = np.block([[cos, -sin], [sin, cos]])
    twist = 2.0 * np.pi * (outer[:, None] + 0.25) * inner[None, :] / length
    twist = np.repeat(twist, channels, axis=0)
    back = first.T / length
    rows = count * channels
    back = np.concatenate([back[:, :rows], back[:, rows:]], axis=0)
    packed = [half for t in (first, back, second, second.T) for half in halves(t)]
    twist = np.concatenate([np.cos(twist), -np.sin(twist)], axis=1).astype(np.float32)
    return np.concatenate(packed, axis=0), twist


def tables_of(table, twist):
    rows = twist.shape[0]
    at, found = 0, []
    for size in (2 * rows, 2 * rows, 2 * LANES, 2 * LANES):
        pair = []
        for half in range(2):
            pair.append(table[at : at + size])
            at += size
        found.append(tuple(pair))
    found[1] = tuple(jnp.concatenate([t[:rows], t[rows:]], axis=1) for t in found[1])
    return (*found, (twist[:, :LANES], twist[:, LANES:]))


def split(value):
    high = value.astype(bf16)
    low = (value - high.astype(f32)).astype(bf16)
    return high, low


def dot(left, right):
    return jnp.dot(left, right, preferred_element_type=f32)


def dot_pairs(left, right):
    return dot(left[0], right[0]) + dot(left[0], right[1]) + dot(left[1], right[0])


def forward(signals, first, second, twist):
    rows = signals[0].shape[0]
    stage = dot_pairs(first, split(jnp.concatenate(signals, axis=1)))
    parts = []
    for i in range(len(signals)):
        re = stage[:rows, i * LANES : (i + 1) * LANES]
        im = stage[rows:, i * LANES : (i + 1) * LANES]
        parts.append(
            jnp.concatenate(
                [re * twist[0] - im * twist[1], re * twist[1] + im * twist[0]], axis=1
            )
        )
    spec = dot_pairs(split(jnp.concatenate(parts, axis=0)), second)
    return [
        (spec[i * rows : (i + 1) * rows, :LANES], spec[i * rows : (i + 1) * rows, LANES:])
        for i in range(len(signals))
    ]


def backward(spectra, first_back, second_back, twist):
    rows = spectra[0][0].shape[0]
    stacked = jnp.concatenate([jnp.concatenate(pair, axis=1) for pair in spectra], axis=0)
    stage = dot_pairs(split(stacked), second_back)
    parts = []
    for i in range(len(spectra)):
        re = stage[i * rows : (i + 1) * rows, :LANES]
        im = stage[i * rows : (i + 1) * rows, LANES:]
        parts.append(
            jnp.concatenate(
                [re * twist[0] + im * twist[1], im * twist[0] - re * twist[1]], axis=0
            )
        )
    out = dot_pairs(first_back, split(jnp.concatenate(parts, axis=1)))
    return [out[:, i * LANES : (i + 1) * LANES] for i in range(len(spectra))]


def times(a, b):
    return (a[0] * b[0] - a[1] * b[1], a[0] * b[1] + a[1] * b[0])


def conj_times(a, b):
    return (a[0] * b[0] + a[1] * b[1], a[0] * b[1] - a[1] * b[0])


def one_hot(order):
    size = order.shape[1]
    place = lax.broadcasted_iota(jnp.int32, (size, size), 0)
    return (place == order).astype(f32).astype(bf16)


def project_kernel(
    features_at,
    order_at,
    cotangent_at,
    w_in_at,
    w_out_at,
    streams_out,
    gather_out,
    features,
    order,
    cotangent,
    w_in,
    w_out,
    done,
):
    copies = [
        pltpu.make_async_copy(source, target, done.at[i])
        for i, (source, target) in enumerate(
            [
                (order_at, order),
                (features_at, features),
                (w_in_at, w_in),
                (cotangent_at, cotangent),
                (w_out_at, w_out),
            ]
        )
    ]
    for copy in copies:
        copy.start()
    width, row_count = features.shape
    copies[0].wait()
    copies[1].wait()
    seq_input = dot(features[...], one_hot(order[...])).astype(bf16)
    copies[2].wait()
    projected = dot(w_in[...], seq_input)
    copies[3].wait()
    copies[4].wait()
    out_grad = lax.dot_general(
        w_out[...], cotangent[...], (((0,), (0,)), ((), ())), preferred_element_type=f32
    )
    if len(streams_out.shape) == 3:
        blocks = streams_out.shape[0]
        parts = [projected[s * width : (s + 1) * width] for s in range(3)] + [out_grad]
        parts = [part.reshape(blocks, width // blocks, row_count) for part in parts]
        streams_out[...] = jnp.concatenate(parts, axis=1).astype(bf16)
    else:
        streams_out[: 3 * width] = projected.astype(bf16)
        streams_out[3 * width :] = out_grad.astype(bf16)
    own = jnp.concatenate([seq_input, cotangent[...]], axis=0)
    gather_out[...] = own


def read_signal(ref, rows):
    if ref.shape[1] == LANES:
        return ref[...]
    return jnp.concatenate(
        [ref[:, i * LANES : (i + 1) * LANES] for i in range(ref.shape[1] // LANES)], axis=0
    )


def write_signal(ref, value):
    if ref.shape[1] == LANES:
        ref[...] = value
        return
    channels = ref.shape[0]
    for i in range(ref.shape[1] // LANES):
        ref[:, i * LANES : (i + 1) * LANES] = value[i * channels : (i + 1) * channels]


def filter_kernel(
    filter_one, filter_two, table, twist, spec_one, spec_two, table_out, twist_out
):
    rows = spec_one.shape[0]
    signals = [read_signal(filter_one, rows), read_signal(filter_two, rows)]
    first, _, second, _, turns = tables_of(table, twist)
    one, two = forward(signals, first, second, turns)
    spec_one[...] = jnp.concatenate(one, axis=1)
    spec_two[...] = jnp.concatenate(two, axis=1)
    table_out[...] = table[...]
    twist_out[...] = twist[...]


def shifted(value, steps, channels):
    if steps == 0:
        return value
    rows, lanes = value.shape
    lane = lax.broadcasted_iota(jnp.int32, value.shape, 1)
    row = lax.broadcasted_iota(jnp.int32, value.shape, 0)
    turned = pltpu.roll(value, steps % lanes, 1)
    if steps > 0:
        carried = jnp.where(row < channels, 0.0, pltpu.roll(turned, channels, 0))
        return jnp.where(lane < steps, carried, turned)
    carried = jnp.where(row >= rows - channels, 0.0, pltpu.roll(turned, rows - channels, 0))
    return jnp.where(lane >= lanes + steps, carried, turned)


def mix_kernel(
    channels,
    scale,
    streams,
    taps,
    spec_one,
    spec_two,
    table,
    twist,
    line,
    short_out,
    product_one,
    product_two,
    *sent_out,
):
    rows = twist.shape[0]
    eight = taps.shape[0]
    first, first_back, second, second_back, twist = tables_of(table, twist)
    if streams.shape[0] == 4 and streams.shape[1] == rows:
        pieces = [streams[s].astype(f32) for s in range(4)]
    else:
        whole = streams[...].astype(f32)
        pieces = [
            whole[:, s * channels : (s + 1) * channels].reshape(rows, LANES) for s in range(4)
        ]
    out_grad = pieces[3]

    def tap(s, k):
        column = jnp.broadcast_to(taps[:, 3 * s + k : 3 * s + k + 1], (eight, LANES))
        column = jnp.broadcast_to(column[None], (rows // eight, eight, LANES))
        return column.reshape(rows, LANES)

    late = [[shifted(pieces[s], k, channels) for k in range(3)] for s in range(3)]
    value, gate_one, gate_two = [
        sum(tap(s, k) * late[s][k] for k in range(3)) for s in range(3)
    ]
    h_one = (spec_one[:, :LANES], spec_one[:, LANES:])
    h_two = (spec_two[:, :LANES], spec_two[:, LANES:])
    value_spec, second_spec = forward([value, out_grad * gate_two], first, second, twist)
    first_mix, grad_first_out = backward(
        [times(h_one, value_spec), conj_times(h_two, second_spec)],
        first_back,
        second_back,
        twist,
    )
    first_spec, grad_first_spec = forward(
        [gate_one * first_mix, gate_one * grad_first_out], first, second, twist
    )
    second_mix, grad_value = backward(
        [times(h_two, first_spec), conj_times(h_one, grad_first_spec)],
        first_back,
        second_back,
        twist,
    )
    product_one[...] = jnp.concatenate(conj_times(value_spec, grad_first_spec), axis=1)
    product_two[...] = jnp.concatenate(conj_times(first_spec, second_spec), axis=1)
    grads = [grad_value, grad_first_out * first_mix, out_grad * second_mix]
    sent = []
    lane = lax.broadcasted_iota(jnp.int32, (eight, LANES), 1)
    short = jnp.zeros((eight, LANES), f32)
    for s in range(3):
        sent.append(sum(tap(s, k) * shifted(grads[s], -k, channels) for k in range(3)))
        for k in range(3):
            folded = (grads[s] * late[s][k]).reshape(rows // eight, eight, LANES).sum(axis=0)
            total = jnp.sum(folded, axis=1, keepdims=True) * scale
            short = jnp.where(lane == 3 * s + k, total, short)
    sent.append(gate_two * second_mix)
    short_out[...] = short
    if len(sent_out) == 1:
        for s in range(4):
            sent_out[0][s] = sent[s].astype(bf16)
        return
    parts = [part.reshape(rows // channels, channels, LANES) for part in sent]
    packed = jnp.concatenate(parts, axis=1).astype(bf16)
    *sent_out, store = sent_out
    lines, plane = store.shape[:2]
    for i in range(lines):
        store[i] = packed[i * plane : (i + 1) * plane]
    for step in range(lines):
        sent_out[step][...] = store[lax.rem(line[0] + step, lines)]


def filter_grads_kernel(scale, product_one, product_two, table, twist, grad_one, grad_two):
    _, first_back, _, second_back, twist = tables_of(table, twist)
    spectra = [(ref[:, :LANES], ref[:, LANES:]) for ref in (product_one, product_two)]
    one, two = backward(spectra, first_back, second_back, twist)
    write_signal(grad_one, one * scale)
    write_signal(grad_two, two * scale)


def member(at, k):
    return jnp.bitwise_xor(at, k)


def weights_kernel(channels, scale, lines, *refs):
    at, short, *refs, partial_out, moved_out = refs
    met, pieces = refs[:lines], refs[lines:]
    plane, width = len(pieces), pieces[0].shape[0] // 2
    height = 4 * channels
    total = jnp.zeros((lines * height, 2 * width), f32)
    step = 2 if plane % 2 == 0 else 1
    for i in range(0, plane, step):
        left = jnp.concatenate(
            [
                jnp.concatenate([m[member(at[1], i + j)] for m in met], axis=0)
                for j in range(step)
            ],
            axis=1,
        )
        right = jnp.concatenate([pieces[i + j][...] for j in range(step)], axis=1)
        total = total + lax.dot_general(
            left, right, (((1,), (1,)), ((), ())), preferred_element_type=f32
        )
    total = total * scale
    size = height * (width // LANES)
    for k in range(lines):
        parts = []
        for h in range(width // LANES):
            low, high = h * LANES, (h + 1) * LANES
            base = k * height
            parts.append(total[base : base + 3 * channels, low:high])
            parts.append(total[base + 3 * channels : base + height, width + low : width + high])
        owner = lax.rem(at[0] + lines - k, lines)
        spot = pl.ds(pl.multiple_of(owner * size, size), size)
        partial_out[spot] = jnp.concatenate(parts, axis=0).astype(bf16)
    tail = jnp.concatenate([short[...]] * lines, axis=0)
    owner = lax.broadcasted_iota(jnp.int32, tail.shape, 0) // channels
    partial_out[lines * size :] = jnp.where(owner == at[0], tail, 0.0).astype(bf16)
    parts = [m[...].astype(f32)[:, : 3 * channels] for m in met]
    moved_out[...] = jnp.concatenate(parts, axis=1).astype(bf16)


def sum_kernel(*refs):
    *partials, out = refs
    out[...] = sum(part[...].astype(f32) for part in partials).astype(bf16)


def unorder(grad_projected, w_in, order):
    grad_seq = lax.dot_general(
        w_in, grad_projected, (((0,), (0,)), ((), ())), preferred_element_type=f32
    ).astype(bf16)
    return lax.dot_general(
        grad_seq, one_hot(order), (((1,), (1,)), ((), ())), preferred_element_type=f32
    ).astype(bf16)


def moved_kernel(channels, lines, at, back, w_in, order, features_out, store):
    plane, width = back.shape[0], w_in.shape[1]
    share = plane * channels
    whole = back[...].astype(f32)
    for k in range(lines):
        owner = lax.rem(at[0] + lines - k, lines)
        for s in range(3):
            start = (3 * k + s) * channels
            spot = pl.ds(pl.multiple_of(s * width + owner * share, share), share)
            store[spot] = whole[:, start : start + channels].reshape(share, LANES)
    features_out[...] = unorder(store[...].astype(bf16), w_in[...], order[...])


def finish_kernel(channels, lines, at, *refs):
    *pieces, w_in_out, w_out_out, short_out, out_rows, short_rows = refs
    width = w_out_out.shape[0]
    share = width // lines
    height = 4 * channels
    size = height * (width // LANES)
    for k, piece in enumerate(pieces):
        rows = piece[...].astype(f32)
        for i in range(lines):
            first = pl.multiple_of(i * share + member(at[1], k) * channels, channels)
            for h in range(width // LANES):
                low, high = h * LANES, (h + 1) * LANES
                base = i * size + h * height
                for s in range(3):
                    spot = pl.ds(pl.multiple_of(s * width + first, channels), channels)
                    start = base + s * channels
                    w_in_out[spot, low:high] = rows[start : start + channels]
                start = base + 3 * channels
                out_rows[pl.ds(first, channels), low:high] = rows[start : start + channels]
            start = lines * size + i * channels
            short_rows[pl.ds(first, channels), :] = rows[start : start + channels]
    w_out_out[...] = out_rows[...].T
    short = short_rows[...].T
    for s in range(3):
        short_out[:, s * width : (s + 1) * width] = short[3 * s : 3 * s + 3, :]


def features_kernel(moved, w_in, order, features_out):
    features_out[...] = unorder(moved[...], w_in[...], order[...])


def swapped(value, plane, distance):
    return lax.ppermute(value, "fft", [(i, i ^ distance) for i in range(plane)])


def spread(value, plane):
    pieces = [value if k == 0 else swapped(value, plane, k) for k in range(0, plane, 2)]
    return [piece for own in pieces for piece in (own, swapped(own, plane, 1))]


def shape(dims, dtype=f32):
    return jax.ShapeDtypeStruct(dims, dtype)


def local(features, sink_order, cotangent, w_in, short_taps, w_out, filter_one, filter_two):
    width, row_count = features.shape
    lines, plane = lax.axis_size("seq"), lax.axis_size("fft")
    blocks = lines * plane
    channels, length = filter_one.shape
    rows = channels * blocks
    scale = 1.0 / math.sqrt(length)
    whole = channels % 8 == 0 and plane % 2 == 0 and plane & (plane - 1) == 0
    table, twist = make_tables(blocks, channels)
    eight = channels if whole else 8
    mine = lax.axis_index(AXES)

    def call(kernel, outs, *args, **options):
        return pl.pallas_call(kernel, out_shape=outs, compiler_params=PARAMS, **options)(*args)

    dims = (blocks, 4 * channels, LANES) if whole else (4 * width, LANES)
    streams, own = pl.pallas_call(
        project_kernel,
        out_shape=(shape(dims, bf16), shape((2 * width, row_count), bf16)),
        in_specs=[pl.BlockSpec(memory_space=pl.ANY)] * 5,
        scratch_shapes=[
            pltpu.VMEM(a.shape, a.dtype)
            for a in (features, sink_order, cotangent, w_in, w_out)
        ]
        + [pltpu.SemaphoreType.DMA((5,))],
        compiler_params=pltpu.CompilerParams(vmem_limit_bytes=60 * 1024 * 1024),
    )(features, sink_order, cotangent, w_in, w_out)
    if not whole:
        streams = streams.reshape(4, blocks, channels, LANES).transpose(1, 0, 2, 3)
        streams = streams.reshape(blocks, 4 * channels, LANES)
    if whole:
        pieces = spread(own, plane)
    else:
        gathered = lax.all_gather(own, AXES, axis=0, tiled=False)
    arrived = lax.all_to_all(streams, AXES, split_axis=0, concat_axis=0, tiled=True)
    taps = lax.dynamic_slice_in_dim(short_taps.reshape(3, width, 3), mine * channels, channels, 1)
    taps = taps.transpose(1, 0, 2).reshape(channels, 9)
    if not whole:
        taps = jnp.tile(taps, (8 // channels, 1))
        arrived = arrived.reshape(blocks, 4, channels, LANES).transpose(1, 0, 2, 3)
        arrived = arrived.reshape(4, rows, LANES)
        filter_one, filter_two = [
            h.reshape(channels, blocks, LANES).transpose(1, 0, 2).reshape(rows, LANES)
            for h in (filter_one, filter_two)
        ]
    spec = shape((rows, 2 * LANES))
    spec_one, spec_two, table, twist = call(
        filter_kernel,
        (spec, spec, shape(table.shape, bf16), shape(twist.shape)),
        filter_one,
        filter_two,
        table,
        twist,
    )
    at = jnp.stack([lax.axis_index("seq"), lax.axis_index("fft")]).astype(jnp.int32)
    scalar = pl.BlockSpec(memory_space=pltpu.SMEM)
    held = pl.BlockSpec(memory_space=pltpu.VMEM)
    chunk = (plane, 4 * channels, LANES)
    dims = [shape(chunk, bf16)] * lines if whole else [shape((4, rows, LANES), bf16)]
    short, product_one, product_two, *sent = call(
        lambda *refs: mix_kernel(channels, scale, *refs),
        (shape((eight, LANES)), spec, spec, *dims),
        arrived,
        taps,
        spec_one,
        spec_two,
        table,
        twist,
        at,
        in_specs=[held] * 6 + [scalar],
        scratch_shapes=[pltpu.VMEM((lines, *chunk), bf16)] if whole else [],
    )
    grad_one, grad_two = call(
        lambda *refs: filter_grads_kernel(scale, *refs),
        (shape(filter_one.shape), shape(filter_two.shape)),
        product_one,
        product_two,
        table,
        twist,
    )
    height = channels * 4 * (width // LANES)
    if whole:
        def ahead(value, steps):
            pairs = [(i, (i + steps) % lines) for i in range(lines)]
            return lax.ppermute(value, "seq", pairs)

        met = [sent[0]] + [ahead(sent[k], k) for k in range(1, lines)]
        size = lines * height + lines * channels
        partial, moved = call(
            lambda *refs: weights_kernel(channels, scale, lines, *refs),
            (
                shape((size, LANES), bf16),
                shape((plane, 3 * lines * channels, LANES), bf16),
            ),
            at,
            short,
            *met,
            *pieces,
            in_specs=[scalar] + [held] * (1 + lines + plane),
        )
        partials = [partial] + [ahead(partial, k) for k in range(1, lines)]
        back = lax.all_to_all(moved, "fft", split_axis=0, concat_axis=0, tiled=True)
        grad_features = call(
            lambda *refs: moved_kernel(channels, lines, *refs),
            shape(features.shape, bf16),
            at,
            back,
            w_in,
            sink_order,
            in_specs=[scalar] + [held] * 3,
            scratch_shapes=[pltpu.VMEM((3 * width, LANES), f32)],
        )
        rows_sum = call(sum_kernel, shape((size, LANES), bf16), *partials)
        grad_w_in, grad_w_out, short = call(
            lambda *refs: finish_kernel(channels, lines, *refs),
            (shape((3 * width, width)), shape((width, width)), shape((3, 3 * width))),
            at,
            *spread(rows_sum, plane),
            in_specs=[scalar] + [held] * plane,
            scratch_shapes=[pltpu.VMEM((width, width), f32), pltpu.VMEM((width, LANES), f32)],
        )
        return (grad_features, grad_w_in, grad_w_out, short.T, grad_one, grad_two)
    sent = sent[0]
    sent = sent.reshape(4, blocks, channels, LANES)
    grad_in = jnp.einsum(
        "sbcp,bwp->scw", sent[:3], gathered[:, :width], preferred_element_type=f32
    )
    grad_out = jnp.einsum(
        "bcp,bwp->cw", sent[3], gathered[:, width:], preferred_element_type=f32
    )
    own = jnp.concatenate([grad_in, grad_out[None]]) * scale
    own = own.reshape(height, LANES)
    short = short.reshape(8 // channels, channels, LANES).sum(axis=0)
    own = jnp.concatenate([own, short]).astype(bf16)
    moved = sent[:3].transpose(1, 0, 2, 3).reshape(blocks, 3 * channels, LANES)
    own = jnp.broadcast_to(own[None], (blocks,) + own.shape)
    packed = jnp.concatenate([moved, own], axis=1)
    back = lax.all_to_all(packed, AXES, split_axis=0, concat_axis=0, tiled=True)
    moved = back[:, : 3 * channels].reshape(blocks, 3, channels, LANES)
    moved = moved.transpose(1, 0, 2, 3).reshape(3 * width, LANES)
    weights = back[:, 3 * channels : 3 * channels + height].astype(f32)
    weights = weights.reshape(blocks, 4, channels, width).transpose(1, 0, 2, 3)
    weights = weights.reshape(4 * width, width)
    short = back[:, 3 * channels + height :, :9].astype(f32).reshape(width, 3, 3)
    short = short.transpose(1, 0, 2).reshape(3 * width, 3)
    grad_features = call(
        features_kernel, shape(features.shape, bf16), moved, w_in, sink_order
    )
    grad_one, grad_two = [
        g.reshape(blocks, channels, LANES).transpose(1, 0, 2).reshape(channels, length)
        for g in (grad_one, grad_two)
    ]
    return (
        grad_features,
        weights[: 3 * width],
        weights[3 * width :].T,
        short,
        grad_one,
        grad_two,
    )


def solution(mesh):
    columns, blocks_first, copied = P(None, AXES), P(AXES, None), P()
    return jax.shard_map(
        local,
        mesh=mesh,
        in_specs=(
            columns,
            blocks_first,
            columns,
            copied,
            copied,
            copied,
            blocks_first,
            blocks_first,
        ),
        out_specs=(columns, copied, copied, copied, blocks_first, blocks_first),
        check_vma=False,
    )
```

profile of v0, /device:TPU:0, one launch (start us, length us, event | category | flops | bytes accessed | tf_op | source)
XLA Modules:
  0.0 64.3 jit_solution(5211280758581035536)
XLA Ops:
  0.6 0.0 copy-start
  0.6 2.3 %shard_map.145 = (bf16[32,32,128]{2,1,0:T(8,128)(2,1)}, bf16[512,128]{1,0:T(8,128)(2,1)}) custom-call(bf16[256,128]{1,0:T(8,128)(2,1)} %features_at.1, s32[1,128]{1,0:T(1,128)} %refs_3_.1, bf16[256,128]{1,0:T(8,128)(2,1)} %cotangent_at.1, bf16[768,256]{1,0:T(8,128)(2,1)} %refs_2_.1, bf16[256,256]{1,0:T(8,128)(2,1)} %w_out_at.1), custom_call_target="tpu_custom_call" | custom-call | tf_op jit(solution)/shard_map/pallas_call | solution.py:436
  3.0 7.3 %all-to-all-start = ((bf16[32,32,128]{2,1,0:T(8,128)(2,1)}), bf16[32,32,128]{2,1,0:T(8,128)(2,1)S(1)}, u32[]{:S(2)}, u32[]{:S(2)}) async-start(bf16[32,32,128]{2,1,0:T(8,128)(2,1)} %get-tuple-element.26), calls=%async_computation | async-start | bytes 524288 | tf_op jit(solution)/shard_map/all_to_all | solution.py:454
  10.3 1.8 %collective-permute-start.4 = (bf16[512,128]{1,0:T(8,128)(2,1)}, bf16[512,128]{1,0:T(8,128)(2,1)S(1)}, u32[]{:S(2)}, u32[]{:S(2)}) collective-permute-start(bf16[512,128]{1,0:T(8,128)(2,1)} %get-tuple-element.36.refs_6_), channel_id=1, source_target_pairs={{0,2},{1,3},{2,0},{3,1},{4,6},{5,7},{6,4},{7,5},{8,10},{9,11},{10,... | collective-permute-start | bytes 393224 | tf_op jit(solution)/shard_map/ppermute | solution.py:408
  12.1 1.5 %collective-permute-start.6 = (bf16[512,128]{1,0:T(8,128)(2,1)}, bf16[512,128]{1,0:T(8,128)(2,1)}, u32[]{:S(2)}, u32[]{:S(2)}) collective-permute-start(bf16[512,128]{1,0:T(8,128)(2,1)} %get-tuple-element.36.refs_6_), channel_id=1, source_target_pairs={{0,4},{1,5},{2,6},{3,7},{4,0},{5,1},{6,2},{7,3},{8,12},{9,13},{10,... | collective-permute-start | bytes 393224 | tf_op jit(solution)/shard_map/ppermute | solution.py:408
  13.6 0.3 collective-permute-start.8
  13.9 0.0 collective-permute-start.3
  13.9 5.1 %collective-permute-done.4.refs_8_ = bf16[512,128]{1,0:T(8,128)(2,1)S(1)} collective-permute-done((bf16[512,128]{1,0:T(8,128)(2,1)}, bf16[512,128]{1,0:T(8,128)(2,1)S(1)}, u32[]{:S(2)}, u32[]{:S(2)}) %collective-permute-start.4) | collective-permute-done | bytes 131104 | tf_op jit(solution)/shard_map/ppermute | solution.py:408
  19.0 0.0 collective-permute-start.5
  19.0 0.0 copy-done
  19.0 0.1 dynamic-slice_bitcast_fusion
  19.1 0.1 copy.19.refs_1_
  19.2 1.4 %copy-done.2 = bf16[3072,256]{1,0:T(8,128)(2,1)S(1)} copy-done((bf16[3072,256]{1,0:T(8,128)(2,1)S(1)}, bf16[3072,256]{1,0:T(8,128)(2,1)}, u32[]{:S(2)}) %copy-start.2) | copy-done | bytes 1572888
  20.6 0.9 %copy-done.3 = f32[256,256]{1,0:T(8,128)S(1)} copy-done((f32[256,256]{1,0:T(8,128)S(1)}, f32[256,256]{1,0:T(8,128)}, u32[]{:S(2)}) %copy-start.3) | copy-done | bytes 262168
  21.5 0.9 %copy-done.4 = f32[8,4096]{1,0:T(8,128)S(1)} copy-done((f32[8,4096]{1,0:T(8,128)S(1)}, f32[8,4096]{1,0:T(8,128)}, u32[]{:S(2)}) %copy-start.4) | copy-done | bytes 131096
  22.4 0.9 %copy-done.5 = f32[8,4096]{1,0:T(8,128)S(1)} copy-done((f32[8,4096]{1,0:T(8,128)S(1)}, f32[8,4096]{1,0:T(8,128)}, u32[]{:S(2)}) %copy-start.5) | copy-done | bytes 131096
  23.3 1.0 %shard_map.146 = (f32[256,256]{1,0:T(8,128)S(1)}, f32[256,256]{1,0:T(8,128)S(1)}, bf16[3072,256]{1,0:T(8,128)(2,1)S(1)}, f32[256,256]{1,0:T(8,128)S(1)}) custom-call(f32[8,4096]{1,0:T(8,128)S(1)} %copy-done.4, f32[8,4096]{1,0:T(8,128)S(1)} %copy-done.5, bf16[3072,256]{1,0:T(8,128)(2,1)S(1)} %copy-done.2, f32[256,256]{1,0:T(8,128)S(1)} %copy-done.3), custom_call_target="tpu_custom_call" | custom-call | tf_op jit(solution)/shard_map/pallas_call | solution.py:433
  24.4 0.0 copy-start.6
  24.4 0.0 collective-permute-done.6.refs_10_
  24.4 0.6 collective-permute-start.7
  25.0 0.0 collective-permute-done.8.refs_12_
  25.0 0.1 collective-permute-start.9
  25.1 0.1 pad_add_fusion.refs_6_.refs_0_
  25.2 0.0 all-to-all-done.refs_0_
  25.2 4.8 %shard_map.147 = (f32[8,128]{1,0:T(8,128)S(1)}, f32[256,256]{1,0:T(8,128)S(1)}, f32[256,256]{1,0:T(8,128)S(1)}, bf16[8,32,128]{2,1,0:T(8,128)(2,1)S(1)}, bf16[8,...) custom-call(bf16[32,32,128]{2,1,0:T(8,128)(2,1)S(1)} %all-to-all-done.refs_0_, ...), custom_call_target="tpu_custom_call" | custom-call | tf_op jit(solution)/shard_map/pallas_call | solution.py:433
  30.0 1.6 %collective-permute-start = (bf16[8,32,128]{2,1,0:T(8,128)(2,1)S(1)}, bf16[8,32,128]{2,1,0:T(8,128)(2,1)S(1)}, u32[]{:S(2)}, u32[]{:S(2)}) collective-permute-start(bf16[8,32,128]{2,1,0:T(8,128)(2,1)S(1)} %get-tuple-element.33), channel_id=1, source_target_pairs={{0,8},{8,16},{16,24},{24,0},{1,9},{9,17},{17,25},{25,1},{2,10},{10... | collective-permute-start | bytes 196616 | tf_op jit(solution)/shard_map/ppermute | solution.py:504
  31.5 0.0 collective-permute-done.3.refs_7_
  31.5 2.5 %collective-permute-start.1 = (bf16[8,32,128]{2,1,0:T(8,128)(2,1)S(1)}, bf16[8,32,128]{2,1,0:T(8,128)(2,1)S(1)}, u32[]{:S(2)}, u32[]{:S(2)}) collective-permute-start(bf16[8,32,128]{2,1,0:T(8,128)(2,1)S(1)} %get-tuple-element.34), channel_id=1, source_target_pairs={{0,16},{8,24},{16,0},{24,8},{1,17},{9,25},{17,1},{25,9},{2,18},{10... | collective-permute-start | bytes 196616 | tf_op jit(solution)/shard_map/ppermute | solution.py:504
  34.0 0.0 collective-permute-done.5.refs_9_
  34.0 1.4 %collective-permute-start.2 = (bf16[8,32,128]{2,1,0:T(8,128)(2,1)S(1)}, bf16[8,32,128]{2,1,0:T(8,128)(2,1)S(1)}, u32[]{:S(2)}, u32[]{:S(2)}) collective-permute-start(bf16[8,32,128]{2,1,0:T(8,128)(2,1)S(1)} %get-tuple-element.35), channel_id=1, source_target_pairs={{0,24},{8,0},{16,8},{24,16},{1,25},{9,1},{17,9},{25,17},{2,26},{10... | collective-permute-start | bytes 196616 | tf_op jit(solution)/shard_map/ppermute | solution.py:504
  35.4 0.0 collective-permute-done.7.refs_11_
  35.4 0.0 collective-permute-done.9.refs_13_
  35.4 1.1 %collective-permute-done.refs_3_ = bf16[8,32,128]{2,1,0:T(8,128)(2,1)S(1)} collective-permute-done((bf16[8,32,128]{2,1,0:T(8,128)(2,1)S(1)}, bf16[8,32,128]{2,1,0:T(8,128)(2,1)S(1)}, u32[]{:S(2)}, u32[]{:S(2)}) %collective-permute-start) | collective-permute-done | bytes 65568 | tf_op jit(solution)/shard_map/ppermute | solution.py:504
  36.5 2.7 %collective-permute-done.1.refs_4_ = bf16[8,32,128]{2,1,0:T(8,128)(2,1)S(1)} collective-permute-done((bf16[8,32,128]{2,1,0:T(8,128)(2,1)S(1)}, bf16[8,32,128]{2,1,0:T(8,128)(2,1)S(1)}, u32[]{:S(2)}, u32[]{:S(2)}) %collective-permute-start.1) | collective-permute-done | bytes 65568 | tf_op jit(solution)/shard_map/ppermute | solution.py:504
  39.1 0.2 collective-permute-done.2.refs_5_
  39.4 0.0 copy-done.6
  39.4 2.3 %shard_map.148 = (bf16[288,128]{1,0:T(8,128)(2,1)S(1)}, bf16[8,96,128]{2,1,0:T(8,128)(2,1)}) custom-call(s32[2]{0:T(128)S(1)} %pad_add_fusion.refs_6_.refs_0_, f32[8,128]{1,0:T(8,128)S(1)} %get-tuple-element.31.refs_1_, bf16[8,32,128]{2,1,0:T(8,128)(2,1)S(1)} %get-tuple-element.32.refs_2_, bf16[8,32,128]{2,1,0:T(8,128)(2,1)S(1)} %collective-permute-done.refs_3_, ...), custom_call_target="tpu_custom_call" | custom-call | tf_op jit(solution)/shard_map/pallas_call | solution.py:433
  41.7 1.6 %collective-permute-start.10 = (bf16[288,128]{1,0:T(8,128)(2,1)S(1)}, bf16[288,128]{1,0:T(8,128)(2,1)S(1)}, u32[]{:S(2)}, u32[]{:S(2)}) collective-permute-start(bf16[288,128]{1,0:T(8,128)(2,1)S(1)} %get-tuple-element.38.refs_0_), channel_id=1, source_target_pairs={{0,8},{8,16},{16,24},{24,0},{1,9},{9,17},{17,25},{25,1},{2,10},{10... | collective-permute-start | bytes 221192 | tf_op jit(solution)/shard_map/ppermute | solution.py:504
  43.3 1.6 %collective-permute-start.11 = (bf16[288,128]{1,0:T(8,128)(2,1)S(1)}, bf16[288,128]{1,0:T(8,128)(2,1)S(1)}, u32[]{:S(2)}, u32[]{:S(2)}) collective-permute-start(bf16[288,128]{1,0:T(8,128)(2,1)S(1)} %get-tuple-element.38.refs_0_), channel_id=1, source_target_pairs={{0,16},{8,24},{16,0},{24,8},{1,17},{9,25},{17,1},{25,9},{2,18},{10... | collective-permute-start | bytes 221192 | tf_op jit(solution)/shard_map/ppermute | solution.py:504
  44.9 0.9 %collective-permute-start.12 = (bf16[288,128]{1,0:T(8,128)(2,1)S(1)}, bf16[288,128]{1,0:T(8,128)(2,1)S(1)}, u32[]{:S(2)}, u32[]{:S(2)}) collective-permute-start(bf16[288,128]{1,0:T(8,128)(2,1)S(1)} %get-tuple-element.38.refs_0_), channel_id=1, source_target_pairs={{0,24},{8,0},{16,8},{24,16},{1,25},{9,1},{17,9},{25,17},{2,26},{10... | collective-permute-start | bytes 221192 | tf_op jit(solution)/shard_map/ppermute | solution.py:504
  45.7 3.4 %all-to-all-start.1 = ((bf16[8,96,128]{2,1,0:T(8,128)(2,1)}), bf16[8,96,128]{2,1,0:T(8,128)(2,1)S(1)}, u32[]{:S(2)}, u32[]{:S(2)}) async-start(bf16[8,96,128]{2,1,0:T(8,128)(2,1)} %get-tuple-element.37), calls=%async_computation.1 | async-start | bytes 393216 | tf_op jit(solution)/shard_map/all_to_all | solution.py:521
  49.1 0.0 collective-permute-done.10.refs_1_
  49.1 1.5 %collective-permute-done.11.refs_2_ = bf16[288,128]{1,0:T(8,128)(2,1)S(1)} collective-permute-done((bf16[288,128]{1,0:T(8,128)(2,1)S(1)}, bf16[288,128]{1,0:T(8,128)(2,1)S(1)}, u32[]{:S(2)}, u32[]{:S(2)}) %collective-permute-start.11) | collective-permute-done | bytes 73760 | tf_op jit(solution)/shard_map/ppermute | solution.py:504
  50.6 0.0 collective-permute-done.12.refs_3_
  50.6 1.1 %collective-permute-start.14 = (bf16[288,128]{1,0:T(8,128)(2,1)S(1)}, bf16[288,128]{1,0:T(8,128)(2,1)S(1)}, u32[]{:S(2)}, u32[]{:S(2)}) collective-permute-start(bf16[288,128]{1,0:T(8,128)(2,1)S(1)} %shard_map.150.refs_1_), channel_id=1, source_target_pairs={{0,2},{1,3},{2,0},{3,1},{4,6},{5,7},{6,4},{7,5},{8,10},{9,11},{10,... | collective-permute-start | bytes 221192 | tf_op jit(solution)/shard_map/ppermute | solution.py:408
  51.8 1.5 %collective-permute-start.16 = (bf16[288,128]{1,0:T(8,128)(2,1)S(1)}, bf16[288,128]{1,0:T(8,128)(2,1)S(1)}, u32[]{:S(2)}, u32[]{:S(2)}) collective-permute-start(bf16[288,128]{1,0:T(8,128)(2,1)S(1)} %shard_map.150.refs_1_), channel_id=1, source_target_pairs={{0,4},{1,5},{2,6},{3,7},{4,0},{5,1},{6,2},{7,3},{8,12},{9,13},{10,... | collective-permute-start | bytes 221192 | tf_op jit(solution)/shard_map/ppermute | solution.py:408
  53.3 0.9 %collective-permute-start.18 = (bf16[288,128]{1,0:T(8,128)(2,1)S(1)}, bf16[288,128]{1,0:T(8,128)(2,1)S(1)}, u32[]{:S(2)}, u32[]{:S(2)}) collective-permute-start(bf16[288,128]{1,0:T(8,128)(2,1)S(1)} %shard_map.150.refs_1_), channel_id=1, source_target_pairs={{0,6},{1,7},{2,4},{3,5},{4,2},{5,3},{6,0},{7,1},{8,14},{9,15},{10,... | collective-permute-start | bytes 221192 | tf_op jit(solution)/shard_map/ppermute | solution.py:408
  54.2 0.0 collective-permute-start.13
  54.2 2.2 %collective-permute-done.14.refs_3_ = bf16[288,128]{1,0:T(8,128)(2,1)S(1)} collective-permute-done((bf16[288,128]{1,0:T(8,128)(2,1)S(1)}, bf16[288,128]{1,0:T(8,128)(2,1)S(1)}, u32[]{:S(2)}, u32[]{:S(2)}) %collective-permute-start.14) | collective-permute-done | bytes 73760 | tf_op jit(solution)/shard_map/ppermute | solution.py:408
  56.4 0.0 collective-permute-start.15
  56.4 0.0 collective-permute-done.16.refs_5_
  56.4 0.5 collective-permute-start.17
  56.9 1.6 %collective-permute-done.18.refs_7_ = bf16[288,128]{1,0:T(8,128)(2,1)S(1)} collective-permute-done((bf16[288,128]{1,0:T(8,128)(2,1)S(1)}, bf16[288,128]{1,0:T(8,128)(2,1)S(1)}, u32[]{:S(2)}, u32[]{:S(2)}) %collective-permute-start.18) | collective-permute-done | bytes 73760 | tf_op jit(solution)/shard_map/ppermute | solution.py:408
  58.5 0.0 collective-permute-start.19
  58.5 1.8 %shard_map.152 = (f32[8,4096]{1,0:T(8,128)}, f32[8,4096]{1,0:T(8,128)}) custom-call(f32[256,256]{1,0:T(8,128)S(1)} %get-tuple-element.42.refs_0_, f32[256,256]{1,0:T(8,128)S(1)} %get-tuple-element.43.refs_1_, bf16[3072,256]{1,0:T(8,128)(2,1)S(1)} %get-tuple-element.29.refs_4_.refs_2_, f32[256,256]{1,0:T(8,128)S(1)} %get-tuple-element.30.refs_5_.refs_3_), custom_call_target="tpu_custom_call" | custom-call | tf_op jit(solution)/shard_map/pallas_call | solution.py:433
  60.3 0.0 all-to-all-done.1.refs_1_
  60.3 0.0 copy-done.1
  60.3 0.7 %copy-done.7 = s32[1,128]{1,0:T(1,128)S(1)} copy-done((s32[1,128]{1,0:T(1,128)S(1)}, s32[1,128]{1,0:T(1,128)}, u32[]{:S(2)}) %copy-start.7) | copy-done | bytes 536
  61.0 1.6 %shard_map.149 = bf16[256,128]{1,0:T(8,128)(2,1)} custom-call(s32[2]{0:T(128)S(1)} %pad_add_fusion.refs_6_.refs_0_, bf16[8,96,128]{2,1,0:T(8,128)(2,1)S(1)} %all-to-all-done.1.refs_1_, bf16[768,256]{1,0:T(8,128)(2,1)S(1)} %copy-done.1, s32[1,128]{1,0:T(1,128)S(1)} %copy-done.7), custom_call_target="tpu_custom_call" | custom-call | tf_op jit(solution)/shard_map/pallas_call | solution.py:433
  62.6 0.0 collective-permute-done.13.refs_2_
  62.6 0.0 collective-permute-done.15.refs_4_
  62.6 0.0 collective-permute-done.17.refs_6_
  62.6 0.0 collective-permute-done.19.refs_8_
  62.6 1.7 %shard_map.151 = (f32[768,256]{1,0:T(8,128)}, f32[256,256]{1,0:T(8,128)}, f32[3,768]{1,0:T(4,128)}) custom-call(s32[2]{0:T(128)S(1)} %pad_add_fusion.refs_6_.refs_0_, bf16[288,128]{1,0:T(8,128)(2,1)S(1)} %shard_map.150.refs_1_, bf16[288,128]{1,0:T(8,128)(2,1)S(1)} %collective-permute-done.13.refs_2_, bf16[288,128]{1,0:T(8,128)(2,1)S(1)} %collective-permute-done.14.refs_3_, ...), custom_call_target="tpu_custom_call" | custom-call | tf_op jit(solution)/shard_map/pallas_call | solution.py:433
  (8 shorter events, 0.1 us)
Async XLA Ops:
  0.6 18.4 %copy-start = (f32[768,3]{0,1:T(4,128)S(1)}, f32[768,3]{0,1:T(4,128)}, u32[]{:S(2)}) copy-start(f32[768,3]{0,1:T(4,128)} %param.14) | copy-start | bytes 27652
  3.0 22.2 %all-to-all-start = ((bf16[32,32,128]{2,1,0:T(8,128)(2,1)}), bf16[32,32,128]{2,1,0:T(8,128)(2,1)S(1)}, u32[]{:S(2)}, u32[]{:S(2)}) async-start(bf16[32,32,128]{2,1,0:T(8,128)(2,1)} %get-tuple-element.26), calls=%async_computation | async-start | bytes 524288 | tf_op jit(solution)/shard_map/all_to_all | solution.py:454
  10.3 8.7 %collective-permute-start.4 = (bf16[512,128]{1,0:T(8,128)(2,1)}, bf16[512,128]{1,0:T(8,128)(2,1)S(1)}, u32[]{:S(2)}, u32[]{:S(2)}) collective-permute-start(bf16[512,128]{1,0:T(8,128)(2,1)} %get-tuple-element.36.refs_6_), channel_id=1, source_target_pairs={{0,2},{1,3},{2,0},{3,1},{4,6},{5,7},{6,4},{7,5},{8,10},{9,11},{10,... | collective-permute-start | bytes 393224 | tf_op jit(solution)/shard_map/ppermute | solution.py:408
  12.1 12.3 %collective-permute-start.6 = (bf16[512,128]{1,0:T(8,128)(2,1)}, bf16[512,128]{1,0:T(8,128)(2,1)}, u32[]{:S(2)}, u32[]{:S(2)}) collective-permute-start(bf16[512,128]{1,0:T(8,128)(2,1)} %get-tuple-element.36.refs_6_), channel_id=1, source_target_pairs={{0,4},{1,5},{2,6},{3,7},{4,0},{5,1},{6,2},{7,3},{8,12},{9,13},{10,... | collective-permute-start | bytes 393224 | tf_op jit(solution)/shard_map/ppermute | solution.py:408
  13.6 11.4 %collective-permute-start.8 = (bf16[512,128]{1,0:T(8,128)(2,1)}, bf16[512,128]{1,0:T(8,128)(2,1)}, u32[]{:S(2)}, u32[]{:S(2)}) collective-permute-start(bf16[512,128]{1,0:T(8,128)(2,1)} %get-tuple-element.36.refs_6_), channel_id=1, source_target_pairs={{0,6},{1,7},{2,4},{3,5},{4,2},{5,3},{6,0},{7,1},{8,14},{9,15},{10,... | collective-permute-start | bytes 393224 | tf_op jit(solution)/shard_map/ppermute | solution.py:408
  13.9 17.7 %collective-permute-start.3 = (bf16[512,128]{1,0:T(8,128)(2,1)}, bf16[512,128]{1,0:T(8,128)(2,1)}, u32[]{:S(2)}, u32[]{:S(2)}) collective-permute-start(bf16[512,128]{1,0:T(8,128)(2,1)} %get-tuple-element.36.refs_6_), channel_id=1, source_target_pairs={{0,1},{1,0},{2,3},{3,2},{4,5},{5,4},{6,7},{7,6},{8,9},{9,8},{10,11... | collective-permute-start | bytes 393224 | tf_op jit(solution)/shard_map/ppermute | solution.py:408
  19.0 15.0 %collective-permute-start.5 = (bf16[512,128]{1,0:T(8,128)(2,1)S(1)}, bf16[512,128]{1,0:T(8,128)(2,1)}, u32[]{:S(2)}, u32[]{:S(2)}) collective-permute-start(bf16[512,128]{1,0:T(8,128)(2,1)S(1)} %collective-permute-done.4.refs_8_), channel_id=1, source_target_pairs={{0,1},{1,0},{2,3},{3,2},{4,5},{5,4},{6,7},{7,6},{8,9},{9,8},{10,11... | collective-permute-start | bytes 393224 | tf_op jit(solution)/shard_map/ppermute | solution.py:408
  19.2 1.4 %copy-start.2 = (bf16[3072,256]{1,0:T(8,128)(2,1)S(1)}, bf16[3072,256]{1,0:T(8,128)(2,1)}, u32[]{:S(2)}) copy-start(bf16[3072,256]{1,0:T(8,128)(2,1)} %constant.18.clone.table) | copy-start | bytes 4718596
  20.6 0.9 %copy-start.3 = (f32[256,256]{1,0:T(8,128)S(1)}, f32[256,256]{1,0:T(8,128)}, u32[]{:S(2)}) copy-start(f32[256,256]{1,0:T(8,128)} %constant.19.clone.twist) | copy-start | bytes 786436
  21.5 0.9 %copy-start.4 = (f32[8,4096]{1,0:T(8,128)S(1)}, f32[8,4096]{1,0:T(8,128)}, u32[]{:S(2)}) copy-start(f32[8,4096]{1,0:T(8,128)} %filter_one.1) | copy-start | bytes 393220
  22.4 0.9 %copy-start.5 = (f32[8,4096]{1,0:T(8,128)S(1)}, f32[8,4096]{1,0:T(8,128)}, u32[]{:S(2)}) copy-start(f32[8,4096]{1,0:T(8,128)} %filter_two.1) | copy-start | bytes 393220
  24.4 15.0 %copy-start.6 = (bf16[512,128]{1,0:T(8,128)(2,1)S(1)}, bf16[512,128]{1,0:T(8,128)(2,1)}, u32[]{:S(2)}) copy-start(bf16[512,128]{1,0:T(8,128)(2,1)} %get-tuple-element.36.refs_6_) | copy-start | bytes 393220
  24.4 11.0 %collective-permute-start.7 = (bf16[512,128]{1,0:T(8,128)(2,1)}, bf16[512,128]{1,0:T(8,128)(2,1)}, u32[]{:S(2)}, u32[]{:S(2)}) collective-permute-start(bf16[512,128]{1,0:T(8,128)(2,1)} %collective-permute-done.6.refs_10_), channel_id=1, source_target_pairs={{0,1},{1,0},{2,3},{3,2},{4,5},{5,4},{6,7},{7,6},{8,9},{9,8},{10,11... | collective-permute-start | bytes 393224 | tf_op jit(solution)/shard_map/ppermute | solution.py:408
  25.0 10.4 %collective-permute-start.9 = (bf16[512,128]{1,0:T(8,128)(2,1)}, bf16[512,128]{1,0:T(8,128)(2,1)}, u32[]{:S(2)}, u32[]{:S(2)}) collective-permute-start(bf16[512,128]{1,0:T(8,128)(2,1)} %collective-permute-done.8.refs_12_), channel_id=1, source_target_pairs={{0,1},{1,0},{2,3},{3,2},{4,5},{5,4},{6,7},{7,6},{8,9},{9,8},{10,11... | collective-permute-start | bytes 393224 | tf_op jit(solution)/shard_map/ppermute | solution.py:408
  30.0 6.5 %collective-permute-start = (bf16[8,32,128]{2,1,0:T(8,128)(2,1)S(1)}, bf16[8,32,128]{2,1,0:T(8,128)(2,1)S(1)}, u32[]{:S(2)}, u32[]{:S(2)}) collective-permute-start(bf16[8,32,128]{2,1,0:T(8,128)(2,1)S(1)} %get-tuple-element.33), channel_id=1, source_target_pairs={{0,8},{8,16},{16,24},{24,0},{1,9},{9,17},{17,25},{25,1},{2,10},{10... | collective-permute-start | bytes 196616 | tf_op jit(solution)/shard_map/ppermute | solution.py:504
  31.5 7.6 %collective-permute-start.1 = (bf16[8,32,128]{2,1,0:T(8,128)(2,1)S(1)}, bf16[8,32,128]{2,1,0:T(8,128)(2,1)S(1)}, u32[]{:S(2)}, u32[]{:S(2)}) collective-permute-start(bf16[8,32,128]{2,1,0:T(8,128)(2,1)S(1)} %get-tuple-element.34), channel_id=1, source_target_pairs={{0,16},{8,24},{16,0},{24,8},{1,17},{9,25},{17,1},{25,9},{2,18},{10... | collective-permute-start | bytes 196616 | tf_op jit(solution)/shard_map/ppermute | solution.py:504
  34.0 5.4 %collective-permute-start.2 = (bf16[8,32,128]{2,1,0:T(8,128)(2,1)S(1)}, bf16[8,32,128]{2,1,0:T(8,128)(2,1)S(1)}, u32[]{:S(2)}, u32[]{:S(2)}) collective-permute-start(bf16[8,32,128]{2,1,0:T(8,128)(2,1)S(1)} %get-tuple-element.35), channel_id=1, source_target_pairs={{0,24},{8,0},{16,8},{24,16},{1,25},{9,1},{17,9},{25,17},{2,26},{10... | collective-permute-start | bytes 196616 | tf_op jit(solution)/shard_map/ppermute | solution.py:504
  41.7 18.7 %copy-start.1 = (bf16[768,256]{1,0:T(8,128)(2,1)S(1)}, bf16[768,256]{1,0:T(8,128)(2,1)}, u32[]{:S(2)}) copy-start(bf16[768,256]{1,0:T(8,128)(2,1)} %refs_2_.1) | copy-start | bytes 1179652
  41.7 7.5 %collective-permute-start.10 = (bf16[288,128]{1,0:T(8,128)(2,1)S(1)}, bf16[288,128]{1,0:T(8,128)(2,1)S(1)}, u32[]{:S(2)}, u32[]{:S(2)}) collective-permute-start(bf16[288,128]{1,0:T(8,128)(2,1)S(1)} %get-tuple-element.38.refs_0_), channel_id=1, source_target_pairs={{0,8},{8,16},{16,24},{24,0},{1,9},{9,17},{17,25},{25,1},{2,10},{10... | collective-permute-start | bytes 221192 | tf_op jit(solution)/shard_map/ppermute | solution.py:504
  43.3 7.3 %collective-permute-start.11 = (bf16[288,128]{1,0:T(8,128)(2,1)S(1)}, bf16[288,128]{1,0:T(8,128)(2,1)S(1)}, u32[]{:S(2)}, u32[]{:S(2)}) collective-permute-start(bf16[288,128]{1,0:T(8,128)(2,1)S(1)} %get-tuple-element.38.refs_0_), channel_id=1, source_target_pairs={{0,16},{8,24},{16,0},{24,8},{1,17},{9,25},{17,1},{25,9},{2,18},{10... | collective-permute-start | bytes 221192 | tf_op jit(solution)/shard_map/ppermute | solution.py:504
  44.9 5.7 %collective-permute-start.12 = (bf16[288,128]{1,0:T(8,128)(2,1)S(1)}, bf16[288,128]{1,0:T(8,128)(2,1)S(1)}, u32[]{:S(2)}, u32[]{:S(2)}) collective-permute-start(bf16[288,128]{1,0:T(8,128)(2,1)S(1)} %get-tuple-element.38.refs_0_), channel_id=1, source_target_pairs={{0,24},{8,0},{16,8},{24,16},{1,25},{9,1},{17,9},{25,17},{2,26},{10... | collective-permute-start | bytes 221192 | tf_op jit(solution)/shard_map/ppermute | solution.py:504
  45.7 14.6 %all-to-all-start.1 = ((bf16[8,96,128]{2,1,0:T(8,128)(2,1)}), bf16[8,96,128]{2,1,0:T(8,128)(2,1)S(1)}, u32[]{:S(2)}, u32[]{:S(2)}) async-start(bf16[8,96,128]{2,1,0:T(8,128)(2,1)} %get-tuple-element.37), calls=%async_computation.1 | async-start | bytes 393216 | tf_op jit(solution)/shard_map/all_to_all | solution.py:521
  50.6 5.8 %collective-permute-start.14 = (bf16[288,128]{1,0:T(8,128)(2,1)S(1)}, bf16[288,128]{1,0:T(8,128)(2,1)S(1)}, u32[]{:S(2)}, u32[]{:S(2)}) collective-permute-start(bf16[288,128]{1,0:T(8,128)(2,1)S(1)} %shard_map.150.refs_1_), channel_id=1, source_target_pairs={{0,2},{1,3},{2,0},{3,1},{4,6},{5,7},{6,4},{7,5},{8,10},{9,11},{10,... | collective-permute-start | bytes 221192 | tf_op jit(solution)/shard_map/ppermute | solution.py:408
  51.8 4.6 %collective-permute-start.16 = (bf16[288,128]{1,0:T(8,128)(2,1)S(1)}, bf16[288,128]{1,0:T(8,128)(2,1)S(1)}, u32[]{:S(2)}, u32[]{:S(2)}) collective-permute-start(bf16[288,128]{1,0:T(8,128)(2,1)S(1)} %shard_map.150.refs_1_), channel_id=1, source_target_pairs={{0,4},{1,5},{2,6},{3,7},{4,0},{5,1},{6,2},{7,3},{8,12},{9,13},{10,... | collective-permute-start | bytes 221192 | tf_op jit(solution)/shard_map/ppermute | solution.py:408
  53.3 5.3 %collective-permute-start.18 = (bf16[288,128]{1,0:T(8,128)(2,1)S(1)}, bf16[288,128]{1,0:T(8,128)(2,1)S(1)}, u32[]{:S(2)}, u32[]{:S(2)}) collective-permute-start(bf16[288,128]{1,0:T(8,128)(2,1)S(1)} %shard_map.150.refs_1_), channel_id=1, source_target_pairs={{0,6},{1,7},{2,4},{3,5},{4,2},{5,3},{6,0},{7,1},{8,14},{9,15},{10,... | collective-permute-start | bytes 221192 | tf_op jit(solution)/shard_map/ppermute | solution.py:408
  54.2 8.4 %collective-permute-start.13 = (bf16[288,128]{1,0:T(8,128)(2,1)S(1)}, bf16[288,128]{1,0:T(8,128)(2,1)S(1)}, u32[]{:S(2)}, u32[]{:S(2)}) collective-permute-start(bf16[288,128]{1,0:T(8,128)(2,1)S(1)} %shard_map.150.refs_1_), channel_id=1, source_target_pairs={{0,1},{1,0},{2,3},{3,2},{4,5},{5,4},{6,7},{7,6},{8,9},{9,8},{10,11... | collective-permute-start | bytes 221192 | tf_op jit(solution)/shard_map/ppermute | solution.py:408
  56.4 6.2 %collective-permute-start.15 = (bf16[288,128]{1,0:T(8,128)(2,1)S(1)}, bf16[288,128]{1,0:T(8,128)(2,1)S(1)}, u32[]{:S(2)}, u32[]{:S(2)}) collective-permute-start(bf16[288,128]{1,0:T(8,128)(2,1)S(1)} %collective-permute-done.14.refs_3_), channel_id=1, source_target_pairs={{0,1},{1,0},{2,3},{3,2},{4,5},{5,4},{6,7},{7,6},{8,9},{9,8},{10,11... | collective-permute-start | bytes 221192 | tf_op jit(solution)/shard_map/ppermute | solution.py:408
  56.4 6.2 %collective-permute-start.17 = (bf16[288,128]{1,0:T(8,128)(2,1)S(1)}, bf16[288,128]{1,0:T(8,128)(2,1)S(1)}, u32[]{:S(2)}, u32[]{:S(2)}) collective-permute-start(bf16[288,128]{1,0:T(8,128)(2,1)S(1)} %collective-permute-done.16.refs_5_), channel_id=1, source_target_pairs={{0,1},{1,0},{2,3},{3,2},{4,5},{5,4},{6,7},{7,6},{8,9},{9,8},{10,11... | collective-permute-start | bytes 221192 | tf_op jit(solution)/shard_map/ppermute | solution.py:408
  58.5 4.1 %collective-permute-start.19 = (bf16[288,128]{1,0:T(8,128)(2,1)S(1)}, bf16[288,128]{1,0:T(8,128)(2,1)S(1)}, u32[]{:S(2)}, u32[]{:S(2)}) collective-permute-start(bf16[288,128]{1,0:T(8,128)(2,1)S(1)} %collective-permute-done.18.refs_7_), channel_id=1, source_target_pairs={{0,1},{1,0},{2,3},{3,2},{4,5},{5,4},{6,7},{7,6},{8,9},{9,8},{10,11... | collective-permute-start | bytes 221192 | tf_op jit(solution)/shard_map/ppermute | solution.py:408
  60.3 0.7 %copy-start.7 = (s32[1,128]{1,0:T(1,128)S(1)}, s32[1,128]{1,0:T(1,128)}, u32[]{:S(2)}) copy-start(s32[1,128]{1,0:T(1,128)} %refs_3_.1) | copy-start | bytes 1540
where the time goes:
time: 64.8 us; the launch traced here: 64.3 us
  starting transfers between devices  28.5 us (44%)
  Pallas kernels  15.6 us (24%)
  waiting for transfers between devices  14.4 us (22%)
  local copies, waits for them, and re-layouts  5.01 us (8%)
  between operations  0.74 us (1%)
    pallas_call x7, Pallas kernels, call(): pl.pallas_call(kernel, out_shape=outs, compiler_params=PARAMS, **options)  13.3 us
    ppermute x6, starting transfers between devices, ahead(): return lax.ppermute(value, 'seq', pairs)  9.5 us
    ppermute x14, waiting for transfers between devices, swapped(): return lax.ppermute(value, 'fft', [(i, i ^ distance) for i in range(plane)])  8.95 us
    ppermute x14, starting transfers between devices, swapped(): return lax.ppermute(value, 'fft', [(i, i ^ distance) for i in range(plane)])  8.29 us
    all_to_all x1, starting transfers between devices, local(): lax.all_to_all(streams, AXES, split_axis=0, concat_axis=0, tiled=True)  7.3 us
    ppermute x6, waiting for transfers between devices, ahead(): return lax.ppermute(value, 'seq', pairs)  5.43 us
    unnamed x16, local copies, waits for them, and re-layouts  4.84 us
    all_to_all x1, starting transfers between devices, local(): back = lax.all_to_all(moved, 'fft', split_axis=0, concat_axis=0, tiled=True)  3.39 us
  transfers between devices with their start and end apart: 22, of which 7 were waited for; matrix products, arithmetic and copies ran while one was open for 0% of the time, Pallas kernels for 14%

commit v1 on v0

--- a/solution.py
+++ b/solution.py
@@ -23,20 +23,16 @@
 
 def make_tables(count, channels):
     length = count * LANES
-    outer = np.arange(count, dtype=np.float64)
+    outer = np.arange(count, dtype=np.float64) + 0.25
     inner = np.arange(LANES, dtype=np.float64)
-    angle = 2.0 * np.pi * (outer[:, None] + 0.25) * outer[None, :] / count
-    first = np.concatenate([np.cos(angle), -np.sin(angle)], axis=0)
-    first = np.kron(first, np.eye(channels))
+    angle = 2.0 * np.pi * outer[:, None] * outer[None, :] / count
+    first = np.kron(np.concatenate([np.cos(angle), np.sin(angle)], axis=0), np.eye(channels))
     turn = 2.0 * np.pi * (inner[:, None] * inner[None, :] % LANES) / LANES
     cos, sin = np.cos(turn), np.sin(turn)
     second = np.block([[cos, -sin], [sin, cos]])
-    twist = 2.0 * np.pi * (outer[:, None] + 0.25) * inner[None, :] / length
+    packed = [half for t in (first, second) for half in halves(t)]
+    twist = 2.0 * np.pi * outer[:, None] * (inner[None, :] - LANES / 4) / length
     twist = np.repeat(twist, channels, axis=0)
-    back = first.T / length
-    rows = count * channels
-    back = np.concatenate([back[:, :rows], back[:, rows:]], axis=0)
-    packed = [half for t in (first, back, second, second.T) for half in halves(t)]
     twist = np.concatenate([np.cos(twist), -np.sin(twist)], axis=1).astype(np.float32)
     return np.concatenate(packed, axis=0), twist
 
@@ -44,14 +40,15 @@
 def tables_of(table, twist):
     rows = twist.shape[0]
     at, found = 0, []
-    for size in (2 * rows, 2 * rows, 2 * LANES, 2 * LANES):
+    for size in (2 * rows, 2 * LANES):
         pair = []
         for half in range(2):
             pair.append(table[at : at + size])
             at += size
         found.append(tuple(pair))
-    found[1] = tuple(jnp.concatenate([t[:rows], t[rows:]], axis=1) for t in found[1])
-    return (*found, (twist[:, :LANES], twist[:, LANES:]))
+    first, second = found
+    back = tuple(jnp.concatenate([t[:rows], t[rows:]], axis=1) for t in first)
+    return first, back, second, (twist[:, :LANES], twist[:, LANES:])
 
 
 def split(value):
@@ -73,11 +70,11 @@
     stage = dot_pairs(first, split(jnp.concatenate(signals, axis=1)))
     parts = []
     for i in range(len(signals)):
-        re = stage[:rows, i * LANES : (i + 1) * LANES]
-        im = stage[rows:, i * LANES : (i + 1) * LANES]
+        cos = stage[:rows, i * LANES : (i + 1) * LANES]
+        sin = stage[rows:, i * LANES : (i + 1) * LANES]
         parts.append(
             jnp.concatenate(
-                [re * twist[0] - im * twist[1], re * twist[1] + im * twist[0]], axis=1
+                [cos * twist[0] + sin * twist[1], cos * twist[1] - sin * twist[0]], axis=1
             )
         )
     spec = dot_pairs(split(jnp.concatenate(parts, axis=0)), second)
@@ -87,29 +84,29 @@
     ]
 
 
-def backward(spectra, first_back, second_back, twist):
+def backward(spectra, back, second, twist):
     rows = spectra[0][0].shape[0]
     stacked = jnp.concatenate([jnp.concatenate(pair, axis=1) for pair in spectra], axis=0)
-    stage = dot_pairs(split(stacked), second_back)
+    stage = dot_pairs(split(stacked), second)
     parts = []
     for i in range(len(spectra)):
         re = stage[i * rows : (i + 1) * rows, :LANES]
         im = stage[i * rows : (i + 1) * rows, LANES:]
         parts.append(
             jnp.concatenate(
-                [re * twist[0] + im * twist[1], im * twist[0] - re * twist[1]], axis=0
+                [re * twist[0] - im * twist[1], re * twist[1] + im * twist[0]], axis=0
             )
         )
-    out = dot_pairs(first_back, split(jnp.concatenate(parts, axis=1)))
+    out = dot_pairs(back, split(jnp.concatenate(parts, axis=1)))
     return [out[:, i * LANES : (i + 1) * LANES] for i in range(len(spectra))]
 
 
 def times(a, b):
-    return (a[0] * b[0] - a[1] * b[1], a[0] * b[1] + a[1] * b[0])
+    return (a[0] * b[0] - a[1] * b[1], -(a[0] * b[1] + a[1] * b[0]))
 
 
 def conj_times(a, b):
-    return (a[0] * b[0] + a[1] * b[1], a[0] * b[1] - a[1] * b[0])
+    return (a[0] * b[0] + a[1] * b[1], a[1] * b[0] - a[0] * b[1])
 
 
 def one_hot(order):
@@ -188,16 +185,30 @@
 
 
 def filter_kernel(
-    filter_one, filter_two, table, twist, spec_one, spec_two, table_out, twist_out
+    length,
+    filter_one,
+    filter_two,
+    table,
+    twist,
+    own,
+    order,
+    spec_one,
+    spec_two,
+    table_out,
+    twist_out,
+    own_out,
+    order_out,
 ):
     rows = spec_one.shape[0]
     signals = [read_signal(filter_one, rows), read_signal(filter_two, rows)]
-    first, _, second, _, turns = tables_of(table, twist)
+    first, _, second, turns = tables_of(table, twist)
     one, two = forward(signals, first, second, turns)
-    spec_one[...] = jnp.concatenate(one, axis=1)
-    spec_two[...] = jnp.concatenate(two, axis=1)
+    spec_one[...] = jnp.concatenate(one, axis=1) * (1.0 / length)
+    spec_two[...] = jnp.concatenate(two, axis=1) * (1.0 / length)
     table_out[...] = table[...]
     twist_out[...] = twist[...]
+    own_out[...] = own[...]
+    order_out[...] = order[...]
 
 
 def shifted(value, steps, channels):
@@ -231,7 +242,7 @@
 ):
     rows = twist.shape[0]
     eight = taps.shape[0]
-    first, first_back, second, second_back, twist = tables_of(table, twist)
+    first, back, second, twist = tables_of(table, twist)
     if streams.shape[0] == 4 and streams.shape[1] == rows:
         pieces = [streams[s].astype(f32) for s in range(4)]
     else:
@@ -255,8 +266,8 @@
     value_spec, second_spec = forward([value, out_grad * gate_two], first, second, twist)
     first_mix, grad_first_out = backward(
         [times(h_one, value_spec), conj_times(h_two, second_spec)],
-        first_back,
-        second_back,
+        back,
+        second,
         twist,
     )
     first_spec, grad_first_spec = forward(
@@ -264,8 +275,8 @@
     )
     second_mix, grad_value = backward(
         [times(h_two, first_spec), conj_times(h_one, grad_first_spec)],
-        first_back,
-        second_back,
+        back,
+        second,
         twist,
     )
     product_one[...] = jnp.concatenate(conj_times(value_spec, grad_first_spec), axis=1)
@@ -296,12 +307,15 @@
         sent_out[step][...] = store[lax.rem(line[0] + step, lines)]
 
 
-def filter_grads_kernel(scale, product_one, product_two, table, twist, grad_one, grad_two):
-    _, first_back, _, second_back, twist = tables_of(table, twist)
+def filter_grads_kernel(
+    scale, product_one, product_two, table, twist, short, grad_one, grad_two, short_out
+):
+    _, back, second, twist = tables_of(table, twist)
     spectra = [(ref[:, :LANES], ref[:, LANES:]) for ref in (product_one, product_two)]
-    one, two = backward(spectra, first_back, second_back, twist)
+    one, two = backward(spectra, back, second, twist)
     write_signal(grad_one, one * scale)
     write_signal(grad_two, two * scale)
+    short_out[...] = short[...]
 
 
 def member(at, k):
@@ -309,7 +323,7 @@
 
 
 def weights_kernel(channels, scale, lines, *refs):
-    at, short, *refs, partial_out, moved_out = refs
+    line, place, short, *refs, partial_out, moved_out = refs
     met, pieces = refs[:lines], refs[lines:]
     plane, width = len(pieces), pieces[0].shape[0] // 2
     height = 4 * channels
@@ -318,7 +332,7 @@
     for i in range(0, plane, step):
         left = jnp.concatenate(
             [
-                jnp.concatenate([m[member(at[1], i + j)] for m in met], axis=0)
+                jnp.concatenate([m[member(place[0], i + j)] for m in met], axis=0)
                 for j in range(step)
             ],
             axis=1,
@@ -336,12 +350,12 @@
             base = k * height
             parts.append(total[base : base + 3 * channels, low:high])
             parts.append(total[base + 3 * channels : base + height, width + low : width + high])
-        owner = lax.rem(at[0] + lines - k, lines)
+        owner = lax.rem(line[0] + lines - k, lines)
         spot = pl.ds(pl.multiple_of(owner * size, size), size)
         partial_out[spot] = jnp.concatenate(parts, axis=0).astype(bf16)
     tail = jnp.concatenate([short[...]] * lines, axis=0)
     owner = lax.broadcasted_iota(jnp.int32, tail.shape, 0) // channels
-    partial_out[lines * size :] = jnp.where(owner == at[0], tail, 0.0).astype(bf16)
+    partial_out[lines * size :] = jnp.where(owner == line[0], tail, 0.0).astype(bf16)
     parts = [m[...].astype(f32)[:, : 3 * channels] for m in met]
     moved_out[...] = jnp.concatenate(parts, axis=1).astype(bf16)
 
@@ -360,12 +374,12 @@
     ).astype(bf16)
 
 
-def moved_kernel(channels, lines, at, back, w_in, order, features_out, store):
+def moved_kernel(channels, lines, line, back, w_in, order, features_out, store):
     plane, width = back.shape[0], w_in.shape[1]
     share = plane * channels
     whole = back[...].astype(f32)
     for k in range(lines):
-        owner = lax.rem(at[0] + lines - k, lines)
+        owner = lax.rem(line[0] + lines - k, lines)
         for s in range(3):
             start = (3 * k + s) * channels
             spot = pl.ds(pl.multiple_of(s * width + owner * share, share), share)
@@ -373,7 +387,7 @@
     features_out[...] = unorder(store[...].astype(bf16), w_in[...], order[...])
 
 
-def finish_kernel(channels, lines, at, *refs):
+def finish_kernel(channels, lines, place, *refs):
     *pieces, w_in_out, w_out_out, short_out, out_rows, short_rows = refs
     width = w_out_out.shape[0]
     share = width // lines
@@ -382,7 +396,7 @@
     for k, piece in enumerate(pieces):
         rows = piece[...].astype(f32)
         for i in range(lines):
-            first = pl.multiple_of(i * share + member(at[1], k) * channels, channels)
+            first = pl.multiple_of(i * share + member(place[0], k) * channels, channels)
             for h in range(width // LANES):
                 low, high = h * LANES, (h + 1) * LANES
                 base = i * size + h * height
@@ -447,10 +461,6 @@
     if not whole:
         streams = streams.reshape(4, blocks, channels, LANES).transpose(1, 0, 2, 3)
         streams = streams.reshape(blocks, 4 * channels, LANES)
-    if whole:
-        pieces = spread(own, plane)
-    else:
-        gathered = lax.all_gather(own, AXES, axis=0, tiled=False)
     arrived = lax.all_to_all(streams, AXES, split_axis=0, concat_axis=0, tiled=True)
     taps = lax.dynamic_slice_in_dim(short_taps.reshape(3, width, 3), mine * channels, channels, 1)
     taps = taps.transpose(1, 0, 2).reshape(channels, 9)
@@ -463,15 +473,25 @@
             for h in (filter_one, filter_two)
         ]
     spec = shape((rows, 2 * LANES))
-    spec_one, spec_two, table, twist = call(
-        filter_kernel,
-        (spec, spec, shape(table.shape, bf16), shape(twist.shape)),
+    spec_one, spec_two, table, twist, own, order = call(
+        lambda *refs: filter_kernel(length, *refs),
+        (
+            spec,
+            spec,
+            shape(table.shape, bf16),
+            shape(twist.shape),
+            shape(own.shape, bf16),
+            shape(sink_order.shape, jnp.int32),
+        ),
         filter_one,
         filter_two,
         table,
         twist,
-    )
-    at = jnp.stack([lax.axis_index("seq"), lax.axis_index("fft")]).astype(jnp.int32)
+        own,
+        sink_order,
+    )
+    line = lax.axis_index("seq").astype(jnp.int32).reshape(1)
+    place = lax.axis_index("fft").astype(jnp.int32).reshape(1)
     scalar = pl.BlockSpec(memory_space=pltpu.SMEM)
     held = pl.BlockSpec(memory_space=pltpu.VMEM)
     chunk = (plane, 4 * channels, LANES)
@@ -485,17 +505,18 @@
         spec_two,
         table,
         twist,
-        at,
+        line,
         in_specs=[held] * 6 + [scalar],
         scratch_shapes=[pltpu.VMEM((lines, *chunk), bf16)] if whole else [],
     )
-    grad_one, grad_two = call(
-        lambda *refs: filter_grads_kernel(scale, *refs),
-        (shape(filter_one.shape), shape(filter_two.shape)),
+    grad_one, grad_two, short = call(
+        lambda *refs: filter_grads_kernel(scale / length, *refs),
+        (shape(filter_one.shape), shape(filter_two.shape), shape(short.shape)),
         product_one,
         product_two,
         table,
         twist,
+        short,
     )
     height = channels * 4 * (width // LANES)
     if whole:
@@ -511,21 +532,22 @@
                 shape((size, LANES), bf16),
                 shape((plane, 3 * lines * channels, LANES), bf16),
             ),
-            at,
+            line,
+            place,
             short,
             *met,
-            *pieces,
-            in_specs=[scalar] + [held] * (1 + lines + plane),
+            *spread(own, plane),
+            in_specs=[scalar] * 2 + [held] * (1 + lines + plane),
         )
         partials = [partial] + [ahead(partial, k) for k in range(1, lines)]
         back = lax.all_to_all(moved, "fft", split_axis=0, concat_axis=0, tiled=True)
         grad_features = call(
             lambda *refs: moved_kernel(channels, lines, *refs),
             shape(features.shape, bf16),
-            at,
+            line,
             back,
             w_in,
-            sink_order,
+            order,
             in_specs=[scalar] + [held] * 3,
             scratch_shapes=[pltpu.VMEM((3 * width, LANES), f32)],
         )
@@ -533,12 +555,13 @@
         grad_w_in, grad_w_out, short = call(
             lambda *refs: finish_kernel(channels, lines, *refs),
             (shape((3 * width, width)), shape((width, width)), shape((3, 3 * width))),
-            at,
+            place,
             *spread(rows_sum, plane),
             in_specs=[scalar] + [held] * plane,
             scratch_shapes=[pltpu.VMEM((width, width), f32), pltpu.VMEM((width, LANES), f32)],
         )
         return (grad_features, grad_w_in, grad_w_out, short.T, grad_one, grad_two)
+    gathered = lax.all_gather(own, AXES, axis=0, tiled=False)
     sent = sent[0]
     sent = sent.reshape(4, blocks, channels, LANES)
     grad_in = jnp.einsum(

time: 64.8 us -> 59.2 us (0.914)
  Pallas kernels: 15.6 us -> 12.8 us
  local copies, waits for them, and re-layouts: 5.01 us -> 2.63 us
  starting transfers between devices: 28.5 us -> 27.3 us
  waiting for transfers between devices: 14.4 us -> 15.4 us
    pallas_call x7, Pallas kernels: 13.3 us -> 10.4 us  [call(): pl.pallas_call(kernel, out_shape=outs, compiler_params=PARAMS, **options)]
    unnamed x16, local copies, waits for them, and re-layouts: 4.84 us -> 2.46 us
    ppermute x14, waiting for transfers between devices: 8.95 us -> 10.5 us  [swapped(): return lax.ppermute(value, 'fft', [(i, i ^ distance) for i in range(plane)])]
    ppermute x14, starting transfers between devices: 8.29 us -> 7.63 us  [swapped(): return lax.ppermute(value, 'fft', [(i, i ^ distance) for i in range(plane)])]
  transfers between devices with their start and end apart: 22 -> 22, of which waited for: 7 -> 8; matrix products, arithmetic and copies ran while one was open for 0% -> 0% of each run, Pallas kernels for 14% -> 14%
where the time goes in v1:
time: 59.2 us; the launch traced here: 58.9 us
  starting transfers between devices  27.3 us (46%)
  waiting for transfers between devices  15.4 us (26%)
  Pallas kernels  12.8 us (22%)
  local copies, waits for them, and re-layouts  2.63 us (4%)
  between operations  0.78 us (1%)
    ppermute x14, waiting for transfers between devices, swapped(): return lax.ppermute(value, 'fft', [(i, i ^ distance) for i in range(plane)])  10.5 us
    pallas_call x7, Pallas kernels, call(): pl.pallas_call(kernel, out_shape=outs, compiler_params=PARAMS, **options)  10.4 us
    ppermute x6, starting transfers between devices, ahead(): return lax.ppermute(value, 'seq', pairs)  8.94 us
    ppermute x14, starting transfers between devices, swapped(): return lax.ppermute(value, 'fft', [(i, i ^ distance) for i in range(plane)])  7.63 us
    all_to_all x1, starting transfers between devices, local(): lax.all_to_all(streams, AXES, split_axis=0, concat_axis=0, tiled=True)  7.3 us
    ppermute x6, waiting for transfers between devices, ahead(): return lax.ppermute(value, 'seq', pairs)  4.91 us
    all_to_all x1, starting transfers between devices, local(): back = lax.all_to_all(moved, 'fft', split_axis=0, concat_axis=0, tiled=True)  3.39 us
    unnamed x16, local copies, waits for them, and re-layouts  2.46 us
  transfers between devices with their start and end apart: 22, of which 8 were waited for; matrix products, arithmetic and copies ran while one was open for 0% of the time, Pallas kernels for 14%

profile of v1, /device:TPU:0, one launch (start us, length us, event | category | flops | bytes accessed | tf_op | source)
XLA Modules:
  0.0 58.9 jit_solution(4154915522010091118)
XLA Ops:
  0.6 0.0 copy-start
  0.6 0.0 copy-start.2
  0.7 2.4 %shard_map.145 = (bf16[32,32,128]{2,1,0:T(8,128)(2,1)}, bf16[512,128]{1,0:T(8,128)(2,1)}) custom-call(bf16[256,128]{1,0:T(8,128)(2,1)} %features_at.1, s32[1,128]{1,0:T(1,128)} %refs_5_.1, bf16[256,128]{1,0:T(8,128)(2,1)} %cotangent_at.1, bf16[768,256]{1,0:T(8,128)(2,1)} %refs_2_.2, bf16[256,256]{1,0:T(8,128)(2,1)} %w_out_at.1), custom_call_target="tpu_custom_call" | custom-call | tf_op jit(solution)/shard_map/pallas_call | solution.py:450
  3.1 0.0 copy-start.3
  3.1 0.0 copy-start.4
  3.1 7.3 %all-to-all-start = ((bf16[32,32,128]{2,1,0:T(8,128)(2,1)}), bf16[32,32,128]{2,1,0:T(8,128)(2,1)S(1)}, u32[]{:S(2)}, u32[]{:S(2)}) async-start(bf16[32,32,128]{2,1,0:T(8,128)(2,1)} %get-tuple-element.29), calls=%async_computation | async-start | bytes 524288 | tf_op jit(solution)/shard_map/all_to_all | solution.py:464
  10.4 0.0 copy-start.7
  10.4 0.0 copy-done.2
  10.4 0.0 copy-done.3
  10.4 0.0 copy-done.4
  10.5 0.6 %copy-done.7 = s32[1,128]{1,0:T(1,128)S(1)} copy-done((s32[1,128]{1,0:T(1,128)S(1)}, s32[1,128]{1,0:T(1,128)}, u32[]{:S(2)}) %copy-start.7) | copy-done | bytes 536
  11.1 0.9 %copy-done.5 = f32[8,4096]{1,0:T(8,128)S(1)} copy-done((f32[8,4096]{1,0:T(8,128)S(1)}, f32[8,4096]{1,0:T(8,128)}, u32[]{:S(2)}) %copy-start.5) | copy-done | bytes 131096
  12.0 0.9 %copy-done.6 = bf16[512,128]{1,0:T(8,128)(2,1)S(1)} copy-done((bf16[512,128]{1,0:T(8,128)(2,1)S(1)}, bf16[512,128]{1,0:T(8,128)(2,1)}, u32[]{:S(2)}) %copy-start.6) | copy-done | bytes 131096
  12.9 1.0 %shard_map.146 = (f32[256,256]{1,0:T(8,128)S(1)}, f32[256,256]{1,0:T(8,128)S(1)}, bf16[1536,256]{1,0:T(8,128)(2,1)S(1)}, f32[256,256]{1,0:T(8,128)S(1)}, bf16[51...) custom-call(f32[8,4096]{1,0:T(8,128)S(1)} %copy-done.4, f32[8,4096]{1,0:T(8,128)S(1)} %copy-done.5, ...), custom_call_target="tpu_custom_call" | custom-call | tf_op jit(solution)/shard_map/pallas_call | solution.py:447
  13.9 2.7 %collective-permute-start.8 = (bf16[512,128]{1,0:T(8,128)(2,1)S(1)}, bf16[512,128]{1,0:T(8,128)(2,1)S(1)}, u32[]{:S(2)}, u32[]{:S(2)}) collective-permute-start(bf16[512,128]{1,0:T(8,128)(2,1)S(1)} %get-tuple-element.43.refs_7_), channel_id=1, source_target_pairs={{0,6},{1,7},{2,4},{3,5},{4,2},{5,3},{6,0},{7,1},{8,14},{9,15},{10,... | collective-permute-start | bytes 393224 | tf_op jit(solution)/shard_map/ppermute | solution.py:422
  16.6 0.6 collective-permute-start.6
  17.2 0.3 collective-permute-start.4
  17.5 0.0 collective-permute-start.3
  17.5 4.5 %collective-permute-done.8.refs_13_ = bf16[512,128]{1,0:T(8,128)(2,1)S(1)} collective-permute-done((bf16[512,128]{1,0:T(8,128)(2,1)S(1)}, bf16[512,128]{1,0:T(8,128)(2,1)S(1)}, u32[]{:S(2)}, u32[]{:S(2)}) %collective-permute-start.8) | collective-permute-done | bytes 131104 | tf_op jit(solution)/shard_map/ppermute | solution.py:422
  21.9 0.0 collective-permute-start.9
  21.9 2.3 %collective-permute-done.6.refs_11_ = bf16[512,128]{1,0:T(8,128)(2,1)S(1)} collective-permute-done((bf16[512,128]{1,0:T(8,128)(2,1)S(1)}, bf16[512,128]{1,0:T(8,128)(2,1)S(1)}, u32[]{:S(2)}, u32[]{:S(2)}) %collective-permute-start.6) | collective-permute-done | bytes 131104 | tf_op jit(solution)/shard_map/ppermute | solution.py:422
  24.2 0.0 collective-permute-start.7
  24.2 0.0 collective-permute-done.4.refs_9_
  24.2 0.5 collective-permute-start.5
  24.7 0.1 dynamic-slice_bitcast_fusion
  24.8 0.1 copy.19.refs_1_
  24.9 0.0 all-to-all-done.refs_0_
  24.9 4.2 %shard_map.147 = (f32[8,128]{1,0:T(8,128)S(1)}, f32[256,256]{1,0:T(8,128)S(1)}, f32[256,256]{1,0:T(8,128)S(1)}, bf16[8,32,128]{2,1,0:T(8,128)(2,1)S(1)}, bf16[8,...) custom-call(bf16[32,32,128]{2,1,0:T(8,128)(2,1)S(1)} %all-to-all-done.refs_0_, ...), custom_call_target="tpu_custom_call" | custom-call | tf_op jit(solution)/shard_map/pallas_call | solution.py:447
  29.1 1.5 %collective-permute-start = (bf16[8,32,128]{2,1,0:T(8,128)(2,1)S(1)}, bf16[8,32,128]{2,1,0:T(8,128)(2,1)S(1)}, u32[]{:S(2)}, u32[]{:S(2)}) collective-permute-start(bf16[8,32,128]{2,1,0:T(8,128)(2,1)S(1)} %get-tuple-element.40), channel_id=1, source_target_pairs={{0,8},{8,16},{16,24},{24,0},{1,9},{9,17},{17,25},{25,1},{2,10},{10... | collective-permute-start | bytes 196616 | tf_op jit(solution)/shard_map/ppermute | solution.py:525
  30.7 0.0 collective-permute-done.3.refs_8_
  30.7 2.1 %collective-permute-start.1 = (bf16[8,32,128]{2,1,0:T(8,128)(2,1)S(1)}, bf16[8,32,128]{2,1,0:T(8,128)(2,1)S(1)}, u32[]{:S(2)}, u32[]{:S(2)}) collective-permute-start(bf16[8,32,128]{2,1,0:T(8,128)(2,1)S(1)} %get-tuple-element.41), channel_id=1, source_target_pairs={{0,16},{8,24},{16,0},{24,8},{1,17},{9,25},{17,1},{25,9},{2,18},{10... | collective-permute-start | bytes 196616 | tf_op jit(solution)/shard_map/ppermute | solution.py:525
  32.8 0.0 collective-permute-done.9.refs_14_
  32.8 1.8 %collective-permute-start.2 = (bf16[8,32,128]{2,1,0:T(8,128)(2,1)S(1)}, bf16[8,32,128]{2,1,0:T(8,128)(2,1)S(1)}, u32[]{:S(2)}, u32[]{:S(2)}) collective-permute-start(bf16[8,32,128]{2,1,0:T(8,128)(2,1)S(1)} %get-tuple-element.42), channel_id=1, source_target_pairs={{0,24},{8,0},{16,8},{24,16},{1,25},{9,1},{17,9},{25,17},{2,26},{10... | collective-permute-start | bytes 196616 | tf_op jit(solution)/shard_map/ppermute | solution.py:525
  34.6 1.8 %shard_map.148 = (f32[8,4096]{1,0:T(8,128)}, f32[8,4096]{1,0:T(8,128)}, f32[8,128]{1,0:T(8,128)S(1)}) custom-call(f32[256,256]{1,0:T(8,128)S(1)} %get-tuple-element.35.refs_0_, f32[256,256]{1,0:T(8,128)S(1)} %get-tuple-element.36.refs_1_, bf16[1536,256]{1,0:T(8,128)(2,1)S(1)} %get-tuple-element.33.refs_4_.refs_2_, ...), custom_call_target="tpu_custom_call" | custom-call | tf_op jit(solution)/shard_map/pallas_call | solution.py:447
  36.3 0.0 collective-permute-done.7.refs_12_
  36.4 0.0 collective-permute-done.5.refs_10_
  36.4 0.0 collective-permute-done.refs_4_
  36.4 1.7 %collective-permute-done.1.refs_5_ = bf16[8,32,128]{2,1,0:T(8,128)(2,1)S(1)} collective-permute-done((bf16[8,32,128]{2,1,0:T(8,128)(2,1)S(1)}, bf16[8,32,128]{2,1,0:T(8,128)(2,1)S(1)}, u32[]{:S(2)}, u32[]{:S(2)}) %collective-permute-start.1) | collective-permute-done | bytes 65568 | tf_op jit(solution)/shard_map/ppermute | solution.py:525
  38.1 0.0 collective-permute-done.2.refs_6_
  38.1 1.1 %shard_map.149 = (bf16[288,128]{1,0:T(8,128)(2,1)S(1)}, bf16[8,96,128]{2,1,0:T(8,128)(2,1)}) custom-call(s32[1]{0:T(128)} %bitcast.refs_6_.refs_0_, s32[1]{0:T(128)} %bitcast.1.refs_1_.refs_0_, f32[8,128]{1,0:T(8,128)S(1)} %get-tuple-element.38.refs_2_, bf16[8,32,128]{2,1,0:T(8,128)(2,1)S(1)} %get-tuple-element.39.refs_3_, ...), custom_call_target="tpu_custom_call" | custom-call | tf_op jit(solution)/shard_map/pallas_call | solution.py:447
  39.1 3.0 %collective-permute-start.12 = (bf16[288,128]{1,0:T(8,128)(2,1)S(1)}, bf16[288,128]{1,0:T(8,128)(2,1)S(1)}, u32[]{:S(2)}, u32[]{:S(2)}) collective-permute-start(bf16[288,128]{1,0:T(8,128)(2,1)S(1)} %get-tuple-element.46.refs_0_), channel_id=1, source_target_pairs={{0,24},{8,0},{16,8},{24,16},{1,25},{9,1},{17,9},{25,17},{2,26},{10... | collective-permute-start | bytes 221192 | tf_op jit(solution)/shard_map/ppermute | solution.py:525
  42.1 0.2 collective-permute-start.11
  42.3 0.3 collective-permute-start.10
  42.7 3.4 %all-to-all-start.1 = ((bf16[8,96,128]{2,1,0:T(8,128)(2,1)}), bf16[8,96,128]{2,1,0:T(8,128)(2,1)S(1)}, u32[]{:S(2)}, u32[]{:S(2)}) async-start(bf16[8,96,128]{2,1,0:T(8,128)(2,1)} %get-tuple-element.44), calls=%async_computation.1 | async-start | bytes 393216 | tf_op jit(solution)/shard_map/all_to_all | solution.py:543
  46.1 0.0 collective-permute-done.12.refs_3_
  46.1 3.2 %collective-permute-done.11.refs_2_ = bf16[288,128]{1,0:T(8,128)(2,1)S(1)} collective-permute-done((bf16[288,128]{1,0:T(8,128)(2,1)S(1)}, bf16[288,128]{1,0:T(8,128)(2,1)S(1)}, u32[]{:S(2)}, u32[]{:S(2)}) %collective-permute-start.11) | collective-permute-done | bytes 73760 | tf_op jit(solution)/shard_map/ppermute | solution.py:525
  49.3 0.0 collective-permute-done.10.refs_1_
  49.3 1.6 %collective-permute-start.18 = (bf16[288,128]{1,0:T(8,128)(2,1)S(1)}, bf16[288,128]{1,0:T(8,128)(2,1)S(1)}, u32[]{:S(2)}, u32[]{:S(2)}) collective-permute-start(bf16[288,128]{1,0:T(8,128)(2,1)S(1)} %shard_map.151.refs_1_), channel_id=1, source_target_pairs={{0,6},{1,7},{2,4},{3,5},{4,2},{5,3},{6,0},{7,1},{8,14},{9,15},{10,... | collective-permute-start | bytes 221192 | tf_op jit(solution)/shard_map/ppermute | solution.py:422
  50.9 1.3 %collective-permute-start.16 = (bf16[288,128]{1,0:T(8,128)(2,1)S(1)}, bf16[288,128]{1,0:T(8,128)(2,1)S(1)}, u32[]{:S(2)}, u32[]{:S(2)}) collective-permute-start(bf16[288,128]{1,0:T(8,128)(2,1)S(1)} %shard_map.151.refs_1_), channel_id=1, source_target_pairs={{0,4},{1,5},{2,6},{3,7},{4,0},{5,1},{6,2},{7,3},{8,12},{9,13},{10,... | collective-permute-start | bytes 221192 | tf_op jit(solution)/shard_map/ppermute | solution.py:422
  52.2 0.7 %collective-permute-start.14 = (bf16[288,128]{1,0:T(8,128)(2,1)S(1)}, bf16[288,128]{1,0:T(8,128)(2,1)S(1)}, u32[]{:S(2)}, u32[]{:S(2)}) collective-permute-start(bf16[288,128]{1,0:T(8,128)(2,1)S(1)} %shard_map.151.refs_1_), channel_id=1, source_target_pairs={{0,2},{1,3},{2,0},{3,1},{4,6},{5,7},{6,4},{7,5},{8,10},{9,11},{10,... | collective-permute-start | bytes 221192 | tf_op jit(solution)/shard_map/ppermute | solution.py:422
  52.9 0.0 collective-permute-start.13
  52.9 1.9 %collective-permute-done.18.refs_7_ = bf16[288,128]{1,0:T(8,128)(2,1)S(1)} collective-permute-done((bf16[288,128]{1,0:T(8,128)(2,1)S(1)}, bf16[288,128]{1,0:T(8,128)(2,1)S(1)}, u32[]{:S(2)}, u32[]{:S(2)}) %collective-permute-start.18) | collective-permute-done | bytes 73760 | tf_op jit(solution)/shard_map/ppermute | solution.py:422
  54.8 0.0 collective-permute-start.19
  54.8 0.8 %collective-permute-done.16.refs_5_ = bf16[288,128]{1,0:T(8,128)(2,1)S(1)} collective-permute-done((bf16[288,128]{1,0:T(8,128)(2,1)S(1)}, bf16[288,128]{1,0:T(8,128)(2,1)S(1)}, u32[]{:S(2)}, u32[]{:S(2)}) %collective-permute-start.16) | collective-permute-done | bytes 73760 | tf_op jit(solution)/shard_map/ppermute | solution.py:422
  55.5 0.0 collective-permute-start.17
  55.5 1.0 %collective-permute-done.14.refs_3_ = bf16[288,128]{1,0:T(8,128)(2,1)S(1)} collective-permute-done((bf16[288,128]{1,0:T(8,128)(2,1)S(1)}, bf16[288,128]{1,0:T(8,128)(2,1)S(1)}, u32[]{:S(2)}, u32[]{:S(2)}) %collective-permute-start.14) | collective-permute-done | bytes 73760 | tf_op jit(solution)/shard_map/ppermute | solution.py:422
  56.5 0.0 collective-permute-start.15
  56.5 0.0 all-to-all-done.1.refs_1_
  56.5 1.1 %shard_map.150 = bf16[256,128]{1,0:T(8,128)(2,1)} custom-call(s32[1]{0:T(128)} %bitcast.refs_6_.refs_0_, bf16[8,96,128]{2,1,0:T(8,128)(2,1)S(1)} %all-to-all-done.1.refs_1_, bf16[768,256]{1,0:T(8,128)(2,1)S(1)} %copy-done.1, s32[1,128]{1,0:T(1,128)S(1)} %get-tuple-element.45.refs_3_), custom_call_target="tpu_custom_call" | custom-call | tf_op jit(solution)/shard_map/pallas_call | solution.py:447
  57.6 0.0 collective-permute-done.13.refs_2_
  57.6 0.0 collective-permute-done.19.refs_8_
  57.6 0.0 collective-permute-done.17.refs_6_
  57.6 0.1 collective-permute-done.15.refs_4_
  57.8 1.1 %shard_map.152 = (f32[768,256]{1,0:T(8,128)}, f32[256,256]{1,0:T(8,128)}, f32[3,768]{1,0:T(4,128)}) custom-call(s32[1]{0:T(128)} %bitcast.1.refs_1_.refs_0_, bf16[288,128]{1,0:T(8,128)(2,1)S(1)} %shard_map.151.refs_1_, bf16[288,128]{1,0:T(8,128)(2,1)S(1)} %collective-permute-done.13.refs_2_, bf16[288,128]{1,0:T(8,128)(2,1)S(1)} %collective-permute-done.14.refs_3_, ...), custom_call_target="tpu_custom_call" | custom-call | tf_op jit(solution)/shard_map/pallas_call | solution.py:447
  (7 shorter events, 0.1 us)
Async XLA Ops:
  0.6 24.1 %copy-start = (f32[768,3]{0,1:T(4,128)S(1)}, f32[768,3]{0,1:T(4,128)}, u32[]{:S(2)}) copy-start(f32[768,3]{0,1:T(4,128)} %param.14) | copy-start | bytes 27652
  0.6 9.8 %copy-start.2 = (bf16[1536,256]{1,0:T(8,128)(2,1)S(1)}, bf16[1536,256]{1,0:T(8,128)(2,1)}, u32[]{:S(2)}) copy-start(bf16[1536,256]{1,0:T(8,128)(2,1)} %constant.18.clone.refs_2_) | copy-start | bytes 2359300
  3.1 7.4 %copy-start.3 = (f32[256,256]{1,0:T(8,128)S(1)}, f32[256,256]{1,0:T(8,128)}, u32[]{:S(2)}) copy-start(f32[256,256]{1,0:T(8,128)} %constant.19.clone.refs_3_) | copy-start | bytes 786436
  3.1 7.4 %copy-start.4 = (f32[8,4096]{1,0:T(8,128)S(1)}, f32[8,4096]{1,0:T(8,128)}, u32[]{:S(2)}) copy-start(f32[8,4096]{1,0:T(8,128)} %refs_0_.1) | copy-start | bytes 393220
  3.1 21.8 %all-to-all-start = ((bf16[32,32,128]{2,1,0:T(8,128)(2,1)}), bf16[32,32,128]{2,1,0:T(8,128)(2,1)S(1)}, u32[]{:S(2)}, u32[]{:S(2)}) async-start(bf16[32,32,128]{2,1,0:T(8,128)(2,1)} %get-tuple-element.29), calls=%async_computation | async-start | bytes 524288 | tf_op jit(solution)/shard_map/all_to_all | solution.py:464
  10.4 0.7 %copy-start.7 = (s32[1,128]{1,0:T(1,128)S(1)}, s32[1,128]{1,0:T(1,128)}, u32[]{:S(2)}) copy-start(s32[1,128]{1,0:T(1,128)} %refs_5_.1) | copy-start | bytes 1540
  11.1 0.9 %copy-start.5 = (f32[8,4096]{1,0:T(8,128)S(1)}, f32[8,4096]{1,0:T(8,128)}, u32[]{:S(2)}) copy-start(f32[8,4096]{1,0:T(8,128)} %refs_1_.1) | copy-start | bytes 393220
  12.0 0.9 %copy-start.6 = (bf16[512,128]{1,0:T(8,128)(2,1)S(1)}, bf16[512,128]{1,0:T(8,128)(2,1)}, u32[]{:S(2)}) copy-start(bf16[512,128]{1,0:T(8,128)(2,1)} %get-tuple-element.30.refs_4_) | copy-start | bytes 393220
  13.9 8.0 %collective-permute-start.8 = (bf16[512,128]{1,0:T(8,128)(2,1)S(1)}, bf16[512,128]{1,0:T(8,128)(2,1)S(1)}, u32[]{:S(2)}, u32[]{:S(2)}) collective-permute-start(bf16[512,128]{1,0:T(8,128)(2,1)S(1)} %get-tuple-element.43.refs_7_), channel_id=1, source_target_pairs={{0,6},{1,7},{2,4},{3,5},{4,2},{5,3},{6,0},{7,1},{8,14},{9,15},{10,... | collective-permute-start | bytes 393224 | tf_op jit(solution)/shard_map/ppermute | solution.py:422
  16.6 7.6 %collective-permute-start.6 = (bf16[512,128]{1,0:T(8,128)(2,1)S(1)}, bf16[512,128]{1,0:T(8,128)(2,1)S(1)}, u32[]{:S(2)}, u32[]{:S(2)}) collective-permute-start(bf16[512,128]{1,0:T(8,128)(2,1)S(1)} %get-tuple-element.43.refs_7_), channel_id=1, source_target_pairs={{0,4},{1,5},{2,6},{3,7},{4,0},{5,1},{6,2},{7,3},{8,12},{9,13},{10,... | collective-permute-start | bytes 393224 | tf_op jit(solution)/shard_map/ppermute | solution.py:422
  17.2 7.0 %collective-permute-start.4 = (bf16[512,128]{1,0:T(8,128)(2,1)S(1)}, bf16[512,128]{1,0:T(8,128)(2,1)S(1)}, u32[]{:S(2)}, u32[]{:S(2)}) collective-permute-start(bf16[512,128]{1,0:T(8,128)(2,1)S(1)} %get-tuple-element.43.refs_7_), channel_id=1, source_target_pairs={{0,2},{1,3},{2,0},{3,1},{4,6},{5,7},{6,4},{7,5},{8,10},{9,11},{10,... | collective-permute-start | bytes 393224 | tf_op jit(solution)/shard_map/ppermute | solution.py:422
  17.5 13.2 %collective-permute-start.3 = (bf16[512,128]{1,0:T(8,128)(2,1)S(1)}, bf16[512,128]{1,0:T(8,128)(2,1)S(1)}, u32[]{:S(2)}, u32[]{:S(2)}) collective-permute-start(bf16[512,128]{1,0:T(8,128)(2,1)S(1)} %get-tuple-element.43.refs_7_), channel_id=1, source_target_pairs={{0,1},{1,0},{2,3},{3,2},{4,5},{5,4},{6,7},{7,6},{8,9},{9,8},{10,11... | collective-permute-start | bytes 393224 | tf_op jit(solution)/shard_map/ppermute | solution.py:422
  21.9 10.8 %collective-permute-start.9 = (bf16[512,128]{1,0:T(8,128)(2,1)S(1)}, bf16[512,128]{1,0:T(8,128)(2,1)S(1)}, u32[]{:S(2)}, u32[]{:S(2)}) collective-permute-start(bf16[512,128]{1,0:T(8,128)(2,1)S(1)} %collective-permute-done.8.refs_13_), channel_id=1, source_target_pairs={{0,1},{1,0},{2,3},{3,2},{4,5},{5,4},{6,7},{7,6},{8,9},{9,8},{10,11... | collective-permute-start | bytes 393224 | tf_op jit(solution)/shard_map/ppermute | solution.py:422
  24.2 12.1 %collective-permute-start.7 = (bf16[512,128]{1,0:T(8,128)(2,1)S(1)}, bf16[512,128]{1,0:T(8,128)(2,1)S(1)}, u32[]{:S(2)}, u32[]{:S(2)}) collective-permute-start(bf16[512,128]{1,0:T(8,128)(2,1)S(1)} %collective-permute-done.6.refs_11_), channel_id=1, source_target_pairs={{0,1},{1,0},{2,3},{3,2},{4,5},{5,4},{6,7},{7,6},{8,9},{9,8},{10,11... | collective-permute-start | bytes 393224 | tf_op jit(solution)/shard_map/ppermute | solution.py:422
  24.2 12.1 %collective-permute-start.5 = (bf16[512,128]{1,0:T(8,128)(2,1)S(1)}, bf16[512,128]{1,0:T(8,128)(2,1)S(1)}, u32[]{:S(2)}, u32[]{:S(2)}) collective-permute-start(bf16[512,128]{1,0:T(8,128)(2,1)S(1)} %collective-permute-done.4.refs_9_), channel_id=1, source_target_pairs={{0,1},{1,0},{2,3},{3,2},{4,5},{5,4},{6,7},{7,6},{8,9},{9,8},{10,11... | collective-permute-start | bytes 393224 | tf_op jit(solution)/shard_map/ppermute | solution.py:422
  29.1 7.2 %collective-permute-start = (bf16[8,32,128]{2,1,0:T(8,128)(2,1)S(1)}, bf16[8,32,128]{2,1,0:T(8,128)(2,1)S(1)}, u32[]{:S(2)}, u32[]{:S(2)}) collective-permute-start(bf16[8,32,128]{2,1,0:T(8,128)(2,1)S(1)} %get-tuple-element.40), channel_id=1, source_target_pairs={{0,8},{8,16},{16,24},{24,0},{1,9},{9,17},{17,25},{25,1},{2,10},{10... | collective-permute-start | bytes 196616 | tf_op jit(solution)/shard_map/ppermute | solution.py:525
  30.7 7.4 %collective-permute-start.1 = (bf16[8,32,128]{2,1,0:T(8,128)(2,1)S(1)}, bf16[8,32,128]{2,1,0:T(8,128)(2,1)S(1)}, u32[]{:S(2)}, u32[]{:S(2)}) collective-permute-start(bf16[8,32,128]{2,1,0:T(8,128)(2,1)S(1)} %get-tuple-element.41), channel_id=1, source_target_pairs={{0,16},{8,24},{16,0},{24,8},{1,17},{9,25},{17,1},{25,9},{2,18},{10... | collective-permute-start | bytes 196616 | tf_op jit(solution)/shard_map/ppermute | solution.py:525
  32.8 5.3 %collective-permute-start.2 = (bf16[8,32,128]{2,1,0:T(8,128)(2,1)S(1)}, bf16[8,32,128]{2,1,0:T(8,128)(2,1)S(1)}, u32[]{:S(2)}, u32[]{:S(2)}) collective-permute-start(bf16[8,32,128]{2,1,0:T(8,128)(2,1)S(1)} %get-tuple-element.42), channel_id=1, source_target_pairs={{0,24},{8,0},{16,8},{24,16},{1,25},{9,1},{17,9},{25,17},{2,26},{10... | collective-permute-start | bytes 196616 | tf_op jit(solution)/shard_map/ppermute | solution.py:525
  39.1 17.4 %copy-start.1 = (bf16[768,256]{1,0:T(8,128)(2,1)S(1)}, bf16[768,256]{1,0:T(8,128)(2,1)}, u32[]{:S(2)}) copy-start(bf16[768,256]{1,0:T(8,128)(2,1)} %refs_2_.2) | copy-start | bytes 1179652
  39.1 6.9 %collective-permute-start.12 = (bf16[288,128]{1,0:T(8,128)(2,1)S(1)}, bf16[288,128]{1,0:T(8,128)(2,1)S(1)}, u32[]{:S(2)}, u32[]{:S(2)}) collective-permute-start(bf16[288,128]{1,0:T(8,128)(2,1)S(1)} %get-tuple-element.46.refs_0_), channel_id=1, source_target_pairs={{0,24},{8,0},{16,8},{24,16},{1,25},{9,1},{17,9},{25,17},{2,26},{10... | collective-permute-start | bytes 221192 | tf_op jit(solution)/shard_map/ppermute | solution.py:525
  42.1 7.2 %collective-permute-start.11 = (bf16[288,128]{1,0:T(8,128)(2,1)S(1)}, bf16[288,128]{1,0:T(8,128)(2,1)S(1)}, u32[]{:S(2)}, u32[]{:S(2)}) collective-permute-start(bf16[288,128]{1,0:T(8,128)(2,1)S(1)} %get-tuple-element.46.refs_0_), channel_id=1, source_target_pairs={{0,16},{8,24},{16,0},{24,8},{1,17},{9,25},{17,1},{25,9},{2,18},{10... | collective-permute-start | bytes 221192 | tf_op jit(solution)/shard_map/ppermute | solution.py:525
  42.3 7.0 %collective-permute-start.10 = (bf16[288,128]{1,0:T(8,128)(2,1)S(1)}, bf16[288,128]{1,0:T(8,128)(2,1)S(1)}, u32[]{:S(2)}, u32[]{:S(2)}) collective-permute-start(bf16[288,128]{1,0:T(8,128)(2,1)S(1)} %get-tuple-element.46.refs_0_), channel_id=1, source_target_pairs={{0,8},{8,16},{16,24},{24,0},{1,9},{9,17},{17,25},{25,1},{2,10},{10... | collective-permute-start | bytes 221192 | tf_op jit(solution)/shard_map/ppermute | solution.py:525
  42.7 13.9 %all-to-all-start.1 = ((bf16[8,96,128]{2,1,0:T(8,128)(2,1)}), bf16[8,96,128]{2,1,0:T(8,128)(2,1)S(1)}, u32[]{:S(2)}, u32[]{:S(2)}) async-start(bf16[8,96,128]{2,1,0:T(8,128)(2,1)} %get-tuple-element.44), calls=%async_computation.1 | async-start | bytes 393216 | tf_op jit(solution)/shard_map/all_to_all | solution.py:543
  49.3 5.4 %collective-permute-start.18 = (bf16[288,128]{1,0:T(8,128)(2,1)S(1)}, bf16[288,128]{1,0:T(8,128)(2,1)S(1)}, u32[]{:S(2)}, u32[]{:S(2)}) collective-permute-start(bf16[288,128]{1,0:T(8,128)(2,1)S(1)} %shard_map.151.refs_1_), channel_id=1, source_target_pairs={{0,6},{1,7},{2,4},{3,5},{4,2},{5,3},{6,0},{7,1},{8,14},{9,15},{10,... | collective-permute-start | bytes 221192 | tf_op jit(solution)/shard_map/ppermute | solution.py:422
  50.9 4.6 %collective-permute-start.16 = (bf16[288,128]{1,0:T(8,128)(2,1)S(1)}, bf16[288,128]{1,0:T(8,128)(2,1)S(1)}, u32[]{:S(2)}, u32[]{:S(2)}) collective-permute-start(bf16[288,128]{1,0:T(8,128)(2,1)S(1)} %shard_map.151.refs_1_), channel_id=1, source_target_pairs={{0,4},{1,5},{2,6},{3,7},{4,0},{5,1},{6,2},{7,3},{8,12},{9,13},{10,... | collective-permute-start | bytes 221192 | tf_op jit(solution)/shard_map/ppermute | solution.py:422
  52.2 4.4 %collective-permute-start.14 = (bf16[288,128]{1,0:T(8,128)(2,1)S(1)}, bf16[288,128]{1,0:T(8,128)(2,1)S(1)}, u32[]{:S(2)}, u32[]{:S(2)}) collective-permute-start(bf16[288,128]{1,0:T(8,128)(2,1)S(1)} %shard_map.151.refs_1_), channel_id=1, source_target_pairs={{0,2},{1,3},{2,0},{3,1},{4,6},{5,7},{6,4},{7,5},{8,10},{9,11},{10,... | collective-permute-start | bytes 221192 | tf_op jit(solution)/shard_map/ppermute | solution.py:422
  52.9 4.7 %collective-permute-start.13 = (bf16[288,128]{1,0:T(8,128)(2,1)S(1)}, bf16[288,128]{1,0:T(8,128)(2,1)S(1)}, u32[]{:S(2)}, u32[]{:S(2)}) collective-permute-start(bf16[288,128]{1,0:T(8,128)(2,1)S(1)} %shard_map.151.refs_1_), channel_id=1, source_target_pairs={{0,1},{1,0},{2,3},{3,2},{4,5},{5,4},{6,7},{7,6},{8,9},{9,8},{10,11... | collective-permute-start | bytes 221192 | tf_op jit(solution)/shard_map/ppermute | solution.py:422
  54.8 2.9 %collective-permute-start.19 = (bf16[288,128]{1,0:T(8,128)(2,1)S(1)}, bf16[288,128]{1,0:T(8,128)(2,1)S(1)}, u32[]{:S(2)}, u32[]{:S(2)}) collective-permute-start(bf16[288,128]{1,0:T(8,128)(2,1)S(1)} %collective-permute-done.18.refs_7_), channel_id=1, source_target_pairs={{0,1},{1,0},{2,3},{3,2},{4,5},{5,4},{6,7},{7,6},{8,9},{9,8},{10,11... | collective-permute-start | bytes 221192 | tf_op jit(solution)/shard_map/ppermute | solution.py:422
  55.5 2.1 %collective-permute-start.17 = (bf16[288,128]{1,0:T(8,128)(2,1)S(1)}, bf16[288,128]{1,0:T(8,128)(2,1)S(1)}, u32[]{:S(2)}, u32[]{:S(2)}) collective-permute-start(bf16[288,128]{1,0:T(8,128)(2,1)S(1)} %collective-permute-done.16.refs_5_), channel_id=1, source_target_pairs={{0,1},{1,0},{2,3},{3,2},{4,5},{5,4},{6,7},{7,6},{8,9},{9,8},{10,11... | collective-permute-start | bytes 221192 | tf_op jit(solution)/shard_map/ppermute | solution.py:422
  56.5 1.3 %collective-permute-start.15 = (bf16[288,128]{1,0:T(8,128)(2,1)S(1)}, bf16[288,128]{1,0:T(8,128)(2,1)S(1)}, u32[]{:S(2)}, u32[]{:S(2)}) collective-permute-start(bf16[288,128]{1,0:T(8,128)(2,1)S(1)} %collective-permute-done.14.refs_3_), channel_id=1, source_target_pairs={{0,1},{1,0},{2,3},{3,2},{4,5},{5,4},{6,7},{7,6},{8,9},{9,8},{10,11... | collective-permute-start | bytes 221192 | tf_op jit(solution)/shard_map/ppermute | solution.py:422

commit v2 on v1

--- a/solution.py
+++ b/solution.py
@@ -304,7 +304,7 @@
     for i in range(lines):
         store[i] = packed[i * plane : (i + 1) * plane]
     for step in range(lines):
-        sent_out[step][...] = store[lax.rem(line[0] + step, lines)]
+        sent_out[step][...] = store[member(line[0], step)]
 
 
 def filter_grads_kernel(
@@ -350,7 +350,7 @@
             base = k * height
             parts.append(total[base : base + 3 * channels, low:high])
             parts.append(total[base + 3 * channels : base + height, width + low : width + high])
-        owner = lax.rem(line[0] + lines - k, lines)
+        owner = member(line[0], k)
         spot = pl.ds(pl.multiple_of(owner * size, size), size)
         partial_out[spot] = jnp.concatenate(parts, axis=0).astype(bf16)
     tail = jnp.concatenate([short[...]] * lines, axis=0)
@@ -379,7 +379,7 @@
     share = plane * channels
     whole = back[...].astype(f32)
     for k in range(lines):
-        owner = lax.rem(line[0] + lines - k, lines)
+        owner = member(line[0], k)
         for s in range(3):
             start = (3 * k + s) * channels
             spot = pl.ds(pl.multiple_of(s * width + owner * share, share), share)
@@ -418,13 +418,13 @@
     features_out[...] = unorder(moved[...], w_in[...], order[...])
 
 
-def swapped(value, plane, distance):
-    return lax.ppermute(value, "fft", [(i, i ^ distance) for i in range(plane)])
+def swapped(value, axis, count, distance):
+    return lax.ppermute(value, axis, [(i, i ^ distance) for i in range(count)])
 
 
 def spread(value, plane):
-    pieces = [value if k == 0 else swapped(value, plane, k) for k in range(0, plane, 2)]
-    return [piece for own in pieces for piece in (own, swapped(own, plane, 1))]
+    pieces = [value if k == 0 else swapped(value, "fft", plane, k) for k in range(0, plane, 2)]
+    return [piece for own in pieces for piece in (own, swapped(own, "fft", plane, 1))]
 
 
 def shape(dims, dtype=f32):
@@ -438,7 +438,8 @@
     channels, length = filter_one.shape
     rows = channels * blocks
     scale = 1.0 / math.sqrt(length)
-    whole = channels % 8 == 0 and plane % 2 == 0 and plane & (plane - 1) == 0
+    powers = all(n > 1 and n & (n - 1) == 0 for n in (lines, plane))
+    whole = channels % 8 == 0 and powers
     table, twist = make_tables(blocks, channels)
     eight = channels if whole else 8
     mine = lax.axis_index(AXES)
@@ -520,11 +521,7 @@
     )
     height = channels * 4 * (width // LANES)
     if whole:
-        def ahead(value, steps):
-            pairs = [(i, (i + steps) % lines) for i in range(lines)]
-            return lax.ppermute(value, "seq", pairs)
-
-        met = [sent[0]] + [ahead(sent[k], k) for k in range(1, lines)]
+        met = [sent[0]] + [swapped(sent[k], "seq", lines, k) for k in range(1, lines)]
         size = lines * height + lines * channels
         partial, moved = call(
             lambda *refs: weights_kernel(channels, scale, lines, *refs),
@@ -536,10 +533,10 @@
             place,
             short,
             *met,
-            *spread(own, plane),
+            *[own] + [swapped(own, "fft", plane, k) for k in range(1, plane)],
             in_specs=[scalar] * 2 + [held] * (1 + lines + plane),
         )
-        partials = [partial] + [ahead(partial, k) for k in range(1, lines)]
+        partials = [partial] + [swapped(partial, "seq", lines, k) for k in range(1, lines)]
         back = lax.all_to_all(moved, "fft", split_axis=0, concat_axis=0, tiled=True)
         grad_features = call(
             lambda *refs: moved_kernel(channels, lines, *refs),

time: 59.2 us -> 60.1 us (1.015)
  starting transfers between devices: 27.3 us -> 31.7 us
  waiting for transfers between devices: 15.4 us -> 11.9 us
    ppermute x20, starting transfers between devices: 16.6 us -> 21 us  [swapped(): return lax.ppermute(value, axis, [(i, i ^ distance) for i in range(count)])]
    ppermute x20, waiting for transfers between devices: 15.4 us -> 11.9 us  [swapped(): return lax.ppermute(value, axis, [(i, i ^ distance) for i in range(count)])]
  transfers between devices with their start and end apart: 22 -> 22, of which waited for: 8 -> 6; matrix products, arithmetic and copies ran while one was open for 0% -> 0% of each run, Pallas kernels for 14% -> 14%
where the time goes in v2:
time: 60.1 us; the launch traced here: 59.8 us
  starting transfers between devices  31.7 us (53%)
  Pallas kernels  12.7 us (21%)
  waiting for transfers between devices  11.9 us (20%)
  local copies, waits for them, and re-layouts  2.63 us (4%)
  between operations  0.79 us (1%)
    ppermute x20, starting transfers between devices, swapped(): return lax.ppermute(value, axis, [(i, i ^ distance) for i in range(count)])  21 us
    ppermute x20, waiting for transfers between devices, swapped(): return lax.ppermute(value, axis, [(i, i ^ distance) for i in range(count)])  11.9 us
    pallas_call x7, Pallas kernels, call(): pl.pallas_call(kernel, out_shape=outs, compiler_params=PARAMS, **options)  10.3 us
    all_to_all x1, starting transfers between devices, local(): lax.all_to_all(streams, AXES, split_axis=0, concat_axis=0, tiled=True)  7.3 us
    all_to_all x1, starting transfers between devices, local(): back = lax.all_to_all(moved, 'fft', split_axis=0, concat_axis=0, tiled=True)  3.39 us
    unnamed x16, local copies, waits for them, and re-layouts  2.46 us
    pallas_call x1, Pallas kernels, local(): pl.pallas_call(project_kernel, out_shape=(shape(dims, bf16), shape((2 * w...  2.41 us
  transfers between devices with their start and end apart: 22, of which 6 were waited for; matrix products, arithmetic and copies ran while one was open for 0% of the time, Pallas kernels for 14%

profile of v2, /device:TPU:0, one launch (start us, length us, event | category | flops | bytes accessed | tf_op | source)
XLA Modules:
  0.0 59.8 jit_solution(9518373639511135769)
XLA Ops:
  0.6 0.0 copy-start
  0.6 0.0 copy-start.2
  0.7 2.4 %shard_map.145 = (bf16[32,32,128]{2,1,0:T(8,128)(2,1)}, bf16[512,128]{1,0:T(8,128)(2,1)}) custom-call(bf16[256,128]{1,0:T(8,128)(2,1)} %features_at.1, s32[1,128]{1,0:T(1,128)} %refs_5_.1, bf16[256,128]{1,0:T(8,128)(2,1)} %cotangent_at.1, bf16[768,256]{1,0:T(8,128)(2,1)} %refs_2_.2, bf16[256,256]{1,0:T(8,128)(2,1)} %w_out_at.1), custom_call_target="tpu_custom_call" | custom-call | tf_op jit(solution)/shard_map/pallas_call | solution.py:451
  3.1 0.0 copy-start.3
  3.1 0.0 copy-start.4
  3.1 7.3 %all-to-all-start = ((bf16[32,32,128]{2,1,0:T(8,128)(2,1)}), bf16[32,32,128]{2,1,0:T(8,128)(2,1)S(1)}, u32[]{:S(2)}, u32[]{:S(2)}) async-start(bf16[32,32,128]{2,1,0:T(8,128)(2,1)} %get-tuple-element.29), calls=%async_computation | async-start | bytes 524288 | tf_op jit(solution)/shard_map/all_to_all | solution.py:465
  10.4 0.0 copy-start.7
  10.4 0.0 copy-done.2
  10.4 0.0 copy-done.3
  10.5 0.6 %copy-done.7 = s32[1,128]{1,0:T(1,128)S(1)} copy-done((s32[1,128]{1,0:T(1,128)S(1)}, s32[1,128]{1,0:T(1,128)}, u32[]{:S(2)}) %copy-start.7) | copy-done | bytes 536
  11.1 0.9 %copy-done.5 = f32[8,4096]{1,0:T(8,128)S(1)} copy-done((f32[8,4096]{1,0:T(8,128)S(1)}, f32[8,4096]{1,0:T(8,128)}, u32[]{:S(2)}) %copy-start.5) | copy-done | bytes 131096
  12.0 0.9 %copy-done.6 = bf16[512,128]{1,0:T(8,128)(2,1)S(1)} copy-done((bf16[512,128]{1,0:T(8,128)(2,1)S(1)}, bf16[512,128]{1,0:T(8,128)(2,1)}, u32[]{:S(2)}) %copy-start.6) | copy-done | bytes 131096
  12.9 1.0 %shard_map.146 = (f32[256,256]{1,0:T(8,128)S(1)}, f32[256,256]{1,0:T(8,128)S(1)}, bf16[1536,256]{1,0:T(8,128)(2,1)S(1)}, f32[256,256]{1,0:T(8,128)S(1)}, bf16[51...) custom-call(f32[8,4096]{1,0:T(8,128)S(1)} %copy-done.4, f32[8,4096]{1,0:T(8,128)S(1)} %copy-done.5, ...), custom_call_target="tpu_custom_call" | custom-call | tf_op jit(solution)/shard_map/pallas_call | solution.py:448
  13.9 2.5 %collective-permute-start.9 = (bf16[512,128]{1,0:T(8,128)(2,1)S(1)}, bf16[512,128]{1,0:T(8,128)(2,1)S(1)}, u32[]{:S(2)}, u32[]{:S(2)}) collective-permute-start(bf16[512,128]{1,0:T(8,128)(2,1)S(1)} %get-tuple-element.43.refs_7_), channel_id=1, source_target_pairs={{0,7},{1,6},{2,5},{3,4},{4,3},{5,2},{6,1},{7,0},{8,15},{9,14},{10,... | collective-permute-start | bytes 393224 | tf_op jit(solution)/shard_map/ppermute | solution.py:422
  16.4 0.4 collective-permute-start.8
  16.8 1.4 %collective-permute-start.7 = (bf16[512,128]{1,0:T(8,128)(2,1)S(1)}, bf16[512,128]{1,0:T(8,128)(2,1)S(1)}, u32[]{:S(2)}, u32[]{:S(2)}) collective-permute-start(bf16[512,128]{1,0:T(8,128)(2,1)S(1)} %get-tuple-element.43.refs_7_), channel_id=1, source_target_pairs={{0,5},{1,4},{2,7},{3,6},{4,1},{5,0},{6,3},{7,2},{8,13},{9,12},{10,... | collective-permute-start | bytes 393224 | tf_op jit(solution)/shard_map/ppermute | solution.py:422
  18.1 0.4 collective-permute-start.6
  18.5 1.4 %collective-permute-start.5 = (bf16[512,128]{1,0:T(8,128)(2,1)S(1)}, bf16[512,128]{1,0:T(8,128)(2,1)S(1)}, u32[]{:S(2)}, u32[]{:S(2)}) collective-permute-start(bf16[512,128]{1,0:T(8,128)(2,1)S(1)} %get-tuple-element.43.refs_7_), channel_id=1, source_target_pairs={{0,3},{1,2},{2,1},{3,0},{4,7},{5,6},{6,5},{7,4},{8,11},{9,10},{10,... | collective-permute-start | bytes 393224 | tf_op jit(solution)/shard_map/ppermute | solution.py:422
  19.9 1.4 %collective-permute-done.9.refs_14_ = bf16[512,128]{1,0:T(8,128)(2,1)S(1)} collective-permute-done((bf16[512,128]{1,0:T(8,128)(2,1)S(1)}, bf16[512,128]{1,0:T(8,128)(2,1)S(1)}, u32[]{:S(2)}, u32[]{:S(2)}) %collective-permute-start.9) | collective-permute-done | bytes 131104 | tf_op jit(solution)/shard_map/ppermute | solution.py:422
  21.3 1.7 %collective-permute-start.4 = (bf16[512,128]{1,0:T(8,128)(2,1)S(1)}, bf16[512,128]{1,0:T(8,128)(2,1)S(1)}, u32[]{:S(2)}, u32[]{:S(2)}) collective-permute-start(bf16[512,128]{1,0:T(8,128)(2,1)S(1)} %get-tuple-element.43.refs_7_), channel_id=1, source_target_pairs={{0,2},{1,3},{2,0},{3,1},{4,6},{5,7},{6,4},{7,5},{8,10},{9,11},{10,... | collective-permute-start | bytes 393224 | tf_op jit(solution)/shard_map/ppermute | solution.py:422
  23.0 1.6 %collective-permute-done.8.refs_13_ = bf16[512,128]{1,0:T(8,128)(2,1)S(1)} collective-permute-done((bf16[512,128]{1,0:T(8,128)(2,1)S(1)}, bf16[512,128]{1,0:T(8,128)(2,1)S(1)}, u32[]{:S(2)}, u32[]{:S(2)}) %collective-permute-start.8) | collective-permute-done | bytes 131104 | tf_op jit(solution)/shard_map/ppermute | solution.py:422
  24.7 0.0 collective-permute-start.3
  24.7 0.1 dynamic-slice_bitcast_fusion
  24.8 0.1 copy.19.refs_1_
  24.8 0.0 all-to-all-done.refs_0_
  24.9 4.2 %shard_map.147 = (f32[8,128]{1,0:T(8,128)S(1)}, f32[256,256]{1,0:T(8,128)S(1)}, f32[256,256]{1,0:T(8,128)S(1)}, bf16[8,32,128]{2,1,0:T(8,128)(2,1)S(1)}, bf16[8,...) custom-call(bf16[32,32,128]{2,1,0:T(8,128)(2,1)S(1)} %all-to-all-done.refs_0_, ...), custom_call_target="tpu_custom_call" | custom-call | tf_op jit(solution)/shard_map/pallas_call | solution.py:448
  29.1 0.0 collective-permute-done.7.refs_12_
  29.1 1.5 %collective-permute-start = (bf16[8,32,128]{2,1,0:T(8,128)(2,1)S(1)}, bf16[8,32,128]{2,1,0:T(8,128)(2,1)S(1)}, u32[]{:S(2)}, u32[]{:S(2)}) collective-permute-start(bf16[8,32,128]{2,1,0:T(8,128)(2,1)S(1)} %get-tuple-element.40), channel_id=1, source_target_pairs={{0,8},{8,0},{16,24},{24,16},{1,9},{9,1},{17,25},{25,17},{2,10},{10... | collective-permute-start | bytes 196616 | tf_op jit(solution)/shard_map/ppermute | solution.py:422
  30.6 0.0 collective-permute-done.6.refs_11_
  30.7 2.2 %collective-permute-start.1 = (bf16[8,32,128]{2,1,0:T(8,128)(2,1)S(1)}, bf16[8,32,128]{2,1,0:T(8,128)(2,1)S(1)}, u32[]{:S(2)}, u32[]{:S(2)}) collective-permute-start(bf16[8,32,128]{2,1,0:T(8,128)(2,1)S(1)} %get-tuple-element.41), channel_id=1, source_target_pairs={{0,16},{8,24},{16,0},{24,8},{1,17},{9,25},{17,1},{25,9},{2,18},{10... | collective-permute-start | bytes 196616 | tf_op jit(solution)/shard_map/ppermute | solution.py:422
  32.9 0.0 collective-permute-done.5.refs_10_
  32.9 1.1 %collective-permute-start.2 = (bf16[8,32,128]{2,1,0:T(8,128)(2,1)S(1)}, bf16[8,32,128]{2,1,0:T(8,128)(2,1)S(1)}, u32[]{:S(2)}, u32[]{:S(2)}) collective-permute-start(bf16[8,32,128]{2,1,0:T(8,128)(2,1)S(1)} %get-tuple-element.42), channel_id=1, source_target_pairs={{0,24},{8,16},{16,8},{24,0},{1,25},{9,17},{17,9},{25,1},{2,26},{10... | collective-permute-start | bytes 196616 | tf_op jit(solution)/shard_map/ppermute | solution.py:422
  34.0 1.8 %shard_map.148 = (f32[8,4096]{1,0:T(8,128)}, f32[8,4096]{1,0:T(8,128)}, f32[8,128]{1,0:T(8,128)S(1)}) custom-call(f32[256,256]{1,0:T(8,128)S(1)} %get-tuple-element.35.refs_0_, f32[256,256]{1,0:T(8,128)S(1)} %get-tuple-element.36.refs_1_, bf16[1536,256]{1,0:T(8,128)(2,1)S(1)} %get-tuple-element.33.refs_4_.refs_2_, ...), custom_call_target="tpu_custom_call" | custom-call | tf_op jit(solution)/shard_map/pallas_call | solution.py:448
  35.8 0.0 collective-permute-done.4.refs_9_
  35.8 0.0 collective-permute-done.3.refs_8_
  35.8 0.0 collective-permute-done.refs_4_
  35.8 3.3 %collective-permute-done.1.refs_5_ = bf16[8,32,128]{2,1,0:T(8,128)(2,1)S(1)} collective-permute-done((bf16[8,32,128]{2,1,0:T(8,128)(2,1)S(1)}, bf16[8,32,128]{2,1,0:T(8,128)(2,1)S(1)}, u32[]{:S(2)}, u32[]{:S(2)}) %collective-permute-start.1) | collective-permute-done | bytes 65568 | tf_op jit(solution)/shard_map/ppermute | solution.py:422
  39.1 0.0 collective-permute-done.2.refs_6_
  39.1 1.1 %shard_map.149 = (bf16[288,128]{1,0:T(8,128)(2,1)S(1)}, bf16[8,96,128]{2,1,0:T(8,128)(2,1)}) custom-call(s32[1]{0:T(128)} %bitcast.refs_6_.refs_0_, s32[1]{0:T(128)} %bitcast.1.refs_1_.refs_0_, f32[8,128]{1,0:T(8,128)S(1)} %get-tuple-element.38.refs_2_, bf16[8,32,128]{2,1,0:T(8,128)(2,1)S(1)} %get-tuple-element.39.refs_3_, ...), custom_call_target="tpu_custom_call" | custom-call | tf_op jit(solution)/shard_map/pallas_call | solution.py:448
  40.2 2.5 %collective-permute-start.12 = (bf16[288,128]{1,0:T(8,128)(2,1)S(1)}, bf16[288,128]{1,0:T(8,128)(2,1)S(1)}, u32[]{:S(2)}, u32[]{:S(2)}) collective-permute-start(bf16[288,128]{1,0:T(8,128)(2,1)S(1)} %get-tuple-element.46.refs_0_), channel_id=1, source_target_pairs={{0,24},{8,16},{16,8},{24,0},{1,25},{9,17},{17,9},{25,1},{2,26},{10... | collective-permute-start | bytes 221192 | tf_op jit(solution)/shard_map/ppermute | solution.py:422
  42.7 0.4 collective-permute-start.11
  43.1 1.4 %collective-permute-start.10 = (bf16[288,128]{1,0:T(8,128)(2,1)S(1)}, bf16[288,128]{1,0:T(8,128)(2,1)S(1)}, u32[]{:S(2)}, u32[]{:S(2)}) collective-permute-start(bf16[288,128]{1,0:T(8,128)(2,1)S(1)} %get-tuple-element.46.refs_0_), channel_id=1, source_target_pairs={{0,8},{8,0},{16,24},{24,16},{1,9},{9,1},{17,25},{25,17},{2,10},{10... | collective-permute-start | bytes 221192 | tf_op jit(solution)/shard_map/ppermute | solution.py:422
  44.6 3.4 %all-to-all-start.1 = ((bf16[8,96,128]{2,1,0:T(8,128)(2,1)}), bf16[8,96,128]{2,1,0:T(8,128)(2,1)S(1)}, u32[]{:S(2)}, u32[]{:S(2)}) async-start(bf16[8,96,128]{2,1,0:T(8,128)(2,1)} %get-tuple-element.44), calls=%async_computation.1 | async-start | bytes 393216 | tf_op jit(solution)/shard_map/all_to_all | solution.py:540
  48.0 0.0 collective-permute-done.12.refs_3_
  48.0 1.6 %collective-permute-done.11.refs_2_ = bf16[288,128]{1,0:T(8,128)(2,1)S(1)} collective-permute-done((bf16[288,128]{1,0:T(8,128)(2,1)S(1)}, bf16[288,128]{1,0:T(8,128)(2,1)S(1)}, u32[]{:S(2)}, u32[]{:S(2)}) %collective-permute-start.11) | collective-permute-done | bytes 73760 | tf_op jit(solution)/shard_map/ppermute | solution.py:422
  49.5 0.0 collective-permute-done.10.refs_1_
  49.6 2.1 %collective-permute-start.18 = (bf16[288,128]{1,0:T(8,128)(2,1)S(1)}, bf16[288,128]{1,0:T(8,128)(2,1)S(1)}, u32[]{:S(2)}, u32[]{:S(2)}) collective-permute-start(bf16[288,128]{1,0:T(8,128)(2,1)S(1)} %shard_map.151.refs_1_), channel_id=1, source_target_pairs={{0,6},{1,7},{2,4},{3,5},{4,2},{5,3},{6,0},{7,1},{8,14},{9,15},{10,... | collective-permute-start | bytes 221192 | tf_op jit(solution)/shard_map/ppermute | solution.py:422
  51.7 0.6 collective-permute-start.16
  52.2 0.9 %collective-permute-start.14 = (bf16[288,128]{1,0:T(8,128)(2,1)S(1)}, bf16[288,128]{1,0:T(8,128)(2,1)S(1)}, u32[]{:S(2)}, u32[]{:S(2)}) collective-permute-start(bf16[288,128]{1,0:T(8,128)(2,1)S(1)} %shard_map.151.refs_1_), channel_id=1, source_target_pairs={{0,2},{1,3},{2,0},{3,1},{4,6},{5,7},{6,4},{7,5},{8,10},{9,11},{10,... | collective-permute-start | bytes 221192 | tf_op jit(solution)/shard_map/ppermute | solution.py:422
  53.1 0.0 collective-permute-start.13
  53.1 3.0 %collective-permute-done.18.refs_7_ = bf16[288,128]{1,0:T(8,128)(2,1)S(1)} collective-permute-done((bf16[288,128]{1,0:T(8,128)(2,1)S(1)}, bf16[288,128]{1,0:T(8,128)(2,1)S(1)}, u32[]{:S(2)}, u32[]{:S(2)}) %collective-permute-start.18) | collective-permute-done | bytes 73760 | tf_op jit(solution)/shard_map/ppermute | solution.py:422
  56.2 0.0 collective-permute-start.19
  56.2 0.8 %collective-permute-done.16.refs_5_ = bf16[288,128]{1,0:T(8,128)(2,1)S(1)} collective-permute-done((bf16[288,128]{1,0:T(8,128)(2,1)S(1)}, bf16[288,128]{1,0:T(8,128)(2,1)S(1)}, u32[]{:S(2)}, u32[]{:S(2)}) %collective-permute-start.16) | collective-permute-done | bytes 73760 | tf_op jit(solution)/shard_map/ppermute | solution.py:422
  57.0 0.0 collective-permute-start.17
  57.0 0.0 collective-permute-done.14.refs_3_
  57.0 0.5 collective-permute-start.15
  57.6 0.0 all-to-all-done.1.refs_1_
  57.6 0.0 copy-done.1
  57.6 1.1 %shard_map.150 = bf16[256,128]{1,0:T(8,128)(2,1)} custom-call(s32[1]{0:T(128)} %bitcast.refs_6_.refs_0_, bf16[8,96,128]{2,1,0:T(8,128)(2,1)S(1)} %all-to-all-done.1.refs_1_, bf16[768,256]{1,0:T(8,128)(2,1)S(1)} %copy-done.1, s32[1,128]{1,0:T(1,128)S(1)} %get-tuple-element.45.refs_3_), custom_call_target="tpu_custom_call" | custom-call | tf_op jit(solution)/shard_map/pallas_call | solution.py:448
  58.6 0.0 collective-permute-done.13.refs_2_
  58.6 0.0 collective-permute-done.19.refs_8_
  58.6 0.0 collective-permute-done.17.refs_6_
  58.6 0.0 collective-permute-done.15.refs_4_
  58.6 1.1 %shard_map.152 = (f32[768,256]{1,0:T(8,128)}, f32[256,256]{1,0:T(8,128)}, f32[3,768]{1,0:T(4,128)}) custom-call(s32[1]{0:T(128)} %bitcast.1.refs_1_.refs_0_, bf16[288,128]{1,0:T(8,128)(2,1)S(1)} %shard_map.151.refs_1_, bf16[288,128]{1,0:T(8,128)(2,1)S(1)} %collective-permute-done.13.refs_2_, bf16[288,128]{1,0:T(8,128)(2,1)S(1)} %collective-permute-done.14.refs_3_, ...), custom_call_target="tpu_custom_call" | custom-call | tf_op jit(solution)/shard_map/pallas_call | solution.py:448
  (7 shorter events, 0.1 us)
Async XLA Ops:
  0.6 24.0 %copy-start = (f32[768,3]{0,1:T(4,128)S(1)}, f32[768,3]{0,1:T(4,128)}, u32[]{:S(2)}) copy-start(f32[768,3]{0,1:T(4,128)} %param.14) | copy-start | bytes 27652
  0.6 9.8 %copy-start.2 = (bf16[1536,256]{1,0:T(8,128)(2,1)S(1)}, bf16[1536,256]{1,0:T(8,128)(2,1)}, u32[]{:S(2)}) copy-start(bf16[1536,256]{1,0:T(8,128)(2,1)} %constant.18.clone.refs_2_) | copy-start | bytes 2359300
  3.1 7.4 %copy-start.3 = (f32[256,256]{1,0:T(8,128)S(1)}, f32[256,256]{1,0:T(8,128)}, u32[]{:S(2)}) copy-start(f32[256,256]{1,0:T(8,128)} %constant.19.clone.refs_3_) | copy-start | bytes 786436
  3.1 7.4 %copy-start.4 = (f32[8,4096]{1,0:T(8,128)S(1)}, f32[8,4096]{1,0:T(8,128)}, u32[]{:S(2)}) copy-start(f32[8,4096]{1,0:T(8,128)} %refs_0_.1) | copy-start | bytes 393220
  3.1 21.8 %all-to-all-start = ((bf16[32,32,128]{2,1,0:T(8,128)(2,1)}), bf16[32,32,128]{2,1,0:T(8,128)(2,1)S(1)}, u32[]{:S(2)}, u32[]{:S(2)}) async-start(bf16[32,32,128]{2,1,0:T(8,128)(2,1)} %get-tuple-element.29), calls=%async_computation | async-start | bytes 524288 | tf_op jit(solution)/shard_map/all_to_all | solution.py:465
  10.4 0.7 %copy-start.7 = (s32[1,128]{1,0:T(1,128)S(1)}, s32[1,128]{1,0:T(1,128)}, u32[]{:S(2)}) copy-start(s32[1,128]{1,0:T(1,128)} %refs_5_.1) | copy-start | bytes 1540
  11.1 0.9 %copy-start.5 = (f32[8,4096]{1,0:T(8,128)S(1)}, f32[8,4096]{1,0:T(8,128)}, u32[]{:S(2)}) copy-start(f32[8,4096]{1,0:T(8,128)} %refs_1_.1) | copy-start | bytes 393220
  12.0 0.9 %copy-start.6 = (bf16[512,128]{1,0:T(8,128)(2,1)S(1)}, bf16[512,128]{1,0:T(8,128)(2,1)}, u32[]{:S(2)}) copy-start(bf16[512,128]{1,0:T(8,128)(2,1)} %get-tuple-element.30.refs_4_) | copy-start | bytes 393220
  13.9 7.4 %collective-permute-start.9 = (bf16[512,128]{1,0:T(8,128)(2,1)S(1)}, bf16[512,128]{1,0:T(8,128)(2,1)S(1)}, u32[]{:S(2)}, u32[]{:S(2)}) collective-permute-start(bf16[512,128]{1,0:T(8,128)(2,1)S(1)} %get-tuple-element.43.refs_7_), channel_id=1, source_target_pairs={{0,7},{1,6},{2,5},{3,4},{4,3},{5,2},{6,1},{7,0},{8,15},{9,14},{10,... | collective-permute-start | bytes 393224 | tf_op jit(solution)/shard_map/ppermute | solution.py:422
  16.4 8.3 %collective-permute-start.8 = (bf16[512,128]{1,0:T(8,128)(2,1)S(1)}, bf16[512,128]{1,0:T(8,128)(2,1)S(1)}, u32[]{:S(2)}, u32[]{:S(2)}) collective-permute-start(bf16[512,128]{1,0:T(8,128)(2,1)S(1)} %get-tuple-element.43.refs_7_), channel_id=1, source_target_pairs={{0,6},{1,7},{2,4},{3,5},{4,2},{5,3},{6,0},{7,1},{8,14},{9,15},{10,... | collective-permute-start | bytes 393224 | tf_op jit(solution)/shard_map/ppermute | solution.py:422
  16.8 12.3 %collective-permute-start.7 = (bf16[512,128]{1,0:T(8,128)(2,1)S(1)}, bf16[512,128]{1,0:T(8,128)(2,1)S(1)}, u32[]{:S(2)}, u32[]{:S(2)}) collective-permute-start(bf16[512,128]{1,0:T(8,128)(2,1)S(1)} %get-tuple-element.43.refs_7_), channel_id=1, source_target_pairs={{0,5},{1,4},{2,7},{3,6},{4,1},{5,0},{6,3},{7,2},{8,13},{9,12},{10,... | collective-permute-start | bytes 393224 | tf_op jit(solution)/shard_map/ppermute | solution.py:422
  18.1 12.5 %collective-permute-start.6 = (bf16[512,128]{1,0:T(8,128)(2,1)S(1)}, bf16[512,128]{1,0:T(8,128)(2,1)S(1)}, u32[]{:S(2)}, u32[]{:S(2)}) collective-permute-start(bf16[512,128]{1,0:T(8,128)(2,1)S(1)} %get-tuple-element.43.refs_7_), channel_id=1, source_target_pairs={{0,4},{1,5},{2,6},{3,7},{4,0},{5,1},{6,2},{7,3},{8,12},{9,13},{10,... | collective-permute-start | bytes 393224 | tf_op jit(solution)/shard_map/ppermute | solution.py:422
  18.5 14.4 %collective-permute-start.5 = (bf16[512,128]{1,0:T(8,128)(2,1)S(1)}, bf16[512,128]{1,0:T(8,128)(2,1)S(1)}, u32[]{:S(2)}, u32[]{:S(2)}) collective-permute-start(bf16[512,128]{1,0:T(8,128)(2,1)S(1)} %get-tuple-element.43.refs_7_), channel_id=1, source_target_pairs={{0,3},{1,2},{2,1},{3,0},{4,7},{5,6},{6,5},{7,4},{8,11},{9,10},{10,... | collective-permute-start | bytes 393224 | tf_op jit(solution)/shard_map/ppermute | solution.py:422
  21.3 14.5 %collective-permute-start.4 = (bf16[512,128]{1,0:T(8,128)(2,1)S(1)}, bf16[512,128]{1,0:T(8,128)(2,1)S(1)}, u32[]{:S(2)}, u32[]{:S(2)}) collective-permute-start(bf16[512,128]{1,0:T(8,128)(2,1)S(1)} %get-tuple-element.43.refs_7_), channel_id=1, source_target_pairs={{0,2},{1,3},{2,0},{3,1},{4,6},{5,7},{6,4},{7,5},{8,10},{9,11},{10,... | collective-permute-start | bytes 393224 | tf_op jit(solution)/shard_map/ppermute | solution.py:422
  24.7 11.1 %collective-permute-start.3 = (bf16[512,128]{1,0:T(8,128)(2,1)S(1)}, bf16[512,128]{1,0:T(8,128)(2,1)S(1)}, u32[]{:S(2)}, u32[]{:S(2)}) collective-permute-start(bf16[512,128]{1,0:T(8,128)(2,1)S(1)} %get-tuple-element.43.refs_7_), channel_id=1, source_target_pairs={{0,1},{1,0},{2,3},{3,2},{4,5},{5,4},{6,7},{7,6},{8,9},{9,8},{10,11... | collective-permute-start | bytes 393224 | tf_op jit(solution)/shard_map/ppermute | solution.py:422
  29.1 6.7 %collective-permute-start = (bf16[8,32,128]{2,1,0:T(8,128)(2,1)S(1)}, bf16[8,32,128]{2,1,0:T(8,128)(2,1)S(1)}, u32[]{:S(2)}, u32[]{:S(2)}) collective-permute-start(bf16[8,32,128]{2,1,0:T(8,128)(2,1)S(1)} %get-tuple-element.40), channel_id=1, source_target_pairs={{0,8},{8,0},{16,24},{24,16},{1,9},{9,1},{17,25},{25,17},{2,10},{10... | collective-permute-start | bytes 196616 | tf_op jit(solution)/shard_map/ppermute | solution.py:422
  30.7 8.4 %collective-permute-start.1 = (bf16[8,32,128]{2,1,0:T(8,128)(2,1)S(1)}, bf16[8,32,128]{2,1,0:T(8,128)(2,1)S(1)}, u32[]{:S(2)}, u32[]{:S(2)}) collective-permute-start(bf16[8,32,128]{2,1,0:T(8,128)(2,1)S(1)} %get-tuple-element.41), channel_id=1, source_target_pairs={{0,16},{8,24},{16,0},{24,8},{1,17},{9,25},{17,1},{25,9},{2,18},{10... | collective-permute-start | bytes 196616 | tf_op jit(solution)/shard_map/ppermute | solution.py:422
  32.9 6.2 %collective-permute-start.2 = (bf16[8,32,128]{2,1,0:T(8,128)(2,1)S(1)}, bf16[8,32,128]{2,1,0:T(8,128)(2,1)S(1)}, u32[]{:S(2)}, u32[]{:S(2)}) collective-permute-start(bf16[8,32,128]{2,1,0:T(8,128)(2,1)S(1)} %get-tuple-element.42), channel_id=1, source_target_pairs={{0,24},{8,16},{16,8},{24,0},{1,25},{9,17},{17,9},{25,1},{2,26},{10... | collective-permute-start | bytes 196616 | tf_op jit(solution)/shard_map/ppermute | solution.py:422
  40.2 17.4 %copy-start.1 = (bf16[768,256]{1,0:T(8,128)(2,1)S(1)}, bf16[768,256]{1,0:T(8,128)(2,1)}, u32[]{:S(2)}) copy-start(bf16[768,256]{1,0:T(8,128)(2,1)} %refs_2_.2) | copy-start | bytes 1179652
  40.2 7.8 %collective-permute-start.12 = (bf16[288,128]{1,0:T(8,128)(2,1)S(1)}, bf16[288,128]{1,0:T(8,128)(2,1)S(1)}, u32[]{:S(2)}, u32[]{:S(2)}) collective-permute-start(bf16[288,128]{1,0:T(8,128)(2,1)S(1)} %get-tuple-element.46.refs_0_), channel_id=1, source_target_pairs={{0,24},{8,16},{16,8},{24,0},{1,25},{9,17},{17,9},{25,1},{2,26},{10... | collective-permute-start | bytes 221192 | tf_op jit(solution)/shard_map/ppermute | solution.py:422
  42.7 6.8 %collective-permute-start.11 = (bf16[288,128]{1,0:T(8,128)(2,1)S(1)}, bf16[288,128]{1,0:T(8,128)(2,1)S(1)}, u32[]{:S(2)}, u32[]{:S(2)}) collective-permute-start(bf16[288,128]{1,0:T(8,128)(2,1)S(1)} %get-tuple-element.46.refs_0_), channel_id=1, source_target_pairs={{0,16},{8,24},{16,0},{24,8},{1,17},{9,25},{17,1},{25,9},{2,18},{10... | collective-permute-start | bytes 221192 | tf_op jit(solution)/shard_map/ppermute | solution.py:422
  43.1 6.4 %collective-permute-start.10 = (bf16[288,128]{1,0:T(8,128)(2,1)S(1)}, bf16[288,128]{1,0:T(8,128)(2,1)S(1)}, u32[]{:S(2)}, u32[]{:S(2)}) collective-permute-start(bf16[288,128]{1,0:T(8,128)(2,1)S(1)} %get-tuple-element.46.refs_0_), channel_id=1, source_target_pairs={{0,8},{8,0},{16,24},{24,16},{1,9},{9,1},{17,25},{25,17},{2,10},{10... | collective-permute-start | bytes 221192 | tf_op jit(solution)/shard_map/ppermute | solution.py:422
  44.6 13.0 %all-to-all-start.1 = ((bf16[8,96,128]{2,1,0:T(8,128)(2,1)}), bf16[8,96,128]{2,1,0:T(8,128)(2,1)S(1)}, u32[]{:S(2)}, u32[]{:S(2)}) async-start(bf16[8,96,128]{2,1,0:T(8,128)(2,1)} %get-tuple-element.44), calls=%async_computation.1 | async-start | bytes 393216 | tf_op jit(solution)/shard_map/all_to_all | solution.py:540
  49.6 6.6 %collective-permute-start.18 = (bf16[288,128]{1,0:T(8,128)(2,1)S(1)}, bf16[288,128]{1,0:T(8,128)(2,1)S(1)}, u32[]{:S(2)}, u32[]{:S(2)}) collective-permute-start(bf16[288,128]{1,0:T(8,128)(2,1)S(1)} %shard_map.151.refs_1_), channel_id=1, source_target_pairs={{0,6},{1,7},{2,4},{3,5},{4,2},{5,3},{6,0},{7,1},{8,14},{9,15},{10,... | collective-permute-start | bytes 221192 | tf_op jit(solution)/shard_map/ppermute | solution.py:422
  51.7 5.4 %collective-permute-start.16 = (bf16[288,128]{1,0:T(8,128)(2,1)S(1)}, bf16[288,128]{1,0:T(8,128)(2,1)S(1)}, u32[]{:S(2)}, u32[]{:S(2)}) collective-permute-start(bf16[288,128]{1,0:T(8,128)(2,1)S(1)} %shard_map.151.refs_1_), channel_id=1, source_target_pairs={{0,4},{1,5},{2,6},{3,7},{4,0},{5,1},{6,2},{7,3},{8,12},{9,13},{10,... | collective-permute-start | bytes 221192 | tf_op jit(solution)/shard_map/ppermute | solution.py:422
  52.2 4.8 %collective-permute-start.14 = (bf16[288,128]{1,0:T(8,128)(2,1)S(1)}, bf16[288,128]{1,0:T(8,128)(2,1)S(1)}, u32[]{:S(2)}, u32[]{:S(2)}) collective-permute-start(bf16[288,128]{1,0:T(8,128)(2,1)S(1)} %shard_map.151.refs_1_), channel_id=1, source_target_pairs={{0,2},{1,3},{2,0},{3,1},{4,6},{5,7},{6,4},{7,5},{8,10},{9,11},{10,... | collective-permute-start | bytes 221192 | tf_op jit(solution)/shard_map/ppermute | solution.py:422
  53.1 5.5 %collective-permute-start.13 = (bf16[288,128]{1,0:T(8,128)(2,1)S(1)}, bf16[288,128]{1,0:T(8,128)(2,1)S(1)}, u32[]{:S(2)}, u32[]{:S(2)}) collective-permute-start(bf16[288,128]{1,0:T(8,128)(2,1)S(1)} %shard_map.151.refs_1_), channel_id=1, source_target_pairs={{0,1},{1,0},{2,3},{3,2},{4,5},{5,4},{6,7},{7,6},{8,9},{9,8},{10,11... | collective-permute-start | bytes 221192 | tf_op jit(solution)/shard_map/ppermute | solution.py:422
  56.2 2.4 %collective-permute-start.19 = (bf16[288,128]{1,0:T(8,128)(2,1)S(1)}, bf16[288,128]{1,0:T(8,128)(2,1)S(1)}, u32[]{:S(2)}, u32[]{:S(2)}) collective-permute-start(bf16[288,128]{1,0:T(8,128)(2,1)S(1)} %collective-permute-done.18.refs_7_), channel_id=1, source_target_pairs={{0,1},{1,0},{2,3},{3,2},{4,5},{5,4},{6,7},{7,6},{8,9},{9,8},{10,11... | collective-permute-start | bytes 221192 | tf_op jit(solution)/shard_map/ppermute | solution.py:422
  57.0 1.6 %collective-permute-start.17 = (bf16[288,128]{1,0:T(8,128)(2,1)S(1)}, bf16[288,128]{1,0:T(8,128)(2,1)S(1)}, u32[]{:S(2)}, u32[]{:S(2)}) collective-permute-start(bf16[288,128]{1,0:T(8,128)(2,1)S(1)} %collective-permute-done.16.refs_5_), channel_id=1, source_target_pairs={{0,1},{1,0},{2,3},{3,2},{4,5},{5,4},{6,7},{7,6},{8,9},{9,8},{10,11... | collective-permute-start | bytes 221192 | tf_op jit(solution)/shard_map/ppermute | solution.py:422
  57.0 1.6 %collective-permute-start.15 = (bf16[288,128]{1,0:T(8,128)(2,1)S(1)}, bf16[288,128]{1,0:T(8,128)(2,1)S(1)}, u32[]{:S(2)}, u32[]{:S(2)}) collective-permute-start(bf16[288,128]{1,0:T(8,128)(2,1)S(1)} %collective-permute-done.14.refs_3_), channel_id=1, source_target_pairs={{0,1},{1,0},{2,3},{3,2},{4,5},{5,4},{6,7},{7,6},{8,9},{9,8},{10,11... | collective-permute-start | bytes 221192 | tf_op jit(solution)/shard_map/ppermute | solution.py:422

commit v3 on v2

--- a/solution.py
+++ b/solution.py
@@ -307,15 +307,16 @@
         sent_out[step][...] = store[member(line[0], step)]
 
 
-def filter_grads_kernel(
-    scale, product_one, product_two, table, twist, short, grad_one, grad_two, short_out
-):
+def filter_grads_kernel(scale, product_one, product_two, table, twist, *refs):
+    count = (len(refs) - 2) // 2
+    passed, (grad_one, grad_two, *passed_out) = refs[:count], refs[count:]
     _, back, second, twist = tables_of(table, twist)
     spectra = [(ref[:, :LANES], ref[:, LANES:]) for ref in (product_one, product_two)]
     one, two = backward(spectra, back, second, twist)
     write_signal(grad_one, one * scale)
     write_signal(grad_two, two * scale)
-    short_out[...] = short[...]
+    for source, target in zip(passed, passed_out):
+        target[...] = source[...]
 
 
 def member(at, k):
@@ -374,7 +375,9 @@
     ).astype(bf16)
 
 
-def moved_kernel(channels, lines, line, back, w_in, order, features_out, store):
+def moved_kernel(
+    channels, lines, line, back, w_in, order, passed, features_out, passed_out, store
+):
     plane, width = back.shape[0], w_in.shape[1]
     share = plane * channels
     whole = back[...].astype(f32)
@@ -384,6 +387,7 @@
             start = (3 * k + s) * channels
             spot = pl.ds(pl.multiple_of(s * width + owner * share, share), share)
             store[spot] = whole[:, start : start + channels].reshape(share, LANES)
+    passed_out[...] = passed[...]
     features_out[...] = unorder(store[...].astype(bf16), w_in[...], order[...])
 
 
@@ -420,11 +424,6 @@
 
 def swapped(value, axis, count, distance):
     return lax.ppermute(value, axis, [(i, i ^ distance) for i in range(count)])
-
-
-def spread(value, plane):
-    pieces = [value if k == 0 else swapped(value, "fft", plane, k) for k in range(0, plane, 2)]
-    return [piece for own in pieces for piece in (own, swapped(own, "fft", plane, 1))]
 
 
 def shape(dims, dtype=f32):
@@ -510,14 +509,21 @@
         in_specs=[held] * 6 + [scalar],
         scratch_shapes=[pltpu.VMEM((lines, *chunk), bf16)] if whole else [],
     )
-    grad_one, grad_two, short = call(
+    passed = [short]
+    if whole:
+        passed += [swapped(own, "fft", plane, k) for k in range(2, plane, 2)]
+    grad_one, grad_two, short, *pieces = call(
         lambda *refs: filter_grads_kernel(scale / length, *refs),
-        (shape(filter_one.shape), shape(filter_two.shape), shape(short.shape)),
+        (
+            shape(filter_one.shape),
+            shape(filter_two.shape),
+            *[shape(a.shape, a.dtype) for a in passed],
+        ),
         product_one,
         product_two,
         table,
         twist,
-        short,
+        *passed,
     )
     height = channels * 4 * (width // LANES)
     if whole:
@@ -533,27 +539,31 @@
             place,
             short,
             *met,
-            *[own] + [swapped(own, "fft", plane, k) for k in range(1, plane)],
+            *[a for piece in (own, *pieces) for a in (piece, swapped(piece, "fft", plane, 1))],
             in_specs=[scalar] * 2 + [held] * (1 + lines + plane),
         )
         partials = [partial] + [swapped(partial, "seq", lines, k) for k in range(1, lines)]
         back = lax.all_to_all(moved, "fft", split_axis=0, concat_axis=0, tiled=True)
-        grad_features = call(
+        rows_sum = call(sum_kernel, shape((size, LANES), bf16), *partials)
+        across = [swapped(rows_sum, "fft", plane, k) for k in range(2, plane, 2)]
+        grad_features, passed = call(
             lambda *refs: moved_kernel(channels, lines, *refs),
-            shape(features.shape, bf16),
+            (shape(features.shape, bf16), shape((size, LANES), bf16)),
             line,
             back,
             w_in,
             order,
-            in_specs=[scalar] + [held] * 3,
+            rows_sum,
+            in_specs=[scalar] + [held] * 4,
             scratch_shapes=[pltpu.VMEM((3 * width, LANES), f32)],
         )
-        rows_sum = call(sum_kernel, shape((size, LANES), bf16), *partials)
+        spread = [rows_sum, swapped(passed, "fft", plane, 1)]
+        spread += [a for piece in across for a in (piece, swapped(piece, "fft", plane, 1))]
         grad_w_in, grad_w_out, short = call(
             lambda *refs: finish_kernel(channels, lines, *refs),
             (shape((3 * width, width)), shape((width, width)), shape((3, 3 * width))),
             place,
-            *spread(rows_sum, plane),
+            *spread,
             in_specs=[scalar] + [held] * plane,
             scratch_shapes=[pltpu.VMEM((width, width), f32), pltpu.VMEM((width, LANES), f32)],
         )

time: 60.1 us -> 64.5 us (1.073)
  waiting for transfers between devices: 11.9 us -> 20.1 us
  starting transfers between devices: 31.7 us -> 27.9 us
    ppermute x20, waiting for transfers between devices: 11.9 us -> 16.8 us  [swapped(): return lax.ppermute(value, axis, [(i, i ^ distance) for i in range(count)])]
    ppermute x20, starting transfers between devices: 21 us -> 17 us  [swapped(): return lax.ppermute(value, axis, [(i, i ^ distance) for i in range(count)])]
    all_to_all x1, waiting for transfers between devices: 0.01 us -> 3.37 us  [local(): lax.all_to_all(streams, AXES, split_axis=0, concat_axis=0, tiled=True)]
  transfers between devices with their start and end apart: 22 -> 22, of which waited for: 6 -> 8; matrix products, arithmetic and copies ran while one was open for 0% -> 0% of each run, Pallas kernels for 14% -> 13%
where the time goes in v3:
time: 64.5 us; the launch traced here: 64.2 us
  starting transfers between devices  27.9 us (43%)
  waiting for transfers between devices  20.1 us (31%)
  Pallas kernels  12.8 us (20%)
  local copies, waits for them, and re-layouts  2.63 us (4%)
  between operations  0.78 us (1%)
    ppermute x20, starting transfers between devices, swapped(): return lax.ppermute(value, axis, [(i, i ^ distance) for i in range(count)])  17 us
    ppermute x20, waiting for transfers between devices, swapped(): return lax.ppermute(value, axis, [(i, i ^ distance) for i in range(count)])  16.8 us
    pallas_call x7, Pallas kernels, call(): pl.pallas_call(kernel, out_shape=outs, compiler_params=PARAMS, **options)  10.3 us
    all_to_all x1, starting transfers between devices, local(): lax.all_to_all(streams, AXES, split_axis=0, concat_axis=0, tiled=True)  7.3 us
    all_to_all x1, starting transfers between devices, local(): back = lax.all_to_all(moved, 'fft', split_axis=0, concat_axis=0, tiled=True)  3.52 us
    all_to_all x1, waiting for transfers between devices, local(): lax.all_to_all(streams, AXES, split_axis=0, concat_axis=0, tiled=True)  3.37 us
    unnamed x16, local copies, waits for them, and re-layouts  2.46 us
    pallas_call x1, Pallas kernels, local(): pl.pallas_call(project_kernel, out_shape=(shape(dims, bf16), shape((2 * w...  2.41 us
  transfers between devices with their start and end apart: 22, of which 8 were waited for; matrix products, arithmetic and copies ran while one was open for 0% of the time, Pallas kernels for 13%

profile of v3, /device:TPU:0, one launch (start us, length us, event | category | flops | bytes accessed | tf_op | source)
XLA Modules:
  0.0 64.2 jit_solution(12428695854698049036)
XLA Ops:
  0.6 0.0 copy-start
  0.6 0.0 copy-start.2
  0.7 2.4 %shard_map.145 = (bf16[32,32,128]{2,1,0:T(8,128)(2,1)}, bf16[512,128]{1,0:T(8,128)(2,1)}) custom-call(bf16[256,128]{1,0:T(8,128)(2,1)} %features_at.1, s32[1,128]{1,0:T(1,128)} %refs_5_.1, bf16[256,128]{1,0:T(8,128)(2,1)} %cotangent_at.1, bf16[768,256]{1,0:T(8,128)(2,1)} %refs_2_.2, bf16[256,256]{1,0:T(8,128)(2,1)} %w_out_at.1), custom_call_target="tpu_custom_call" | custom-call | tf_op jit(solution)/shard_map/pallas_call | solution.py:450
  3.1 0.0 copy-start.3
  3.1 0.0 copy-start.4
  3.1 7.3 %all-to-all-start = ((bf16[32,32,128]{2,1,0:T(8,128)(2,1)}), bf16[32,32,128]{2,1,0:T(8,128)(2,1)S(1)}, u32[]{:S(2)}, u32[]{:S(2)}) async-start(bf16[32,32,128]{2,1,0:T(8,128)(2,1)} %get-tuple-element.34), calls=%async_computation | async-start | bytes 524288 | tf_op jit(solution)/shard_map/all_to_all | solution.py:464
  10.4 0.0 copy-start.7
  10.4 0.0 copy-done.2
  10.4 0.0 copy-done.3
  10.4 0.0 copy-done.4
  10.5 0.6 copy-done.7
  11.1 0.9 %copy-done.5 = f32[8,4096]{1,0:T(8,128)S(1)} copy-done((f32[8,4096]{1,0:T(8,128)S(1)}, f32[8,4096]{1,0:T(8,128)}, u32[]{:S(2)}) %copy-start.5) | copy-done | bytes 131096
  12.0 0.9 %copy-done.6 = bf16[512,128]{1,0:T(8,128)(2,1)S(1)} copy-done((bf16[512,128]{1,0:T(8,128)(2,1)S(1)}, bf16[512,128]{1,0:T(8,128)(2,1)}, u32[]{:S(2)}) %copy-start.6) | copy-done | bytes 131096
  12.9 1.0 %shard_map.146 = (f32[256,256]{1,0:T(8,128)S(1)}, f32[256,256]{1,0:T(8,128)S(1)}, bf16[1536,256]{1,0:T(8,128)(2,1)S(1)}, f32[256,256]{1,0:T(8,128)S(1)}, bf16[51...) custom-call(f32[8,4096]{1,0:T(8,128)S(1)} %copy-done.4, f32[8,4096]{1,0:T(8,128)S(1)} %copy-done.5, ...), custom_call_target="tpu_custom_call" | custom-call | tf_op jit(solution)/shard_map/pallas_call | solution.py:447
  13.9 1.8 %collective-permute-start = (bf16[512,128]{1,0:T(8,128)(2,1)S(1)}, bf16[512,128]{1,0:T(8,128)(2,1)S(1)}, u32[]{:S(2)}, u32[]{:S(2)}) collective-permute-start(bf16[512,128]{1,0:T(8,128)(2,1)S(1)} %get-tuple-element.43.refs_7_), channel_id=1, source_target_pairs={{0,2},{1,3},{2,0},{3,1},{4,6},{5,7},{6,4},{7,5},{8,10},{9,11},{10,... | collective-permute-start | bytes 393224 | tf_op jit(solution)/shard_map/ppermute | solution.py:426
  15.7 1.5 %collective-permute-start.1 = (bf16[512,128]{1,0:T(8,128)(2,1)S(1)}, bf16[512,128]{1,0:T(8,128)(2,1)S(1)}, u32[]{:S(2)}, u32[]{:S(2)}) collective-permute-start(bf16[512,128]{1,0:T(8,128)(2,1)S(1)} %get-tuple-element.43.refs_7_), channel_id=1, source_target_pairs={{0,4},{1,5},{2,6},{3,7},{4,0},{5,1},{6,2},{7,3},{8,12},{9,13},{10,... | collective-permute-start | bytes 393224 | tf_op jit(solution)/shard_map/ppermute | solution.py:426
  17.2 0.3 collective-permute-start.2
  17.5 0.0 collective-permute-start.6
  17.5 0.1 dynamic-slice_bitcast_fusion
  17.6 0.1 copy.19.refs_1_
  17.6 3.4 %all-to-all-done.refs_0_ = bf16[32,32,128]{2,1,0:T(8,128)(2,1)S(1)} async-done(((bf16[32,32,128]{2,1,0:T(8,128)(2,1)}), bf16[32,32,128]{2,1,0:T(8,128)(2,1)S(1)}, u32[]{:S(2)}, u32[]{:S(2)}) %all-to-all-start) | async-done | bytes 262176 | tf_op jit(solution)/shard_map/all_to_all | solution.py:464
  21.0 4.2 %shard_map.147 = (f32[8,128]{1,0:T(8,128)S(1)}, f32[256,256]{1,0:T(8,128)S(1)}, f32[256,256]{1,0:T(8,128)S(1)}, bf16[8,32,128]{2,1,0:T(8,128)(2,1)S(1)}, bf16[8,...) custom-call(bf16[32,32,128]{2,1,0:T(8,128)(2,1)S(1)} %all-to-all-done.refs_0_, ...), custom_call_target="tpu_custom_call" | custom-call | tf_op jit(solution)/shard_map/pallas_call | solution.py:447
  25.3 1.2 %collective-permute-start.3 = (bf16[8,32,128]{2,1,0:T(8,128)(2,1)S(1)}, bf16[8,32,128]{2,1,0:T(8,128)(2,1)S(1)}, u32[]{:S(2)}, u32[]{:S(2)}) collective-permute-start(bf16[8,32,128]{2,1,0:T(8,128)(2,1)S(1)} %get-tuple-element.46), channel_id=1, source_target_pairs={{0,8},{8,0},{16,24},{24,16},{1,9},{9,1},{17,25},{25,17},{2,10},{10... | collective-permute-start | bytes 196616 | tf_op jit(solution)/shard_map/ppermute | solution.py:426
  26.4 0.0 collective-permute-done.refs_5_
  26.4 0.0 collective-permute-done.1.refs_6_
  26.4 0.0 collective-permute-done.2.refs_7_
  26.5 1.8 %shard_map.148 = (f32[8,4096]{1,0:T(8,128)}, f32[8,4096]{1,0:T(8,128)}, f32[8,128]{1,0:T(8,128)S(1)}, bf16[512,128]{1,0:T(8,128)(2,1)S(1)}, bf16[512,128]{1,0:T(8,128)(2,1)S(1)}, /*index=5*/bf16[512,128]{1,0:T(8,128)(2,1)S(1)}) custom-call(f32[256,256]{1,0:T(8,128)S(1)} %get-tuple-element.40.refs_0_, f32[256,256]{1,0:T(8,128)S(1)} %get-tuple-element.41.refs_1_, ...), custom_call_target="tpu_custom_call" | custom-call | tf_op jit(solution)/shard_map/pallas_call | solution.py:447
  28.2 0.0 collective-permute-start.7
  28.2 0.5 collective-permute-start.8
  28.8 0.0 collective-permute-start.9
  28.8 0.0 collective-permute-done.6.refs_8_
  28.8 0.8 %collective-permute-start.4 = (bf16[8,32,128]{2,1,0:T(8,128)(2,1)S(1)}, bf16[8,32,128]{2,1,0:T(8,128)(2,1)S(1)}, u32[]{:S(2)}, u32[]{:S(2)}) collective-permute-start(bf16[8,32,128]{2,1,0:T(8,128)(2,1)S(1)} %get-tuple-element.47), channel_id=1, source_target_pairs={{0,16},{8,24},{16,0},{24,8},{1,17},{9,25},{17,1},{25,9},{2,18},{10... | collective-permute-start | bytes 196616 | tf_op jit(solution)/shard_map/ppermute | solution.py:426
  29.6 0.0 collective-permute-done.3.refs_4_
  29.6 2.4 %collective-permute-start.5 = (bf16[8,32,128]{2,1,0:T(8,128)(2,1)S(1)}, bf16[8,32,128]{2,1,0:T(8,128)(2,1)S(1)}, u32[]{:S(2)}, u32[]{:S(2)}) collective-permute-start(bf16[8,32,128]{2,1,0:T(8,128)(2,1)S(1)} %get-tuple-element.48), channel_id=1, source_target_pairs={{0,24},{8,16},{16,8},{24,0},{1,25},{9,17},{17,9},{25,1},{2,26},{10... | collective-permute-start | bytes 196616 | tf_op jit(solution)/shard_map/ppermute | solution.py:426
  32.0 5.3 %collective-permute-done.4.refs_5_ = bf16[8,32,128]{2,1,0:T(8,128)(2,1)S(1)} collective-permute-done((bf16[8,32,128]{2,1,0:T(8,128)(2,1)S(1)}, bf16[8,32,128]{2,1,0:T(8,128)(2,1)S(1)}, u32[]{:S(2)}, u32[]{:S(2)}) %collective-permute-start.4) | collective-permute-done | bytes 65568 | tf_op jit(solution)/shard_map/ppermute | solution.py:426
  37.3 0.0 collective-permute-done.5.refs_6_
  37.3 0.0 collective-permute-done.7.refs_10_
  37.3 0.0 collective-permute-done.8.refs_12_
  37.3 0.0 collective-permute-done.9.refs_14_
  37.4 1.1 %shard_map.149 = (bf16[288,128]{1,0:T(8,128)(2,1)S(1)}, bf16[8,96,128]{2,1,0:T(8,128)(2,1)}) custom-call(s32[1]{0:T(128)} %bitcast.refs_6_.refs_0_, s32[1]{0:T(128)} %bitcast.1.refs_1_.refs_0_, f32[8,128]{1,0:T(8,128)S(1)} %get-tuple-element.44.refs_2_, bf16[8,32,128]{2,1,0:T(8,128)(2,1)S(1)} %get-tuple-element.45.refs_3_, ...), custom_call_target="tpu_custom_call" | custom-call | tf_op jit(solution)/shard_map/pallas_call | solution.py:447
  38.4 3.5 %all-to-all-start.1 = ((bf16[8,96,128]{2,1,0:T(8,128)(2,1)}), bf16[8,96,128]{2,1,0:T(8,128)(2,1)S(1)}, u32[]{:S(2)}, u32[]{:S(2)}) async-start(bf16[8,96,128]{2,1,0:T(8,128)(2,1)} %get-tuple-element.52), calls=%async_computation.1 | async-start | bytes 393216 | tf_op jit(solution)/shard_map/all_to_all | solution.py:546
  42.0 1.7 %collective-permute-start.10 = (bf16[288,128]{1,0:T(8,128)(2,1)S(1)}, bf16[288,128]{1,0:T(8,128)(2,1)S(1)}, u32[]{:S(2)}, u32[]{:S(2)}) collective-permute-start(bf16[288,128]{1,0:T(8,128)(2,1)S(1)} %get-tuple-element.54.refs_0_), channel_id=1, source_target_pairs={{0,8},{8,0},{16,24},{24,16},{1,9},{9,1},{17,25},{25,17},{2,10},{10... | collective-permute-start | bytes 221192 | tf_op jit(solution)/shard_map/ppermute | solution.py:426
  43.6 0.0 collective-permute-start.11
  43.7 2.7 %collective-permute-start.12 = (bf16[288,128]{1,0:T(8,128)(2,1)S(1)}, bf16[288,128]{1,0:T(8,128)(2,1)S(1)}, u32[]{:S(2)}, u32[]{:S(2)}) collective-permute-start(bf16[288,128]{1,0:T(8,128)(2,1)S(1)} %get-tuple-element.54.refs_0_), channel_id=1, source_target_pairs={{0,24},{8,16},{16,8},{24,0},{1,25},{9,17},{17,9},{25,1},{2,26},{10... | collective-permute-start | bytes 221192 | tf_op jit(solution)/shard_map/ppermute | solution.py:426
  46.4 0.1 collective-permute-done.10.refs_1_
  46.6 5.4 %collective-permute-done.11.refs_2_ = bf16[288,128]{1,0:T(8,128)(2,1)S(1)} collective-permute-done((bf16[288,128]{1,0:T(8,128)(2,1)S(1)}, bf16[288,128]{1,0:T(8,128)(2,1)S(1)}, u32[]{:S(2)}, u32[]{:S(2)}) %collective-permute-start.11) | collective-permute-done | bytes 73760 | tf_op jit(solution)/shard_map/ppermute | solution.py:426
  51.9 0.0 collective-permute-done.12.refs_3_
  52.0 1.9 %collective-permute-start.14 = (bf16[288,128]{1,0:T(8,128)(2,1)S(1)}, bf16[288,128]{1,0:T(8,128)(2,1)S(1)}, u32[]{:S(2)}, u32[]{:S(2)}) collective-permute-start(bf16[288,128]{1,0:T(8,128)(2,1)S(1)} %shard_map.150.refs_4_.refs_1_), channel_id=1, source_target_pairs={{0,2},{1,3},{2,0},{3,1},{4,6},{5,7},{6,4},{7,5},{8,10},{9,11},{10,... | collective-permute-start | bytes 221192 | tf_op jit(solution)/shard_map/ppermute | solution.py:426
  53.8 1.5 %collective-permute-start.16 = (bf16[288,128]{1,0:T(8,128)(2,1)S(1)}, bf16[288,128]{1,0:T(8,128)(2,1)S(1)}, u32[]{:S(2)}, u32[]{:S(2)}) collective-permute-start(bf16[288,128]{1,0:T(8,128)(2,1)S(1)} %shard_map.150.refs_4_.refs_1_), channel_id=1, source_target_pairs={{0,4},{1,5},{2,6},{3,7},{4,0},{5,1},{6,2},{7,3},{8,12},{9,13},{10,... | collective-permute-start | bytes 221192 | tf_op jit(solution)/shard_map/ppermute | solution.py:426
  55.3 0.2 collective-permute-start.18
  55.5 0.9 %collective-permute-done.14.refs_3_ = bf16[288,128]{1,0:T(8,128)(2,1)S(1)} collective-permute-done((bf16[288,128]{1,0:T(8,128)(2,1)S(1)}, bf16[288,128]{1,0:T(8,128)(2,1)S(1)}, u32[]{:S(2)}, u32[]{:S(2)}) %collective-permute-start.14) | collective-permute-done | bytes 73760 | tf_op jit(solution)/shard_map/ppermute | solution.py:426
  56.4 0.0 collective-permute-start.15
  56.4 2.6 %collective-permute-done.16.refs_5_ = bf16[288,128]{1,0:T(8,128)(2,1)S(1)} collective-permute-done((bf16[288,128]{1,0:T(8,128)(2,1)S(1)}, bf16[288,128]{1,0:T(8,128)(2,1)S(1)}, u32[]{:S(2)}, u32[]{:S(2)}) %collective-permute-start.16) | collective-permute-done | bytes 73760 | tf_op jit(solution)/shard_map/ppermute | solution.py:426
  59.0 0.0 collective-permute-start.17
  59.0 1.6 %collective-permute-done.18.refs_7_ = bf16[288,128]{1,0:T(8,128)(2,1)S(1)} collective-permute-done((bf16[288,128]{1,0:T(8,128)(2,1)S(1)}, bf16[288,128]{1,0:T(8,128)(2,1)S(1)}, u32[]{:S(2)}, u32[]{:S(2)}) %collective-permute-start.18) | collective-permute-done | bytes 73760 | tf_op jit(solution)/shard_map/ppermute | solution.py:426
  60.6 0.0 collective-permute-start.19
  60.6 0.0 all-to-all-done.1.refs_1_
  60.6 1.1 %shard_map.151 = (bf16[256,128]{1,0:T(8,128)(2,1)}, bf16[288,128]{1,0:T(8,128)(2,1)S(1)}) custom-call(s32[1]{0:T(128)} %bitcast.refs_6_.refs_0_, bf16[8,96,128]{2,1,0:T(8,128)(2,1)S(1)} %all-to-all-done.1.refs_1_, bf16[768,256]{1,0:T(8,128)(2,1)S(1)} %copy-done.1, s32[1,128]{1,0:T(1,128)S(1)} %get-tuple-element.53.refs_3_, ...), custom_call_target="tpu_custom_call" | custom-call | tf_op jit(solution)/shard_map/pallas_call | solution.py:447
  61.6 0.5 collective-permute-start.13
  62.1 0.0 collective-permute-done.15.refs_4_
  62.1 0.0 collective-permute-done.17.refs_6_
  62.1 0.0 collective-permute-done.19.refs_8_
  62.2 0.9 %collective-permute-done.13.refs_2_ = bf16[288,128]{1,0:T(8,128)(2,1)S(1)} collective-permute-done((bf16[288,128]{1,0:T(8,128)(2,1)S(1)}, bf16[288,128]{1,0:T(8,128)(2,1)S(1)}, u32[]{:S(2)}, u32[]{:S(2)}) %collective-permute-start.13) | collective-permute-done | bytes 73760 | tf_op jit(solution)/shard_map/ppermute | solution.py:426
  63.1 1.1 %shard_map.152 = (f32[768,256]{1,0:T(8,128)}, f32[256,256]{1,0:T(8,128)}, f32[3,768]{1,0:T(4,128)}) custom-call(s32[1]{0:T(128)} %bitcast.1.refs_1_.refs_0_, bf16[288,128]{1,0:T(8,128)(2,1)S(1)} %shard_map.150.refs_4_.refs_1_, bf16[288,128]{1,0:T(8,128)(2,1)S(1)} %collective-permute-done.13.refs_2_, bf16[288,128]{1,0:T(8,128)(2,1)S(1)} %collective-permute-done.14.refs_3_, ...), custom_call_target="tpu_custom_call" | custom-call | tf_op jit(solution)/shard_map/pallas_call | solution.py:447
  (7 shorter events, 0.1 us)
Async XLA Ops:
  0.6 16.8 %copy-start = (f32[768,3]{0,1:T(4,128)S(1)}, f32[768,3]{0,1:T(4,128)}, u32[]{:S(2)}) copy-start(f32[768,3]{0,1:T(4,128)} %param.14) | copy-start | bytes 27652
  0.6 9.8 %copy-start.2 = (bf16[1536,256]{1,0:T(8,128)(2,1)S(1)}, bf16[1536,256]{1,0:T(8,128)(2,1)}, u32[]{:S(2)}) copy-start(bf16[1536,256]{1,0:T(8,128)(2,1)} %constant.18.clone.refs_2_) | copy-start | bytes 2359300
  3.1 7.4 %copy-start.3 = (f32[256,256]{1,0:T(8,128)S(1)}, f32[256,256]{1,0:T(8,128)}, u32[]{:S(2)}) copy-start(f32[256,256]{1,0:T(8,128)} %constant.19.clone.refs_3_) | copy-start | bytes 786436
  3.1 7.4 %copy-start.4 = (f32[8,4096]{1,0:T(8,128)S(1)}, f32[8,4096]{1,0:T(8,128)}, u32[]{:S(2)}) copy-start(f32[8,4096]{1,0:T(8,128)} %refs_0_.1) | copy-start | bytes 393220
  3.1 17.9 %all-to-all-start = ((bf16[32,32,128]{2,1,0:T(8,128)(2,1)}), bf16[32,32,128]{2,1,0:T(8,128)(2,1)S(1)}, u32[]{:S(2)}, u32[]{:S(2)}) async-start(bf16[32,32,128]{2,1,0:T(8,128)(2,1)} %get-tuple-element.34), calls=%async_computation | async-start | bytes 524288 | tf_op jit(solution)/shard_map/all_to_all | solution.py:464
  10.4 0.7 %copy-start.7 = (s32[1,128]{1,0:T(1,128)S(1)}, s32[1,128]{1,0:T(1,128)}, u32[]{:S(2)}) copy-start(s32[1,128]{1,0:T(1,128)} %refs_5_.1) | copy-start | bytes 1540
  11.1 0.9 %copy-start.5 = (f32[8,4096]{1,0:T(8,128)S(1)}, f32[8,4096]{1,0:T(8,128)}, u32[]{:S(2)}) copy-start(f32[8,4096]{1,0:T(8,128)} %refs_1_.1) | copy-start | bytes 393220
  12.0 0.9 %copy-start.6 = (bf16[512,128]{1,0:T(8,128)(2,1)S(1)}, bf16[512,128]{1,0:T(8,128)(2,1)}, u32[]{:S(2)}) copy-start(bf16[512,128]{1,0:T(8,128)(2,1)} %get-tuple-element.35.refs_4_) | copy-start | bytes 393220
  13.9 12.5 %collective-permute-start = (bf16[512,128]{1,0:T(8,128)(2,1)S(1)}, bf16[512,128]{1,0:T(8,128)(2,1)S(1)}, u32[]{:S(2)}, u32[]{:S(2)}) collective-permute-start(bf16[512,128]{1,0:T(8,128)(2,1)S(1)} %get-tuple-element.43.refs_7_), channel_id=1, source_target_pairs={{0,2},{1,3},{2,0},{3,1},{4,6},{5,7},{6,4},{7,5},{8,10},{9,11},{10,... | collective-permute-start | bytes 393224 | tf_op jit(solution)/shard_map/ppermute | solution.py:426
  15.7 10.7 %collective-permute-start.1 = (bf16[512,128]{1,0:T(8,128)(2,1)S(1)}, bf16[512,128]{1,0:T(8,128)(2,1)S(1)}, u32[]{:S(2)}, u32[]{:S(2)}) collective-permute-start(bf16[512,128]{1,0:T(8,128)(2,1)S(1)} %get-tuple-element.43.refs_7_), channel_id=1, source_target_pairs={{0,4},{1,5},{2,6},{3,7},{4,0},{5,1},{6,2},{7,3},{8,12},{9,13},{10,... | collective-permute-start | bytes 393224 | tf_op jit(solution)/shard_map/ppermute | solution.py:426
  17.2 9.2 %collective-permute-start.2 = (bf16[512,128]{1,0:T(8,128)(2,1)S(1)}, bf16[512,128]{1,0:T(8,128)(2,1)S(1)}, u32[]{:S(2)}, u32[]{:S(2)}) collective-permute-start(bf16[512,128]{1,0:T(8,128)(2,1)S(1)} %get-tuple-element.43.refs_7_), channel_id=1, source_target_pairs={{0,6},{1,7},{2,4},{3,5},{4,2},{5,3},{6,0},{7,1},{8,14},{9,15},{10,... | collective-permute-start | bytes 393224 | tf_op jit(solution)/shard_map/ppermute | solution.py:426
  17.5 11.3 %collective-permute-start.6 = (bf16[512,128]{1,0:T(8,128)(2,1)S(1)}, bf16[512,128]{1,0:T(8,128)(2,1)S(1)}, u32[]{:S(2)}, u32[]{:S(2)}) collective-permute-start(bf16[512,128]{1,0:T(8,128)(2,1)S(1)} %get-tuple-element.43.refs_7_), channel_id=1, source_target_pairs={{0,1},{1,0},{2,3},{3,2},{4,5},{5,4},{6,7},{7,6},{8,9},{9,8},{10,11... | collective-permute-start | bytes 393224 | tf_op jit(solution)/shard_map/ppermute | solution.py:426
  25.3 4.3 %collective-permute-start.3 = (bf16[8,32,128]{2,1,0:T(8,128)(2,1)S(1)}, bf16[8,32,128]{2,1,0:T(8,128)(2,1)S(1)}, u32[]{:S(2)}, u32[]{:S(2)}) collective-permute-start(bf16[8,32,128]{2,1,0:T(8,128)(2,1)S(1)} %get-tuple-element.46), channel_id=1, source_target_pairs={{0,8},{8,0},{16,24},{24,16},{1,9},{9,1},{17,25},{25,17},{2,10},{10... | collective-permute-start | bytes 196616 | tf_op jit(solution)/shard_map/ppermute | solution.py:426
  28.2 9.1 %collective-permute-start.7 = (bf16[512,128]{1,0:T(8,128)(2,1)S(1)}, bf16[512,128]{1,0:T(8,128)(2,1)S(1)}, u32[]{:S(2)}, u32[]{:S(2)}) collective-permute-start(bf16[512,128]{1,0:T(8,128)(2,1)S(1)} %get-tuple-element.49.refs_9_), channel_id=1, source_target_pairs={{0,1},{1,0},{2,3},{3,2},{4,5},{5,4},{6,7},{7,6},{8,9},{9,8},{10,11... | collective-permute-start | bytes 393224 | tf_op jit(solution)/shard_map/ppermute | solution.py:426
  28.2 9.1 %collective-permute-start.8 = (bf16[512,128]{1,0:T(8,128)(2,1)S(1)}, bf16[512,128]{1,0:T(8,128)(2,1)S(1)}, u32[]{:S(2)}, u32[]{:S(2)}) collective-permute-start(bf16[512,128]{1,0:T(8,128)(2,1)S(1)} %get-tuple-element.50.refs_11_), channel_id=1, source_target_pairs={{0,1},{1,0},{2,3},{3,2},{4,5},{5,4},{6,7},{7,6},{8,9},{9,8},{10,11... | collective-permute-start | bytes 393224 | tf_op jit(solution)/shard_map/ppermute | solution.py:426
  28.8 8.6 %collective-permute-start.9 = (bf16[512,128]{1,0:T(8,128)(2,1)S(1)}, bf16[512,128]{1,0:T(8,128)(2,1)S(1)}, u32[]{:S(2)}, u32[]{:S(2)}) collective-permute-start(bf16[512,128]{1,0:T(8,128)(2,1)S(1)} %get-tuple-element.51.refs_13_), channel_id=1, source_target_pairs={{0,1},{1,0},{2,3},{3,2},{4,5},{5,4},{6,7},{7,6},{8,9},{9,8},{10,11... | collective-permute-start | bytes 393224 | tf_op jit(solution)/shard_map/ppermute | solution.py:426
  28.8 8.6 %collective-permute-start.4 = (bf16[8,32,128]{2,1,0:T(8,128)(2,1)S(1)}, bf16[8,32,128]{2,1,0:T(8,128)(2,1)S(1)}, u32[]{:S(2)}, u32[]{:S(2)}) collective-permute-start(bf16[8,32,128]{2,1,0:T(8,128)(2,1)S(1)} %get-tuple-element.47), channel_id=1, source_target_pairs={{0,16},{8,24},{16,0},{24,8},{1,17},{9,25},{17,1},{25,9},{2,18},{10... | collective-permute-start | bytes 196616 | tf_op jit(solution)/shard_map/ppermute | solution.py:426
  29.6 7.8 %collective-permute-start.5 = (bf16[8,32,128]{2,1,0:T(8,128)(2,1)S(1)}, bf16[8,32,128]{2,1,0:T(8,128)(2,1)S(1)}, u32[]{:S(2)}, u32[]{:S(2)}) collective-permute-start(bf16[8,32,128]{2,1,0:T(8,128)(2,1)S(1)} %get-tuple-element.48), channel_id=1, source_target_pairs={{0,24},{8,16},{16,8},{24,0},{1,25},{9,17},{17,9},{25,1},{2,26},{10... | collective-permute-start | bytes 196616 | tf_op jit(solution)/shard_map/ppermute | solution.py:426
  38.4 22.1 %copy-start.1 = (bf16[768,256]{1,0:T(8,128)(2,1)S(1)}, bf16[768,256]{1,0:T(8,128)(2,1)}, u32[]{:S(2)}) copy-start(bf16[768,256]{1,0:T(8,128)(2,1)} %refs_2_.2) | copy-start | bytes 1179652
  38.4 22.1 %all-to-all-start.1 = ((bf16[8,96,128]{2,1,0:T(8,128)(2,1)}), bf16[8,96,128]{2,1,0:T(8,128)(2,1)S(1)}, u32[]{:S(2)}, u32[]{:S(2)}) async-start(bf16[8,96,128]{2,1,0:T(8,128)(2,1)} %get-tuple-element.52), calls=%async_computation.1 | async-start | bytes 393216 | tf_op jit(solution)/shard_map/all_to_all | solution.py:546
  42.0 4.6 %collective-permute-start.10 = (bf16[288,128]{1,0:T(8,128)(2,1)S(1)}, bf16[288,128]{1,0:T(8,128)(2,1)S(1)}, u32[]{:S(2)}, u32[]{:S(2)}) collective-permute-start(bf16[288,128]{1,0:T(8,128)(2,1)S(1)} %get-tuple-element.54.refs_0_), channel_id=1, source_target_pairs={{0,8},{8,0},{16,24},{24,16},{1,9},{9,1},{17,25},{25,17},{2,10},{10... | collective-permute-start | bytes 221192 | tf_op jit(solution)/shard_map/ppermute | solution.py:426
  43.6 8.3 %collective-permute-start.11 = (bf16[288,128]{1,0:T(8,128)(2,1)S(1)}, bf16[288,128]{1,0:T(8,128)(2,1)S(1)}, u32[]{:S(2)}, u32[]{:S(2)}) collective-permute-start(bf16[288,128]{1,0:T(8,128)(2,1)S(1)} %get-tuple-element.54.refs_0_), channel_id=1, source_target_pairs={{0,16},{8,24},{16,0},{24,8},{1,17},{9,25},{17,1},{25,9},{2,18},{10... | collective-permute-start | bytes 221192 | tf_op jit(solution)/shard_map/ppermute | solution.py:426
  43.7 8.2 %collective-permute-start.12 = (bf16[288,128]{1,0:T(8,128)(2,1)S(1)}, bf16[288,128]{1,0:T(8,128)(2,1)S(1)}, u32[]{:S(2)}, u32[]{:S(2)}) collective-permute-start(bf16[288,128]{1,0:T(8,128)(2,1)S(1)} %get-tuple-element.54.refs_0_), channel_id=1, source_target_pairs={{0,24},{8,16},{16,8},{24,0},{1,25},{9,17},{17,9},{25,1},{2,26},{10... | collective-permute-start | bytes 221192 | tf_op jit(solution)/shard_map/ppermute | solution.py:426
  52.0 4.4 %collective-permute-start.14 = (bf16[288,128]{1,0:T(8,128)(2,1)S(1)}, bf16[288,128]{1,0:T(8,128)(2,1)S(1)}, u32[]{:S(2)}, u32[]{:S(2)}) collective-permute-start(bf16[288,128]{1,0:T(8,128)(2,1)S(1)} %shard_map.150.refs_4_.refs_1_), channel_id=1, source_target_pairs={{0,2},{1,3},{2,0},{3,1},{4,6},{5,7},{6,4},{7,5},{8,10},{9,11},{10,... | collective-permute-start | bytes 221192 | tf_op jit(solution)/shard_map/ppermute | solution.py:426
  53.8 5.1 %collective-permute-start.16 = (bf16[288,128]{1,0:T(8,128)(2,1)S(1)}, bf16[288,128]{1,0:T(8,128)(2,1)S(1)}, u32[]{:S(2)}, u32[]{:S(2)}) collective-permute-start(bf16[288,128]{1,0:T(8,128)(2,1)S(1)} %shard_map.150.refs_4_.refs_1_), channel_id=1, source_target_pairs={{0,4},{1,5},{2,6},{3,7},{4,0},{5,1},{6,2},{7,3},{8,12},{9,13},{10,... | collective-permute-start | bytes 221192 | tf_op jit(solution)/shard_map/ppermute | solution.py:426
  55.3 5.3 %collective-permute-start.18 = (bf16[288,128]{1,0:T(8,128)(2,1)S(1)}, bf16[288,128]{1,0:T(8,128)(2,1)S(1)}, u32[]{:S(2)}, u32[]{:S(2)}) collective-permute-start(bf16[288,128]{1,0:T(8,128)(2,1)S(1)} %shard_map.150.refs_4_.refs_1_), channel_id=1, source_target_pairs={{0,6},{1,7},{2,4},{3,5},{4,2},{5,3},{6,0},{7,1},{8,14},{9,15},{10,... | collective-permute-start | bytes 221192 | tf_op jit(solution)/shard_map/ppermute | solution.py:426
  56.4 5.8 %collective-permute-start.15 = (bf16[288,128]{1,0:T(8,128)(2,1)S(1)}, bf16[288,128]{1,0:T(8,128)(2,1)S(1)}, u32[]{:S(2)}, u32[]{:S(2)}) collective-permute-start(bf16[288,128]{1,0:T(8,128)(2,1)S(1)} %collective-permute-done.14.refs_3_), channel_id=1, source_target_pairs={{0,1},{1,0},{2,3},{3,2},{4,5},{5,4},{6,7},{7,6},{8,9},{9,8},{10,11... | collective-permute-start | bytes 221192 | tf_op jit(solution)/shard_map/ppermute | solution.py:426
  59.0 3.2 %collective-permute-start.17 = (bf16[288,128]{1,0:T(8,128)(2,1)S(1)}, bf16[288,128]{1,0:T(8,128)(2,1)S(1)}, u32[]{:S(2)}, u32[]{:S(2)}) collective-permute-start(bf16[288,128]{1,0:T(8,128)(2,1)S(1)} %collective-permute-done.16.refs_5_), channel_id=1, source_target_pairs={{0,1},{1,0},{2,3},{3,2},{4,5},{5,4},{6,7},{7,6},{8,9},{9,8},{10,11... | collective-permute-start | bytes 221192 | tf_op jit(solution)/shard_map/ppermute | solution.py:426
  60.6 1.6 %collective-permute-start.19 = (bf16[288,128]{1,0:T(8,128)(2,1)S(1)}, bf16[288,128]{1,0:T(8,128)(2,1)S(1)}, u32[]{:S(2)}, u32[]{:S(2)}) collective-permute-start(bf16[288,128]{1,0:T(8,128)(2,1)S(1)} %collective-permute-done.18.refs_7_), channel_id=1, source_target_pairs={{0,1},{1,0},{2,3},{3,2},{4,5},{5,4},{6,7},{7,6},{8,9},{9,8},{10,11... | collective-permute-start | bytes 221192 | tf_op jit(solution)/shard_map/ppermute | solution.py:426
  61.6 1.4 %collective-permute-start.13 = (bf16[288,128]{1,0:T(8,128)(2,1)S(1)}, bf16[288,128]{1,0:T(8,128)(2,1)S(1)}, u32[]{:S(2)}, u32[]{:S(2)}) collective-permute-start(bf16[288,128]{1,0:T(8,128)(2,1)S(1)} %get-tuple-element.56), channel_id=1, source_target_pairs={{0,1},{1,0},{2,3},{3,2},{4,5},{5,4},{6,7},{7,6},{8,9},{9,8},{10,11... | collective-permute-start | bytes 221192 | tf_op jit(solution)/shard_map/ppermute | solution.py:426

commit v4 on v1

--- a/solution.py
+++ b/solution.py
@@ -190,13 +190,11 @@
     filter_two,
     table,
     twist,
-    own,
     order,
     spec_one,
     spec_two,
     table_out,
     twist_out,
-    own_out,
     order_out,
 ):
     rows = spec_one.shape[0]
@@ -207,8 +205,13 @@
     spec_two[...] = jnp.concatenate(two, axis=1) * (1.0 / length)
     table_out[...] = table[...]
     twist_out[...] = twist[...]
-    own_out[...] = own[...]
     order_out[...] = order[...]
+
+
+def pass_kernel(after, *refs):
+    count = len(refs) // 2
+    for source, target in zip(refs[:count], refs[count:]):
+        target[...] = source[...]
 
 
 def shifted(value, steps, channels):
@@ -473,23 +476,24 @@
             for h in (filter_one, filter_two)
         ]
     spec = shape((rows, 2 * LANES))
-    spec_one, spec_two, table, twist, own, order = call(
+    spec_one, spec_two, table, twist, order = call(
         lambda *refs: filter_kernel(length, *refs),
         (
             spec,
             spec,
             shape(table.shape, bf16),
             shape(twist.shape),
-            shape(own.shape, bf16),
             shape(sink_order.shape, jnp.int32),
         ),
         filter_one,
         filter_two,
         table,
         twist,
-        own,
         sink_order,
     )
+    if whole:
+        pieces = [swapped(own, plane, k) for k in range(2, plane, 2)]
+        pieces = call(pass_kernel, [shape(own.shape, bf16)] * len(pieces), order, *pieces)
     line = lax.axis_index("seq").astype(jnp.int32).reshape(1)
     place = lax.axis_index("fft").astype(jnp.int32).reshape(1)
     scalar = pl.BlockSpec(memory_space=pltpu.SMEM)
@@ -536,7 +540,7 @@
             place,
             short,
             *met,
-            *spread(own, plane),
+            *[a for p in (own, *pieces) for a in (p, swapped(p, plane, 1))],
             in_specs=[scalar] * 2 + [held] * (1 + lines + plane),
         )
         partials = [partial] + [ahead(partial, k) for k in range(1, lines)]

time: 59.2 us -> 57.8 us (0.976)
  local copies, waits for them, and re-layouts: 2.63 us -> 1.11 us
  starting transfers between devices: 27.3 us -> 28.3 us
  waiting for transfers between devices: 15.4 us -> 14.5 us
    unnamed x16, local copies, waits for them, and re-layouts: 2.46 us -> 0.94 us
    ppermute x6, waiting for transfers between devices: 4.91 us -> 3.86 us  [ahead(): return lax.ppermute(value, 'seq', pairs)]
    ppermute x14, starting transfers between devices: 7.63 us -> 8.27 us  [swapped(): return lax.ppermute(value, 'fft', [(i, i ^ distance) for i in range(plane)])]
    pallas_call x7 -> x8, Pallas kernels: 10.4 us -> 10.4 us  [call(): pl.pallas_call(kernel, out_shape=outs, compiler_params=PARAMS, **options)]
  transfers between devices with their start and end apart: 22 -> 22, of which waited for: 8 -> 9; matrix products, arithmetic and copies ran while one was open for 0% -> 0% of each run, Pallas kernels for 14% -> 14%
where the time goes in v4:
time: 57.8 us; the launch traced here: 57.5 us
  starting transfers between devices  28.3 us (49%)
  waiting for transfers between devices  14.5 us (25%)
  Pallas kernels  12.8 us (22%)
  local copies, waits for them, and re-layouts  1.11 us (2%)
  between operations  0.8 us (1%)
    ppermute x14, waiting for transfers between devices, swapped(): return lax.ppermute(value, 'fft', [(i, i ^ distance) for i in range(plane)])  10.7 us
    pallas_call x8, Pallas kernels, call(): pl.pallas_call(kernel, out_shape=outs, compiler_params=PARAMS, **options)  10.4 us
    ppermute x6, starting transfers between devices, ahead(): return lax.ppermute(value, 'seq', pairs)  9.29 us
    ppermute x14, starting transfers between devices, swapped(): return lax.ppermute(value, 'fft', [(i, i ^ distance) for i in range(plane)])  8.27 us
    all_to_all x1, starting transfers between devices, local(): lax.all_to_all(streams, AXES, split_axis=0, concat_axis=0, tiled=True)  7.3 us
    ppermute x6, waiting for transfers between devices, ahead(): return lax.ppermute(value, 'seq', pairs)  3.86 us
    all_to_all x1, starting transfers between devices, local(): back = lax.all_to_all(moved, 'fft', split_axis=0, concat_axis=0, tiled=True)  3.39 us
    pallas_call x1, Pallas kernels, local(): pl.pallas_call(project_kernel, out_shape=(shape(dims, bf16), shape((2 * w...  2.41 us
  transfers between devices with their start and end apart: 22, of which 9 were waited for; matrix products, arithmetic and copies ran while one was open for 0% of the time, Pallas kernels for 14%

profile of v4, /device:TPU:0, one launch (start us, length us, event | category | flops | bytes accessed | tf_op | source)
XLA Modules:
  0.0 57.5 jit_solution(5620823750123832214)
XLA Ops:
  0.6 0.0 copy-start
  0.6 0.0 copy-start.2
  0.7 2.4 %shard_map.145 = (bf16[32,32,128]{2,1,0:T(8,128)(2,1)}, bf16[512,128]{1,0:T(8,128)(2,1)}) custom-call(bf16[256,128]{1,0:T(8,128)(2,1)} %features_at.1, s32[1,128]{1,0:T(1,128)} %refs_4_.1, bf16[256,128]{1,0:T(8,128)(2,1)} %cotangent_at.1, bf16[768,256]{1,0:T(8,128)(2,1)} %refs_2_.2, bf16[256,256]{1,0:T(8,128)(2,1)} %w_out_at.1), custom_call_target="tpu_custom_call" | custom-call | tf_op jit(solution)/shard_map/pallas_call | solution.py:453
  3.1 0.0 copy-start.3
  3.1 0.0 copy-start.4
  3.1 7.3 %all-to-all-start = ((bf16[32,32,128]{2,1,0:T(8,128)(2,1)}), bf16[32,32,128]{2,1,0:T(8,128)(2,1)S(1)}, u32[]{:S(2)}, u32[]{:S(2)}) async-start(bf16[32,32,128]{2,1,0:T(8,128)(2,1)} %get-tuple-element.31), calls=%async_computation | async-start | bytes 524288 | tf_op jit(solution)/shard_map/all_to_all | solution.py:467
  10.4 0.0 copy-start.7
  10.4 1.8 %collective-permute-start.4 = (bf16[512,128]{1,0:T(8,128)(2,1)}, bf16[512,128]{1,0:T(8,128)(2,1)S(1)}, u32[]{:S(2)}, u32[]{:S(2)}) collective-permute-start(bf16[512,128]{1,0:T(8,128)(2,1)} %get-tuple-element.44.refs_7_), channel_id=1, source_target_pairs={{0,2},{1,3},{2,0},{3,1},{4,6},{5,7},{6,4},{7,5},{8,10},{9,11},{10,... | collective-permute-start | bytes 393224 | tf_op jit(solution)/shard_map/ppermute | solution.py:425
  12.3 1.5 %collective-permute-start.5 = (bf16[512,128]{1,0:T(8,128)(2,1)}, bf16[512,128]{1,0:T(8,128)(2,1)S(1)}, u32[]{:S(2)}, u32[]{:S(2)}) collective-permute-start(bf16[512,128]{1,0:T(8,128)(2,1)} %get-tuple-element.44.refs_7_), channel_id=1, source_target_pairs={{0,4},{1,5},{2,6},{3,7},{4,0},{5,1},{6,2},{7,3},{8,12},{9,13},{10,... | collective-permute-start | bytes 393224 | tf_op jit(solution)/shard_map/ppermute | solution.py:425
  13.7 0.3 collective-permute-start.6
  14.0 0.0 collective-permute-start.3
  14.0 0.0 copy-done.2
  14.0 0.0 copy-done.3
  14.0 0.0 copy-done.4
  14.0 0.0 copy-done.7
  14.0 0.0 copy-start.5
  14.0 0.9 %copy-done.5 = f32[8,4096]{1,0:T(8,128)S(1)} copy-done((f32[8,4096]{1,0:T(8,128)S(1)}, f32[8,4096]{1,0:T(8,128)}, u32[]{:S(2)}) %copy-start.5) | copy-done | bytes 131096
  14.9 1.0 %shard_map.146 = (f32[256,256]{1,0:T(8,128)S(1)}, f32[256,256]{1,0:T(8,128)S(1)}, bf16[1536,256]{1,0:T(8,128)(2,1)S(1)}, f32[256,256]{1,0:T(8,128)S(1)}, s32[1,128]{1,0:T(1,128)S(1)}) custom-call(f32[8,4096]{1,0:T(8,128)S(1)} %copy-done.4, f32[8,4096]{1,0:T(8,128)S(1)} %copy-done.5, bf16[1536,256]{1,0:T(8,128)(2,1)S(1)} %copy-done.2, ...), custom_call_target="tpu_custom_call" | custom-call | tf_op jit(solution)/shard_map/pallas_call | solution.py:450
  15.9 3.2 %collective-permute-done.4.refs_0_ = bf16[512,128]{1,0:T(8,128)(2,1)S(1)} collective-permute-done((bf16[512,128]{1,0:T(8,128)(2,1)}, bf16[512,128]{1,0:T(8,128)(2,1)S(1)}, u32[]{:S(2)}, u32[]{:S(2)}) %collective-permute-start.4) | collective-permute-done | bytes 131104 | tf_op jit(solution)/shard_map/ppermute | solution.py:425
  19.1 2.1 %collective-permute-done.5.refs_1_ = bf16[512,128]{1,0:T(8,128)(2,1)S(1)} collective-permute-done((bf16[512,128]{1,0:T(8,128)(2,1)}, bf16[512,128]{1,0:T(8,128)(2,1)S(1)}, u32[]{:S(2)}, u32[]{:S(2)}) %collective-permute-start.5) | collective-permute-done | bytes 131104 | tf_op jit(solution)/shard_map/ppermute | solution.py:425
  21.2 1.6 %collective-permute-done.6.refs_2_ = bf16[512,128]{1,0:T(8,128)(2,1)S(1)} collective-permute-done((bf16[512,128]{1,0:T(8,128)(2,1)}, bf16[512,128]{1,0:T(8,128)(2,1)S(1)}, u32[]{:S(2)}, u32[]{:S(2)}) %collective-permute-start.6) | collective-permute-done | bytes 131104 | tf_op jit(solution)/shard_map/ppermute | solution.py:425
  22.8 0.1 collective-permute-start.7
  22.9 0.5 collective-permute-start.8
  23.4 0.1 collective-permute-start.9
  23.5 0.1 dynamic-slice_bitcast_fusion
  23.6 0.1 copy.19.refs_1_
  23.6 0.0 all-to-all-done.refs_0_
  23.6 4.2 %shard_map.147 = (f32[8,128]{1,0:T(8,128)S(1)}, f32[256,256]{1,0:T(8,128)S(1)}, f32[256,256]{1,0:T(8,128)S(1)}, bf16[8,32,128]{2,1,0:T(8,128)(2,1)S(1)}, bf16[8,...) custom-call(bf16[32,32,128]{2,1,0:T(8,128)(2,1)S(1)} %all-to-all-done.refs_0_, ...), custom_call_target="tpu_custom_call" | custom-call | tf_op jit(solution)/shard_map/pallas_call | solution.py:450
  27.9 1.3 %collective-permute-start = (bf16[8,32,128]{2,1,0:T(8,128)(2,1)S(1)}, bf16[8,32,128]{2,1,0:T(8,128)(2,1)S(1)}, u32[]{:S(2)}, u32[]{:S(2)}) collective-permute-start(bf16[8,32,128]{2,1,0:T(8,128)(2,1)S(1)} %get-tuple-element.41), channel_id=1, source_target_pairs={{0,8},{8,16},{16,24},{24,0},{1,9},{9,17},{17,25},{25,1},{2,10},{10... | collective-permute-start | bytes 196616 | tf_op jit(solution)/shard_map/ppermute | solution.py:529
  29.2 0.0 collective-permute-done.3.refs_8_
  29.2 2.4 %collective-permute-start.1 = (bf16[8,32,128]{2,1,0:T(8,128)(2,1)S(1)}, bf16[8,32,128]{2,1,0:T(8,128)(2,1)S(1)}, u32[]{:S(2)}, u32[]{:S(2)}) collective-permute-start(bf16[8,32,128]{2,1,0:T(8,128)(2,1)S(1)} %get-tuple-element.42), channel_id=1, source_target_pairs={{0,16},{8,24},{16,0},{24,8},{1,17},{9,25},{17,1},{25,9},{2,18},{10... | collective-permute-start | bytes 196616 | tf_op jit(solution)/shard_map/ppermute | solution.py:529
  31.6 0.0 collective-permute-done.7.refs_10_
  31.6 1.5 %collective-permute-start.2 = (bf16[8,32,128]{2,1,0:T(8,128)(2,1)S(1)}, bf16[8,32,128]{2,1,0:T(8,128)(2,1)S(1)}, u32[]{:S(2)}, u32[]{:S(2)}) collective-permute-start(bf16[8,32,128]{2,1,0:T(8,128)(2,1)S(1)} %get-tuple-element.43), channel_id=1, source_target_pairs={{0,24},{8,0},{16,8},{24,16},{1,25},{9,1},{17,9},{25,17},{2,26},{10... | collective-permute-start | bytes 196616 | tf_op jit(solution)/shard_map/ppermute | solution.py:529
  33.1 1.8 %shard_map.148 = (f32[8,4096]{1,0:T(8,128)}, f32[8,4096]{1,0:T(8,128)}, f32[8,128]{1,0:T(8,128)S(1)}) custom-call(f32[256,256]{1,0:T(8,128)S(1)} %get-tuple-element.36.refs_0_, f32[256,256]{1,0:T(8,128)S(1)} %get-tuple-element.37.refs_1_, bf16[1536,256]{1,0:T(8,128)(2,1)S(1)} %get-tuple-element.34.refs_4_.refs_2_, ...), custom_call_target="tpu_custom_call" | custom-call | tf_op jit(solution)/shard_map/pallas_call | solution.py:450
  34.9 0.0 collective-permute-done.8.refs_12_
  34.9 0.0 collective-permute-done.9.refs_14_
  34.9 0.0 collective-permute-done.refs_4_
  34.9 2.2 %collective-permute-done.1.refs_5_ = bf16[8,32,128]{2,1,0:T(8,128)(2,1)S(1)} collective-permute-done((bf16[8,32,128]{2,1,0:T(8,128)(2,1)S(1)}, bf16[8,32,128]{2,1,0:T(8,128)(2,1)S(1)}, u32[]{:S(2)}, u32[]{:S(2)}) %collective-permute-start.1) | collective-permute-done | bytes 65568 | tf_op jit(solution)/shard_map/ppermute | solution.py:529
  37.1 0.1 collective-permute-done.2.refs_6_
  37.2 1.1 %shard_map.150 = (bf16[288,128]{1,0:T(8,128)(2,1)S(1)}, bf16[8,96,128]{2,1,0:T(8,128)(2,1)}) custom-call(s32[1]{0:T(128)} %bitcast.refs_6_.refs_0_, s32[1]{0:T(128)} %bitcast.1.refs_1_.refs_0_, f32[8,128]{1,0:T(8,128)S(1)} %get-tuple-element.39.refs_2_, bf16[8,32,128]{2,1,0:T(8,128)(2,1)S(1)} %get-tuple-element.40.refs_3_, ...), custom_call_target="tpu_custom_call" | custom-call | tf_op jit(solution)/shard_map/pallas_call | solution.py:450
  38.3 1.7 %collective-permute-start.10 = (bf16[288,128]{1,0:T(8,128)(2,1)S(1)}, bf16[288,128]{1,0:T(8,128)(2,1)S(1)}, u32[]{:S(2)}, u32[]{:S(2)}) collective-permute-start(bf16[288,128]{1,0:T(8,128)(2,1)S(1)} %get-tuple-element.50.refs_0_), channel_id=1, source_target_pairs={{0,8},{8,16},{16,24},{24,0},{1,9},{9,17},{17,25},{25,1},{2,10},{10... | collective-permute-start | bytes 221192 | tf_op jit(solution)/shard_map/ppermute | solution.py:529
  40.0 1.3 %collective-permute-start.11 = (bf16[288,128]{1,0:T(8,128)(2,1)S(1)}, bf16[288,128]{1,0:T(8,128)(2,1)S(1)}, u32[]{:S(2)}, u32[]{:S(2)}) collective-permute-start(bf16[288,128]{1,0:T(8,128)(2,1)S(1)} %get-tuple-element.50.refs_0_), channel_id=1, source_target_pairs={{0,16},{8,24},{16,0},{24,8},{1,17},{9,25},{17,1},{25,9},{2,18},{10... | collective-permute-start | bytes 221192 | tf_op jit(solution)/shard_map/ppermute | solution.py:529
  41.3 1.0 %collective-permute-start.12 = (bf16[288,128]{1,0:T(8,128)(2,1)S(1)}, bf16[288,128]{1,0:T(8,128)(2,1)S(1)}, u32[]{:S(2)}, u32[]{:S(2)}) collective-permute-start(bf16[288,128]{1,0:T(8,128)(2,1)S(1)} %get-tuple-element.50.refs_0_), channel_id=1, source_target_pairs={{0,24},{8,0},{16,8},{24,16},{1,25},{9,1},{17,9},{25,17},{2,26},{10... | collective-permute-start | bytes 221192 | tf_op jit(solution)/shard_map/ppermute | solution.py:529
  42.4 3.4 %all-to-all-start.1 = ((bf16[8,96,128]{2,1,0:T(8,128)(2,1)}), bf16[8,96,128]{2,1,0:T(8,128)(2,1)S(1)}, u32[]{:S(2)}, u32[]{:S(2)}) async-start(bf16[8,96,128]{2,1,0:T(8,128)(2,1)} %get-tuple-element.49), calls=%async_computation.1 | async-start | bytes 393216 | tf_op jit(solution)/shard_map/all_to_all | solution.py:547
  45.8 0.0 collective-permute-done.10.refs_1_
  45.8 1.5 %collective-permute-done.11.refs_2_ = bf16[288,128]{1,0:T(8,128)(2,1)S(1)} collective-permute-done((bf16[288,128]{1,0:T(8,128)(2,1)S(1)}, bf16[288,128]{1,0:T(8,128)(2,1)S(1)}, u32[]{:S(2)}, u32[]{:S(2)}) %collective-permute-start.11) | collective-permute-done | bytes 73760 | tf_op jit(solution)/shard_map/ppermute | solution.py:529
  47.3 0.0 collective-permute-done.12.refs_3_
  47.4 1.0 %collective-permute-start.14 = (bf16[288,128]{1,0:T(8,128)(2,1)S(1)}, bf16[288,128]{1,0:T(8,128)(2,1)S(1)}, u32[]{:S(2)}, u32[]{:S(2)}) collective-permute-start(bf16[288,128]{1,0:T(8,128)(2,1)S(1)} %shard_map.152.refs_1_), channel_id=1, source_target_pairs={{0,2},{1,3},{2,0},{3,1},{4,6},{5,7},{6,4},{7,5},{8,10},{9,11},{10,... | collective-permute-start | bytes 221192 | tf_op jit(solution)/shard_map/ppermute | solution.py:425
  48.4 0.9 %collective-permute-start.16 = (bf16[288,128]{1,0:T(8,128)(2,1)S(1)}, bf16[288,128]{1,0:T(8,128)(2,1)S(1)}, u32[]{:S(2)}, u32[]{:S(2)}) collective-permute-start(bf16[288,128]{1,0:T(8,128)(2,1)S(1)} %shard_map.152.refs_1_), channel_id=1, source_target_pairs={{0,4},{1,5},{2,6},{3,7},{4,0},{5,1},{6,2},{7,3},{8,12},{9,13},{10,... | collective-permute-start | bytes 221192 | tf_op jit(solution)/shard_map/ppermute | solution.py:425
  49.3 1.6 %collective-permute-start.18 = (bf16[288,128]{1,0:T(8,128)(2,1)S(1)}, bf16[288,128]{1,0:T(8,128)(2,1)S(1)}, u32[]{:S(2)}, u32[]{:S(2)}) collective-permute-start(bf16[288,128]{1,0:T(8,128)(2,1)S(1)} %shard_map.152.refs_1_), channel_id=1, source_target_pairs={{0,6},{1,7},{2,4},{3,5},{4,2},{5,3},{6,0},{7,1},{8,14},{9,15},{10,... | collective-permute-start | bytes 221192 | tf_op jit(solution)/shard_map/ppermute | solution.py:425
  50.9 0.0 collective-permute-start.13
  50.9 2.1 %collective-permute-done.14.refs_3_ = bf16[288,128]{1,0:T(8,128)(2,1)S(1)} collective-permute-done((bf16[288,128]{1,0:T(8,128)(2,1)S(1)}, bf16[288,128]{1,0:T(8,128)(2,1)S(1)}, u32[]{:S(2)}, u32[]{:S(2)}) %collective-permute-start.14) | collective-permute-done | bytes 73760 | tf_op jit(solution)/shard_map/ppermute | solution.py:425
  53.1 0.0 collective-permute-start.15
  53.1 0.0 collective-permute-done.16.refs_5_
  53.1 0.5 collective-permute-start.17
  53.6 1.5 %collective-permute-done.18.refs_7_ = bf16[288,128]{1,0:T(8,128)(2,1)S(1)} collective-permute-done((bf16[288,128]{1,0:T(8,128)(2,1)S(1)}, bf16[288,128]{1,0:T(8,128)(2,1)S(1)}, u32[]{:S(2)}, u32[]{:S(2)}) %collective-permute-start.18) | collective-permute-done | bytes 73760 | tf_op jit(solution)/shard_map/ppermute | solution.py:425
  55.1 0.0 collective-permute-start.19
  55.1 0.0 all-to-all-done.1.refs_1_
  55.1 1.1 %shard_map.151 = bf16[256,128]{1,0:T(8,128)(2,1)} custom-call(s32[1]{0:T(128)} %bitcast.refs_6_.refs_0_, bf16[8,96,128]{2,1,0:T(8,128)(2,1)S(1)} %all-to-all-done.1.refs_1_, bf16[768,256]{1,0:T(8,128)(2,1)S(1)} %copy-done.1, s32[1,128]{1,0:T(1,128)S(1)} %get-tuple-element.45.after.refs_3_), custom_call_target="tpu_custom_call" | custom-call | tf_op jit(solution)/shard_map/pallas_call | solution.py:450
  56.2 0.0 collective-permute-done.13.refs_2_
  56.2 0.0 collective-permute-done.15.refs_4_
  56.2 0.0 collective-permute-done.17.refs_6_
  56.2 0.1 collective-permute-done.19.refs_8_
  56.4 1.1 %shard_map.153 = (f32[768,256]{1,0:T(8,128)}, f32[256,256]{1,0:T(8,128)}, f32[3,768]{1,0:T(4,128)}) custom-call(s32[1]{0:T(128)} %bitcast.1.refs_1_.refs_0_, bf16[288,128]{1,0:T(8,128)(2,1)S(1)} %shard_map.152.refs_1_, bf16[288,128]{1,0:T(8,128)(2,1)S(1)} %collective-permute-done.13.refs_2_, bf16[288,128]{1,0:T(8,128)(2,1)S(1)} %collective-permute-done.14.refs_3_, ...), custom_call_target="tpu_custom_call" | custom-call | tf_op jit(solution)/shard_map/pallas_call | solution.py:450
  (8 shorter events, 0.1 us)
Async XLA Ops:
  0.6 22.8 %copy-start = (f32[768,3]{0,1:T(4,128)S(1)}, f32[768,3]{0,1:T(4,128)}, u32[]{:S(2)}) copy-start(f32[768,3]{0,1:T(4,128)} %param.14) | copy-start | bytes 27652
  0.6 13.3 %copy-start.2 = (bf16[1536,256]{1,0:T(8,128)(2,1)S(1)}, bf16[1536,256]{1,0:T(8,128)(2,1)}, u32[]{:S(2)}) copy-start(bf16[1536,256]{1,0:T(8,128)(2,1)} %constant.18.clone.refs_2_) | copy-start | bytes 2359300
  3.1 10.9 %copy-start.3 = (f32[256,256]{1,0:T(8,128)S(1)}, f32[256,256]{1,0:T(8,128)}, u32[]{:S(2)}) copy-start(f32[256,256]{1,0:T(8,128)} %constant.19.clone.refs_3_) | copy-start | bytes 786436
  3.1 10.9 %copy-start.4 = (f32[8,4096]{1,0:T(8,128)S(1)}, f32[8,4096]{1,0:T(8,128)}, u32[]{:S(2)}) copy-start(f32[8,4096]{1,0:T(8,128)} %refs_0_.1) | copy-start | bytes 393220
  3.1 20.5 %all-to-all-start = ((bf16[32,32,128]{2,1,0:T(8,128)(2,1)}), bf16[32,32,128]{2,1,0:T(8,128)(2,1)S(1)}, u32[]{:S(2)}, u32[]{:S(2)}) async-start(bf16[32,32,128]{2,1,0:T(8,128)(2,1)} %get-tuple-element.31), calls=%async_computation | async-start | bytes 524288 | tf_op jit(solution)/shard_map/all_to_all | solution.py:467
  10.4 3.6 %copy-start.7 = (s32[1,128]{1,0:T(1,128)S(1)}, s32[1,128]{1,0:T(1,128)}, u32[]{:S(2)}) copy-start(s32[1,128]{1,0:T(1,128)} %refs_4_.1) | copy-start | bytes 1540
  10.4 8.7 %collective-permute-start.4 = (bf16[512,128]{1,0:T(8,128)(2,1)}, bf16[512,128]{1,0:T(8,128)(2,1)S(1)}, u32[]{:S(2)}, u32[]{:S(2)}) collective-permute-start(bf16[512,128]{1,0:T(8,128)(2,1)} %get-tuple-element.44.refs_7_), channel_id=1, source_target_pairs={{0,2},{1,3},{2,0},{3,1},{4,6},{5,7},{6,4},{7,5},{8,10},{9,11},{10,... | collective-permute-start | bytes 393224 | tf_op jit(solution)/shard_map/ppermute | solution.py:425
  12.3 8.9 %collective-permute-start.5 = (bf16[512,128]{1,0:T(8,128)(2,1)}, bf16[512,128]{1,0:T(8,128)(2,1)S(1)}, u32[]{:S(2)}, u32[]{:S(2)}) collective-permute-start(bf16[512,128]{1,0:T(8,128)(2,1)} %get-tuple-element.44.refs_7_), channel_id=1, source_target_pairs={{0,4},{1,5},{2,6},{3,7},{4,0},{5,1},{6,2},{7,3},{8,12},{9,13},{10,... | collective-permute-start | bytes 393224 | tf_op jit(solution)/shard_map/ppermute | solution.py:425
  13.7 9.0 %collective-permute-start.6 = (bf16[512,128]{1,0:T(8,128)(2,1)}, bf16[512,128]{1,0:T(8,128)(2,1)S(1)}, u32[]{:S(2)}, u32[]{:S(2)}) collective-permute-start(bf16[512,128]{1,0:T(8,128)(2,1)} %get-tuple-element.44.refs_7_), channel_id=1, source_target_pairs={{0,6},{1,7},{2,4},{3,5},{4,2},{5,3},{6,0},{7,1},{8,14},{9,15},{10,... | collective-permute-start | bytes 393224 | tf_op jit(solution)/shard_map/ppermute | solution.py:425
  14.0 15.2 %collective-permute-start.3 = (bf16[512,128]{1,0:T(8,128)(2,1)}, bf16[512,128]{1,0:T(8,128)(2,1)S(1)}, u32[]{:S(2)}, u32[]{:S(2)}) collective-permute-start(bf16[512,128]{1,0:T(8,128)(2,1)} %get-tuple-element.44.refs_7_), channel_id=1, source_target_pairs={{0,1},{1,0},{2,3},{3,2},{4,5},{5,4},{6,7},{7,6},{8,9},{9,8},{10,11... | collective-permute-start | bytes 393224 | tf_op jit(solution)/shard_map/ppermute | solution.py:425
  14.0 0.9 %copy-start.5 = (f32[8,4096]{1,0:T(8,128)S(1)}, f32[8,4096]{1,0:T(8,128)}, u32[]{:S(2)}) copy-start(f32[8,4096]{1,0:T(8,128)} %refs_1_.1) | copy-start | bytes 393220
  22.8 8.8 %collective-permute-start.7 = (bf16[512,128]{1,0:T(8,128)(2,1)S(1)}, bf16[512,128]{1,0:T(8,128)(2,1)S(1)}, u32[]{:S(2)}, u32[]{:S(2)}) collective-permute-start(bf16[512,128]{1,0:T(8,128)(2,1)S(1)} %get-tuple-element.46.refs_9_), channel_id=1, source_target_pairs={{0,1},{1,0},{2,3},{3,2},{4,5},{5,4},{6,7},{7,6},{8,9},{9,8},{10,11... | collective-permute-start | bytes 393224 | tf_op jit(solution)/shard_map/ppermute | solution.py:425
  22.9 12.0 %collective-permute-start.8 = (bf16[512,128]{1,0:T(8,128)(2,1)S(1)}, bf16[512,128]{1,0:T(8,128)(2,1)S(1)}, u32[]{:S(2)}, u32[]{:S(2)}) collective-permute-start(bf16[512,128]{1,0:T(8,128)(2,1)S(1)} %get-tuple-element.47.refs_11_), channel_id=1, source_target_pairs={{0,1},{1,0},{2,3},{3,2},{4,5},{5,4},{6,7},{7,6},{8,9},{9,8},{10,11... | collective-permute-start | bytes 393224 | tf_op jit(solution)/shard_map/ppermute | solution.py:425
  23.4 11.5 %collective-permute-start.9 = (bf16[512,128]{1,0:T(8,128)(2,1)S(1)}, bf16[512,128]{1,0:T(8,128)(2,1)S(1)}, u32[]{:S(2)}, u32[]{:S(2)}) collective-permute-start(bf16[512,128]{1,0:T(8,128)(2,1)S(1)} %get-tuple-element.48.refs_13_), channel_id=1, source_target_pairs={{0,1},{1,0},{2,3},{3,2},{4,5},{5,4},{6,7},{7,6},{8,9},{9,8},{10,11... | collective-permute-start | bytes 393224 | tf_op jit(solution)/shard_map/ppermute | solution.py:425
  27.9 7.0 %collective-permute-start = (bf16[8,32,128]{2,1,0:T(8,128)(2,1)S(1)}, bf16[8,32,128]{2,1,0:T(8,128)(2,1)S(1)}, u32[]{:S(2)}, u32[]{:S(2)}) collective-permute-start(bf16[8,32,128]{2,1,0:T(8,128)(2,1)S(1)} %get-tuple-element.41), channel_id=1, source_target_pairs={{0,8},{8,16},{16,24},{24,0},{1,9},{9,17},{17,25},{25,1},{2,10},{10... | collective-permute-start | bytes 196616 | tf_op jit(solution)/shard_map/ppermute | solution.py:529
  29.2 7.9 %collective-permute-start.1 = (bf16[8,32,128]{2,1,0:T(8,128)(2,1)S(1)}, bf16[8,32,128]{2,1,0:T(8,128)(2,1)S(1)}, u32[]{:S(2)}, u32[]{:S(2)}) collective-permute-start(bf16[8,32,128]{2,1,0:T(8,128)(2,1)S(1)} %get-tuple-element.42), channel_id=1, source_target_pairs={{0,16},{8,24},{16,0},{24,8},{1,17},{9,25},{17,1},{25,9},{2,18},{10... | collective-permute-start | bytes 196616 | tf_op jit(solution)/shard_map/ppermute | solution.py:529
  31.6 5.6 %collective-permute-start.2 = (bf16[8,32,128]{2,1,0:T(8,128)(2,1)S(1)}, bf16[8,32,128]{2,1,0:T(8,128)(2,1)S(1)}, u32[]{:S(2)}, u32[]{:S(2)}) collective-permute-start(bf16[8,32,128]{2,1,0:T(8,128)(2,1)S(1)} %get-tuple-element.43), channel_id=1, source_target_pairs={{0,24},{8,0},{16,8},{24,16},{1,25},{9,1},{17,9},{25,17},{2,26},{10... | collective-permute-start | bytes 196616 | tf_op jit(solution)/shard_map/ppermute | solution.py:529
  33.1 4.1 %copy-start.6 = (bf16[512,128]{1,0:T(8,128)(2,1)S(1)}, bf16[512,128]{1,0:T(8,128)(2,1)}, u32[]{:S(2)}) copy-start(bf16[512,128]{1,0:T(8,128)(2,1)} %get-tuple-element.44.refs_7_) | copy-start | bytes 393220
  38.3 16.8 %copy-start.1 = (bf16[768,256]{1,0:T(8,128)(2,1)S(1)}, bf16[768,256]{1,0:T(8,128)(2,1)}, u32[]{:S(2)}) copy-start(bf16[768,256]{1,0:T(8,128)(2,1)} %refs_2_.2) | copy-start | bytes 1179652
  38.3 7.5 %collective-permute-start.10 = (bf16[288,128]{1,0:T(8,128)(2,1)S(1)}, bf16[288,128]{1,0:T(8,128)(2,1)S(1)}, u32[]{:S(2)}, u32[]{:S(2)}) collective-permute-start(bf16[288,128]{1,0:T(8,128)(2,1)S(1)} %get-tuple-element.50.refs_0_), channel_id=1, source_target_pairs={{0,8},{8,16},{16,24},{24,0},{1,9},{9,17},{17,25},{25,1},{2,10},{10... | collective-permute-start | bytes 221192 | tf_op jit(solution)/shard_map/ppermute | solution.py:529
  40.0 7.3 %collective-permute-start.11 = (bf16[288,128]{1,0:T(8,128)(2,1)S(1)}, bf16[288,128]{1,0:T(8,128)(2,1)S(1)}, u32[]{:S(2)}, u32[]{:S(2)}) collective-permute-start(bf16[288,128]{1,0:T(8,128)(2,1)S(1)} %get-tuple-element.50.refs_0_), channel_id=1, source_target_pairs={{0,16},{8,24},{16,0},{24,8},{1,17},{9,25},{17,1},{25,9},{2,18},{10... | collective-permute-start | bytes 221192 | tf_op jit(solution)/shard_map/ppermute | solution.py:529
  41.3 6.0 %collective-permute-start.12 = (bf16[288,128]{1,0:T(8,128)(2,1)S(1)}, bf16[288,128]{1,0:T(8,128)(2,1)S(1)}, u32[]{:S(2)}, u32[]{:S(2)}) collective-permute-start(bf16[288,128]{1,0:T(8,128)(2,1)S(1)} %get-tuple-element.50.refs_0_), channel_id=1, source_target_pairs={{0,24},{8,0},{16,8},{24,16},{1,25},{9,1},{17,9},{25,17},{2,26},{10... | collective-permute-start | bytes 221192 | tf_op jit(solution)/shard_map/ppermute | solution.py:529
  42.4 12.7 %all-to-all-start.1 = ((bf16[8,96,128]{2,1,0:T(8,128)(2,1)}), bf16[8,96,128]{2,1,0:T(8,128)(2,1)S(1)}, u32[]{:S(2)}, u32[]{:S(2)}) async-start(bf16[8,96,128]{2,1,0:T(8,128)(2,1)} %get-tuple-element.49), calls=%async_computation.1 | async-start | bytes 393216 | tf_op jit(solution)/shard_map/all_to_all | solution.py:547
  47.4 5.7 %collective-permute-start.14 = (bf16[288,128]{1,0:T(8,128)(2,1)S(1)}, bf16[288,128]{1,0:T(8,128)(2,1)S(1)}, u32[]{:S(2)}, u32[]{:S(2)}) collective-permute-start(bf16[288,128]{1,0:T(8,128)(2,1)S(1)} %shard_map.152.refs_1_), channel_id=1, source_target_pairs={{0,2},{1,3},{2,0},{3,1},{4,6},{5,7},{6,4},{7,5},{8,10},{9,11},{10,... | collective-permute-start | bytes 221192 | tf_op jit(solution)/shard_map/ppermute | solution.py:425
  48.4 4.7 %collective-permute-start.16 = (bf16[288,128]{1,0:T(8,128)(2,1)S(1)}, bf16[288,128]{1,0:T(8,128)(2,1)S(1)}, u32[]{:S(2)}, u32[]{:S(2)}) collective-permute-start(bf16[288,128]{1,0:T(8,128)(2,1)S(1)} %shard_map.152.refs_1_), channel_id=1, source_target_pairs={{0,4},{1,5},{2,6},{3,7},{4,0},{5,1},{6,2},{7,3},{8,12},{9,13},{10,... | collective-permute-start | bytes 221192 | tf_op jit(solution)/shard_map/ppermute | solution.py:425
  49.3 5.8 %collective-permute-start.18 = (bf16[288,128]{1,0:T(8,128)(2,1)S(1)}, bf16[288,128]{1,0:T(8,128)(2,1)S(1)}, u32[]{:S(2)}, u32[]{:S(2)}) collective-permute-start(bf16[288,128]{1,0:T(8,128)(2,1)S(1)} %shard_map.152.refs_1_), channel_id=1, source_target_pairs={{0,6},{1,7},{2,4},{3,5},{4,2},{5,3},{6,0},{7,1},{8,14},{9,15},{10,... | collective-permute-start | bytes 221192 | tf_op jit(solution)/shard_map/ppermute | solution.py:425
  50.9 5.3 %collective-permute-start.13 = (bf16[288,128]{1,0:T(8,128)(2,1)S(1)}, bf16[288,128]{1,0:T(8,128)(2,1)S(1)}, u32[]{:S(2)}, u32[]{:S(2)}) collective-permute-start(bf16[288,128]{1,0:T(8,128)(2,1)S(1)} %shard_map.152.refs_1_), channel_id=1, source_target_pairs={{0,1},{1,0},{2,3},{3,2},{4,5},{5,4},{6,7},{7,6},{8,9},{9,8},{10,11... | collective-permute-start | bytes 221192 | tf_op jit(solution)/shard_map/ppermute | solution.py:425
  53.1 3.1 %collective-permute-start.15 = (bf16[288,128]{1,0:T(8,128)(2,1)S(1)}, bf16[288,128]{1,0:T(8,128)(2,1)S(1)}, u32[]{:S(2)}, u32[]{:S(2)}) collective-permute-start(bf16[288,128]{1,0:T(8,128)(2,1)S(1)} %collective-permute-done.14.refs_3_), channel_id=1, source_target_pairs={{0,1},{1,0},{2,3},{3,2},{4,5},{5,4},{6,7},{7,6},{8,9},{9,8},{10,11... | collective-permute-start | bytes 221192 | tf_op jit(solution)/shard_map/ppermute | solution.py:425
  53.1 3.1 %collective-permute-start.17 = (bf16[288,128]{1,0:T(8,128)(2,1)S(1)}, bf16[288,128]{1,0:T(8,128)(2,1)S(1)}, u32[]{:S(2)}, u32[]{:S(2)}) collective-permute-start(bf16[288,128]{1,0:T(8,128)(2,1)S(1)} %collective-permute-done.16.refs_5_), channel_id=1, source_target_pairs={{0,1},{1,0},{2,3},{3,2},{4,5},{5,4},{6,7},{7,6},{8,9},{9,8},{10,11... | collective-permute-start | bytes 221192 | tf_op jit(solution)/shard_map/ppermute | solution.py:425
  55.1 1.3 %collective-permute-start.19 = (bf16[288,128]{1,0:T(8,128)(2,1)S(1)}, bf16[288,128]{1,0:T(8,128)(2,1)S(1)}, u32[]{:S(2)}, u32[]{:S(2)}) collective-permute-start(bf16[288,128]{1,0:T(8,128)(2,1)S(1)} %collective-permute-done.18.refs_7_), channel_id=1, source_target_pairs={{0,1},{1,0},{2,3},{3,2},{4,5},{5,4},{6,7},{7,6},{8,9},{9,8},{10,11... | collective-permute-start | bytes 221192 | tf_op jit(solution)/shard_map/ppermute | solution.py:425

commit v5 on v4

--- a/solution.py
+++ b/solution.py
@@ -62,7 +62,9 @@
 
 
 def dot_pairs(left, right):
-    return dot(left[0], right[0]) + dot(left[0], right[1]) + dot(left[1], right[0])
+    deep_left = jnp.concatenate([left[0], left[0], left[1]], axis=1)
+    deep_right = jnp.concatenate([right[0], right[1], right[0]], axis=0)
+    return dot(deep_left, deep_right)
 
 
 def forward(signals, first, second, twist):
@@ -491,9 +493,6 @@
         twist,
         sink_order,
     )
-    if whole:
-        pieces = [swapped(own, plane, k) for k in range(2, plane, 2)]
-        pieces = call(pass_kernel, [shape(own.shape, bf16)] * len(pieces), order, *pieces)
     line = lax.axis_index("seq").astype(jnp.int32).reshape(1)
     place = lax.axis_index("fft").astype(jnp.int32).reshape(1)
     scalar = pl.BlockSpec(memory_space=pltpu.SMEM)
@@ -513,6 +512,12 @@
         in_specs=[held] * 6 + [scalar],
         scratch_shapes=[pltpu.VMEM((lines, *chunk), bf16)] if whole else [],
     )
+    if whole:
+        pieces = [swapped(own, plane, k) for k in (1, *range(2, plane, 2))]
+        beside, *pieces = call(
+            pass_kernel, [shape(own.shape, bf16)] * len(pieces), short, *pieces
+        )
+        pieces = [own, beside] + [a for p in pieces for a in (p, swapped(p, plane, 1))]
     grad_one, grad_two, short = call(
         lambda *refs: filter_grads_kernel(scale / length, *refs),
         (shape(filter_one.shape), shape(filter_two.shape), shape(short.shape)),
@@ -540,7 +545,7 @@
             place,
             short,
             *met,
-            *[a for p in (own, *pieces) for a in (p, swapped(p, plane, 1))],
+            *pieces,
             in_specs=[scalar] * 2 + [held] * (1 + lines + plane),
         )
         partials = [partial] + [ahead(partial, k) for k in range(1, lines)]

time: 57.8 us -> 56.4 us (0.976)
  starting transfers between devices: 28.3 us -> 25 us
  local copies, waits for them, and re-layouts: 1.11 us -> 2.27 us
  waiting for transfers between devices: 14.5 us -> 15.2 us
    ppermute x14, waiting for transfers between devices: 10.7 us -> 4.79 us  [swapped(): return lax.ppermute(value, 'fft', [(i, i ^ distance) for i in range(plane)])]
    all_to_all x1, waiting for transfers between devices: 0.01 us -> 3.55 us  [local(): lax.all_to_all(streams, AXES, split_axis=0, concat_axis=0, tiled=True)]
    ppermute x6, starting transfers between devices: 9.29 us -> 5.77 us  [ahead(): return lax.ppermute(value, 'seq', pairs)]
    ppermute x6, waiting for transfers between devices: 3.86 us -> 6.86 us  [ahead(): return lax.ppermute(value, 'seq', pairs)]
    unnamed x16 -> x20, local copies, waits for them, and re-layouts: 0.94 us -> 2.1 us
  transfers between devices with their start and end apart: 22 -> 22, of which waited for: 9 -> 8; matrix products, arithmetic and copies ran while one was open for 0% -> 0% of each run, Pallas kernels for 14% -> 15%
where the time goes in v5:
time: 56.4 us; the launch traced here: 56.1 us
  starting transfers between devices  25 us (44%)
  waiting for transfers between devices  15.2 us (27%)
  Pallas kernels  12.8 us (23%)
  local copies, waits for them, and re-layouts  2.27 us (4%)
  between operations  0.81 us (1%)
    pallas_call x8, Pallas kernels, call(): pl.pallas_call(kernel, out_shape=outs, compiler_params=PARAMS, **options)  10.4 us
    ppermute x14, starting transfers between devices, swapped(): return lax.ppermute(value, 'fft', [(i, i ^ distance) for i in range(plane)])  8.52 us
    all_to_all x1, starting transfers between devices, local(): lax.all_to_all(streams, AXES, split_axis=0, concat_axis=0, tiled=True)  7.3 us
    ppermute x6, waiting for transfers between devices, ahead(): return lax.ppermute(value, 'seq', pairs)  6.86 us
    ppermute x6, starting transfers between devices, ahead(): return lax.ppermute(value, 'seq', pairs)  5.77 us
    ppermute x14, waiting for transfers between devices, swapped(): return lax.ppermute(value, 'fft', [(i, i ^ distance) for i in range(plane)])  4.79 us
    all_to_all x1, waiting for transfers between devices, local(): lax.all_to_all(streams, AXES, split_axis=0, concat_axis=0, tiled=True)  3.55 us
    all_to_all x1, starting transfers between devices, local(): back = lax.all_to_all(moved, 'fft', split_axis=0, concat_axis=0, tiled=True)  3.39 us
  transfers between devices with their start and end apart: 22, of which 8 were waited for; matrix products, arithmetic and copies ran while one was open for 0% of the time, Pallas kernels for 15%

profile of v5, /device:TPU:0, one launch (start us, length us, event | category | flops | bytes accessed | tf_op | source)
XLA Modules:
  0.0 56.1 jit_solution(5656847187297953877)
XLA Ops:
  0.6 0.0 copy-start
  0.6 0.0 copy-start.2
  0.7 2.4 %shard_map.145 = (bf16[32,32,128]{2,1,0:T(8,128)(2,1)}, bf16[512,128]{1,0:T(8,128)(2,1)}) custom-call(bf16[256,128]{1,0:T(8,128)(2,1)} %features_at.1, s32[1,128]{1,0:T(1,128)} %refs_4_.1, bf16[256,128]{1,0:T(8,128)(2,1)} %cotangent_at.1, bf16[768,256]{1,0:T(8,128)(2,1)} %refs_2_.2, bf16[256,256]{1,0:T(8,128)(2,1)} %w_out_at.1), custom_call_target="tpu_custom_call" | custom-call | tf_op jit(solution)/shard_map/pallas_call | solution.py:455
  3.1 0.0 copy-start.3
  3.1 0.0 copy-start.4
  3.1 7.3 %all-to-all-start = ((bf16[32,32,128]{2,1,0:T(8,128)(2,1)}), bf16[32,32,128]{2,1,0:T(8,128)(2,1)S(1)}, u32[]{:S(2)}, u32[]{:S(2)}) async-start(bf16[32,32,128]{2,1,0:T(8,128)(2,1)} %get-tuple-element.32), calls=%async_computation | async-start | bytes 524288 | tf_op jit(solution)/shard_map/all_to_all | solution.py:469
  10.4 0.3 collective-permute-start.3
  10.7 1.7 %collective-permute-start.4 = (bf16[512,128]{1,0:T(8,128)(2,1)}, bf16[512,128]{1,0:T(8,128)(2,1)S(1)}, u32[]{:S(2)}, u32[]{:S(2)}) collective-permute-start(bf16[512,128]{1,0:T(8,128)(2,1)} %get-tuple-element.45.refs_7_), channel_id=1, source_target_pairs={{0,2},{1,3},{2,0},{3,1},{4,6},{5,7},{6,4},{7,5},{8,10},{9,11},{10,... | collective-permute-start | bytes 393224 | tf_op jit(solution)/shard_map/ppermute | solution.py:427
  12.4 1.5 %collective-permute-start.5 = (bf16[512,128]{1,0:T(8,128)(2,1)}, bf16[512,128]{1,0:T(8,128)(2,1)S(1)}, u32[]{:S(2)}, u32[]{:S(2)}) collective-permute-start(bf16[512,128]{1,0:T(8,128)(2,1)} %get-tuple-element.45.refs_7_), channel_id=1, source_target_pairs={{0,4},{1,5},{2,6},{3,7},{4,0},{5,1},{6,2},{7,3},{8,12},{9,13},{10,... | collective-permute-start | bytes 393224 | tf_op jit(solution)/shard_map/ppermute | solution.py:427
  13.9 0.3 collective-permute-start.6
  14.2 0.0 copy-done
  14.2 0.1 dynamic-slice_bitcast_fusion
  14.3 0.1 copy.19.refs_1_
  14.4 0.9 %copy-done.5 = f32[8,4096]{1,0:T(8,128)S(1)} copy-done((f32[8,4096]{1,0:T(8,128)S(1)}, f32[8,4096]{1,0:T(8,128)}, u32[]{:S(2)}) %copy-start.5) | copy-done | bytes 131096
  15.3 0.7 %copy-done.7 = s32[1,128]{1,0:T(1,128)S(1)} copy-done((s32[1,128]{1,0:T(1,128)S(1)}, s32[1,128]{1,0:T(1,128)}, u32[]{:S(2)}) %copy-start.7) | copy-done | bytes 536
  16.0 1.0 %shard_map.146 = (f32[256,256]{1,0:T(8,128)S(1)}, f32[256,256]{1,0:T(8,128)S(1)}, bf16[1536,256]{1,0:T(8,128)(2,1)S(1)}, f32[256,256]{1,0:T(8,128)S(1)}, s32[1,128]{1,0:T(1,128)S(1)}) custom-call(f32[8,4096]{1,0:T(8,128)S(1)} %copy-done.4, f32[8,4096]{1,0:T(8,128)S(1)} %copy-done.5, bf16[1536,256]{1,0:T(8,128)(2,1)S(1)} %copy-done.2, ...), custom_call_target="tpu_custom_call" | custom-call | tf_op jit(solution)/shard_map/pallas_call | solution.py:452
  17.0 0.0 copy-start.8
  17.0 0.5 copy-done.8
  17.5 3.6 %all-to-all-done.refs_0_ = bf16[32,32,128]{2,1,0:T(8,128)(2,1)S(1)} async-done(((bf16[32,32,128]{2,1,0:T(8,128)(2,1)}), bf16[32,32,128]{2,1,0:T(8,128)(2,1)S(1)}, u32[]{:S(2)}, u32[]{:S(2)}) %all-to-all-start) | async-done | bytes 262176 | tf_op jit(solution)/shard_map/all_to_all | solution.py:469
  21.1 4.2 %shard_map.147 = (f32[8,128]{1,0:T(8,128)S(1)}, f32[256,256]{1,0:T(8,128)S(1)}, f32[256,256]{1,0:T(8,128)S(1)}, bf16[8,32,128]{2,1,0:T(8,128)(2,1)S(1)}, bf16[8,...) custom-call(bf16[32,32,128]{2,1,0:T(8,128)(2,1)S(1)} %all-to-all-done.refs_0_, ...), custom_call_target="tpu_custom_call" | custom-call | tf_op jit(solution)/shard_map/pallas_call | solution.py:452
  25.3 1.0 %collective-permute-start = (bf16[8,32,128]{2,1,0:T(8,128)(2,1)S(1)}, bf16[8,32,128]{2,1,0:T(8,128)(2,1)S(1)}, u32[]{:S(2)}, u32[]{:S(2)}) collective-permute-start(bf16[8,32,128]{2,1,0:T(8,128)(2,1)S(1)} %get-tuple-element.42), channel_id=1, source_target_pairs={{0,8},{8,16},{16,24},{24,0},{1,9},{9,17},{17,25},{25,1},{2,10},{10... | collective-permute-start | bytes 196616 | tf_op jit(solution)/shard_map/ppermute | solution.py:534
  26.3 0.0 collective-permute-done.3.refs_0_
  26.3 0.0 collective-permute-done.4.refs_1_
  26.3 0.0 collective-permute-done.5.refs_2_
  26.3 0.0 collective-permute-done.6.refs_3_
  26.4 0.1 collective-permute-start.7
  26.4 0.5 collective-permute-start.8
  26.9 0.1 collective-permute-start.9
  27.0 0.9 %collective-permute-start.1 = (bf16[8,32,128]{2,1,0:T(8,128)(2,1)S(1)}, bf16[8,32,128]{2,1,0:T(8,128)(2,1)S(1)}, u32[]{:S(2)}, u32[]{:S(2)}) collective-permute-start(bf16[8,32,128]{2,1,0:T(8,128)(2,1)S(1)} %get-tuple-element.43), channel_id=1, source_target_pairs={{0,16},{8,24},{16,0},{24,8},{1,17},{9,25},{17,1},{25,9},{2,18},{10... | collective-permute-start | bytes 196616 | tf_op jit(solution)/shard_map/ppermute | solution.py:534
  27.9 3.8 %collective-permute-done.refs_4_ = bf16[8,32,128]{2,1,0:T(8,128)(2,1)S(1)} collective-permute-done((bf16[8,32,128]{2,1,0:T(8,128)(2,1)S(1)}, bf16[8,32,128]{2,1,0:T(8,128)(2,1)S(1)}, u32[]{:S(2)}, u32[]{:S(2)}) %collective-permute-start) | collective-permute-done | bytes 65568 | tf_op jit(solution)/shard_map/ppermute | solution.py:534
  31.8 0.0 collective-permute-start.2
  31.8 1.8 %shard_map.148 = (f32[8,4096]{1,0:T(8,128)}, f32[8,4096]{1,0:T(8,128)}, f32[8,128]{1,0:T(8,128)S(1)}) custom-call(f32[256,256]{1,0:T(8,128)S(1)} %get-tuple-element.37.refs_0_, f32[256,256]{1,0:T(8,128)S(1)} %get-tuple-element.38.refs_1_, bf16[1536,256]{1,0:T(8,128)(2,1)S(1)} %get-tuple-element.35.refs_4_.refs_2_, ...), custom_call_target="tpu_custom_call" | custom-call | tf_op jit(solution)/shard_map/pallas_call | solution.py:452
  33.6 0.7 %collective-permute-done.1.refs_5_ = bf16[8,32,128]{2,1,0:T(8,128)(2,1)S(1)} collective-permute-done((bf16[8,32,128]{2,1,0:T(8,128)(2,1)S(1)}, bf16[8,32,128]{2,1,0:T(8,128)(2,1)S(1)}, u32[]{:S(2)}, u32[]{:S(2)}) %collective-permute-start.1) | collective-permute-done | bytes 65568 | tf_op jit(solution)/shard_map/ppermute | solution.py:534
  34.3 1.7 %collective-permute-done.2.refs_6_ = bf16[8,32,128]{2,1,0:T(8,128)(2,1)S(1)} collective-permute-done((bf16[8,32,128]{2,1,0:T(8,128)(2,1)S(1)}, bf16[8,32,128]{2,1,0:T(8,128)(2,1)S(1)}, u32[]{:S(2)}, u32[]{:S(2)}) %collective-permute-start.2) | collective-permute-done | bytes 65568 | tf_op jit(solution)/shard_map/ppermute | solution.py:534
  36.0 0.0 collective-permute-done.7.refs_10_
  36.0 0.0 collective-permute-done.8.refs_12_
  36.0 0.0 collective-permute-done.9.refs_14_
  36.1 1.1 %shard_map.150 = (bf16[288,128]{1,0:T(8,128)(2,1)S(1)}, bf16[8,96,128]{2,1,0:T(8,128)(2,1)}) custom-call(s32[1]{0:T(128)} %bitcast.refs_6_.refs_0_, s32[1]{0:T(128)} %bitcast.1.refs_1_.refs_0_, f32[8,128]{1,0:T(8,128)S(1)} %get-tuple-element.40.refs_2_, bf16[8,32,128]{2,1,0:T(8,128)(2,1)S(1)} %get-tuple-element.41.refs_3_, ...), custom_call_target="tpu_custom_call" | custom-call | tf_op jit(solution)/shard_map/pallas_call | solution.py:452
  37.1 0.2 collective-permute-start.10
  37.3 2.2 %collective-permute-start.11 = (bf16[288,128]{1,0:T(8,128)(2,1)S(1)}, bf16[288,128]{1,0:T(8,128)(2,1)S(1)}, u32[]{:S(2)}, u32[]{:S(2)}) collective-permute-start(bf16[288,128]{1,0:T(8,128)(2,1)S(1)} %get-tuple-element.52.refs_0_), channel_id=1, source_target_pairs={{0,16},{8,24},{16,0},{24,8},{1,17},{9,25},{17,1},{25,9},{2,18},{10... | collective-permute-start | bytes 221192 | tf_op jit(solution)/shard_map/ppermute | solution.py:534
  39.5 1.5 %collective-permute-start.12 = (bf16[288,128]{1,0:T(8,128)(2,1)S(1)}, bf16[288,128]{1,0:T(8,128)(2,1)S(1)}, u32[]{:S(2)}, u32[]{:S(2)}) collective-permute-start(bf16[288,128]{1,0:T(8,128)(2,1)S(1)} %get-tuple-element.52.refs_0_), channel_id=1, source_target_pairs={{0,24},{8,0},{16,8},{24,16},{1,25},{9,1},{17,9},{25,17},{2,26},{10... | collective-permute-start | bytes 221192 | tf_op jit(solution)/shard_map/ppermute | solution.py:534
  41.0 3.4 %all-to-all-start.1 = ((bf16[8,96,128]{2,1,0:T(8,128)(2,1)}), bf16[8,96,128]{2,1,0:T(8,128)(2,1)S(1)}, u32[]{:S(2)}, u32[]{:S(2)}) async-start(bf16[8,96,128]{2,1,0:T(8,128)(2,1)} %get-tuple-element.50), calls=%async_computation.1 | async-start | bytes 393216 | tf_op jit(solution)/shard_map/all_to_all | solution.py:552
  44.4 0.0 collective-permute-done.10.refs_1_
  44.4 0.5 collective-permute-done.11.refs_2_
  44.9 0.0 collective-permute-done.12.refs_3_
  45.0 0.0 copy-start.9
  45.0 1.5 %collective-permute-start.14 = (bf16[288,128]{1,0:T(8,128)(2,1)S(1)}, bf16[288,128]{1,0:T(8,128)(2,1)S(1)}, u32[]{:S(2)}, u32[]{:S(2)}) collective-permute-start(bf16[288,128]{1,0:T(8,128)(2,1)S(1)} %shard_map.152.refs_1_), channel_id=1, source_target_pairs={{0,2},{1,3},{2,0},{3,1},{4,6},{5,7},{6,4},{7,5},{8,10},{9,11},{10,... | collective-permute-start | bytes 221192 | tf_op jit(solution)/shard_map/ppermute | solution.py:427
  46.4 1.5 %collective-permute-start.16 = (bf16[288,128]{1,0:T(8,128)(2,1)S(1)}, bf16[288,128]{1,0:T(8,128)(2,1)S(1)}, u32[]{:S(2)}, u32[]{:S(2)}) collective-permute-start(bf16[288,128]{1,0:T(8,128)(2,1)S(1)} %shard_map.152.refs_1_), channel_id=1, source_target_pairs={{0,4},{1,5},{2,6},{3,7},{4,0},{5,1},{6,2},{7,3},{8,12},{9,13},{10,... | collective-permute-start | bytes 221192 | tf_op jit(solution)/shard_map/ppermute | solution.py:427
  47.9 0.6 %collective-permute-start.18 = (bf16[288,128]{1,0:T(8,128)(2,1)S(1)}, bf16[288,128]{1,0:T(8,128)(2,1)S(1)}, u32[]{:S(2)}, u32[]{:S(2)}) collective-permute-start(bf16[288,128]{1,0:T(8,128)(2,1)S(1)} %shard_map.152.refs_1_), channel_id=1, source_target_pairs={{0,6},{1,7},{2,4},{3,5},{4,2},{5,3},{6,0},{7,1},{8,14},{9,15},{10,... | collective-permute-start | bytes 221192 | tf_op jit(solution)/shard_map/ppermute | solution.py:427
  48.5 0.0 collective-permute-start.13
  48.5 3.1 %collective-permute-done.14.refs_3_ = bf16[288,128]{1,0:T(8,128)(2,1)S(1)} collective-permute-done((bf16[288,128]{1,0:T(8,128)(2,1)S(1)}, bf16[288,128]{1,0:T(8,128)(2,1)S(1)}, u32[]{:S(2)}, u32[]{:S(2)}) %collective-permute-start.14) | collective-permute-done | bytes 73760 | tf_op jit(solution)/shard_map/ppermute | solution.py:427
  51.7 0.0 collective-permute-start.15
  51.7 0.0 collective-permute-done.16.refs_5_
  51.7 0.5 collective-permute-start.17
  52.2 1.5 %collective-permute-done.18.refs_7_ = bf16[288,128]{1,0:T(8,128)(2,1)S(1)} collective-permute-done((bf16[288,128]{1,0:T(8,128)(2,1)S(1)}, bf16[288,128]{1,0:T(8,128)(2,1)S(1)}, u32[]{:S(2)}, u32[]{:S(2)}) %collective-permute-start.18) | collective-permute-done | bytes 73760 | tf_op jit(solution)/shard_map/ppermute | solution.py:427
  53.7 0.0 collective-permute-start.19
  53.7 0.0 all-to-all-done.1.refs_1_
  53.7 0.0 copy-done.9
  53.7 1.1 %shard_map.151 = bf16[256,128]{1,0:T(8,128)(2,1)} custom-call(s32[1]{0:T(128)} %bitcast.refs_6_.refs_0_, bf16[8,96,128]{2,1,0:T(8,128)(2,1)S(1)} %all-to-all-done.1.refs_1_, bf16[768,256]{1,0:T(8,128)(2,1)S(1)} %copy-done.1, s32[1,128]{1,0:T(1,128)S(1)} %copy-done.9), custom_call_target="tpu_custom_call" | custom-call | tf_op jit(solution)/shard_map/pallas_call | solution.py:452
  54.8 0.0 collective-permute-done.13.refs_2_
  54.8 0.0 collective-permute-done.15.refs_4_
  54.8 0.0 collective-permute-done.17.refs_6_
  54.8 0.1 collective-permute-done.19.refs_8_
  55.0 1.1 %shard_map.153 = (f32[768,256]{1,0:T(8,128)}, f32[256,256]{1,0:T(8,128)}, f32[3,768]{1,0:T(4,128)}) custom-call(s32[1]{0:T(128)} %bitcast.1.refs_1_.refs_0_, bf16[288,128]{1,0:T(8,128)(2,1)S(1)} %shard_map.152.refs_1_, bf16[288,128]{1,0:T(8,128)(2,1)S(1)} %collective-permute-done.13.refs_2_, bf16[288,128]{1,0:T(8,128)(2,1)S(1)} %collective-permute-done.14.refs_3_, ...), custom_call_target="tpu_custom_call" | custom-call | tf_op jit(solution)/shard_map/pallas_call | solution.py:452
  (12 shorter events, 0.1 us)
Async XLA Ops:
  0.6 13.6 %copy-start = (f32[768,3]{0,1:T(4,128)S(1)}, f32[768,3]{0,1:T(4,128)}, u32[]{:S(2)}) copy-start(f32[768,3]{0,1:T(4,128)} %param.14) | copy-start | bytes 27652
  0.6 13.7 %copy-start.2 = (bf16[1536,256]{1,0:T(8,128)(2,1)S(1)}, bf16[1536,256]{1,0:T(8,128)(2,1)}, u32[]{:S(2)}) copy-start(bf16[1536,256]{1,0:T(8,128)(2,1)} %constant.18.clone.refs_2_) | copy-start | bytes 2359300
  3.1 11.3 %copy-start.3 = (f32[256,256]{1,0:T(8,128)S(1)}, f32[256,256]{1,0:T(8,128)}, u32[]{:S(2)}) copy-start(f32[256,256]{1,0:T(8,128)} %constant.19.clone.refs_3_) | copy-start | bytes 786436
  3.1 11.3 %copy-start.4 = (f32[8,4096]{1,0:T(8,128)S(1)}, f32[8,4096]{1,0:T(8,128)}, u32[]{:S(2)}) copy-start(f32[8,4096]{1,0:T(8,128)} %refs_0_.1) | copy-start | bytes 393220
  3.1 18.0 %all-to-all-start = ((bf16[32,32,128]{2,1,0:T(8,128)(2,1)}), bf16[32,32,128]{2,1,0:T(8,128)(2,1)S(1)}, u32[]{:S(2)}, u32[]{:S(2)}) async-start(bf16[32,32,128]{2,1,0:T(8,128)(2,1)} %get-tuple-element.32), calls=%async_computation | async-start | bytes 524288 | tf_op jit(solution)/shard_map/all_to_all | solution.py:469
  10.4 15.9 %collective-permute-start.3 = (bf16[512,128]{1,0:T(8,128)(2,1)}, bf16[512,128]{1,0:T(8,128)(2,1)S(1)}, u32[]{:S(2)}, u32[]{:S(2)}) collective-permute-start(bf16[512,128]{1,0:T(8,128)(2,1)} %get-tuple-element.45.refs_7_), channel_id=1, source_target_pairs={{0,1},{1,0},{2,3},{3,2},{4,5},{5,4},{6,7},{7,6},{8,9},{9,8},{10,11... | collective-permute-start | bytes 393224 | tf_op jit(solution)/shard_map/ppermute | solution.py:427
  10.7 15.6 %collective-permute-start.4 = (bf16[512,128]{1,0:T(8,128)(2,1)}, bf16[512,128]{1,0:T(8,128)(2,1)S(1)}, u32[]{:S(2)}, u32[]{:S(2)}) collective-permute-start(bf16[512,128]{1,0:T(8,128)(2,1)} %get-tuple-element.45.refs_7_), channel_id=1, source_target_pairs={{0,2},{1,3},{2,0},{3,1},{4,6},{5,7},{6,4},{7,5},{8,10},{9,11},{10,... | collective-permute-start | bytes 393224 | tf_op jit(solution)/shard_map/ppermute | solution.py:427
  12.4 13.9 %collective-permute-start.5 = (bf16[512,128]{1,0:T(8,128)(2,1)}, bf16[512,128]{1,0:T(8,128)(2,1)S(1)}, u32[]{:S(2)}, u32[]{:S(2)}) collective-permute-start(bf16[512,128]{1,0:T(8,128)(2,1)} %get-tuple-element.45.refs_7_), channel_id=1, source_target_pairs={{0,4},{1,5},{2,6},{3,7},{4,0},{5,1},{6,2},{7,3},{8,12},{9,13},{10,... | collective-permute-start | bytes 393224 | tf_op jit(solution)/shard_map/ppermute | solution.py:427
  13.9 12.4 %collective-permute-start.6 = (bf16[512,128]{1,0:T(8,128)(2,1)}, bf16[512,128]{1,0:T(8,128)(2,1)S(1)}, u32[]{:S(2)}, u32[]{:S(2)}) collective-permute-start(bf16[512,128]{1,0:T(8,128)(2,1)} %get-tuple-element.45.refs_7_), channel_id=1, source_target_pairs={{0,6},{1,7},{2,4},{3,5},{4,2},{5,3},{6,0},{7,1},{8,14},{9,15},{10,... | collective-permute-start | bytes 393224 | tf_op jit(solution)/shard_map/ppermute | solution.py:427
  14.4 0.9 %copy-start.5 = (f32[8,4096]{1,0:T(8,128)S(1)}, f32[8,4096]{1,0:T(8,128)}, u32[]{:S(2)}) copy-start(f32[8,4096]{1,0:T(8,128)} %refs_1_.1) | copy-start | bytes 393220
  15.3 0.7 %copy-start.7 = (s32[1,128]{1,0:T(1,128)S(1)}, s32[1,128]{1,0:T(1,128)}, u32[]{:S(2)}) copy-start(s32[1,128]{1,0:T(1,128)} %refs_4_.1) | copy-start | bytes 1540
  17.0 0.5 copy-start.8
  25.3 6.5 %collective-permute-start = (bf16[8,32,128]{2,1,0:T(8,128)(2,1)S(1)}, bf16[8,32,128]{2,1,0:T(8,128)(2,1)S(1)}, u32[]{:S(2)}, u32[]{:S(2)}) collective-permute-start(bf16[8,32,128]{2,1,0:T(8,128)(2,1)S(1)} %get-tuple-element.42), channel_id=1, source_target_pairs={{0,8},{8,16},{16,24},{24,0},{1,9},{9,17},{17,25},{25,1},{2,10},{10... | collective-permute-start | bytes 196616 | tf_op jit(solution)/shard_map/ppermute | solution.py:534
  26.4 9.7 %collective-permute-start.7 = (bf16[512,128]{1,0:T(8,128)(2,1)S(1)}, bf16[512,128]{1,0:T(8,128)(2,1)S(1)}, u32[]{:S(2)}, u32[]{:S(2)}) collective-permute-start(bf16[512,128]{1,0:T(8,128)(2,1)S(1)} %get-tuple-element.47.refs_9_), channel_id=1, source_target_pairs={{0,1},{1,0},{2,3},{3,2},{4,5},{5,4},{6,7},{7,6},{8,9},{9,8},{10,11... | collective-permute-start | bytes 393224 | tf_op jit(solution)/shard_map/ppermute | solution.py:427
  26.4 9.6 %collective-permute-start.8 = (bf16[512,128]{1,0:T(8,128)(2,1)S(1)}, bf16[512,128]{1,0:T(8,128)(2,1)S(1)}, u32[]{:S(2)}, u32[]{:S(2)}) collective-permute-start(bf16[512,128]{1,0:T(8,128)(2,1)S(1)} %get-tuple-element.48.refs_11_), channel_id=1, source_target_pairs={{0,1},{1,0},{2,3},{3,2},{4,5},{5,4},{6,7},{7,6},{8,9},{9,8},{10,11... | collective-permute-start | bytes 393224 | tf_op jit(solution)/shard_map/ppermute | solution.py:427
  26.9 9.1 %collective-permute-start.9 = (bf16[512,128]{1,0:T(8,128)(2,1)S(1)}, bf16[512,128]{1,0:T(8,128)(2,1)S(1)}, u32[]{:S(2)}, u32[]{:S(2)}) collective-permute-start(bf16[512,128]{1,0:T(8,128)(2,1)S(1)} %get-tuple-element.49.refs_13_), channel_id=1, source_target_pairs={{0,1},{1,0},{2,3},{3,2},{4,5},{5,4},{6,7},{7,6},{8,9},{9,8},{10,11... | collective-permute-start | bytes 393224 | tf_op jit(solution)/shard_map/ppermute | solution.py:427
  27.0 7.3 %collective-permute-start.1 = (bf16[8,32,128]{2,1,0:T(8,128)(2,1)S(1)}, bf16[8,32,128]{2,1,0:T(8,128)(2,1)S(1)}, u32[]{:S(2)}, u32[]{:S(2)}) collective-permute-start(bf16[8,32,128]{2,1,0:T(8,128)(2,1)S(1)} %get-tuple-element.43), channel_id=1, source_target_pairs={{0,16},{8,24},{16,0},{24,8},{1,17},{9,25},{17,1},{25,9},{2,18},{10... | collective-permute-start | bytes 196616 | tf_op jit(solution)/shard_map/ppermute | solution.py:534
  31.8 4.3 %collective-permute-start.2 = (bf16[8,32,128]{2,1,0:T(8,128)(2,1)S(1)}, bf16[8,32,128]{2,1,0:T(8,128)(2,1)S(1)}, u32[]{:S(2)}, u32[]{:S(2)}) collective-permute-start(bf16[8,32,128]{2,1,0:T(8,128)(2,1)S(1)} %get-tuple-element.44), channel_id=1, source_target_pairs={{0,24},{8,0},{16,8},{24,16},{1,25},{9,1},{17,9},{25,17},{2,26},{10... | collective-permute-start | bytes 196616 | tf_op jit(solution)/shard_map/ppermute | solution.py:534
  31.8 4.3 %copy-start.6 = (bf16[512,128]{1,0:T(8,128)(2,1)S(1)}, bf16[512,128]{1,0:T(8,128)(2,1)}, u32[]{:S(2)}) copy-start(bf16[512,128]{1,0:T(8,128)(2,1)} %get-tuple-element.45.refs_7_) | copy-start | bytes 393220
  37.1 16.6 %copy-start.1 = (bf16[768,256]{1,0:T(8,128)(2,1)S(1)}, bf16[768,256]{1,0:T(8,128)(2,1)}, u32[]{:S(2)}) copy-start(bf16[768,256]{1,0:T(8,128)(2,1)} %refs_2_.2) | copy-start | bytes 1179652
  37.1 7.2 %collective-permute-start.10 = (bf16[288,128]{1,0:T(8,128)(2,1)S(1)}, bf16[288,128]{1,0:T(8,128)(2,1)S(1)}, u32[]{:S(2)}, u32[]{:S(2)}) collective-permute-start(bf16[288,128]{1,0:T(8,128)(2,1)S(1)} %get-tuple-element.52.refs_0_), channel_id=1, source_target_pairs={{0,8},{8,16},{16,24},{24,0},{1,9},{9,17},{17,25},{25,1},{2,10},{10... | collective-permute-start | bytes 221192 | tf_op jit(solution)/shard_map/ppermute | solution.py:534
  37.3 7.6 %collective-permute-start.11 = (bf16[288,128]{1,0:T(8,128)(2,1)S(1)}, bf16[288,128]{1,0:T(8,128)(2,1)S(1)}, u32[]{:S(2)}, u32[]{:S(2)}) collective-permute-start(bf16[288,128]{1,0:T(8,128)(2,1)S(1)} %get-tuple-element.52.refs_0_), channel_id=1, source_target_pairs={{0,16},{8,24},{16,0},{24,8},{1,17},{9,25},{17,1},{25,9},{2,18},{10... | collective-permute-start | bytes 221192 | tf_op jit(solution)/shard_map/ppermute | solution.py:534
  39.5 5.4 %collective-permute-start.12 = (bf16[288,128]{1,0:T(8,128)(2,1)S(1)}, bf16[288,128]{1,0:T(8,128)(2,1)S(1)}, u32[]{:S(2)}, u32[]{:S(2)}) collective-permute-start(bf16[288,128]{1,0:T(8,128)(2,1)S(1)} %get-tuple-element.52.refs_0_), channel_id=1, source_target_pairs={{0,24},{8,0},{16,8},{24,16},{1,25},{9,1},{17,9},{25,17},{2,26},{10... | collective-permute-start | bytes 221192 | tf_op jit(solution)/shard_map/ppermute | solution.py:534
  41.0 12.7 %all-to-all-start.1 = ((bf16[8,96,128]{2,1,0:T(8,128)(2,1)}), bf16[8,96,128]{2,1,0:T(8,128)(2,1)S(1)}, u32[]{:S(2)}, u32[]{:S(2)}) async-start(bf16[8,96,128]{2,1,0:T(8,128)(2,1)} %get-tuple-element.50), calls=%async_computation.1 | async-start | bytes 393216 | tf_op jit(solution)/shard_map/all_to_all | solution.py:552
  45.0 8.7 %copy-start.9 = (s32[1,128]{1,0:T(1,128)S(1)}, s32[1,128]{1,0:T(1,128)}, u32[]{:S(2)}) copy-start(s32[1,128]{1,0:T(1,128)} %copy-done.8) | copy-start | bytes 1540
  45.0 6.7 %collective-permute-start.14 = (bf16[288,128]{1,0:T(8,128)(2,1)S(1)}, bf16[288,128]{1,0:T(8,128)(2,1)S(1)}, u32[]{:S(2)}, u32[]{:S(2)}) collective-permute-start(bf16[288,128]{1,0:T(8,128)(2,1)S(1)} %shard_map.152.refs_1_), channel_id=1, source_target_pairs={{0,2},{1,3},{2,0},{3,1},{4,6},{5,7},{6,4},{7,5},{8,10},{9,11},{10,... | collective-permute-start | bytes 221192 | tf_op jit(solution)/shard_map/ppermute | solution.py:427
  46.4 5.2 %collective-permute-start.16 = (bf16[288,128]{1,0:T(8,128)(2,1)S(1)}, bf16[288,128]{1,0:T(8,128)(2,1)S(1)}, u32[]{:S(2)}, u32[]{:S(2)}) collective-permute-start(bf16[288,128]{1,0:T(8,128)(2,1)S(1)} %shard_map.152.refs_1_), channel_id=1, source_target_pairs={{0,4},{1,5},{2,6},{3,7},{4,0},{5,1},{6,2},{7,3},{8,12},{9,13},{10,... | collective-permute-start | bytes 221192 | tf_op jit(solution)/shard_map/ppermute | solution.py:427
  47.9 5.8 %collective-permute-start.18 = (bf16[288,128]{1,0:T(8,128)(2,1)S(1)}, bf16[288,128]{1,0:T(8,128)(2,1)S(1)}, u32[]{:S(2)}, u32[]{:S(2)}) collective-permute-start(bf16[288,128]{1,0:T(8,128)(2,1)S(1)} %shard_map.152.refs_1_), channel_id=1, source_target_pairs={{0,6},{1,7},{2,4},{3,5},{4,2},{5,3},{6,0},{7,1},{8,14},{9,15},{10,... | collective-permute-start | bytes 221192 | tf_op jit(solution)/shard_map/ppermute | solution.py:427
  48.5 6.3 %collective-permute-start.13 = (bf16[288,128]{1,0:T(8,128)(2,1)S(1)}, bf16[288,128]{1,0:T(8,128)(2,1)S(1)}, u32[]{:S(2)}, u32[]{:S(2)}) collective-permute-start(bf16[288,128]{1,0:T(8,128)(2,1)S(1)} %shard_map.152.refs_1_), channel_id=1, source_target_pairs={{0,1},{1,0},{2,3},{3,2},{4,5},{5,4},{6,7},{7,6},{8,9},{9,8},{10,11... | collective-permute-start | bytes 221192 | tf_op jit(solution)/shard_map/ppermute | solution.py:427
  51.7 3.2 %collective-permute-start.15 = (bf16[288,128]{1,0:T(8,128)(2,1)S(1)}, bf16[288,128]{1,0:T(8,128)(2,1)S(1)}, u32[]{:S(2)}, u32[]{:S(2)}) collective-permute-start(bf16[288,128]{1,0:T(8,128)(2,1)S(1)} %collective-permute-done.14.refs_3_), channel_id=1, source_target_pairs={{0,1},{1,0},{2,3},{3,2},{4,5},{5,4},{6,7},{7,6},{8,9},{9,8},{10,11... | collective-permute-start | bytes 221192 | tf_op jit(solution)/shard_map/ppermute | solution.py:427
  51.7 3.2 %collective-permute-start.17 = (bf16[288,128]{1,0:T(8,128)(2,1)S(1)}, bf16[288,128]{1,0:T(8,128)(2,1)S(1)}, u32[]{:S(2)}, u32[]{:S(2)}) collective-permute-start(bf16[288,128]{1,0:T(8,128)(2,1)S(1)} %collective-permute-done.16.refs_5_), channel_id=1, source_target_pairs={{0,1},{1,0},{2,3},{3,2},{4,5},{5,4},{6,7},{7,6},{8,9},{9,8},{10,11... | collective-permute-start | bytes 221192 | tf_op jit(solution)/shard_map/ppermute | solution.py:427
  53.7 1.3 %collective-permute-start.19 = (bf16[288,128]{1,0:T(8,128)(2,1)S(1)}, bf16[288,128]{1,0:T(8,128)(2,1)S(1)}, u32[]{:S(2)}, u32[]{:S(2)}) collective-permute-start(bf16[288,128]{1,0:T(8,128)(2,1)S(1)} %collective-permute-done.18.refs_7_), channel_id=1, source_target_pairs={{0,1},{1,0},{2,3},{3,2},{4,5},{5,4},{6,7},{7,6},{8,9},{9,8},{10,11... | collective-permute-start | bytes 221192 | tf_op jit(solution)/shard_map/ppermute | solution.py:427

commit v6 on v5

--- a/solution.py
+++ b/solution.py
@@ -210,10 +210,10 @@
     order_out[...] = order[...]
 
 
-def pass_kernel(after, *refs):
-    count = len(refs) // 2
-    for source, target in zip(refs[:count], refs[count:]):
-        target[...] = source[...]
+def stack_kernel(after, *refs):
+    *sources, out = refs
+    for i, source in enumerate(sources):
+        out[i] = source[...]
 
 
 def shifted(value, steps, channels):
@@ -329,8 +329,11 @@
 
 def weights_kernel(channels, scale, lines, *refs):
     line, place, short, *refs, partial_out, moved_out = refs
-    met, pieces = refs[:lines], refs[lines:]
-    plane, width = len(pieces), pieces[0].shape[0] // 2
+    met, (own, beside, across, over) = refs[:lines], refs[lines:]
+    pieces = [own[...], beside[...]]
+    for i in range(across.shape[0]):
+        pieces += [across[i], over[i]]
+    plane, width = len(pieces), own.shape[0] // 2
     height = 4 * channels
     total = jnp.zeros((lines * height, 2 * width), f32)
     step = 2 if plane % 2 == 0 else 1
@@ -342,7 +345,7 @@
             ],
             axis=1,
         )
-        right = jnp.concatenate([pieces[i + j][...] for j in range(step)], axis=1)
+        right = jnp.concatenate([pieces[i + j] for j in range(step)], axis=1)
         total = total + lax.dot_general(
             left, right, (((1,), (1,)), ((), ())), preferred_element_type=f32
         )
@@ -513,11 +516,9 @@
         scratch_shapes=[pltpu.VMEM((lines, *chunk), bf16)] if whole else [],
     )
     if whole:
-        pieces = [swapped(own, plane, k) for k in (1, *range(2, plane, 2))]
-        beside, *pieces = call(
-            pass_kernel, [shape(own.shape, bf16)] * len(pieces), short, *pieces
-        )
-        pieces = [own, beside] + [a for p in pieces for a in (p, swapped(p, plane, 1))]
+        across = [swapped(own, plane, k) for k in range(2, plane, 2)]
+        across = call(stack_kernel, shape((len(across), *own.shape), bf16), short, *across)
+        pieces = (own, swapped(own, plane, 1), across, swapped(across, plane, 1))
     grad_one, grad_two, short = call(
         lambda *refs: filter_grads_kernel(scale / length, *refs),
         (shape(filter_one.shape), shape(filter_two.shape), shape(short.shape)),
@@ -546,7 +547,7 @@
             short,
             *met,
             *pieces,
-            in_specs=[scalar] * 2 + [held] * (1 + lines + plane),
+            in_specs=[scalar] * 2 + [held] * (1 + lines + len(pieces)),
         )
         partials = [partial] + [ahead(partial, k) for k in range(1, lines)]
         back = lax.all_to_all(moved, "fft", split_axis=0, concat_axis=0, tiled=True)

time: 56.4 us -> 56.1 us (level)
  waiting for transfers between devices: 15.2 us -> 14.6 us
    ppermute x14 -> x12, waiting for transfers between devices: 4.79 us -> 2.89 us  [swapped(): return lax.ppermute(value, 'fft', [(i, i ^ distance) for i in range(plane)])]
    ppermute x14 -> x12, starting transfers between devices: 8.52 us -> 7.33 us  [swapped(): return lax.ppermute(value, 'fft', [(i, i ^ distance) for i in range(plane)])]
    ppermute x6, starting transfers between devices: 5.77 us -> 6.96 us  [ahead(): return lax.ppermute(value, 'seq', pairs)]
    all_to_all x1, waiting for transfers between devices: 3.55 us -> 4.42 us  [local(): lax.all_to_all(streams, AXES, split_axis=0, concat_axis=0, tiled=True)]
    unnamed x20 -> x16, local copies, waits for them, and re-layouts: 2.1 us -> 2.29 us
  transfers between devices with their start and end apart: 22 -> 20, of which waited for: 8 -> 9; matrix products, arithmetic and copies ran while one was open for 0% -> 0% of each run, Pallas kernels for 15% -> 15%
where the time goes in v6:
time: 56.1 us; the launch traced here: 55.6 us
  starting transfers between devices  25 us (45%)
  waiting for transfers between devices  14.6 us (26%)
  Pallas kernels  12.8 us (23%)
  local copies, waits for them, and re-layouts  2.45 us (4%)
  between operations  0.77 us (1%)
    pallas_call x8, Pallas kernels, call(): pl.pallas_call(kernel, out_shape=outs, compiler_params=PARAMS, **options)  10.4 us
    ppermute x12, starting transfers between devices, swapped(): return lax.ppermute(value, 'fft', [(i, i ^ distance) for i in range(plane)])  7.33 us
    all_to_all x1, starting transfers between devices, local(): lax.all_to_all(streams, AXES, split_axis=0, concat_axis=0, tiled=True)  7.3 us
    ppermute x6, waiting for transfers between devices, ahead(): return lax.ppermute(value, 'seq', pairs)  7.29 us
    ppermute x6, starting transfers between devices, ahead(): return lax.ppermute(value, 'seq', pairs)  6.96 us
    all_to_all x1, waiting for transfers between devices, local(): lax.all_to_all(streams, AXES, split_axis=0, concat_axis=0, tiled=True)  4.42 us
    all_to_all x1, starting transfers between devices, local(): back = lax.all_to_all(moved, 'fft', split_axis=0, concat_axis=0, tiled=True)  3.39 us
    ppermute x12, waiting for transfers between devices, swapped(): return lax.ppermute(value, 'fft', [(i, i ^ distance) for i in range(plane)])  2.89 us
  transfers between devices with their start and end apart: 20, of which 9 were waited for; matrix products, arithmetic and copies ran while one was open for 0% of the time, Pallas kernels for 15%

profile of v6, /device:TPU:0, one launch (start us, length us, event | category | flops | bytes accessed | tf_op | source)
XLA Modules:
  0.0 55.6 jit_solution(17793097345469486831)
XLA Ops:
  0.6 0.0 copy-start
  0.6 0.0 copy-start.2
  0.7 2.4 %shard_map.145 = (bf16[32,32,128]{2,1,0:T(8,128)(2,1)}, bf16[512,128]{1,0:T(8,128)(2,1)}) custom-call(bf16[256,128]{1,0:T(8,128)(2,1)} %features_at.1, s32[1,128]{1,0:T(1,128)} %refs_4_.1, bf16[256,128]{1,0:T(8,128)(2,1)} %cotangent_at.1, bf16[768,256]{1,0:T(8,128)(2,1)} %refs_2_.2, bf16[256,256]{1,0:T(8,128)(2,1)} %w_out_at.1), custom_call_target="tpu_custom_call" | custom-call | tf_op jit(solution)/shard_map/pallas_call | solution.py:458
  3.1 0.0 copy-start.3
  3.1 0.0 copy-start.4
  3.1 7.3 %all-to-all-start = ((bf16[32,32,128]{2,1,0:T(8,128)(2,1)}), bf16[32,32,128]{2,1,0:T(8,128)(2,1)S(1)}, u32[]{:S(2)}, u32[]{:S(2)}) async-start(bf16[32,32,128]{2,1,0:T(8,128)(2,1)} %get-tuple-element.28), calls=%async_computation | async-start | bytes 524288 | tf_op jit(solution)/shard_map/all_to_all | solution.py:472
  10.4 1.8 %collective-permute-start.4 = (bf16[512,128]{1,0:T(8,128)(2,1)}, bf16[512,128]{1,0:T(8,128)(2,1)S(1)}, u32[]{:S(2)}, u32[]{:S(2)}) collective-permute-start(bf16[512,128]{1,0:T(8,128)(2,1)} %get-tuple-element.41.refs_7_), channel_id=1, source_target_pairs={{0,2},{1,3},{2,0},{3,1},{4,6},{5,7},{6,4},{7,5},{8,10},{9,11},{10,... | collective-permute-start | bytes 393224 | tf_op jit(solution)/shard_map/ppermute | solution.py:430
  12.2 1.5 %collective-permute-start.5 = (bf16[512,128]{1,0:T(8,128)(2,1)}, bf16[512,128]{1,0:T(8,128)(2,1)S(1)}, u32[]{:S(2)}, u32[]{:S(2)}) collective-permute-start(bf16[512,128]{1,0:T(8,128)(2,1)} %get-tuple-element.41.refs_7_), channel_id=1, source_target_pairs={{0,4},{1,5},{2,6},{3,7},{4,0},{5,1},{6,2},{7,3},{8,12},{9,13},{10,... | collective-permute-start | bytes 393224 | tf_op jit(solution)/shard_map/ppermute | solution.py:430
  13.7 0.3 collective-permute-start.6
  14.0 0.0 copy-done
  14.0 0.1 dynamic-slice_bitcast_fusion
  14.1 0.0 copy-start.7
  14.1 0.1 copy.19.refs_1_
  14.1 0.0 copy-done.2
  14.1 0.0 copy-done.3
  14.1 0.0 copy-done.4
  14.1 0.6 %copy-done.7 = s32[1,128]{1,0:T(1,128)S(1)} copy-done((s32[1,128]{1,0:T(1,128)S(1)}, s32[1,128]{1,0:T(1,128)}, u32[]{:S(2)}) %copy-start.7) | copy-done | bytes 536
  14.7 0.0 copy-start.5
  14.7 0.9 %copy-done.5 = f32[8,4096]{1,0:T(8,128)S(1)} copy-done((f32[8,4096]{1,0:T(8,128)S(1)}, f32[8,4096]{1,0:T(8,128)}, u32[]{:S(2)}) %copy-start.5) | copy-done | bytes 131096
  15.6 1.0 %shard_map.146 = (f32[256,256]{1,0:T(8,128)S(1)}, f32[256,256]{1,0:T(8,128)S(1)}, bf16[1536,256]{1,0:T(8,128)(2,1)S(1)}, f32[256,256]{1,0:T(8,128)S(1)}, s32[1,128]{1,0:T(1,128)S(1)}) custom-call(f32[8,4096]{1,0:T(8,128)S(1)} %copy-done.4, f32[8,4096]{1,0:T(8,128)S(1)} %copy-done.5, bf16[1536,256]{1,0:T(8,128)(2,1)S(1)} %copy-done.2, ...), custom_call_target="tpu_custom_call" | custom-call | tf_op jit(solution)/shard_map/pallas_call | solution.py:455
  16.6 4.4 %all-to-all-done.refs_0_ = bf16[32,32,128]{2,1,0:T(8,128)(2,1)S(1)} async-done(((bf16[32,32,128]{2,1,0:T(8,128)(2,1)}), bf16[32,32,128]{2,1,0:T(8,128)(2,1)S(1)}, u32[]{:S(2)}, u32[]{:S(2)}) %all-to-all-start) | async-done | bytes 262176 | tf_op jit(solution)/shard_map/all_to_all | solution.py:472
  21.1 4.2 %shard_map.147 = (f32[8,128]{1,0:T(8,128)S(1)}, f32[256,256]{1,0:T(8,128)S(1)}, f32[256,256]{1,0:T(8,128)S(1)}, bf16[8,32,128]{2,1,0:T(8,128)(2,1)S(1)}, bf16[8,...) custom-call(bf16[32,32,128]{2,1,0:T(8,128)(2,1)S(1)} %all-to-all-done.refs_0_, ...), custom_call_target="tpu_custom_call" | custom-call | tf_op jit(solution)/shard_map/pallas_call | solution.py:455
  25.3 0.0 collective-permute-done.4.refs_0_
  25.3 0.0 collective-permute-done.5.refs_1_
  25.3 0.0 collective-permute-done.6.refs_2_
  25.3 0.0 copy-start.6
  25.3 0.1 collective-permute-start.7
  25.4 0.8 %copy-done.6 = bf16[512,128]{1,0:T(8,128)(2,1)S(1)} copy-done((bf16[512,128]{1,0:T(8,128)(2,1)S(1)}, bf16[512,128]{1,0:T(8,128)(2,1)}, u32[]{:S(2)}) %copy-start.6) | copy-done | bytes 131096
  26.2 0.0 collective-permute-start.3
  26.2 1.0 %collective-permute-start = (bf16[8,32,128]{2,1,0:T(8,128)(2,1)S(1)}, bf16[8,32,128]{2,1,0:T(8,128)(2,1)S(1)}, u32[]{:S(2)}, u32[]{:S(2)}) collective-permute-start(bf16[8,32,128]{2,1,0:T(8,128)(2,1)S(1)} %get-tuple-element.38), channel_id=1, source_target_pairs={{0,8},{8,16},{16,24},{24,0},{1,9},{9,17},{17,25},{25,1},{2,10},{10... | collective-permute-start | bytes 196616 | tf_op jit(solution)/shard_map/ppermute | solution.py:535
  27.2 0.9 %collective-permute-start.1 = (bf16[8,32,128]{2,1,0:T(8,128)(2,1)S(1)}, bf16[8,32,128]{2,1,0:T(8,128)(2,1)S(1)}, u32[]{:S(2)}, u32[]{:S(2)}) collective-permute-start(bf16[8,32,128]{2,1,0:T(8,128)(2,1)S(1)} %get-tuple-element.39), channel_id=1, source_target_pairs={{0,16},{8,24},{16,0},{24,8},{1,17},{9,25},{17,1},{25,9},{2,18},{10... | collective-permute-start | bytes 196616 | tf_op jit(solution)/shard_map/ppermute | solution.py:535
  28.1 2.0 %collective-permute-start.2 = (bf16[8,32,128]{2,1,0:T(8,128)(2,1)S(1)}, bf16[8,32,128]{2,1,0:T(8,128)(2,1)S(1)}, u32[]{:S(2)}, u32[]{:S(2)}) collective-permute-start(bf16[8,32,128]{2,1,0:T(8,128)(2,1)S(1)} %get-tuple-element.40), channel_id=1, source_target_pairs={{0,24},{8,0},{16,8},{24,16},{1,25},{9,1},{17,9},{25,17},{2,26},{10... | collective-permute-start | bytes 196616 | tf_op jit(solution)/shard_map/ppermute | solution.py:535
  30.1 1.8 %shard_map.148 = (f32[8,4096]{1,0:T(8,128)}, f32[8,4096]{1,0:T(8,128)}, f32[8,128]{1,0:T(8,128)S(1)}) custom-call(f32[256,256]{1,0:T(8,128)S(1)} %get-tuple-element.33.refs_0_, f32[256,256]{1,0:T(8,128)S(1)} %get-tuple-element.34.refs_1_, bf16[1536,256]{1,0:T(8,128)(2,1)S(1)} %get-tuple-element.31.refs_4_.refs_2_, ...), custom_call_target="tpu_custom_call" | custom-call | tf_op jit(solution)/shard_map/pallas_call | solution.py:455
  31.8 0.0 collective-permute-done.3.refs_8_
  31.8 1.2 %collective-permute-done.refs_4_ = bf16[8,32,128]{2,1,0:T(8,128)(2,1)S(1)} collective-permute-done((bf16[8,32,128]{2,1,0:T(8,128)(2,1)S(1)}, bf16[8,32,128]{2,1,0:T(8,128)(2,1)S(1)}, u32[]{:S(2)}, u32[]{:S(2)}) %collective-permute-start) | collective-permute-done | bytes 65568 | tf_op jit(solution)/shard_map/ppermute | solution.py:535
  33.0 2.4 %collective-permute-done.1.refs_5_ = bf16[8,32,128]{2,1,0:T(8,128)(2,1)S(1)} collective-permute-done((bf16[8,32,128]{2,1,0:T(8,128)(2,1)S(1)}, bf16[8,32,128]{2,1,0:T(8,128)(2,1)S(1)}, u32[]{:S(2)}, u32[]{:S(2)}) %collective-permute-start.1) | collective-permute-done | bytes 65568 | tf_op jit(solution)/shard_map/ppermute | solution.py:535
  35.4 0.0 collective-permute-done.2.refs_6_
  35.4 0.0 collective-permute-done.7.refs_10_
  35.4 1.1 %shard_map.150 = (bf16[288,128]{1,0:T(8,128)(2,1)S(1)}, bf16[8,96,128]{2,1,0:T(8,128)(2,1)}) custom-call(s32[1]{0:T(128)} %bitcast.refs_6_.refs_0_, s32[1]{0:T(128)} %bitcast.1.refs_1_.refs_0_, f32[8,128]{1,0:T(8,128)S(1)} %get-tuple-element.36.refs_2_, bf16[8,32,128]{2,1,0:T(8,128)(2,1)S(1)} %get-tuple-element.37.refs_3_, ...), custom_call_target="tpu_custom_call" | custom-call | tf_op jit(solution)/shard_map/pallas_call | solution.py:455
  36.5 2.2 %collective-permute-start.10 = (bf16[288,128]{1,0:T(8,128)(2,1)S(1)}, bf16[288,128]{1,0:T(8,128)(2,1)S(1)}, u32[]{:S(2)}, u32[]{:S(2)}) collective-permute-start(bf16[288,128]{1,0:T(8,128)(2,1)S(1)} %get-tuple-element.44.refs_0_), channel_id=1, source_target_pairs={{0,24},{8,0},{16,8},{24,16},{1,25},{9,1},{17,9},{25,17},{2,26},{10... | collective-permute-start | bytes 221192 | tf_op jit(solution)/shard_map/ppermute | solution.py:535
  38.7 0.0 collective-permute-start.8
  38.7 0.9 %collective-permute-start.9 = (bf16[288,128]{1,0:T(8,128)(2,1)S(1)}, bf16[288,128]{1,0:T(8,128)(2,1)S(1)}, u32[]{:S(2)}, u32[]{:S(2)}) collective-permute-start(bf16[288,128]{1,0:T(8,128)(2,1)S(1)} %get-tuple-element.44.refs_0_), channel_id=1, source_target_pairs={{0,16},{8,24},{16,0},{24,8},{1,17},{9,25},{17,1},{25,9},{2,18},{10... | collective-permute-start | bytes 221192 | tf_op jit(solution)/shard_map/ppermute | solution.py:535
  39.6 3.4 %all-to-all-start.1 = ((bf16[8,96,128]{2,1,0:T(8,128)(2,1)}), bf16[8,96,128]{2,1,0:T(8,128)(2,1)S(1)}, u32[]{:S(2)}, u32[]{:S(2)}) async-start(bf16[8,96,128]{2,1,0:T(8,128)(2,1)} %get-tuple-element.42), calls=%async_computation.1 | async-start | bytes 393216 | tf_op jit(solution)/shard_map/all_to_all | solution.py:553
  43.0 0.0 collective-permute-done.10.refs_3_
  43.0 2.2 %collective-permute-done.8.refs_1_ = bf16[288,128]{1,0:T(8,128)(2,1)S(1)} collective-permute-done((bf16[288,128]{1,0:T(8,128)(2,1)S(1)}, bf16[288,128]{1,0:T(8,128)(2,1)S(1)}, u32[]{:S(2)}, u32[]{:S(2)}) %collective-permute-start.8) | collective-permute-done | bytes 73760 | tf_op jit(solution)/shard_map/ppermute | solution.py:535
  45.2 1.5 %collective-permute-done.9.refs_2_ = bf16[288,128]{1,0:T(8,128)(2,1)S(1)} collective-permute-done((bf16[288,128]{1,0:T(8,128)(2,1)S(1)}, bf16[288,128]{1,0:T(8,128)(2,1)S(1)}, u32[]{:S(2)}, u32[]{:S(2)}) %collective-permute-start.9) | collective-permute-done | bytes 73760 | tf_op jit(solution)/shard_map/ppermute | solution.py:535
  46.8 0.3 collective-permute-start.12
  47.0 0.9 %collective-permute-start.14 = (bf16[288,128]{1,0:T(8,128)(2,1)S(1)}, bf16[288,128]{1,0:T(8,128)(2,1)S(1)}, u32[]{:S(2)}, u32[]{:S(2)}) collective-permute-start(bf16[288,128]{1,0:T(8,128)(2,1)S(1)} %shard_map.152.refs_1_), channel_id=1, source_target_pairs={{0,4},{1,5},{2,6},{3,7},{4,0},{5,1},{6,2},{7,3},{8,12},{9,13},{10,... | collective-permute-start | bytes 221192 | tf_op jit(solution)/shard_map/ppermute | solution.py:430
  47.9 2.4 %collective-permute-start.16 = (bf16[288,128]{1,0:T(8,128)(2,1)S(1)}, bf16[288,128]{1,0:T(8,128)(2,1)S(1)}, u32[]{:S(2)}, u32[]{:S(2)}) collective-permute-start(bf16[288,128]{1,0:T(8,128)(2,1)S(1)} %shard_map.152.refs_1_), channel_id=1, source_target_pairs={{0,6},{1,7},{2,4},{3,5},{4,2},{5,3},{6,0},{7,1},{8,14},{9,15},{10,... | collective-permute-start | bytes 221192 | tf_op jit(solution)/shard_map/ppermute | solution.py:430
  50.3 0.0 collective-permute-start.11
  50.3 0.9 %collective-permute-done.12.refs_3_ = bf16[288,128]{1,0:T(8,128)(2,1)S(1)} collective-permute-done((bf16[288,128]{1,0:T(8,128)(2,1)S(1)}, bf16[288,128]{1,0:T(8,128)(2,1)S(1)}, u32[]{:S(2)}, u32[]{:S(2)}) %collective-permute-start.12) | collective-permute-done | bytes 73760 | tf_op jit(solution)/shard_map/ppermute | solution.py:430
  51.2 0.0 collective-permute-start.13
  51.2 0.4 collective-permute-done.14.refs_5_
  51.6 0.1 collective-permute-start.15
  51.7 1.5 %collective-permute-done.16.refs_7_ = bf16[288,128]{1,0:T(8,128)(2,1)S(1)} collective-permute-done((bf16[288,128]{1,0:T(8,128)(2,1)S(1)}, bf16[288,128]{1,0:T(8,128)(2,1)S(1)}, u32[]{:S(2)}, u32[]{:S(2)}) %collective-permute-start.16) | collective-permute-done | bytes 73760 | tf_op jit(solution)/shard_map/ppermute | solution.py:430
  53.2 0.0 collective-permute-start.17
  53.2 0.0 all-to-all-done.1.refs_1_
  53.2 0.0 copy-done.1
  53.2 1.1 %shard_map.151 = bf16[256,128]{1,0:T(8,128)(2,1)} custom-call(s32[1]{0:T(128)} %bitcast.refs_6_.refs_0_, bf16[8,96,128]{2,1,0:T(8,128)(2,1)S(1)} %all-to-all-done.1.refs_1_, bf16[768,256]{1,0:T(8,128)(2,1)S(1)} %copy-done.1, s32[1,128]{1,0:T(1,128)S(1)} %get-tuple-element.43.refs_3_), custom_call_target="tpu_custom_call" | custom-call | tf_op jit(solution)/shard_map/pallas_call | solution.py:455
  54.3 0.0 collective-permute-done.11.refs_2_
  54.3 0.0 collective-permute-done.13.refs_4_
  54.3 0.0 collective-permute-done.15.refs_6_
  54.3 0.1 collective-permute-done.17.refs_8_
  54.5 1.1 %shard_map.153 = (f32[768,256]{1,0:T(8,128)}, f32[256,256]{1,0:T(8,128)}, f32[3,768]{1,0:T(4,128)}) custom-call(s32[1]{0:T(128)} %bitcast.1.refs_1_.refs_0_, bf16[288,128]{1,0:T(8,128)(2,1)S(1)} %shard_map.152.refs_1_, bf16[288,128]{1,0:T(8,128)(2,1)S(1)} %collective-permute-done.11.refs_2_, bf16[288,128]{1,0:T(8,128)(2,1)S(1)} %collective-permute-done.12.refs_3_, ...), custom_call_target="tpu_custom_call" | custom-call | tf_op jit(solution)/shard_map/pallas_call | solution.py:455
  (4 shorter events, 0.1 us)
Async XLA Ops:
  0.6 13.3 %copy-start = (f32[768,3]{0,1:T(4,128)S(1)}, f32[768,3]{0,1:T(4,128)}, u32[]{:S(2)}) copy-start(f32[768,3]{0,1:T(4,128)} %param.14) | copy-start | bytes 27652
  0.6 13.5 %copy-start.2 = (bf16[1536,256]{1,0:T(8,128)(2,1)S(1)}, bf16[1536,256]{1,0:T(8,128)(2,1)}, u32[]{:S(2)}) copy-start(bf16[1536,256]{1,0:T(8,128)(2,1)} %constant.18.clone.refs_2_) | copy-start | bytes 2359300
  3.1 11.1 %copy-start.3 = (f32[256,256]{1,0:T(8,128)S(1)}, f32[256,256]{1,0:T(8,128)}, u32[]{:S(2)}) copy-start(f32[256,256]{1,0:T(8,128)} %constant.19.clone.refs_3_) | copy-start | bytes 786436
  3.1 11.1 %copy-start.4 = (f32[8,4096]{1,0:T(8,128)S(1)}, f32[8,4096]{1,0:T(8,128)}, u32[]{:S(2)}) copy-start(f32[8,4096]{1,0:T(8,128)} %refs_0_.1) | copy-start | bytes 393220
  3.1 18.0 %all-to-all-start = ((bf16[32,32,128]{2,1,0:T(8,128)(2,1)}), bf16[32,32,128]{2,1,0:T(8,128)(2,1)S(1)}, u32[]{:S(2)}, u32[]{:S(2)}) async-start(bf16[32,32,128]{2,1,0:T(8,128)(2,1)} %get-tuple-element.28), calls=%async_computation | async-start | bytes 524288 | tf_op jit(solution)/shard_map/all_to_all | solution.py:472
  10.4 14.9 %collective-permute-start.4 = (bf16[512,128]{1,0:T(8,128)(2,1)}, bf16[512,128]{1,0:T(8,128)(2,1)S(1)}, u32[]{:S(2)}, u32[]{:S(2)}) collective-permute-start(bf16[512,128]{1,0:T(8,128)(2,1)} %get-tuple-element.41.refs_7_), channel_id=1, source_target_pairs={{0,2},{1,3},{2,0},{3,1},{4,6},{5,7},{6,4},{7,5},{8,10},{9,11},{10,... | collective-permute-start | bytes 393224 | tf_op jit(solution)/shard_map/ppermute | solution.py:430
  12.2 13.0 %collective-permute-start.5 = (bf16[512,128]{1,0:T(8,128)(2,1)}, bf16[512,128]{1,0:T(8,128)(2,1)S(1)}, u32[]{:S(2)}, u32[]{:S(2)}) collective-permute-start(bf16[512,128]{1,0:T(8,128)(2,1)} %get-tuple-element.41.refs_7_), channel_id=1, source_target_pairs={{0,4},{1,5},{2,6},{3,7},{4,0},{5,1},{6,2},{7,3},{8,12},{9,13},{10,... | collective-permute-start | bytes 393224 | tf_op jit(solution)/shard_map/ppermute | solution.py:430
  13.7 11.6 %collective-permute-start.6 = (bf16[512,128]{1,0:T(8,128)(2,1)}, bf16[512,128]{1,0:T(8,128)(2,1)S(1)}, u32[]{:S(2)}, u32[]{:S(2)}) collective-permute-start(bf16[512,128]{1,0:T(8,128)(2,1)} %get-tuple-element.41.refs_7_), channel_id=1, source_target_pairs={{0,6},{1,7},{2,4},{3,5},{4,2},{5,3},{6,0},{7,1},{8,14},{9,15},{10,... | collective-permute-start | bytes 393224 | tf_op jit(solution)/shard_map/ppermute | solution.py:430
  14.1 0.7 %copy-start.7 = (s32[1,128]{1,0:T(1,128)S(1)}, s32[1,128]{1,0:T(1,128)}, u32[]{:S(2)}) copy-start(s32[1,128]{1,0:T(1,128)} %refs_4_.1) | copy-start | bytes 1540
  14.7 0.9 %copy-start.5 = (f32[8,4096]{1,0:T(8,128)S(1)}, f32[8,4096]{1,0:T(8,128)}, u32[]{:S(2)}) copy-start(f32[8,4096]{1,0:T(8,128)} %refs_1_.1) | copy-start | bytes 393220
  25.3 0.9 %copy-start.6 = (bf16[512,128]{1,0:T(8,128)(2,1)S(1)}, bf16[512,128]{1,0:T(8,128)(2,1)}, u32[]{:S(2)}) copy-start(bf16[512,128]{1,0:T(8,128)(2,1)} %get-tuple-element.41.refs_7_) | copy-start | bytes 393220
  25.3 10.1 %collective-permute-start.7 = (bf16[3,512,128]{2,1,0:T(8,128)(2,1)S(1)}, bf16[3,512,128]{2,1,0:T(8,128)(2,1)S(1)}, u32[]{:S(2)}, u32[]{:S(2)}) collective-permute-start(bf16[3,512,128]{2,1,0:T(8,128)(2,1)S(1)} %shard_map.149.refs_9_), channel_id=1, source_target_pairs={{0,1},{1,0},{2,3},{3,2},{4,5},{5,4},{6,7},{7,6},{8,9},{9,8},{10,11... | collective-permute-start | bytes 1179656 | tf_op jit(solution)/shard_map/ppermute | solution.py:430
  26.2 5.6 %collective-permute-start.3 = (bf16[512,128]{1,0:T(8,128)(2,1)S(1)}, bf16[512,128]{1,0:T(8,128)(2,1)S(1)}, u32[]{:S(2)}, u32[]{:S(2)}) collective-permute-start(bf16[512,128]{1,0:T(8,128)(2,1)S(1)} %copy-done.6), channel_id=1, source_target_pairs={{0,1},{1,0},{2,3},{3,2},{4,5},{5,4},{6,7},{7,6},{8,9},{9,8},{10,11... | collective-permute-start | bytes 393224 | tf_op jit(solution)/shard_map/ppermute | solution.py:430
  26.2 6.8 %collective-permute-start = (bf16[8,32,128]{2,1,0:T(8,128)(2,1)S(1)}, bf16[8,32,128]{2,1,0:T(8,128)(2,1)S(1)}, u32[]{:S(2)}, u32[]{:S(2)}) collective-permute-start(bf16[8,32,128]{2,1,0:T(8,128)(2,1)S(1)} %get-tuple-element.38), channel_id=1, source_target_pairs={{0,8},{8,16},{16,24},{24,0},{1,9},{9,17},{17,25},{25,1},{2,10},{10... | collective-permute-start | bytes 196616 | tf_op jit(solution)/shard_map/ppermute | solution.py:535
  27.2 8.2 %collective-permute-start.1 = (bf16[8,32,128]{2,1,0:T(8,128)(2,1)S(1)}, bf16[8,32,128]{2,1,0:T(8,128)(2,1)S(1)}, u32[]{:S(2)}, u32[]{:S(2)}) collective-permute-start(bf16[8,32,128]{2,1,0:T(8,128)(2,1)S(1)} %get-tuple-element.39), channel_id=1, source_target_pairs={{0,16},{8,24},{16,0},{24,8},{1,17},{9,25},{17,1},{25,9},{2,18},{10... | collective-permute-start | bytes 196616 | tf_op jit(solution)/shard_map/ppermute | solution.py:535
  28.1 7.3 %collective-permute-start.2 = (bf16[8,32,128]{2,1,0:T(8,128)(2,1)S(1)}, bf16[8,32,128]{2,1,0:T(8,128)(2,1)S(1)}, u32[]{:S(2)}, u32[]{:S(2)}) collective-permute-start(bf16[8,32,128]{2,1,0:T(8,128)(2,1)S(1)} %get-tuple-element.40), channel_id=1, source_target_pairs={{0,24},{8,0},{16,8},{24,16},{1,25},{9,1},{17,9},{25,17},{2,26},{10... | collective-permute-start | bytes 196616 | tf_op jit(solution)/shard_map/ppermute | solution.py:535
  36.5 16.7 %copy-start.1 = (bf16[768,256]{1,0:T(8,128)(2,1)S(1)}, bf16[768,256]{1,0:T(8,128)(2,1)}, u32[]{:S(2)}) copy-start(bf16[768,256]{1,0:T(8,128)(2,1)} %refs_2_.2) | copy-start | bytes 1179652
  36.5 6.5 %collective-permute-start.10 = (bf16[288,128]{1,0:T(8,128)(2,1)S(1)}, bf16[288,128]{1,0:T(8,128)(2,1)S(1)}, u32[]{:S(2)}, u32[]{:S(2)}) collective-permute-start(bf16[288,128]{1,0:T(8,128)(2,1)S(1)} %get-tuple-element.44.refs_0_), channel_id=1, source_target_pairs={{0,24},{8,0},{16,8},{24,16},{1,25},{9,1},{17,9},{25,17},{2,26},{10... | collective-permute-start | bytes 221192 | tf_op jit(solution)/shard_map/ppermute | solution.py:535
  38.7 6.5 %collective-permute-start.8 = (bf16[288,128]{1,0:T(8,128)(2,1)S(1)}, bf16[288,128]{1,0:T(8,128)(2,1)S(1)}, u32[]{:S(2)}, u32[]{:S(2)}) collective-permute-start(bf16[288,128]{1,0:T(8,128)(2,1)S(1)} %get-tuple-element.44.refs_0_), channel_id=1, source_target_pairs={{0,8},{8,16},{16,24},{24,0},{1,9},{9,17},{17,25},{25,1},{2,10},{10... | collective-permute-start | bytes 221192 | tf_op jit(solution)/shard_map/ppermute | solution.py:535
  38.7 8.0 %collective-permute-start.9 = (bf16[288,128]{1,0:T(8,128)(2,1)S(1)}, bf16[288,128]{1,0:T(8,128)(2,1)S(1)}, u32[]{:S(2)}, u32[]{:S(2)}) collective-permute-start(bf16[288,128]{1,0:T(8,128)(2,1)S(1)} %get-tuple-element.44.refs_0_), channel_id=1, source_target_pairs={{0,16},{8,24},{16,0},{24,8},{1,17},{9,25},{17,1},{25,9},{2,18},{10... | collective-permute-start | bytes 221192 | tf_op jit(solution)/shard_map/ppermute | solution.py:535
  39.6 13.6 %all-to-all-start.1 = ((bf16[8,96,128]{2,1,0:T(8,128)(2,1)}), bf16[8,96,128]{2,1,0:T(8,128)(2,1)S(1)}, u32[]{:S(2)}, u32[]{:S(2)}) async-start(bf16[8,96,128]{2,1,0:T(8,128)(2,1)} %get-tuple-element.42), calls=%async_computation.1 | async-start | bytes 393216 | tf_op jit(solution)/shard_map/all_to_all | solution.py:553
  46.8 4.4 %collective-permute-start.12 = (bf16[288,128]{1,0:T(8,128)(2,1)S(1)}, bf16[288,128]{1,0:T(8,128)(2,1)S(1)}, u32[]{:S(2)}, u32[]{:S(2)}) collective-permute-start(bf16[288,128]{1,0:T(8,128)(2,1)S(1)} %shard_map.152.refs_1_), channel_id=1, source_target_pairs={{0,2},{1,3},{2,0},{3,1},{4,6},{5,7},{6,4},{7,5},{8,10},{9,11},{10,... | collective-permute-start | bytes 221192 | tf_op jit(solution)/shard_map/ppermute | solution.py:430
  47.0 4.5 %collective-permute-start.14 = (bf16[288,128]{1,0:T(8,128)(2,1)S(1)}, bf16[288,128]{1,0:T(8,128)(2,1)S(1)}, u32[]{:S(2)}, u32[]{:S(2)}) collective-permute-start(bf16[288,128]{1,0:T(8,128)(2,1)S(1)} %shard_map.152.refs_1_), channel_id=1, source_target_pairs={{0,4},{1,5},{2,6},{3,7},{4,0},{5,1},{6,2},{7,3},{8,12},{9,13},{10,... | collective-permute-start | bytes 221192 | tf_op jit(solution)/shard_map/ppermute | solution.py:430
  47.9 5.3 %collective-permute-start.16 = (bf16[288,128]{1,0:T(8,128)(2,1)S(1)}, bf16[288,128]{1,0:T(8,128)(2,1)S(1)}, u32[]{:S(2)}, u32[]{:S(2)}) collective-permute-start(bf16[288,128]{1,0:T(8,128)(2,1)S(1)} %shard_map.152.refs_1_), channel_id=1, source_target_pairs={{0,6},{1,7},{2,4},{3,5},{4,2},{5,3},{6,0},{7,1},{8,14},{9,15},{10,... | collective-permute-start | bytes 221192 | tf_op jit(solution)/shard_map/ppermute | solution.py:430
  50.3 4.0 %collective-permute-start.11 = (bf16[288,128]{1,0:T(8,128)(2,1)S(1)}, bf16[288,128]{1,0:T(8,128)(2,1)S(1)}, u32[]{:S(2)}, u32[]{:S(2)}) collective-permute-start(bf16[288,128]{1,0:T(8,128)(2,1)S(1)} %shard_map.152.refs_1_), channel_id=1, source_target_pairs={{0,1},{1,0},{2,3},{3,2},{4,5},{5,4},{6,7},{7,6},{8,9},{9,8},{10,11... | collective-permute-start | bytes 221192 | tf_op jit(solution)/shard_map/ppermute | solution.py:430
  51.2 3.1 %collective-permute-start.13 = (bf16[288,128]{1,0:T(8,128)(2,1)S(1)}, bf16[288,128]{1,0:T(8,128)(2,1)S(1)}, u32[]{:S(2)}, u32[]{:S(2)}) collective-permute-start(bf16[288,128]{1,0:T(8,128)(2,1)S(1)} %collective-permute-done.12.refs_3_), channel_id=1, source_target_pairs={{0,1},{1,0},{2,3},{3,2},{4,5},{5,4},{6,7},{7,6},{8,9},{9,8},{10,11... | collective-permute-start | bytes 221192 | tf_op jit(solution)/shard_map/ppermute | solution.py:430
  51.6 2.7 %collective-permute-start.15 = (bf16[288,128]{1,0:T(8,128)(2,1)S(1)}, bf16[288,128]{1,0:T(8,128)(2,1)S(1)}, u32[]{:S(2)}, u32[]{:S(2)}) collective-permute-start(bf16[288,128]{1,0:T(8,128)(2,1)S(1)} %collective-permute-done.14.refs_5_), channel_id=1, source_target_pairs={{0,1},{1,0},{2,3},{3,2},{4,5},{5,4},{6,7},{7,6},{8,9},{9,8},{10,11... | collective-permute-start | bytes 221192 | tf_op jit(solution)/shard_map/ppermute | solution.py:430
  53.2 1.3 %collective-permute-start.17 = (bf16[288,128]{1,0:T(8,128)(2,1)S(1)}, bf16[288,128]{1,0:T(8,128)(2,1)S(1)}, u32[]{:S(2)}, u32[]{:S(2)}) collective-permute-start(bf16[288,128]{1,0:T(8,128)(2,1)S(1)} %collective-permute-done.16.refs_7_), channel_id=1, source_target_pairs={{0,1},{1,0},{2,3},{3,2},{4,5},{5,4},{6,7},{7,6},{8,9},{9,8},{10,11... | collective-permute-start | bytes 221192 | tf_op jit(solution)/shard_map/ppermute | solution.py:430

commit v7 on v6

--- a/solution.py
+++ b/solution.py
@@ -79,21 +79,15 @@
                 [cos * twist[0] + sin * twist[1], cos * twist[1] - sin * twist[0]], axis=1
             )
         )
-    spec = dot_pairs(split(jnp.concatenate(parts, axis=0)), second)
-    return [
-        (spec[i * rows : (i + 1) * rows, :LANES], spec[i * rows : (i + 1) * rows, LANES:])
-        for i in range(len(signals))
-    ]
+    specs = [dot_pairs(split(part), second) for part in parts]
+    return [(spec[:, :LANES], spec[:, LANES:]) for spec in specs]
 
 
 def backward(spectra, back, second, twist):
-    rows = spectra[0][0].shape[0]
-    stacked = jnp.concatenate([jnp.concatenate(pair, axis=1) for pair in spectra], axis=0)
-    stage = dot_pairs(split(stacked), second)
     parts = []
-    for i in range(len(spectra)):
-        re = stage[i * rows : (i + 1) * rows, :LANES]
-        im = stage[i * rows : (i + 1) * rows, LANES:]
+    for pair in spectra:
+        stage = dot_pairs(split(jnp.concatenate(pair, axis=1)), second)
+        re, im = stage[:, :LANES], stage[:, LANES:]
         parts.append(
             jnp.concatenate(
                 [re * twist[0] - im * twist[1], re * twist[1] + im * twist[0]], axis=0
@@ -328,12 +322,11 @@
 
 
 def weights_kernel(channels, scale, lines, *refs):
-    line, place, short, *refs, partial_out, moved_out = refs
-    met, (own, beside, across, over) = refs[:lines], refs[lines:]
-    pieces = [own[...], beside[...]]
-    for i in range(across.shape[0]):
+    line, place, short, *met, across, over, partial_out = refs
+    pieces = [over[0], across[0]]
+    for i in range(1, across.shape[0]):
         pieces += [across[i], over[i]]
-    plane, width = len(pieces), own.shape[0] // 2
+    plane, width = len(pieces), across.shape[1] // 2
     height = 4 * channels
     total = jnp.zeros((lines * height, 2 * width), f32)
     step = 2 if plane % 2 == 0 else 1
@@ -364,6 +357,10 @@
     tail = jnp.concatenate([short[...]] * lines, axis=0)
     owner = lax.broadcasted_iota(jnp.int32, tail.shape, 0) // channels
     partial_out[lines * size :] = jnp.where(owner == line[0], tail, 0.0).astype(bf16)
+
+
+def return_kernel(channels, *refs):
+    *met, after, moved_out = refs
     parts = [m[...].astype(f32)[:, : 3 * channels] for m in met]
     moved_out[...] = jnp.concatenate(parts, axis=1).astype(bf16)
 
@@ -516,9 +513,9 @@
         scratch_shapes=[pltpu.VMEM((lines, *chunk), bf16)] if whole else [],
     )
     if whole:
-        across = [swapped(own, plane, k) for k in range(2, plane, 2)]
+        across = [swapped(own, plane, k) for k in (1, *range(2, plane, 2))]
         across = call(stack_kernel, shape((len(across), *own.shape), bf16), short, *across)
-        pieces = (own, swapped(own, plane, 1), across, swapped(across, plane, 1))
+        pieces = (across, swapped(across, plane, 1))
     grad_one, grad_two, short = call(
         lambda *refs: filter_grads_kernel(scale / length, *refs),
         (shape(filter_one.shape), shape(filter_two.shape), shape(short.shape)),
@@ -536,18 +533,21 @@
 
         met = [sent[0]] + [ahead(sent[k], k) for k in range(1, lines)]
         size = lines * height + lines * channels
-        partial, moved = call(
+        partial = call(
             lambda *refs: weights_kernel(channels, scale, lines, *refs),
-            (
-                shape((size, LANES), bf16),
-                shape((plane, 3 * lines * channels, LANES), bf16),
-            ),
+            shape((size, LANES), bf16),
             line,
             place,
             short,
             *met,
             *pieces,
             in_specs=[scalar] * 2 + [held] * (1 + lines + len(pieces)),
+        )
+        moved = call(
+            lambda *refs: return_kernel(channels, *refs),
+            shape((plane, 3 * lines * channels, LANES), bf16),
+            *met,
+            partial,
         )
         partials = [partial] + [ahead(partial, k) for k in range(1, lines)]
         back = lax.all_to_all(moved, "fft", split_axis=0, concat_axis=0, tiled=True)

time: 56.1 us -> 55.1 us (0.982)
  the two profiles are of different devices: /device:TPU:0 before, /device:TPU:9 now
where the time goes in v7:
time: 55.1 us; the launch traced here: 54.7 us
  starting transfers between devices  28.8 us (52%)
  Pallas kernels  12.5 us (23%)
  waiting for transfers between devices  10.4 us (19%)
  local copies, waits for them, and re-layouts  2.27 us (4%)
  between operations  0.81 us (1%)
    ppermute x12, starting transfers between devices, swapped(): return lax.ppermute(value, 'fft', [(i, i ^ distance) for i in range(plane)])  10.5 us
    pallas_call x9, Pallas kernels, call(): pl.pallas_call(kernel, out_shape=outs, compiler_params=PARAMS, **options)  10 us
    ppermute x6, starting transfers between devices, ahead(): return lax.ppermute(value, 'seq', pairs)  7.09 us
    all_to_all x1, starting transfers between devices, local(): lax.all_to_all(streams, AXES, split_axis=0, concat_axis=0, tiled=True)  6.36 us
    all_to_all x1, starting transfers between devices, local(): back = lax.all_to_all(moved, 'fft', split_axis=0, concat_axis=0, tiled=True)  4.85 us
    ppermute x6, waiting for transfers between devices, ahead(): return lax.ppermute(value, 'seq', pairs)  4.57 us
    ppermute x12, waiting for transfers between devices, swapped(): return lax.ppermute(value, 'fft', [(i, i ^ distance) for i in range(plane)])  3.45 us
    pallas_call x1, Pallas kernels, local(): pl.pallas_call(project_kernel, out_shape=(shape(dims, bf16), shape((2 * w...  2.41 us
  transfers between devices with their start and end apart: 20, of which 5 were waited for; matrix products, arithmetic and copies ran while one was open for 0% of the time, Pallas kernels for 15%

profile of v7, /device:TPU:9, one launch (start us, length us, event | category | flops | bytes accessed | tf_op | source)
XLA Modules:
  0.0 54.7 jit_solution(14016903975680354683)
XLA Ops:
  0.6 0.0 copy-start
  0.6 0.0 copy-start.2
  0.7 2.4 %shard_map.145 = (bf16[32,32,128]{2,1,0:T(8,128)(2,1)}, bf16[512,128]{1,0:T(8,128)(2,1)}) custom-call(bf16[256,128]{1,0:T(8,128)(2,1)} %features_at.1, s32[1,128]{1,0:T(1,128)} %refs_4_.1, bf16[256,128]{1,0:T(8,128)(2,1)} %cotangent_at.1, bf16[768,256]{1,0:T(8,128)(2,1)} %refs_2_.2, bf16[256,256]{1,0:T(8,128)(2,1)} %w_out_at.1), custom_call_target="tpu_custom_call" | custom-call | tf_op jit(solution)/shard_map/pallas_call | solution.py:455
  3.1 0.0 copy-start.3
  3.1 0.0 copy-start.4
  3.1 6.4 %all-to-all-start = ((bf16[32,32,128]{2,1,0:T(8,128)(2,1)}), bf16[32,32,128]{2,1,0:T(8,128)(2,1)S(1)}, u32[]{:S(2)}, u32[]{:S(2)}) async-start(bf16[32,32,128]{2,1,0:T(8,128)(2,1)} %get-tuple-element.26), calls=%async_computation | async-start | bytes 524288 | tf_op jit(solution)/shard_map/all_to_all | solution.py:469
  9.5 0.4 collective-permute-start.3
  9.9 1.2 %collective-permute-start.4 = (bf16[512,128]{1,0:T(8,128)(2,1)}, bf16[512,128]{1,0:T(8,128)(2,1)S(1)}, u32[]{:S(2)}, u32[]{:S(2)}) collective-permute-start(bf16[512,128]{1,0:T(8,128)(2,1)} %get-tuple-element.39), channel_id=1, source_target_pairs={{0,2},{1,3},{2,0},{3,1},{4,6},{5,7},{6,4},{7,5},{8,10},{9,11},{10,... | collective-permute-start | bytes 393224 | tf_op jit(solution)/shard_map/ppermute | solution.py:427
  11.1 1.2 %collective-permute-start.5 = (bf16[512,128]{1,0:T(8,128)(2,1)}, bf16[512,128]{1,0:T(8,128)(2,1)S(1)}, u32[]{:S(2)}, u32[]{:S(2)}) collective-permute-start(bf16[512,128]{1,0:T(8,128)(2,1)} %get-tuple-element.39), channel_id=1, source_target_pairs={{0,4},{1,5},{2,6},{3,7},{4,0},{5,1},{6,2},{7,3},{8,12},{9,13},{10,... | collective-permute-start | bytes 393224 | tf_op jit(solution)/shard_map/ppermute | solution.py:427
  12.3 0.3 collective-permute-start.6
  12.5 0.0 copy-done
  12.5 0.1 dynamic-slice_bitcast_fusion
  12.6 0.1 copy.19.refs_1_
  12.7 0.0 copy-done.2
  12.7 0.0 copy-done.3
  12.7 0.0 copy-done.4
  12.7 0.9 %copy-done.5 = f32[8,4096]{1,0:T(8,128)S(1)} copy-done((f32[8,4096]{1,0:T(8,128)S(1)}, f32[8,4096]{1,0:T(8,128)}, u32[]{:S(2)}) %copy-start.5) | copy-done | bytes 131096
  13.6 0.7 %copy-done.6 = s32[1,128]{1,0:T(1,128)S(1)} copy-done((s32[1,128]{1,0:T(1,128)S(1)}, s32[1,128]{1,0:T(1,128)}, u32[]{:S(2)}) %copy-start.6) | copy-done | bytes 536
  14.3 1.0 %shard_map.146 = (f32[256,256]{1,0:T(8,128)S(1)}, f32[256,256]{1,0:T(8,128)S(1)}, bf16[1536,256]{1,0:T(8,128)(2,1)S(1)}, f32[256,256]{1,0:T(8,128)S(1)}, s32[1,128]{1,0:T(1,128)S(1)}) custom-call(f32[8,4096]{1,0:T(8,128)S(1)} %copy-done.4, f32[8,4096]{1,0:T(8,128)S(1)} %copy-done.5, bf16[1536,256]{1,0:T(8,128)(2,1)S(1)} %copy-done.2, ...), custom_call_target="tpu_custom_call" | custom-call | tf_op jit(solution)/shard_map/pallas_call | solution.py:452
  15.3 0.0 copy-start.7
  15.3 0.5 copy-done.7
  15.8 2.4 %all-to-all-done.refs_0_ = bf16[32,32,128]{2,1,0:T(8,128)(2,1)S(1)} async-done(((bf16[32,32,128]{2,1,0:T(8,128)(2,1)}), bf16[32,32,128]{2,1,0:T(8,128)(2,1)S(1)}, u32[]{:S(2)}, u32[]{:S(2)}) %all-to-all-start) | async-done | bytes 262176 | tf_op jit(solution)/shard_map/all_to_all | solution.py:469
  18.2 3.7 %shard_map.147 = (f32[8,128]{1,0:T(8,128)S(1)}, f32[256,256]{1,0:T(8,128)S(1)}, f32[256,256]{1,0:T(8,128)S(1)}, bf16[8,32,128]{2,1,0:T(8,128)(2,1)S(1)}, bf16[8,...) custom-call(bf16[32,32,128]{2,1,0:T(8,128)(2,1)S(1)} %all-to-all-done.refs_0_, ...), custom_call_target="tpu_custom_call" | custom-call | tf_op jit(solution)/shard_map/pallas_call | solution.py:452
  21.9 0.0 collective-permute-done.3.refs_0_
  21.9 0.0 collective-permute-done.4.refs_1_
  21.9 0.0 collective-permute-done.5.refs_2_
  21.9 0.0 collective-permute-done.6.refs_3_
  22.0 1.5 %collective-permute-start.7 = (bf16[4,512,128]{2,1,0:T(8,128)(2,1)S(1)}, bf16[4,512,128]{2,1,0:T(8,128)(2,1)S(1)}, u32[]{:S(2)}, u32[]{:S(2)}) collective-permute-start(bf16[4,512,128]{2,1,0:T(8,128)(2,1)S(1)} %shard_map.149.refs_7_), channel_id=1, source_target_pairs={{0,1},{1,0},{2,3},{3,2},{4,5},{5,4},{6,7},{7,6},{8,9},{9,8},{10,11... | collective-permute-start | bytes 1572872 | tf_op jit(solution)/shard_map/ppermute | solution.py:427
  23.5 0.0 collective-permute-start
  23.5 2.9 %collective-permute-start.1 = (bf16[8,32,128]{2,1,0:T(8,128)(2,1)S(1)}, bf16[8,32,128]{2,1,0:T(8,128)(2,1)S(1)}, u32[]{:S(2)}, u32[]{:S(2)}) collective-permute-start(bf16[8,32,128]{2,1,0:T(8,128)(2,1)S(1)} %get-tuple-element.33), channel_id=1, source_target_pairs={{0,16},{8,24},{16,0},{24,8},{1,17},{9,25},{17,1},{25,9},{2,18},{10... | collective-permute-start | bytes 196616 | tf_op jit(solution)/shard_map/ppermute | solution.py:532
  26.4 0.0 collective-permute-start.2
  26.4 1.8 %shard_map.148 = (f32[8,4096]{1,0:T(8,128)}, f32[8,4096]{1,0:T(8,128)}, f32[8,128]{1,0:T(8,128)S(1)}) custom-call(f32[256,256]{1,0:T(8,128)S(1)} %get-tuple-element.35.refs_0_, f32[256,256]{1,0:T(8,128)S(1)} %get-tuple-element.36.refs_1_, bf16[1536,256]{1,0:T(8,128)(2,1)S(1)} %get-tuple-element.29.refs_4_.refs_2_, ...), custom_call_target="tpu_custom_call" | custom-call | tf_op jit(solution)/shard_map/pallas_call | solution.py:452
  28.2 0.0 collective-permute-done.refs_4_.refs_1_
  28.2 2.4 %collective-permute-done.1.refs_5_.refs_2_ = bf16[8,32,128]{2,1,0:T(8,128)(2,1)S(1)} collective-permute-done((bf16[8,32,128]{2,1,0:T(8,128)(2,1)S(1)}, bf16[8,32,128]{2,1,0:T(8,128)(2,1)S(1)}, u32[]{:S(2)}, u32[]{:S(2)}) %collective-permute-start.1) | collective-permute-done | bytes 65568 | tf_op jit(solution)/shard_map/ppermute | solution.py:532
  30.6 2.2 %collective-permute-done.2.refs_6_.refs_3_ = bf16[8,32,128]{2,1,0:T(8,128)(2,1)S(1)} collective-permute-done((bf16[8,32,128]{2,1,0:T(8,128)(2,1)S(1)}, bf16[8,32,128]{2,1,0:T(8,128)(2,1)S(1)}, u32[]{:S(2)}, u32[]{:S(2)}) %collective-permute-start.2) | collective-permute-done | bytes 65568 | tf_op jit(solution)/shard_map/ppermute | solution.py:532
  32.7 0.0 collective-permute-done.7.refs_8_
  32.7 0.5 shard_map.150.refs_4_.refs_0_
  33.2 0.1 collective-permute-start.10
  33.3 1.5 %collective-permute-start.8 = (bf16[288,128]{1,0:T(8,128)(2,1)S(1)}, bf16[288,128]{1,0:T(8,128)(2,1)S(1)}, u32[]{:S(2)}, u32[]{:S(2)}) collective-permute-start(bf16[288,128]{1,0:T(8,128)(2,1)S(1)} %shard_map.150.refs_4_.refs_0_), channel_id=1, source_target_pairs={{0,8},{8,16},{16,24},{24,0},{1,9},{9,17},{17,25},{25,1},{2,10},{10... | collective-permute-start | bytes 221192 | tf_op jit(solution)/shard_map/ppermute | solution.py:532
  34.7 2.7 %collective-permute-start.9 = (bf16[288,128]{1,0:T(8,128)(2,1)S(1)}, bf16[288,128]{1,0:T(8,128)(2,1)S(1)}, u32[]{:S(2)}, u32[]{:S(2)}) collective-permute-start(bf16[288,128]{1,0:T(8,128)(2,1)S(1)} %shard_map.150.refs_4_.refs_0_), channel_id=1, source_target_pairs={{0,16},{8,24},{16,0},{24,8},{1,17},{9,25},{17,1},{25,9},{2,18},{10... | collective-permute-start | bytes 221192 | tf_op jit(solution)/shard_map/ppermute | solution.py:532
  37.5 0.7 %shard_map.151 = bf16[8,96,128]{2,1,0:T(8,128)(2,1)} custom-call(bf16[8,32,128]{2,1,0:T(8,128)(2,1)S(1)} %get-tuple-element.31.refs_3_.refs_0_, bf16[8,32,128]{2,1,0:T(8,128)(2,1)S(1)} %collective-permute-done.refs_4_.refs_1_, bf16[8,32,128]{2,1,0:T(8,128)(2,1)S(1)} %collective-permute-done.1.refs_5_.refs_2_, ...), custom_call_target="tpu_custom_call" | custom-call | tf_op jit(solution)/shard_map/pallas_call | solution.py:452
  38.2 4.9 %all-to-all-start.1 = ((bf16[8,96,128]{2,1,0:T(8,128)(2,1)}), bf16[8,96,128]{2,1,0:T(8,128)(2,1)S(1)}, u32[]{:S(2)}, u32[]{:S(2)}) async-start(bf16[8,96,128]{2,1,0:T(8,128)(2,1)} %shard_map.151), calls=%async_computation.1 | async-start | bytes 393216 | tf_op jit(solution)/shard_map/all_to_all | solution.py:553
  43.0 0.0 collective-permute-done.10.refs_3_
  43.0 0.0 collective-permute-done.8.refs_1_
  43.1 0.0 collective-permute-done.9.refs_2_
  43.1 0.0 copy-start.8
  43.1 1.5 %collective-permute-start.12 = (bf16[288,128]{1,0:T(8,128)(2,1)S(1)}, bf16[288,128]{1,0:T(8,128)(2,1)S(1)}, u32[]{:S(2)}, u32[]{:S(2)}) collective-permute-start(bf16[288,128]{1,0:T(8,128)(2,1)S(1)} %shard_map.153.refs_1_), channel_id=1, source_target_pairs={{0,2},{1,3},{2,0},{3,1},{4,6},{5,7},{6,4},{7,5},{8,10},{9,11},{10,... | collective-permute-start | bytes 221192 | tf_op jit(solution)/shard_map/ppermute | solution.py:427
  44.6 1.2 %collective-permute-start.14 = (bf16[288,128]{1,0:T(8,128)(2,1)S(1)}, bf16[288,128]{1,0:T(8,128)(2,1)S(1)}, u32[]{:S(2)}, u32[]{:S(2)}) collective-permute-start(bf16[288,128]{1,0:T(8,128)(2,1)S(1)} %shard_map.153.refs_1_), channel_id=1, source_target_pairs={{0,4},{1,5},{2,6},{3,7},{4,0},{5,1},{6,2},{7,3},{8,12},{9,13},{10,... | collective-permute-start | bytes 221192 | tf_op jit(solution)/shard_map/ppermute | solution.py:427
  45.8 0.1 collective-permute-start.16
  45.8 1.0 %collective-permute-start.11 = (bf16[288,128]{1,0:T(8,128)(2,1)S(1)}, bf16[288,128]{1,0:T(8,128)(2,1)S(1)}, u32[]{:S(2)}, u32[]{:S(2)}) collective-permute-start(bf16[288,128]{1,0:T(8,128)(2,1)S(1)} %shard_map.153.refs_1_), channel_id=1, source_target_pairs={{0,1},{1,0},{2,3},{3,2},{4,5},{5,4},{6,7},{7,6},{8,9},{9,8},{10,11... | collective-permute-start | bytes 221192 | tf_op jit(solution)/shard_map/ppermute | solution.py:427
  46.8 2.3 %collective-permute-done.12.refs_3_ = bf16[288,128]{1,0:T(8,128)(2,1)S(1)} collective-permute-done((bf16[288,128]{1,0:T(8,128)(2,1)S(1)}, bf16[288,128]{1,0:T(8,128)(2,1)S(1)}, u32[]{:S(2)}, u32[]{:S(2)}) %collective-permute-start.12) | collective-permute-done | bytes 73760 | tf_op jit(solution)/shard_map/ppermute | solution.py:427
  49.1 1.3 %collective-permute-start.13 = (bf16[288,128]{1,0:T(8,128)(2,1)S(1)}, bf16[288,128]{1,0:T(8,128)(2,1)S(1)}, u32[]{:S(2)}, u32[]{:S(2)}) collective-permute-start(bf16[288,128]{1,0:T(8,128)(2,1)S(1)} %collective-permute-done.12.refs_3_), channel_id=1, source_target_pairs={{0,1},{1,0},{2,3},{3,2},{4,5},{5,4},{6,7},{7,6},{8,9},{9,8},{10,11... | collective-permute-start | bytes 221192 | tf_op jit(solution)/shard_map/ppermute | solution.py:427
  50.4 0.0 collective-permute-done.14.refs_5_
  50.4 0.0 collective-permute-start.15
  50.4 1.2 %collective-permute-done.16.refs_7_ = bf16[288,128]{1,0:T(8,128)(2,1)S(1)} collective-permute-done((bf16[288,128]{1,0:T(8,128)(2,1)S(1)}, bf16[288,128]{1,0:T(8,128)(2,1)S(1)}, u32[]{:S(2)}, u32[]{:S(2)}) %collective-permute-start.16) | collective-permute-done | bytes 73760 | tf_op jit(solution)/shard_map/ppermute | solution.py:427
  51.6 0.9 %collective-permute-start.17 = (bf16[288,128]{1,0:T(8,128)(2,1)S(1)}, bf16[288,128]{1,0:T(8,128)(2,1)S(1)}, u32[]{:S(2)}, u32[]{:S(2)}) collective-permute-start(bf16[288,128]{1,0:T(8,128)(2,1)S(1)} %collective-permute-done.16.refs_7_), channel_id=1, source_target_pairs={{0,1},{1,0},{2,3},{3,2},{4,5},{5,4},{6,7},{7,6},{8,9},{9,8},{10,11... | collective-permute-start | bytes 221192 | tf_op jit(solution)/shard_map/ppermute | solution.py:427
  52.5 0.0 all-to-all-done.1.refs_1_
  52.5 0.0 copy-done.1
  52.5 1.1 %shard_map.152 = bf16[256,128]{1,0:T(8,128)(2,1)} custom-call(s32[1]{0:T(128)} %bitcast.refs_6_.refs_0_, bf16[8,96,128]{2,1,0:T(8,128)(2,1)S(1)} %all-to-all-done.1.refs_1_, bf16[768,256]{1,0:T(8,128)(2,1)S(1)} %copy-done.1, s32[1,128]{1,0:T(1,128)S(1)} %copy-done.8), custom_call_target="tpu_custom_call" | custom-call | tf_op jit(solution)/shard_map/pallas_call | solution.py:452
  53.6 0.0 collective-permute-done.11.refs_2_
  53.6 0.0 collective-permute-done.13.refs_4_
  53.6 0.0 collective-permute-done.15.refs_6_
  53.6 0.0 collective-permute-done.17.refs_8_
  53.6 1.1 %shard_map.154 = (f32[768,256]{1,0:T(8,128)}, f32[256,256]{1,0:T(8,128)}, f32[3,768]{1,0:T(4,128)}) custom-call(s32[1]{0:T(128)} %bitcast.3.refs_1_.refs_0_, bf16[288,128]{1,0:T(8,128)(2,1)S(1)} %shard_map.153.refs_1_, bf16[288,128]{1,0:T(8,128)(2,1)S(1)} %collective-permute-done.11.refs_2_, bf16[288,128]{1,0:T(8,128)(2,1)S(1)} %collective-permute-done.12.refs_3_, ...), custom_call_target="tpu_custom_call" | custom-call | tf_op jit(solution)/shard_map/pallas_call | solution.py:452
  (7 shorter events, 0.1 us)
Async XLA Ops:
  0.6 11.9 %copy-start = (f32[768,3]{0,1:T(4,128)S(1)}, f32[768,3]{0,1:T(4,128)}, u32[]{:S(2)}) copy-start(f32[768,3]{0,1:T(4,128)} %param.14) | copy-start | bytes 27652
  0.6 12.1 %copy-start.2 = (bf16[1536,256]{1,0:T(8,128)(2,1)S(1)}, bf16[1536,256]{1,0:T(8,128)(2,1)}, u32[]{:S(2)}) copy-start(bf16[1536,256]{1,0:T(8,128)(2,1)} %constant.18.clone.refs_2_) | copy-start | bytes 2359300
  3.1 9.6 %copy-start.3 = (f32[256,256]{1,0:T(8,128)S(1)}, f32[256,256]{1,0:T(8,128)}, u32[]{:S(2)}) copy-start(f32[256,256]{1,0:T(8,128)} %constant.19.clone.refs_3_) | copy-start | bytes 786436
  3.1 9.6 %copy-start.4 = (f32[8,4096]{1,0:T(8,128)S(1)}, f32[8,4096]{1,0:T(8,128)}, u32[]{:S(2)}) copy-start(f32[8,4096]{1,0:T(8,128)} %refs_0_.1) | copy-start | bytes 393220
  3.1 15.1 %all-to-all-start = ((bf16[32,32,128]{2,1,0:T(8,128)(2,1)}), bf16[32,32,128]{2,1,0:T(8,128)(2,1)S(1)}, u32[]{:S(2)}, u32[]{:S(2)}) async-start(bf16[32,32,128]{2,1,0:T(8,128)(2,1)} %get-tuple-element.26), calls=%async_computation | async-start | bytes 524288 | tf_op jit(solution)/shard_map/all_to_all | solution.py:469
  9.5 12.4 %collective-permute-start.3 = (bf16[512,128]{1,0:T(8,128)(2,1)}, bf16[512,128]{1,0:T(8,128)(2,1)S(1)}, u32[]{:S(2)}, u32[]{:S(2)}) collective-permute-start(bf16[512,128]{1,0:T(8,128)(2,1)} %get-tuple-element.39), channel_id=1, source_target_pairs={{0,1},{1,0},{2,3},{3,2},{4,5},{5,4},{6,7},{7,6},{8,9},{9,8},{10,11... | collective-permute-start | bytes 393224 | tf_op jit(solution)/shard_map/ppermute | solution.py:427
  9.9 12.0 %collective-permute-start.4 = (bf16[512,128]{1,0:T(8,128)(2,1)}, bf16[512,128]{1,0:T(8,128)(2,1)S(1)}, u32[]{:S(2)}, u32[]{:S(2)}) collective-permute-start(bf16[512,128]{1,0:T(8,128)(2,1)} %get-tuple-element.39), channel_id=1, source_target_pairs={{0,2},{1,3},{2,0},{3,1},{4,6},{5,7},{6,4},{7,5},{8,10},{9,11},{10,... | collective-permute-start | bytes 393224 | tf_op jit(solution)/shard_map/ppermute | solution.py:427
  11.1 10.8 %collective-permute-start.5 = (bf16[512,128]{1,0:T(8,128)(2,1)}, bf16[512,128]{1,0:T(8,128)(2,1)S(1)}, u32[]{:S(2)}, u32[]{:S(2)}) collective-permute-start(bf16[512,128]{1,0:T(8,128)(2,1)} %get-tuple-element.39), channel_id=1, source_target_pairs={{0,4},{1,5},{2,6},{3,7},{4,0},{5,1},{6,2},{7,3},{8,12},{9,13},{10,... | collective-permute-start | bytes 393224 | tf_op jit(solution)/shard_map/ppermute | solution.py:427
  12.3 9.7 %collective-permute-start.6 = (bf16[512,128]{1,0:T(8,128)(2,1)}, bf16[512,128]{1,0:T(8,128)(2,1)S(1)}, u32[]{:S(2)}, u32[]{:S(2)}) collective-permute-start(bf16[512,128]{1,0:T(8,128)(2,1)} %get-tuple-element.39), channel_id=1, source_target_pairs={{0,6},{1,7},{2,4},{3,5},{4,2},{5,3},{6,0},{7,1},{8,14},{9,15},{10,... | collective-permute-start | bytes 393224 | tf_op jit(solution)/shard_map/ppermute | solution.py:427
  12.7 0.9 %copy-start.5 = (f32[8,4096]{1,0:T(8,128)S(1)}, f32[8,4096]{1,0:T(8,128)}, u32[]{:S(2)}) copy-start(f32[8,4096]{1,0:T(8,128)} %refs_1_.1) | copy-start | bytes 393220
  13.6 0.7 %copy-start.6 = (s32[1,128]{1,0:T(1,128)S(1)}, s32[1,128]{1,0:T(1,128)}, u32[]{:S(2)}) copy-start(s32[1,128]{1,0:T(1,128)} %refs_4_.1) | copy-start | bytes 1540
  15.3 0.5 copy-start.7
  22.0 10.8 %collective-permute-start.7 = (bf16[4,512,128]{2,1,0:T(8,128)(2,1)S(1)}, bf16[4,512,128]{2,1,0:T(8,128)(2,1)S(1)}, u32[]{:S(2)}, u32[]{:S(2)}) collective-permute-start(bf16[4,512,128]{2,1,0:T(8,128)(2,1)S(1)} %shard_map.149.refs_7_), channel_id=1, source_target_pairs={{0,1},{1,0},{2,3},{3,2},{4,5},{5,4},{6,7},{7,6},{8,9},{9,8},{10,11... | collective-permute-start | bytes 1572872 | tf_op jit(solution)/shard_map/ppermute | solution.py:427
  23.5 4.6 %collective-permute-start = (bf16[8,32,128]{2,1,0:T(8,128)(2,1)S(1)}, bf16[8,32,128]{2,1,0:T(8,128)(2,1)S(1)}, u32[]{:S(2)}, u32[]{:S(2)}) collective-permute-start(bf16[8,32,128]{2,1,0:T(8,128)(2,1)S(1)} %get-tuple-element.32), channel_id=1, source_target_pairs={{0,8},{8,16},{16,24},{24,0},{1,9},{9,17},{17,25},{25,1},{2,10},{10... | collective-permute-start | bytes 196616 | tf_op jit(solution)/shard_map/ppermute | solution.py:532
  23.5 7.0 %collective-permute-start.1 = (bf16[8,32,128]{2,1,0:T(8,128)(2,1)S(1)}, bf16[8,32,128]{2,1,0:T(8,128)(2,1)S(1)}, u32[]{:S(2)}, u32[]{:S(2)}) collective-permute-start(bf16[8,32,128]{2,1,0:T(8,128)(2,1)S(1)} %get-tuple-element.33), channel_id=1, source_target_pairs={{0,16},{8,24},{16,0},{24,8},{1,17},{9,25},{17,1},{25,9},{2,18},{10... | collective-permute-start | bytes 196616 | tf_op jit(solution)/shard_map/ppermute | solution.py:532
  26.4 6.3 %collective-permute-start.2 = (bf16[8,32,128]{2,1,0:T(8,128)(2,1)S(1)}, bf16[8,32,128]{2,1,0:T(8,128)(2,1)S(1)}, u32[]{:S(2)}, u32[]{:S(2)}) collective-permute-start(bf16[8,32,128]{2,1,0:T(8,128)(2,1)S(1)} %get-tuple-element.34), channel_id=1, source_target_pairs={{0,24},{8,0},{16,8},{24,16},{1,25},{9,1},{17,9},{25,17},{2,26},{10... | collective-permute-start | bytes 196616 | tf_op jit(solution)/shard_map/ppermute | solution.py:532
  33.2 9.8 %collective-permute-start.10 = (bf16[288,128]{1,0:T(8,128)(2,1)S(1)}, bf16[288,128]{1,0:T(8,128)(2,1)S(1)}, u32[]{:S(2)}, u32[]{:S(2)}) collective-permute-start(bf16[288,128]{1,0:T(8,128)(2,1)S(1)} %shard_map.150.refs_4_.refs_0_), channel_id=1, source_target_pairs={{0,24},{8,0},{16,8},{24,16},{1,25},{9,1},{17,9},{25,17},{2,26},{10... | collective-permute-start | bytes 221192 | tf_op jit(solution)/shard_map/ppermute | solution.py:532
  33.3 9.8 %collective-permute-start.8 = (bf16[288,128]{1,0:T(8,128)(2,1)S(1)}, bf16[288,128]{1,0:T(8,128)(2,1)S(1)}, u32[]{:S(2)}, u32[]{:S(2)}) collective-permute-start(bf16[288,128]{1,0:T(8,128)(2,1)S(1)} %shard_map.150.refs_4_.refs_0_), channel_id=1, source_target_pairs={{0,8},{8,16},{16,24},{24,0},{1,9},{9,17},{17,25},{25,1},{2,10},{10... | collective-permute-start | bytes 221192 | tf_op jit(solution)/shard_map/ppermute | solution.py:532
  34.7 8.3 %collective-permute-start.9 = (bf16[288,128]{1,0:T(8,128)(2,1)S(1)}, bf16[288,128]{1,0:T(8,128)(2,1)S(1)}, u32[]{:S(2)}, u32[]{:S(2)}) collective-permute-start(bf16[288,128]{1,0:T(8,128)(2,1)S(1)} %shard_map.150.refs_4_.refs_0_), channel_id=1, source_target_pairs={{0,16},{8,24},{16,0},{24,8},{1,17},{9,25},{17,1},{25,9},{2,18},{10... | collective-permute-start | bytes 221192 | tf_op jit(solution)/shard_map/ppermute | solution.py:532
  38.2 14.3 %copy-start.1 = (bf16[768,256]{1,0:T(8,128)(2,1)S(1)}, bf16[768,256]{1,0:T(8,128)(2,1)}, u32[]{:S(2)}) copy-start(bf16[768,256]{1,0:T(8,128)(2,1)} %refs_2_.2) | copy-start | bytes 1179652
  38.2 14.3 %all-to-all-start.1 = ((bf16[8,96,128]{2,1,0:T(8,128)(2,1)}), bf16[8,96,128]{2,1,0:T(8,128)(2,1)S(1)}, u32[]{:S(2)}, u32[]{:S(2)}) async-start(bf16[8,96,128]{2,1,0:T(8,128)(2,1)} %shard_map.151), calls=%async_computation.1 | async-start | bytes 393216 | tf_op jit(solution)/shard_map/all_to_all | solution.py:553
  43.1 9.4 %copy-start.8 = (s32[1,128]{1,0:T(1,128)S(1)}, s32[1,128]{1,0:T(1,128)}, u32[]{:S(2)}) copy-start(s32[1,128]{1,0:T(1,128)} %copy-done.7) | copy-start | bytes 1540
  43.1 6.0 %collective-permute-start.12 = (bf16[288,128]{1,0:T(8,128)(2,1)S(1)}, bf16[288,128]{1,0:T(8,128)(2,1)S(1)}, u32[]{:S(2)}, u32[]{:S(2)}) collective-permute-start(bf16[288,128]{1,0:T(8,128)(2,1)S(1)} %shard_map.153.refs_1_), channel_id=1, source_target_pairs={{0,2},{1,3},{2,0},{3,1},{4,6},{5,7},{6,4},{7,5},{8,10},{9,11},{10,... | collective-permute-start | bytes 221192 | tf_op jit(solution)/shard_map/ppermute | solution.py:427
  44.6 5.9 %collective-permute-start.14 = (bf16[288,128]{1,0:T(8,128)(2,1)S(1)}, bf16[288,128]{1,0:T(8,128)(2,1)S(1)}, u32[]{:S(2)}, u32[]{:S(2)}) collective-permute-start(bf16[288,128]{1,0:T(8,128)(2,1)S(1)} %shard_map.153.refs_1_), channel_id=1, source_target_pairs={{0,4},{1,5},{2,6},{3,7},{4,0},{5,1},{6,2},{7,3},{8,12},{9,13},{10,... | collective-permute-start | bytes 221192 | tf_op jit(solution)/shard_map/ppermute | solution.py:427
  45.8 5.8 %collective-permute-start.16 = (bf16[288,128]{1,0:T(8,128)(2,1)S(1)}, bf16[288,128]{1,0:T(8,128)(2,1)S(1)}, u32[]{:S(2)}, u32[]{:S(2)}) collective-permute-start(bf16[288,128]{1,0:T(8,128)(2,1)S(1)} %shard_map.153.refs_1_), channel_id=1, source_target_pairs={{0,6},{1,7},{2,4},{3,5},{4,2},{5,3},{6,0},{7,1},{8,14},{9,15},{10,... | collective-permute-start | bytes 221192 | tf_op jit(solution)/shard_map/ppermute | solution.py:427
  45.8 7.8 %collective-permute-start.11 = (bf16[288,128]{1,0:T(8,128)(2,1)S(1)}, bf16[288,128]{1,0:T(8,128)(2,1)S(1)}, u32[]{:S(2)}, u32[]{:S(2)}) collective-permute-start(bf16[288,128]{1,0:T(8,128)(2,1)S(1)} %shard_map.153.refs_1_), channel_id=1, source_target_pairs={{0,1},{1,0},{2,3},{3,2},{4,5},{5,4},{6,7},{7,6},{8,9},{9,8},{10,11... | collective-permute-start | bytes 221192 | tf_op jit(solution)/shard_map/ppermute | solution.py:427
  49.1 4.5 %collective-permute-start.13 = (bf16[288,128]{1,0:T(8,128)(2,1)S(1)}, bf16[288,128]{1,0:T(8,128)(2,1)S(1)}, u32[]{:S(2)}, u32[]{:S(2)}) collective-permute-start(bf16[288,128]{1,0:T(8,128)(2,1)S(1)} %collective-permute-done.12.refs_3_), channel_id=1, source_target_pairs={{0,1},{1,0},{2,3},{3,2},{4,5},{5,4},{6,7},{7,6},{8,9},{9,8},{10,11... | collective-permute-start | bytes 221192 | tf_op jit(solution)/shard_map/ppermute | solution.py:427
  50.4 3.2 %collective-permute-start.15 = (bf16[288,128]{1,0:T(8,128)(2,1)S(1)}, bf16[288,128]{1,0:T(8,128)(2,1)S(1)}, u32[]{:S(2)}, u32[]{:S(2)}) collective-permute-start(bf16[288,128]{1,0:T(8,128)(2,1)S(1)} %collective-permute-done.14.refs_5_), channel_id=1, source_target_pairs={{0,1},{1,0},{2,3},{3,2},{4,5},{5,4},{6,7},{7,6},{8,9},{9,8},{10,11... | collective-permute-start | bytes 221192 | tf_op jit(solution)/shard_map/ppermute | solution.py:427
  51.6 2.0 %collective-permute-start.17 = (bf16[288,128]{1,0:T(8,128)(2,1)S(1)}, bf16[288,128]{1,0:T(8,128)(2,1)S(1)}, u32[]{:S(2)}, u32[]{:S(2)}) collective-permute-start(bf16[288,128]{1,0:T(8,128)(2,1)S(1)} %collective-permute-done.16.refs_7_), channel_id=1, source_target_pairs={{0,1},{1,0},{2,3},{3,2},{4,5},{5,4},{6,7},{7,6},{8,9},{9,8},{10,11... | collective-permute-start | bytes 221192 | tf_op jit(solution)/shard_map/ppermute | solution.py:427

commit v8 on v7

--- a/solution.py
+++ b/solution.py
@@ -10,6 +10,7 @@
 
 AXES = ("seq", "fft")
 LANES = 128
+TAPS = 16
 bf16 = jnp.bfloat16
 f32 = jnp.float32
 PARAMS = pltpu.CompilerParams(vmem_limit_bytes=24 * 1024 * 1024)
@@ -262,22 +263,20 @@
     ]
     h_one = (spec_one[:, :LANES], spec_one[:, LANES:])
     h_two = (spec_two[:, :LANES], spec_two[:, LANES:])
-    value_spec, second_spec = forward([value, out_grad * gate_two], first, second, twist)
-    first_mix, grad_first_out = backward(
-        [times(h_one, value_spec), conj_times(h_two, second_spec)],
-        back,
-        second,
-        twist,
-    )
-    first_spec, grad_first_spec = forward(
-        [gate_one * first_mix, gate_one * grad_first_out], first, second, twist
-    )
-    second_mix, grad_value = backward(
-        [times(h_two, first_spec), conj_times(h_one, grad_first_spec)],
-        back,
-        second,
-        twist,
-    )
+
+    def spectrum(signal):
+        return forward([signal], first, second, twist)[0]
+
+    def signal_of(spec):
+        return backward([spec], back, second, twist)[0]
+
+    value_spec, second_spec = spectrum(value), spectrum(out_grad * gate_two)
+    first_mix = signal_of(times(h_one, value_spec))
+    grad_first_out = signal_of(conj_times(h_two, second_spec))
+    first_spec = spectrum(gate_one * first_mix)
+    grad_first_spec = spectrum(gate_one * grad_first_out)
+    second_mix = signal_of(times(h_two, first_spec))
+    grad_value = signal_of(conj_times(h_one, grad_first_spec))
     product_one[...] = jnp.concatenate(conj_times(value_spec, grad_first_spec), axis=1)
     product_two[...] = jnp.concatenate(conj_times(first_spec, second_spec), axis=1)
     grads = [grad_value, grad_first_out * first_mix, out_grad * second_mix]
@@ -354,9 +353,9 @@
         owner = lax.rem(line[0] + lines - k, lines)
         spot = pl.ds(pl.multiple_of(owner * size, size), size)
         partial_out[spot] = jnp.concatenate(parts, axis=0).astype(bf16)
-    tail = jnp.concatenate([short[...]] * lines, axis=0)
-    owner = lax.broadcasted_iota(jnp.int32, tail.shape, 0) // channels
-    partial_out[lines * size :] = jnp.where(owner == line[0], tail, 0.0).astype(bf16)
+    tail = pltpu.roll(short[...], line[0] * TAPS, 1)
+    tail = jnp.concatenate([tail, jnp.zeros_like(tail)], axis=0)
+    partial_out[lines * size :] = tail.astype(bf16)
 
 
 def return_kernel(channels, *refs):
@@ -411,8 +410,10 @@
                     w_in_out[spot, low:high] = rows[start : start + channels]
                 start = base + 3 * channels
                 out_rows[pl.ds(first, channels), low:high] = rows[start : start + channels]
-            start = lines * size + i * channels
-            short_rows[pl.ds(first, channels), :] = rows[start : start + channels]
+            start = lines * size
+            short_rows[pl.ds(first, channels), :] = pltpu.roll(
+                rows[start : start + channels], (LANES - i * TAPS) % LANES, 1
+            )
     w_out_out[...] = out_rows[...].T
     short = short_rows[...].T
     for s in range(3):
@@ -532,7 +533,7 @@
             return lax.ppermute(value, "seq", pairs)
 
         met = [sent[0]] + [ahead(sent[k], k) for k in range(1, lines)]
-        size = lines * height + lines * channels
+        size = lines * height + 2 * channels
         partial = call(
             lambda *refs: weights_kernel(channels, scale, lines, *refs),
             shape((size, LANES), bf16),

time: 55.1 us -> 56.7 us (1.029)
  Pallas kernels: 12.5 us -> 14.2 us
    pallas_call x9, Pallas kernels: 10 us -> 11.8 us  [call(): pl.pallas_call(kernel, out_shape=outs, compiler_params=PARAMS, **options)]
  transfers between devices with their start and end apart: 20 -> 20, of which waited for: 5 -> 5; matrix products, arithmetic and copies ran while one was open for 0% -> 0% of each run, Pallas kernels for 15% -> 18%
where the time goes in v8:
time: 56.7 us; the launch traced here: 56.4 us
  starting transfers between devices  28.8 us (51%)
  Pallas kernels  14.2 us (25%)
  waiting for transfers between devices  10.2 us (18%)
  local copies, waits for them, and re-layouts  2.27 us (4%)
  between operations  0.81 us (1%)
    pallas_call x9, Pallas kernels, call(): pl.pallas_call(kernel, out_shape=outs, compiler_params=PARAMS, **options)  11.8 us
    ppermute x12, starting transfers between devices, swapped(): return lax.ppermute(value, 'fft', [(i, i ^ distance) for i in range(plane)])  10.5 us
    ppermute x6, starting transfers between devices, ahead(): return lax.ppermute(value, 'seq', pairs)  7.07 us
    all_to_all x1, starting transfers between devices, local(): lax.all_to_all(streams, AXES, split_axis=0, concat_axis=0, tiled=True)  6.36 us
    all_to_all x1, starting transfers between devices, local(): back = lax.all_to_all(moved, 'fft', split_axis=0, concat_axis=0, tiled=True)  4.86 us
    ppermute x6, waiting for transfers between devices, ahead(): return lax.ppermute(value, 'seq', pairs)  4.58 us
    ppermute x12, waiting for transfers between devices, swapped(): return lax.ppermute(value, 'fft', [(i, i ^ distance) for i in range(plane)])  3.27 us
    pallas_call x1, Pallas kernels, local(): pl.pallas_call(project_kernel, out_shape=(shape(dims, bf16), shape((2 * w...  2.41 us
  transfers between devices with their start and end apart: 20, of which 5 were waited for; matrix products, arithmetic and copies ran while one was open for 0% of the time, Pallas kernels for 18%

profile of v8, /device:TPU:9, one launch (start us, length us, event | category | flops | bytes accessed | tf_op | source)
XLA Modules:
  0.0 56.4 jit_solution(13273898998153146124)
XLA Ops:
  0.6 0.0 copy-start
  0.6 0.0 copy-start.2
  0.7 2.4 %shard_map.145 = (bf16[32,32,128]{2,1,0:T(8,128)(2,1)}, bf16[512,128]{1,0:T(8,128)(2,1)}) custom-call(bf16[256,128]{1,0:T(8,128)(2,1)} %features_at.1, s32[1,128]{1,0:T(1,128)} %refs_4_.1, bf16[256,128]{1,0:T(8,128)(2,1)} %cotangent_at.1, bf16[768,256]{1,0:T(8,128)(2,1)} %refs_2_.2, bf16[256,256]{1,0:T(8,128)(2,1)} %w_out_at.1), custom_call_target="tpu_custom_call" | custom-call | tf_op jit(solution)/shard_map/pallas_call | solution.py:456
  3.1 0.0 copy-start.3
  3.1 0.0 copy-start.4
  3.1 6.4 %all-to-all-start = ((bf16[32,32,128]{2,1,0:T(8,128)(2,1)}), bf16[32,32,128]{2,1,0:T(8,128)(2,1)S(1)}, u32[]{:S(2)}, u32[]{:S(2)}) async-start(bf16[32,32,128]{2,1,0:T(8,128)(2,1)} %get-tuple-element.26), calls=%async_computation | async-start | bytes 524288 | tf_op jit(solution)/shard_map/all_to_all | solution.py:470
  9.5 0.4 collective-permute-start.3
  9.9 1.2 %collective-permute-start.4 = (bf16[512,128]{1,0:T(8,128)(2,1)}, bf16[512,128]{1,0:T(8,128)(2,1)S(1)}, u32[]{:S(2)}, u32[]{:S(2)}) collective-permute-start(bf16[512,128]{1,0:T(8,128)(2,1)} %get-tuple-element.39), channel_id=1, source_target_pairs={{0,2},{1,3},{2,0},{3,1},{4,6},{5,7},{6,4},{7,5},{8,10},{9,11},{10,... | collective-permute-start | bytes 393224 | tf_op jit(solution)/shard_map/ppermute | solution.py:428
  11.1 1.2 %collective-permute-start.5 = (bf16[512,128]{1,0:T(8,128)(2,1)}, bf16[512,128]{1,0:T(8,128)(2,1)S(1)}, u32[]{:S(2)}, u32[]{:S(2)}) collective-permute-start(bf16[512,128]{1,0:T(8,128)(2,1)} %get-tuple-element.39), channel_id=1, source_target_pairs={{0,4},{1,5},{2,6},{3,7},{4,0},{5,1},{6,2},{7,3},{8,12},{9,13},{10,... | collective-permute-start | bytes 393224 | tf_op jit(solution)/shard_map/ppermute | solution.py:428
  12.3 0.3 collective-permute-start.6
  12.5 0.0 copy-done
  12.5 0.1 dynamic-slice_bitcast_fusion
  12.6 0.1 copy.19.refs_1_
  12.7 0.0 copy-done.2
  12.7 0.0 copy-done.3
  12.7 0.0 copy-done.4
  12.7 0.9 %copy-done.5 = f32[8,4096]{1,0:T(8,128)S(1)} copy-done((f32[8,4096]{1,0:T(8,128)S(1)}, f32[8,4096]{1,0:T(8,128)}, u32[]{:S(2)}) %copy-start.5) | copy-done | bytes 131096
  13.6 0.7 %copy-done.6 = s32[1,128]{1,0:T(1,128)S(1)} copy-done((s32[1,128]{1,0:T(1,128)S(1)}, s32[1,128]{1,0:T(1,128)}, u32[]{:S(2)}) %copy-start.6) | copy-done | bytes 536
  14.3 1.0 %shard_map.146 = (f32[256,256]{1,0:T(8,128)S(1)}, f32[256,256]{1,0:T(8,128)S(1)}, bf16[1536,256]{1,0:T(8,128)(2,1)S(1)}, f32[256,256]{1,0:T(8,128)S(1)}, s32[1,128]{1,0:T(1,128)S(1)}) custom-call(f32[8,4096]{1,0:T(8,128)S(1)} %copy-done.4, f32[8,4096]{1,0:T(8,128)S(1)} %copy-done.5, bf16[1536,256]{1,0:T(8,128)(2,1)S(1)} %copy-done.2, ...), custom_call_target="tpu_custom_call" | custom-call | tf_op jit(solution)/shard_map/pallas_call | solution.py:453
  15.3 0.0 copy-start.7
  15.3 0.5 copy-done.7
  15.8 2.4 %all-to-all-done.refs_0_ = bf16[32,32,128]{2,1,0:T(8,128)(2,1)S(1)} async-done(((bf16[32,32,128]{2,1,0:T(8,128)(2,1)}), bf16[32,32,128]{2,1,0:T(8,128)(2,1)S(1)}, u32[]{:S(2)}, u32[]{:S(2)}) %all-to-all-start) | async-done | bytes 262176 | tf_op jit(solution)/shard_map/all_to_all | solution.py:470
  18.2 5.5 %shard_map.147 = (f32[8,128]{1,0:T(8,128)S(1)}, f32[256,256]{1,0:T(8,128)S(1)}, f32[256,256]{1,0:T(8,128)S(1)}, bf16[8,32,128]{2,1,0:T(8,128)(2,1)S(1)}, bf16[8,...) custom-call(bf16[32,32,128]{2,1,0:T(8,128)(2,1)S(1)} %all-to-all-done.refs_0_, ...), custom_call_target="tpu_custom_call" | custom-call | tf_op jit(solution)/shard_map/pallas_call | solution.py:453
  23.7 0.0 collective-permute-done.3.refs_0_
  23.7 0.0 collective-permute-done.4.refs_1_
  23.7 0.0 collective-permute-done.5.refs_2_
  23.7 0.0 collective-permute-done.6.refs_3_
  23.8 1.6 %collective-permute-start.7 = (bf16[4,512,128]{2,1,0:T(8,128)(2,1)S(1)}, bf16[4,512,128]{2,1,0:T(8,128)(2,1)S(1)}, u32[]{:S(2)}, u32[]{:S(2)}) collective-permute-start(bf16[4,512,128]{2,1,0:T(8,128)(2,1)S(1)} %shard_map.149.refs_7_), channel_id=1, source_target_pairs={{0,1},{1,0},{2,3},{3,2},{4,5},{5,4},{6,7},{7,6},{8,9},{9,8},{10,11... | collective-permute-start | bytes 1572872 | tf_op jit(solution)/shard_map/ppermute | solution.py:428
  25.3 0.0 collective-permute-start
  25.3 2.8 %collective-permute-start.1 = (bf16[8,32,128]{2,1,0:T(8,128)(2,1)S(1)}, bf16[8,32,128]{2,1,0:T(8,128)(2,1)S(1)}, u32[]{:S(2)}, u32[]{:S(2)}) collective-permute-start(bf16[8,32,128]{2,1,0:T(8,128)(2,1)S(1)} %get-tuple-element.33), channel_id=1, source_target_pairs={{0,16},{8,24},{16,0},{24,8},{1,17},{9,25},{17,1},{25,9},{2,18},{10... | collective-permute-start | bytes 196616 | tf_op jit(solution)/shard_map/ppermute | solution.py:533
  28.2 0.0 collective-permute-start.2
  28.2 1.8 %shard_map.148 = (f32[8,4096]{1,0:T(8,128)}, f32[8,4096]{1,0:T(8,128)}, f32[8,128]{1,0:T(8,128)S(1)}) custom-call(f32[256,256]{1,0:T(8,128)S(1)} %get-tuple-element.35.refs_0_, f32[256,256]{1,0:T(8,128)S(1)} %get-tuple-element.36.refs_1_, bf16[1536,256]{1,0:T(8,128)(2,1)S(1)} %get-tuple-element.29.refs_4_.refs_2_, ...), custom_call_target="tpu_custom_call" | custom-call | tf_op jit(solution)/shard_map/pallas_call | solution.py:453
  30.0 0.0 collective-permute-done.refs_4_.refs_1_
  30.0 2.4 %collective-permute-done.1.refs_5_.refs_2_ = bf16[8,32,128]{2,1,0:T(8,128)(2,1)S(1)} collective-permute-done((bf16[8,32,128]{2,1,0:T(8,128)(2,1)S(1)}, bf16[8,32,128]{2,1,0:T(8,128)(2,1)S(1)}, u32[]{:S(2)}, u32[]{:S(2)}) %collective-permute-start.1) | collective-permute-done | bytes 65568 | tf_op jit(solution)/shard_map/ppermute | solution.py:533
  32.3 2.2 %collective-permute-done.2.refs_6_.refs_3_ = bf16[8,32,128]{2,1,0:T(8,128)(2,1)S(1)} collective-permute-done((bf16[8,32,128]{2,1,0:T(8,128)(2,1)S(1)}, bf16[8,32,128]{2,1,0:T(8,128)(2,1)S(1)}, u32[]{:S(2)}, u32[]{:S(2)}) %collective-permute-start.2) | collective-permute-done | bytes 65568 | tf_op jit(solution)/shard_map/ppermute | solution.py:533
  34.5 0.0 collective-permute-done.7.refs_8_
  34.5 0.5 shard_map.150.refs_4_.refs_0_
  35.0 0.1 collective-permute-start.10
  35.1 1.5 %collective-permute-start.8 = (bf16[272,128]{1,0:T(8,128)(2,1)S(1)}, bf16[272,128]{1,0:T(8,128)(2,1)S(1)}, u32[]{:S(2)}, u32[]{:S(2)}) collective-permute-start(bf16[272,128]{1,0:T(8,128)(2,1)S(1)} %shard_map.150.refs_4_.refs_0_), channel_id=1, source_target_pairs={{0,8},{8,16},{16,24},{24,0},{1,9},{9,17},{17,25},{25,1},{2,10},{10... | collective-permute-start | bytes 208904 | tf_op jit(solution)/shard_map/ppermute | solution.py:533
  36.5 2.7 %collective-permute-start.9 = (bf16[272,128]{1,0:T(8,128)(2,1)S(1)}, bf16[272,128]{1,0:T(8,128)(2,1)S(1)}, u32[]{:S(2)}, u32[]{:S(2)}) collective-permute-start(bf16[272,128]{1,0:T(8,128)(2,1)S(1)} %shard_map.150.refs_4_.refs_0_), channel_id=1, source_target_pairs={{0,16},{8,24},{16,0},{24,8},{1,17},{9,25},{17,1},{25,9},{2,18},{10... | collective-permute-start | bytes 208904 | tf_op jit(solution)/shard_map/ppermute | solution.py:533
  39.3 0.7 %shard_map.151 = bf16[8,96,128]{2,1,0:T(8,128)(2,1)} custom-call(bf16[8,32,128]{2,1,0:T(8,128)(2,1)S(1)} %get-tuple-element.31.refs_3_.refs_0_, bf16[8,32,128]{2,1,0:T(8,128)(2,1)S(1)} %collective-permute-done.refs_4_.refs_1_, bf16[8,32,128]{2,1,0:T(8,128)(2,1)S(1)} %collective-permute-done.1.refs_5_.refs_2_, ...), custom_call_target="tpu_custom_call" | custom-call | tf_op jit(solution)/shard_map/pallas_call | solution.py:453
  40.0 4.9 %all-to-all-start.1 = ((bf16[8,96,128]{2,1,0:T(8,128)(2,1)}), bf16[8,96,128]{2,1,0:T(8,128)(2,1)S(1)}, u32[]{:S(2)}, u32[]{:S(2)}) async-start(bf16[8,96,128]{2,1,0:T(8,128)(2,1)} %shard_map.151), calls=%async_computation.1 | async-start | bytes 393216 | tf_op jit(solution)/shard_map/all_to_all | solution.py:554
  44.8 0.0 collective-permute-done.10.refs_3_
  44.8 0.0 collective-permute-done.8.refs_1_
  44.8 0.0 collective-permute-done.9.refs_2_
  44.9 0.0 copy-start.8
  44.9 1.5 %collective-permute-start.12 = (bf16[272,128]{1,0:T(8,128)(2,1)S(1)}, bf16[272,128]{1,0:T(8,128)(2,1)S(1)}, u32[]{:S(2)}, u32[]{:S(2)}) collective-permute-start(bf16[272,128]{1,0:T(8,128)(2,1)S(1)} %shard_map.153.refs_1_), channel_id=1, source_target_pairs={{0,2},{1,3},{2,0},{3,1},{4,6},{5,7},{6,4},{7,5},{8,10},{9,11},{10,... | collective-permute-start | bytes 208904 | tf_op jit(solution)/shard_map/ppermute | solution.py:428
  46.4 1.2 %collective-permute-start.14 = (bf16[272,128]{1,0:T(8,128)(2,1)S(1)}, bf16[272,128]{1,0:T(8,128)(2,1)S(1)}, u32[]{:S(2)}, u32[]{:S(2)}) collective-permute-start(bf16[272,128]{1,0:T(8,128)(2,1)S(1)} %shard_map.153.refs_1_), channel_id=1, source_target_pairs={{0,4},{1,5},{2,6},{3,7},{4,0},{5,1},{6,2},{7,3},{8,12},{9,13},{10,... | collective-permute-start | bytes 208904 | tf_op jit(solution)/shard_map/ppermute | solution.py:428
  47.6 0.1 collective-permute-start.16
  47.6 1.0 %collective-permute-start.11 = (bf16[272,128]{1,0:T(8,128)(2,1)S(1)}, bf16[272,128]{1,0:T(8,128)(2,1)S(1)}, u32[]{:S(2)}, u32[]{:S(2)}) collective-permute-start(bf16[272,128]{1,0:T(8,128)(2,1)S(1)} %shard_map.153.refs_1_), channel_id=1, source_target_pairs={{0,1},{1,0},{2,3},{3,2},{4,5},{5,4},{6,7},{7,6},{8,9},{9,8},{10,11... | collective-permute-start | bytes 208904 | tf_op jit(solution)/shard_map/ppermute | solution.py:428
  48.6 2.2 %collective-permute-done.12.refs_3_ = bf16[272,128]{1,0:T(8,128)(2,1)S(1)} collective-permute-done((bf16[272,128]{1,0:T(8,128)(2,1)S(1)}, bf16[272,128]{1,0:T(8,128)(2,1)S(1)}, u32[]{:S(2)}, u32[]{:S(2)}) %collective-permute-start.12) | collective-permute-done | bytes 69664 | tf_op jit(solution)/shard_map/ppermute | solution.py:428
  50.8 1.3 %collective-permute-start.13 = (bf16[272,128]{1,0:T(8,128)(2,1)S(1)}, bf16[272,128]{1,0:T(8,128)(2,1)S(1)}, u32[]{:S(2)}, u32[]{:S(2)}) collective-permute-start(bf16[272,128]{1,0:T(8,128)(2,1)S(1)} %collective-permute-done.12.refs_3_), channel_id=1, source_target_pairs={{0,1},{1,0},{2,3},{3,2},{4,5},{5,4},{6,7},{7,6},{8,9},{9,8},{10,11... | collective-permute-start | bytes 208904 | tf_op jit(solution)/shard_map/ppermute | solution.py:428
  52.1 0.0 collective-permute-done.14.refs_5_
  52.1 0.0 collective-permute-start.15
  52.1 1.1 %collective-permute-done.16.refs_7_ = bf16[272,128]{1,0:T(8,128)(2,1)S(1)} collective-permute-done((bf16[272,128]{1,0:T(8,128)(2,1)S(1)}, bf16[272,128]{1,0:T(8,128)(2,1)S(1)}, u32[]{:S(2)}, u32[]{:S(2)}) %collective-permute-start.16) | collective-permute-done | bytes 69664 | tf_op jit(solution)/shard_map/ppermute | solution.py:428
  53.2 0.9 %collective-permute-start.17 = (bf16[272,128]{1,0:T(8,128)(2,1)S(1)}, bf16[272,128]{1,0:T(8,128)(2,1)S(1)}, u32[]{:S(2)}, u32[]{:S(2)}) collective-permute-start(bf16[272,128]{1,0:T(8,128)(2,1)S(1)} %collective-permute-done.16.refs_7_), channel_id=1, source_target_pairs={{0,1},{1,0},{2,3},{3,2},{4,5},{5,4},{6,7},{7,6},{8,9},{9,8},{10,11... | collective-permute-start | bytes 208904 | tf_op jit(solution)/shard_map/ppermute | solution.py:428
  54.1 0.0 all-to-all-done.1.refs_1_
  54.1 0.0 copy-done.8
  54.1 1.1 %shard_map.152 = bf16[256,128]{1,0:T(8,128)(2,1)} custom-call(s32[1]{0:T(128)} %bitcast.refs_6_.refs_0_, bf16[8,96,128]{2,1,0:T(8,128)(2,1)S(1)} %all-to-all-done.1.refs_1_, bf16[768,256]{1,0:T(8,128)(2,1)S(1)} %copy-done.1, s32[1,128]{1,0:T(1,128)S(1)} %copy-done.8), custom_call_target="tpu_custom_call" | custom-call | tf_op jit(solution)/shard_map/pallas_call | solution.py:453
  55.2 0.0 collective-permute-done.11.refs_2_
  55.2 0.0 collective-permute-done.13.refs_4_
  55.2 0.0 collective-permute-done.15.refs_6_
  55.2 0.0 collective-permute-done.17.refs_8_
  55.2 1.1 %shard_map.154 = (f32[768,256]{1,0:T(8,128)}, f32[256,256]{1,0:T(8,128)}, f32[3,768]{1,0:T(4,128)}) custom-call(s32[1]{0:T(128)} %bitcast.3.refs_1_.refs_0_, bf16[272,128]{1,0:T(8,128)(2,1)S(1)} %shard_map.153.refs_1_, bf16[272,128]{1,0:T(8,128)(2,1)S(1)} %collective-permute-done.11.refs_2_, bf16[272,128]{1,0:T(8,128)(2,1)S(1)} %collective-permute-done.12.refs_3_, ...), custom_call_target="tpu_custom_call" | custom-call | tf_op jit(solution)/shard_map/pallas_call | solution.py:453
  (7 shorter events, 0.1 us)
Async XLA Ops:
  0.6 11.9 %copy-start = (f32[768,3]{0,1:T(4,128)S(1)}, f32[768,3]{0,1:T(4,128)}, u32[]{:S(2)}) copy-start(f32[768,3]{0,1:T(4,128)} %param.14) | copy-start | bytes 27652
  0.6 12.1 %copy-start.2 = (bf16[1536,256]{1,0:T(8,128)(2,1)S(1)}, bf16[1536,256]{1,0:T(8,128)(2,1)}, u32[]{:S(2)}) copy-start(bf16[1536,256]{1,0:T(8,128)(2,1)} %constant.18.clone.refs_2_) | copy-start | bytes 2359300
  3.1 9.6 %copy-start.3 = (f32[256,256]{1,0:T(8,128)S(1)}, f32[256,256]{1,0:T(8,128)}, u32[]{:S(2)}) copy-start(f32[256,256]{1,0:T(8,128)} %constant.19.clone.refs_3_) | copy-start | bytes 786436
  3.1 9.6 %copy-start.4 = (f32[8,4096]{1,0:T(8,128)S(1)}, f32[8,4096]{1,0:T(8,128)}, u32[]{:S(2)}) copy-start(f32[8,4096]{1,0:T(8,128)} %refs_0_.1) | copy-start | bytes 393220
  3.1 15.1 %all-to-all-start = ((bf16[32,32,128]{2,1,0:T(8,128)(2,1)}), bf16[32,32,128]{2,1,0:T(8,128)(2,1)S(1)}, u32[]{:S(2)}, u32[]{:S(2)}) async-start(bf16[32,32,128]{2,1,0:T(8,128)(2,1)} %get-tuple-element.26), calls=%async_computation | async-start | bytes 524288 | tf_op jit(solution)/shard_map/all_to_all | solution.py:470
  9.5 14.2 %collective-permute-start.3 = (bf16[512,128]{1,0:T(8,128)(2,1)}, bf16[512,128]{1,0:T(8,128)(2,1)S(1)}, u32[]{:S(2)}, u32[]{:S(2)}) collective-permute-start(bf16[512,128]{1,0:T(8,128)(2,1)} %get-tuple-element.39), channel_id=1, source_target_pairs={{0,1},{1,0},{2,3},{3,2},{4,5},{5,4},{6,7},{7,6},{8,9},{9,8},{10,11... | collective-permute-start | bytes 393224 | tf_op jit(solution)/shard_map/ppermute | solution.py:428
  9.9 13.8 %collective-permute-start.4 = (bf16[512,128]{1,0:T(8,128)(2,1)}, bf16[512,128]{1,0:T(8,128)(2,1)S(1)}, u32[]{:S(2)}, u32[]{:S(2)}) collective-permute-start(bf16[512,128]{1,0:T(8,128)(2,1)} %get-tuple-element.39), channel_id=1, source_target_pairs={{0,2},{1,3},{2,0},{3,1},{4,6},{5,7},{6,4},{7,5},{8,10},{9,11},{10,... | collective-permute-start | bytes 393224 | tf_op jit(solution)/shard_map/ppermute | solution.py:428
  11.1 12.6 %collective-permute-start.5 = (bf16[512,128]{1,0:T(8,128)(2,1)}, bf16[512,128]{1,0:T(8,128)(2,1)S(1)}, u32[]{:S(2)}, u32[]{:S(2)}) collective-permute-start(bf16[512,128]{1,0:T(8,128)(2,1)} %get-tuple-element.39), channel_id=1, source_target_pairs={{0,4},{1,5},{2,6},{3,7},{4,0},{5,1},{6,2},{7,3},{8,12},{9,13},{10,... | collective-permute-start | bytes 393224 | tf_op jit(solution)/shard_map/ppermute | solution.py:428
  12.3 11.5 %collective-permute-start.6 = (bf16[512,128]{1,0:T(8,128)(2,1)}, bf16[512,128]{1,0:T(8,128)(2,1)S(1)}, u32[]{:S(2)}, u32[]{:S(2)}) collective-permute-start(bf16[512,128]{1,0:T(8,128)(2,1)} %get-tuple-element.39), channel_id=1, source_target_pairs={{0,6},{1,7},{2,4},{3,5},{4,2},{5,3},{6,0},{7,1},{8,14},{9,15},{10,... | collective-permute-start | bytes 393224 | tf_op jit(solution)/shard_map/ppermute | solution.py:428
  12.7 0.9 %copy-start.5 = (f32[8,4096]{1,0:T(8,128)S(1)}, f32[8,4096]{1,0:T(8,128)}, u32[]{:S(2)}) copy-start(f32[8,4096]{1,0:T(8,128)} %refs_1_.1) | copy-start | bytes 393220
  13.6 0.7 %copy-start.6 = (s32[1,128]{1,0:T(1,128)S(1)}, s32[1,128]{1,0:T(1,128)}, u32[]{:S(2)}) copy-start(s32[1,128]{1,0:T(1,128)} %refs_4_.1) | copy-start | bytes 1540
  15.3 0.5 copy-start.7
  23.8 10.8 %collective-permute-start.7 = (bf16[4,512,128]{2,1,0:T(8,128)(2,1)S(1)}, bf16[4,512,128]{2,1,0:T(8,128)(2,1)S(1)}, u32[]{:S(2)}, u32[]{:S(2)}) collective-permute-start(bf16[4,512,128]{2,1,0:T(8,128)(2,1)S(1)} %shard_map.149.refs_7_), channel_id=1, source_target_pairs={{0,1},{1,0},{2,3},{3,2},{4,5},{5,4},{6,7},{7,6},{8,9},{9,8},{10,11... | collective-permute-start | bytes 1572872 | tf_op jit(solution)/shard_map/ppermute | solution.py:428
  25.3 4.6 %collective-permute-start = (bf16[8,32,128]{2,1,0:T(8,128)(2,1)S(1)}, bf16[8,32,128]{2,1,0:T(8,128)(2,1)S(1)}, u32[]{:S(2)}, u32[]{:S(2)}) collective-permute-start(bf16[8,32,128]{2,1,0:T(8,128)(2,1)S(1)} %get-tuple-element.32), channel_id=1, source_target_pairs={{0,8},{8,16},{16,24},{24,0},{1,9},{9,17},{17,25},{25,1},{2,10},{10... | collective-permute-start | bytes 196616 | tf_op jit(solution)/shard_map/ppermute | solution.py:533
  25.3 7.0 %collective-permute-start.1 = (bf16[8,32,128]{2,1,0:T(8,128)(2,1)S(1)}, bf16[8,32,128]{2,1,0:T(8,128)(2,1)S(1)}, u32[]{:S(2)}, u32[]{:S(2)}) collective-permute-start(bf16[8,32,128]{2,1,0:T(8,128)(2,1)S(1)} %get-tuple-element.33), channel_id=1, source_target_pairs={{0,16},{8,24},{16,0},{24,8},{1,17},{9,25},{17,1},{25,9},{2,18},{10... | collective-permute-start | bytes 196616 | tf_op jit(solution)/shard_map/ppermute | solution.py:533
  28.2 6.4 %collective-permute-start.2 = (bf16[8,32,128]{2,1,0:T(8,128)(2,1)S(1)}, bf16[8,32,128]{2,1,0:T(8,128)(2,1)S(1)}, u32[]{:S(2)}, u32[]{:S(2)}) collective-permute-start(bf16[8,32,128]{2,1,0:T(8,128)(2,1)S(1)} %get-tuple-element.34), channel_id=1, source_target_pairs={{0,24},{8,0},{16,8},{24,16},{1,25},{9,1},{17,9},{25,17},{2,26},{10... | collective-permute-start | bytes 196616 | tf_op jit(solution)/shard_map/ppermute | solution.py:533
  35.0 9.8 %collective-permute-start.10 = (bf16[272,128]{1,0:T(8,128)(2,1)S(1)}, bf16[272,128]{1,0:T(8,128)(2,1)S(1)}, u32[]{:S(2)}, u32[]{:S(2)}) collective-permute-start(bf16[272,128]{1,0:T(8,128)(2,1)S(1)} %shard_map.150.refs_4_.refs_0_), channel_id=1, source_target_pairs={{0,24},{8,0},{16,8},{24,16},{1,25},{9,1},{17,9},{25,17},{2,26},{10... | collective-permute-start | bytes 208904 | tf_op jit(solution)/shard_map/ppermute | solution.py:533
  35.1 9.7 %collective-permute-start.8 = (bf16[272,128]{1,0:T(8,128)(2,1)S(1)}, bf16[272,128]{1,0:T(8,128)(2,1)S(1)}, u32[]{:S(2)}, u32[]{:S(2)}) collective-permute-start(bf16[272,128]{1,0:T(8,128)(2,1)S(1)} %shard_map.150.refs_4_.refs_0_), channel_id=1, source_target_pairs={{0,8},{8,16},{16,24},{24,0},{1,9},{9,17},{17,25},{25,1},{2,10},{10... | collective-permute-start | bytes 208904 | tf_op jit(solution)/shard_map/ppermute | solution.py:533
  36.5 8.3 %collective-permute-start.9 = (bf16[272,128]{1,0:T(8,128)(2,1)S(1)}, bf16[272,128]{1,0:T(8,128)(2,1)S(1)}, u32[]{:S(2)}, u32[]{:S(2)}) collective-permute-start(bf16[272,128]{1,0:T(8,128)(2,1)S(1)} %shard_map.150.refs_4_.refs_0_), channel_id=1, source_target_pairs={{0,16},{8,24},{16,0},{24,8},{1,17},{9,25},{17,1},{25,9},{2,18},{10... | collective-permute-start | bytes 208904 | tf_op jit(solution)/shard_map/ppermute | solution.py:533
  40.0 14.1 %copy-start.1 = (bf16[768,256]{1,0:T(8,128)(2,1)S(1)}, bf16[768,256]{1,0:T(8,128)(2,1)}, u32[]{:S(2)}) copy-start(bf16[768,256]{1,0:T(8,128)(2,1)} %refs_2_.2) | copy-start | bytes 1179652
  40.0 14.1 %all-to-all-start.1 = ((bf16[8,96,128]{2,1,0:T(8,128)(2,1)}), bf16[8,96,128]{2,1,0:T(8,128)(2,1)S(1)}, u32[]{:S(2)}, u32[]{:S(2)}) async-start(bf16[8,96,128]{2,1,0:T(8,128)(2,1)} %shard_map.151), calls=%async_computation.1 | async-start | bytes 393216 | tf_op jit(solution)/shard_map/all_to_all | solution.py:554
  44.9 9.2 %copy-start.8 = (s32[1,128]{1,0:T(1,128)S(1)}, s32[1,128]{1,0:T(1,128)}, u32[]{:S(2)}) copy-start(s32[1,128]{1,0:T(1,128)} %copy-done.7) | copy-start | bytes 1540
  44.9 5.9 %collective-permute-start.12 = (bf16[272,128]{1,0:T(8,128)(2,1)S(1)}, bf16[272,128]{1,0:T(8,128)(2,1)S(1)}, u32[]{:S(2)}, u32[]{:S(2)}) collective-permute-start(bf16[272,128]{1,0:T(8,128)(2,1)S(1)} %shard_map.153.refs_1_), channel_id=1, source_target_pairs={{0,2},{1,3},{2,0},{3,1},{4,6},{5,7},{6,4},{7,5},{8,10},{9,11},{10,... | collective-permute-start | bytes 208904 | tf_op jit(solution)/shard_map/ppermute | solution.py:428
  46.4 5.8 %collective-permute-start.14 = (bf16[272,128]{1,0:T(8,128)(2,1)S(1)}, bf16[272,128]{1,0:T(8,128)(2,1)S(1)}, u32[]{:S(2)}, u32[]{:S(2)}) collective-permute-start(bf16[272,128]{1,0:T(8,128)(2,1)S(1)} %shard_map.153.refs_1_), channel_id=1, source_target_pairs={{0,4},{1,5},{2,6},{3,7},{4,0},{5,1},{6,2},{7,3},{8,12},{9,13},{10,... | collective-permute-start | bytes 208904 | tf_op jit(solution)/shard_map/ppermute | solution.py:428
  47.6 5.6 %collective-permute-start.16 = (bf16[272,128]{1,0:T(8,128)(2,1)S(1)}, bf16[272,128]{1,0:T(8,128)(2,1)S(1)}, u32[]{:S(2)}, u32[]{:S(2)}) collective-permute-start(bf16[272,128]{1,0:T(8,128)(2,1)S(1)} %shard_map.153.refs_1_), channel_id=1, source_target_pairs={{0,6},{1,7},{2,4},{3,5},{4,2},{5,3},{6,0},{7,1},{8,14},{9,15},{10,... | collective-permute-start | bytes 208904 | tf_op jit(solution)/shard_map/ppermute | solution.py:428
  47.6 7.6 %collective-permute-start.11 = (bf16[272,128]{1,0:T(8,128)(2,1)S(1)}, bf16[272,128]{1,0:T(8,128)(2,1)S(1)}, u32[]{:S(2)}, u32[]{:S(2)}) collective-permute-start(bf16[272,128]{1,0:T(8,128)(2,1)S(1)} %shard_map.153.refs_1_), channel_id=1, source_target_pairs={{0,1},{1,0},{2,3},{3,2},{4,5},{5,4},{6,7},{7,6},{8,9},{9,8},{10,11... | collective-permute-start | bytes 208904 | tf_op jit(solution)/shard_map/ppermute | solution.py:428
  50.8 4.4 %collective-permute-start.13 = (bf16[272,128]{1,0:T(8,128)(2,1)S(1)}, bf16[272,128]{1,0:T(8,128)(2,1)S(1)}, u32[]{:S(2)}, u32[]{:S(2)}) collective-permute-start(bf16[272,128]{1,0:T(8,128)(2,1)S(1)} %collective-permute-done.12.refs_3_), channel_id=1, source_target_pairs={{0,1},{1,0},{2,3},{3,2},{4,5},{5,4},{6,7},{7,6},{8,9},{9,8},{10,11... | collective-permute-start | bytes 208904 | tf_op jit(solution)/shard_map/ppermute | solution.py:428
  52.1 3.1 %collective-permute-start.15 = (bf16[272,128]{1,0:T(8,128)(2,1)S(1)}, bf16[272,128]{1,0:T(8,128)(2,1)S(1)}, u32[]{:S(2)}, u32[]{:S(2)}) collective-permute-start(bf16[272,128]{1,0:T(8,128)(2,1)S(1)} %collective-permute-done.14.refs_5_), channel_id=1, source_target_pairs={{0,1},{1,0},{2,3},{3,2},{4,5},{5,4},{6,7},{7,6},{8,9},{9,8},{10,11... | collective-permute-start | bytes 208904 | tf_op jit(solution)/shard_map/ppermute | solution.py:428
  53.2 2.0 %collective-permute-start.17 = (bf16[272,128]{1,0:T(8,128)(2,1)S(1)}, bf16[272,128]{1,0:T(8,128)(2,1)S(1)}, u32[]{:S(2)}, u32[]{:S(2)}) collective-permute-start(bf16[272,128]{1,0:T(8,128)(2,1)S(1)} %collective-permute-done.16.refs_7_), channel_id=1, source_target_pairs={{0,1},{1,0},{2,3},{3,2},{4,5},{5,4},{6,7},{7,6},{8,9},{9,8},{10,11... | collective-permute-start | bytes 208904 | tf_op jit(solution)/shard_map/ppermute | solution.py:428

commit v9 on v7

--- a/solution.py
+++ b/solution.py
@@ -10,6 +10,7 @@
 
 AXES = ("seq", "fft")
 LANES = 128
+TAPS = 16
 bf16 = jnp.bfloat16
 f32 = jnp.float32
 PARAMS = pltpu.CompilerParams(vmem_limit_bytes=24 * 1024 * 1024)
@@ -354,9 +355,9 @@
         owner = lax.rem(line[0] + lines - k, lines)
         spot = pl.ds(pl.multiple_of(owner * size, size), size)
         partial_out[spot] = jnp.concatenate(parts, axis=0).astype(bf16)
-    tail = jnp.concatenate([short[...]] * lines, axis=0)
-    owner = lax.broadcasted_iota(jnp.int32, tail.shape, 0) // channels
-    partial_out[lines * size :] = jnp.where(owner == line[0], tail, 0.0).astype(bf16)
+    tail = pltpu.roll(short[...], line[0] * TAPS, 1)
+    tail = jnp.concatenate([tail, jnp.zeros_like(tail)], axis=0)
+    partial_out[lines * size :] = tail.astype(bf16)
 
 
 def return_kernel(channels, *refs):
@@ -411,8 +412,10 @@
                     w_in_out[spot, low:high] = rows[start : start + channels]
                 start = base + 3 * channels
                 out_rows[pl.ds(first, channels), low:high] = rows[start : start + channels]
-            start = lines * size + i * channels
-            short_rows[pl.ds(first, channels), :] = rows[start : start + channels]
+            start = lines * size
+            short_rows[pl.ds(first, channels), :] = pltpu.roll(
+                rows[start : start + channels], (LANES - i * TAPS) % LANES, 1
+            )
     w_out_out[...] = out_rows[...].T
     short = short_rows[...].T
     for s in range(3):
@@ -532,7 +535,7 @@
             return lax.ppermute(value, "seq", pairs)
 
         met = [sent[0]] + [ahead(sent[k], k) for k in range(1, lines)]
-        size = lines * height + lines * channels
+        size = lines * height + 2 * channels
         partial = call(
             lambda *refs: weights_kernel(channels, scale, lines, *refs),
             shape((size, LANES), bf16),

time: 55.1 us -> 54.9 us (level)
  no operation moved by 1% of the time
where the time goes in v9:
time: 54.9 us; the launch traced here: 54.6 us
  starting transfers between devices  28.8 us (52%)
  Pallas kernels  12.5 us (23%)
  waiting for transfers between devices  10.2 us (19%)
  local copies, waits for them, and re-layouts  2.27 us (4%)
  between operations  0.81 us (1%)
    ppermute x12, starting transfers between devices, swapped(): return lax.ppermute(value, 'fft', [(i, i ^ distance) for i in range(plane)])  10.5 us
    pallas_call x9, Pallas kernels, call(): pl.pallas_call(kernel, out_shape=outs, compiler_params=PARAMS, **options)  10 us
    ppermute x6, starting transfers between devices, ahead(): return lax.ppermute(value, 'seq', pairs)  7.09 us
    all_to_all x1, starting transfers between devices, local(): lax.all_to_all(streams, AXES, split_axis=0, concat_axis=0, tiled=True)  6.36 us
    all_to_all x1, starting transfers between devices, local(): back = lax.all_to_all(moved, 'fft', split_axis=0, concat_axis=0, tiled=True)  4.85 us
    ppermute x6, waiting for transfers between devices, ahead(): return lax.ppermute(value, 'seq', pairs)  4.57 us
    ppermute x12, waiting for transfers between devices, swapped(): return lax.ppermute(value, 'fft', [(i, i ^ distance) for i in range(plane)])  3.27 us
    pallas_call x1, Pallas kernels, local(): pl.pallas_call(project_kernel, out_shape=(shape(dims, bf16), shape((2 * w...  2.41 us
  transfers between devices with their start and end apart: 20, of which 5 were waited for; matrix products, arithmetic and copies ran while one was open for 0% of the time, Pallas kernels for 15%

profile of v9, /device:TPU:9, one launch (start us, length us, event | category | flops | bytes accessed | tf_op | source)
XLA Modules:
  0.0 54.6 jit_solution(2609226938113508960)
XLA Ops:
  0.6 0.0 copy-start
  0.6 0.0 copy-start.2
  0.7 2.4 %shard_map.145 = (bf16[32,32,128]{2,1,0:T(8,128)(2,1)}, bf16[512,128]{1,0:T(8,128)(2,1)}) custom-call(bf16[256,128]{1,0:T(8,128)(2,1)} %features_at.1, s32[1,128]{1,0:T(1,128)} %refs_4_.1, bf16[256,128]{1,0:T(8,128)(2,1)} %cotangent_at.1, bf16[768,256]{1,0:T(8,128)(2,1)} %refs_2_.2, bf16[256,256]{1,0:T(8,128)(2,1)} %w_out_at.1), custom_call_target="tpu_custom_call" | custom-call | tf_op jit(solution)/shard_map/pallas_call | solution.py:458
  3.1 0.0 copy-start.3
  3.1 0.0 copy-start.4
  3.1 6.4 %all-to-all-start = ((bf16[32,32,128]{2,1,0:T(8,128)(2,1)}), bf16[32,32,128]{2,1,0:T(8,128)(2,1)S(1)}, u32[]{:S(2)}, u32[]{:S(2)}) async-start(bf16[32,32,128]{2,1,0:T(8,128)(2,1)} %get-tuple-element.26), calls=%async_computation | async-start | bytes 524288 | tf_op jit(solution)/shard_map/all_to_all | solution.py:472
  9.5 0.4 collective-permute-start.3
  9.9 1.2 %collective-permute-start.4 = (bf16[512,128]{1,0:T(8,128)(2,1)}, bf16[512,128]{1,0:T(8,128)(2,1)S(1)}, u32[]{:S(2)}, u32[]{:S(2)}) collective-permute-start(bf16[512,128]{1,0:T(8,128)(2,1)} %get-tuple-element.39), channel_id=1, source_target_pairs={{0,2},{1,3},{2,0},{3,1},{4,6},{5,7},{6,4},{7,5},{8,10},{9,11},{10,... | collective-permute-start | bytes 393224 | tf_op jit(solution)/shard_map/ppermute | solution.py:430
  11.1 1.2 %collective-permute-start.5 = (bf16[512,128]{1,0:T(8,128)(2,1)}, bf16[512,128]{1,0:T(8,128)(2,1)S(1)}, u32[]{:S(2)}, u32[]{:S(2)}) collective-permute-start(bf16[512,128]{1,0:T(8,128)(2,1)} %get-tuple-element.39), channel_id=1, source_target_pairs={{0,4},{1,5},{2,6},{3,7},{4,0},{5,1},{6,2},{7,3},{8,12},{9,13},{10,... | collective-permute-start | bytes 393224 | tf_op jit(solution)/shard_map/ppermute | solution.py:430
  12.3 0.3 collective-permute-start.6
  12.5 0.0 copy-done
  12.5 0.1 dynamic-slice_bitcast_fusion
  12.6 0.1 copy.19.refs_1_
  12.7 0.0 copy-done.2
  12.7 0.0 copy-done.3
  12.7 0.0 copy-done.4
  12.7 0.9 %copy-done.5 = f32[8,4096]{1,0:T(8,128)S(1)} copy-done((f32[8,4096]{1,0:T(8,128)S(1)}, f32[8,4096]{1,0:T(8,128)}, u32[]{:S(2)}) %copy-start.5) | copy-done | bytes 131096
  13.6 0.7 %copy-done.6 = s32[1,128]{1,0:T(1,128)S(1)} copy-done((s32[1,128]{1,0:T(1,128)S(1)}, s32[1,128]{1,0:T(1,128)}, u32[]{:S(2)}) %copy-start.6) | copy-done | bytes 536
  14.3 1.0 %shard_map.146 = (f32[256,256]{1,0:T(8,128)S(1)}, f32[256,256]{1,0:T(8,128)S(1)}, bf16[1536,256]{1,0:T(8,128)(2,1)S(1)}, f32[256,256]{1,0:T(8,128)S(1)}, s32[1,128]{1,0:T(1,128)S(1)}) custom-call(f32[8,4096]{1,0:T(8,128)S(1)} %copy-done.4, f32[8,4096]{1,0:T(8,128)S(1)} %copy-done.5, bf16[1536,256]{1,0:T(8,128)(2,1)S(1)} %copy-done.2, ...), custom_call_target="tpu_custom_call" | custom-call | tf_op jit(solution)/shard_map/pallas_call | solution.py:455
  15.3 0.0 copy-start.7
  15.3 0.5 copy-done.7
  15.8 2.4 %all-to-all-done.refs_0_ = bf16[32,32,128]{2,1,0:T(8,128)(2,1)S(1)} async-done(((bf16[32,32,128]{2,1,0:T(8,128)(2,1)}), bf16[32,32,128]{2,1,0:T(8,128)(2,1)S(1)}, u32[]{:S(2)}, u32[]{:S(2)}) %all-to-all-start) | async-done | bytes 262176 | tf_op jit(solution)/shard_map/all_to_all | solution.py:472
  18.2 3.7 %shard_map.147 = (f32[8,128]{1,0:T(8,128)S(1)}, f32[256,256]{1,0:T(8,128)S(1)}, f32[256,256]{1,0:T(8,128)S(1)}, bf16[8,32,128]{2,1,0:T(8,128)(2,1)S(1)}, bf16[8,...) custom-call(bf16[32,32,128]{2,1,0:T(8,128)(2,1)S(1)} %all-to-all-done.refs_0_, ...), custom_call_target="tpu_custom_call" | custom-call | tf_op jit(solution)/shard_map/pallas_call | solution.py:455
  21.9 0.0 collective-permute-done.3.refs_0_
  21.9 0.0 collective-permute-done.4.refs_1_
  21.9 0.0 collective-permute-done.5.refs_2_
  21.9 0.0 collective-permute-done.6.refs_3_
  22.0 1.5 %collective-permute-start.7 = (bf16[4,512,128]{2,1,0:T(8,128)(2,1)S(1)}, bf16[4,512,128]{2,1,0:T(8,128)(2,1)S(1)}, u32[]{:S(2)}, u32[]{:S(2)}) collective-permute-start(bf16[4,512,128]{2,1,0:T(8,128)(2,1)S(1)} %shard_map.149.refs_7_), channel_id=1, source_target_pairs={{0,1},{1,0},{2,3},{3,2},{4,5},{5,4},{6,7},{7,6},{8,9},{9,8},{10,11... | collective-permute-start | bytes 1572872 | tf_op jit(solution)/shard_map/ppermute | solution.py:430
  23.5 0.0 collective-permute-start
  23.5 2.9 %collective-permute-start.1 = (bf16[8,32,128]{2,1,0:T(8,128)(2,1)S(1)}, bf16[8,32,128]{2,1,0:T(8,128)(2,1)S(1)}, u32[]{:S(2)}, u32[]{:S(2)}) collective-permute-start(bf16[8,32,128]{2,1,0:T(8,128)(2,1)S(1)} %get-tuple-element.33), channel_id=1, source_target_pairs={{0,16},{8,24},{16,0},{24,8},{1,17},{9,25},{17,1},{25,9},{2,18},{10... | collective-permute-start | bytes 196616 | tf_op jit(solution)/shard_map/ppermute | solution.py:535
  26.4 0.0 collective-permute-start.2
  26.4 1.8 %shard_map.148 = (f32[8,4096]{1,0:T(8,128)}, f32[8,4096]{1,0:T(8,128)}, f32[8,128]{1,0:T(8,128)S(1)}) custom-call(f32[256,256]{1,0:T(8,128)S(1)} %get-tuple-element.35.refs_0_, f32[256,256]{1,0:T(8,128)S(1)} %get-tuple-element.36.refs_1_, bf16[1536,256]{1,0:T(8,128)(2,1)S(1)} %get-tuple-element.29.refs_4_.refs_2_, ...), custom_call_target="tpu_custom_call" | custom-call | tf_op jit(solution)/shard_map/pallas_call | solution.py:455
  28.2 0.0 collective-permute-done.refs_4_.refs_1_
  28.2 2.4 %collective-permute-done.1.refs_5_.refs_2_ = bf16[8,32,128]{2,1,0:T(8,128)(2,1)S(1)} collective-permute-done((bf16[8,32,128]{2,1,0:T(8,128)(2,1)S(1)}, bf16[8,32,128]{2,1,0:T(8,128)(2,1)S(1)}, u32[]{:S(2)}, u32[]{:S(2)}) %collective-permute-start.1) | collective-permute-done | bytes 65568 | tf_op jit(solution)/shard_map/ppermute | solution.py:535
  30.6 2.2 %collective-permute-done.2.refs_6_.refs_3_ = bf16[8,32,128]{2,1,0:T(8,128)(2,1)S(1)} collective-permute-done((bf16[8,32,128]{2,1,0:T(8,128)(2,1)S(1)}, bf16[8,32,128]{2,1,0:T(8,128)(2,1)S(1)}, u32[]{:S(2)}, u32[]{:S(2)}) %collective-permute-start.2) | collective-permute-done | bytes 65568 | tf_op jit(solution)/shard_map/ppermute | solution.py:535
  32.7 0.0 collective-permute-done.7.refs_8_
  32.7 0.5 shard_map.150.refs_4_.refs_0_
  33.2 0.1 collective-permute-start.10
  33.3 1.5 %collective-permute-start.8 = (bf16[272,128]{1,0:T(8,128)(2,1)S(1)}, bf16[272,128]{1,0:T(8,128)(2,1)S(1)}, u32[]{:S(2)}, u32[]{:S(2)}) collective-permute-start(bf16[272,128]{1,0:T(8,128)(2,1)S(1)} %shard_map.150.refs_4_.refs_0_), channel_id=1, source_target_pairs={{0,8},{8,16},{16,24},{24,0},{1,9},{9,17},{17,25},{25,1},{2,10},{10... | collective-permute-start | bytes 208904 | tf_op jit(solution)/shard_map/ppermute | solution.py:535
  34.7 2.7 %collective-permute-start.9 = (bf16[272,128]{1,0:T(8,128)(2,1)S(1)}, bf16[272,128]{1,0:T(8,128)(2,1)S(1)}, u32[]{:S(2)}, u32[]{:S(2)}) collective-permute-start(bf16[272,128]{1,0:T(8,128)(2,1)S(1)} %shard_map.150.refs_4_.refs_0_), channel_id=1, source_target_pairs={{0,16},{8,24},{16,0},{24,8},{1,17},{9,25},{17,1},{25,9},{2,18},{10... | collective-permute-start | bytes 208904 | tf_op jit(solution)/shard_map/ppermute | solution.py:535
  37.5 0.7 %shard_map.151 = bf16[8,96,128]{2,1,0:T(8,128)(2,1)} custom-call(bf16[8,32,128]{2,1,0:T(8,128)(2,1)S(1)} %get-tuple-element.31.refs_3_.refs_0_, bf16[8,32,128]{2,1,0:T(8,128)(2,1)S(1)} %collective-permute-done.refs_4_.refs_1_, bf16[8,32,128]{2,1,0:T(8,128)(2,1)S(1)} %collective-permute-done.1.refs_5_.refs_2_, ...), custom_call_target="tpu_custom_call" | custom-call | tf_op jit(solution)/shard_map/pallas_call | solution.py:455
  38.2 4.9 %all-to-all-start.1 = ((bf16[8,96,128]{2,1,0:T(8,128)(2,1)}), bf16[8,96,128]{2,1,0:T(8,128)(2,1)S(1)}, u32[]{:S(2)}, u32[]{:S(2)}) async-start(bf16[8,96,128]{2,1,0:T(8,128)(2,1)} %shard_map.151), calls=%async_computation.1 | async-start | bytes 393216 | tf_op jit(solution)/shard_map/all_to_all | solution.py:556
  43.0 0.0 collective-permute-done.10.refs_3_
  43.0 0.0 collective-permute-done.8.refs_1_
  43.1 0.0 collective-permute-done.9.refs_2_
  43.1 0.0 copy-start.8
  43.1 1.5 %collective-permute-start.12 = (bf16[272,128]{1,0:T(8,128)(2,1)S(1)}, bf16[272,128]{1,0:T(8,128)(2,1)S(1)}, u32[]{:S(2)}, u32[]{:S(2)}) collective-permute-start(bf16[272,128]{1,0:T(8,128)(2,1)S(1)} %shard_map.153.refs_1_), channel_id=1, source_target_pairs={{0,2},{1,3},{2,0},{3,1},{4,6},{5,7},{6,4},{7,5},{8,10},{9,11},{10,... | collective-permute-start | bytes 208904 | tf_op jit(solution)/shard_map/ppermute | solution.py:430
  44.6 1.2 %collective-permute-start.14 = (bf16[272,128]{1,0:T(8,128)(2,1)S(1)}, bf16[272,128]{1,0:T(8,128)(2,1)S(1)}, u32[]{:S(2)}, u32[]{:S(2)}) collective-permute-start(bf16[272,128]{1,0:T(8,128)(2,1)S(1)} %shard_map.153.refs_1_), channel_id=1, source_target_pairs={{0,4},{1,5},{2,6},{3,7},{4,0},{5,1},{6,2},{7,3},{8,12},{9,13},{10,... | collective-permute-start | bytes 208904 | tf_op jit(solution)/shard_map/ppermute | solution.py:430
  45.8 0.1 collective-permute-start.16
  45.8 1.0 %collective-permute-start.11 = (bf16[272,128]{1,0:T(8,128)(2,1)S(1)}, bf16[272,128]{1,0:T(8,128)(2,1)S(1)}, u32[]{:S(2)}, u32[]{:S(2)}) collective-permute-start(bf16[272,128]{1,0:T(8,128)(2,1)S(1)} %shard_map.153.refs_1_), channel_id=1, source_target_pairs={{0,1},{1,0},{2,3},{3,2},{4,5},{5,4},{6,7},{7,6},{8,9},{9,8},{10,11... | collective-permute-start | bytes 208904 | tf_op jit(solution)/shard_map/ppermute | solution.py:430
  46.8 2.2 %collective-permute-done.12.refs_3_ = bf16[272,128]{1,0:T(8,128)(2,1)S(1)} collective-permute-done((bf16[272,128]{1,0:T(8,128)(2,1)S(1)}, bf16[272,128]{1,0:T(8,128)(2,1)S(1)}, u32[]{:S(2)}, u32[]{:S(2)}) %collective-permute-start.12) | collective-permute-done | bytes 69664 | tf_op jit(solution)/shard_map/ppermute | solution.py:430
  49.0 1.3 %collective-permute-start.13 = (bf16[272,128]{1,0:T(8,128)(2,1)S(1)}, bf16[272,128]{1,0:T(8,128)(2,1)S(1)}, u32[]{:S(2)}, u32[]{:S(2)}) collective-permute-start(bf16[272,128]{1,0:T(8,128)(2,1)S(1)} %collective-permute-done.12.refs_3_), channel_id=1, source_target_pairs={{0,1},{1,0},{2,3},{3,2},{4,5},{5,4},{6,7},{7,6},{8,9},{9,8},{10,11... | collective-permute-start | bytes 208904 | tf_op jit(solution)/shard_map/ppermute | solution.py:430
  50.4 0.0 collective-permute-done.14.refs_5_
  50.4 0.0 collective-permute-start.15
  50.4 1.1 %collective-permute-done.16.refs_7_ = bf16[272,128]{1,0:T(8,128)(2,1)S(1)} collective-permute-done((bf16[272,128]{1,0:T(8,128)(2,1)S(1)}, bf16[272,128]{1,0:T(8,128)(2,1)S(1)}, u32[]{:S(2)}, u32[]{:S(2)}) %collective-permute-start.16) | collective-permute-done | bytes 69664 | tf_op jit(solution)/shard_map/ppermute | solution.py:430
  51.4 0.9 %collective-permute-start.17 = (bf16[272,128]{1,0:T(8,128)(2,1)S(1)}, bf16[272,128]{1,0:T(8,128)(2,1)S(1)}, u32[]{:S(2)}, u32[]{:S(2)}) collective-permute-start(bf16[272,128]{1,0:T(8,128)(2,1)S(1)} %collective-permute-done.16.refs_7_), channel_id=1, source_target_pairs={{0,1},{1,0},{2,3},{3,2},{4,5},{5,4},{6,7},{7,6},{8,9},{9,8},{10,11... | collective-permute-start | bytes 208904 | tf_op jit(solution)/shard_map/ppermute | solution.py:430
  52.3 0.0 all-to-all-done.1.refs_1_
  52.3 0.0 copy-done.1
  52.3 1.1 %shard_map.152 = bf16[256,128]{1,0:T(8,128)(2,1)} custom-call(s32[1]{0:T(128)} %bitcast.refs_6_.refs_0_, bf16[8,96,128]{2,1,0:T(8,128)(2,1)S(1)} %all-to-all-done.1.refs_1_, bf16[768,256]{1,0:T(8,128)(2,1)S(1)} %copy-done.1, s32[1,128]{1,0:T(1,128)S(1)} %copy-done.8), custom_call_target="tpu_custom_call" | custom-call | tf_op jit(solution)/shard_map/pallas_call | solution.py:455
  53.4 0.0 collective-permute-done.11.refs_2_
  53.4 0.0 collective-permute-done.13.refs_4_
  53.4 0.0 collective-permute-done.15.refs_6_
  53.4 0.0 collective-permute-done.17.refs_8_
  53.4 1.1 %shard_map.154 = (f32[768,256]{1,0:T(8,128)}, f32[256,256]{1,0:T(8,128)}, f32[3,768]{1,0:T(4,128)}) custom-call(s32[1]{0:T(128)} %bitcast.3.refs_1_.refs_0_, bf16[272,128]{1,0:T(8,128)(2,1)S(1)} %shard_map.153.refs_1_, bf16[272,128]{1,0:T(8,128)(2,1)S(1)} %collective-permute-done.11.refs_2_, bf16[272,128]{1,0:T(8,128)(2,1)S(1)} %collective-permute-done.12.refs_3_, ...), custom_call_target="tpu_custom_call" | custom-call | tf_op jit(solution)/shard_map/pallas_call | solution.py:455
  (7 shorter events, 0.1 us)
Async XLA Ops:
  0.6 11.9 %copy-start = (f32[768,3]{0,1:T(4,128)S(1)}, f32[768,3]{0,1:T(4,128)}, u32[]{:S(2)}) copy-start(f32[768,3]{0,1:T(4,128)} %param.14) | copy-start | bytes 27652
  0.6 12.1 %copy-start.2 = (bf16[1536,256]{1,0:T(8,128)(2,1)S(1)}, bf16[1536,256]{1,0:T(8,128)(2,1)}, u32[]{:S(2)}) copy-start(bf16[1536,256]{1,0:T(8,128)(2,1)} %constant.18.clone.refs_2_) | copy-start | bytes 2359300
  3.1 9.6 %copy-start.3 = (f32[256,256]{1,0:T(8,128)S(1)}, f32[256,256]{1,0:T(8,128)}, u32[]{:S(2)}) copy-start(f32[256,256]{1,0:T(8,128)} %constant.19.clone.refs_3_) | copy-start | bytes 786436
  3.1 9.6 %copy-start.4 = (f32[8,4096]{1,0:T(8,128)S(1)}, f32[8,4096]{1,0:T(8,128)}, u32[]{:S(2)}) copy-start(f32[8,4096]{1,0:T(8,128)} %refs_0_.1) | copy-start | bytes 393220
  3.1 15.1 %all-to-all-start = ((bf16[32,32,128]{2,1,0:T(8,128)(2,1)}), bf16[32,32,128]{2,1,0:T(8,128)(2,1)S(1)}, u32[]{:S(2)}, u32[]{:S(2)}) async-start(bf16[32,32,128]{2,1,0:T(8,128)(2,1)} %get-tuple-element.26), calls=%async_computation | async-start | bytes 524288 | tf_op jit(solution)/shard_map/all_to_all | solution.py:472
  9.5 12.4 %collective-permute-start.3 = (bf16[512,128]{1,0:T(8,128)(2,1)}, bf16[512,128]{1,0:T(8,128)(2,1)S(1)}, u32[]{:S(2)}, u32[]{:S(2)}) collective-permute-start(bf16[512,128]{1,0:T(8,128)(2,1)} %get-tuple-element.39), channel_id=1, source_target_pairs={{0,1},{1,0},{2,3},{3,2},{4,5},{5,4},{6,7},{7,6},{8,9},{9,8},{10,11... | collective-permute-start | bytes 393224 | tf_op jit(solution)/shard_map/ppermute | solution.py:430
  9.9 12.0 %collective-permute-start.4 = (bf16[512,128]{1,0:T(8,128)(2,1)}, bf16[512,128]{1,0:T(8,128)(2,1)S(1)}, u32[]{:S(2)}, u32[]{:S(2)}) collective-permute-start(bf16[512,128]{1,0:T(8,128)(2,1)} %get-tuple-element.39), channel_id=1, source_target_pairs={{0,2},{1,3},{2,0},{3,1},{4,6},{5,7},{6,4},{7,5},{8,10},{9,11},{10,... | collective-permute-start | bytes 393224 | tf_op jit(solution)/shard_map/ppermute | solution.py:430
  11.1 10.8 %collective-permute-start.5 = (bf16[512,128]{1,0:T(8,128)(2,1)}, bf16[512,128]{1,0:T(8,128)(2,1)S(1)}, u32[]{:S(2)}, u32[]{:S(2)}) collective-permute-start(bf16[512,128]{1,0:T(8,128)(2,1)} %get-tuple-element.39), channel_id=1, source_target_pairs={{0,4},{1,5},{2,6},{3,7},{4,0},{5,1},{6,2},{7,3},{8,12},{9,13},{10,... | collective-permute-start | bytes 393224 | tf_op jit(solution)/shard_map/ppermute | solution.py:430
  12.3 9.7 %collective-permute-start.6 = (bf16[512,128]{1,0:T(8,128)(2,1)}, bf16[512,128]{1,0:T(8,128)(2,1)S(1)}, u32[]{:S(2)}, u32[]{:S(2)}) collective-permute-start(bf16[512,128]{1,0:T(8,128)(2,1)} %get-tuple-element.39), channel_id=1, source_target_pairs={{0,6},{1,7},{2,4},{3,5},{4,2},{5,3},{6,0},{7,1},{8,14},{9,15},{10,... | collective-permute-start | bytes 393224 | tf_op jit(solution)/shard_map/ppermute | solution.py:430
  12.7 0.9 %copy-start.5 = (f32[8,4096]{1,0:T(8,128)S(1)}, f32[8,4096]{1,0:T(8,128)}, u32[]{:S(2)}) copy-start(f32[8,4096]{1,0:T(8,128)} %refs_1_.1) | copy-start | bytes 393220
  13.6 0.7 %copy-start.6 = (s32[1,128]{1,0:T(1,128)S(1)}, s32[1,128]{1,0:T(1,128)}, u32[]{:S(2)}) copy-start(s32[1,128]{1,0:T(1,128)} %refs_4_.1) | copy-start | bytes 1540
  15.3 0.5 copy-start.7
  22.0 10.8 %collective-permute-start.7 = (bf16[4,512,128]{2,1,0:T(8,128)(2,1)S(1)}, bf16[4,512,128]{2,1,0:T(8,128)(2,1)S(1)}, u32[]{:S(2)}, u32[]{:S(2)}) collective-permute-start(bf16[4,512,128]{2,1,0:T(8,128)(2,1)S(1)} %shard_map.149.refs_7_), channel_id=1, source_target_pairs={{0,1},{1,0},{2,3},{3,2},{4,5},{5,4},{6,7},{7,6},{8,9},{9,8},{10,11... | collective-permute-start | bytes 1572872 | tf_op jit(solution)/shard_map/ppermute | solution.py:430
  23.5 4.6 %collective-permute-start = (bf16[8,32,128]{2,1,0:T(8,128)(2,1)S(1)}, bf16[8,32,128]{2,1,0:T(8,128)(2,1)S(1)}, u32[]{:S(2)}, u32[]{:S(2)}) collective-permute-start(bf16[8,32,128]{2,1,0:T(8,128)(2,1)S(1)} %get-tuple-element.32), channel_id=1, source_target_pairs={{0,8},{8,16},{16,24},{24,0},{1,9},{9,17},{17,25},{25,1},{2,10},{10... | collective-permute-start | bytes 196616 | tf_op jit(solution)/shard_map/ppermute | solution.py:535
  23.5 7.0 %collective-permute-start.1 = (bf16[8,32,128]{2,1,0:T(8,128)(2,1)S(1)}, bf16[8,32,128]{2,1,0:T(8,128)(2,1)S(1)}, u32[]{:S(2)}, u32[]{:S(2)}) collective-permute-start(bf16[8,32,128]{2,1,0:T(8,128)(2,1)S(1)} %get-tuple-element.33), channel_id=1, source_target_pairs={{0,16},{8,24},{16,0},{24,8},{1,17},{9,25},{17,1},{25,9},{2,18},{10... | collective-permute-start | bytes 196616 | tf_op jit(solution)/shard_map/ppermute | solution.py:535
  26.4 6.3 %collective-permute-start.2 = (bf16[8,32,128]{2,1,0:T(8,128)(2,1)S(1)}, bf16[8,32,128]{2,1,0:T(8,128)(2,1)S(1)}, u32[]{:S(2)}, u32[]{:S(2)}) collective-permute-start(bf16[8,32,128]{2,1,0:T(8,128)(2,1)S(1)} %get-tuple-element.34), channel_id=1, source_target_pairs={{0,24},{8,0},{16,8},{24,16},{1,25},{9,1},{17,9},{25,17},{2,26},{10... | collective-permute-start | bytes 196616 | tf_op jit(solution)/shard_map/ppermute | solution.py:535
  33.2 9.8 %collective-permute-start.10 = (bf16[272,128]{1,0:T(8,128)(2,1)S(1)}, bf16[272,128]{1,0:T(8,128)(2,1)S(1)}, u32[]{:S(2)}, u32[]{:S(2)}) collective-permute-start(bf16[272,128]{1,0:T(8,128)(2,1)S(1)} %shard_map.150.refs_4_.refs_0_), channel_id=1, source_target_pairs={{0,24},{8,0},{16,8},{24,16},{1,25},{9,1},{17,9},{25,17},{2,26},{10... | collective-permute-start | bytes 208904 | tf_op jit(solution)/shard_map/ppermute | solution.py:535
  33.3 9.8 %collective-permute-start.8 = (bf16[272,128]{1,0:T(8,128)(2,1)S(1)}, bf16[272,128]{1,0:T(8,128)(2,1)S(1)}, u32[]{:S(2)}, u32[]{:S(2)}) collective-permute-start(bf16[272,128]{1,0:T(8,128)(2,1)S(1)} %shard_map.150.refs_4_.refs_0_), channel_id=1, source_target_pairs={{0,8},{8,16},{16,24},{24,0},{1,9},{9,17},{17,25},{25,1},{2,10},{10... | collective-permute-start | bytes 208904 | tf_op jit(solution)/shard_map/ppermute | solution.py:535
  34.7 8.3 %collective-permute-start.9 = (bf16[272,128]{1,0:T(8,128)(2,1)S(1)}, bf16[272,128]{1,0:T(8,128)(2,1)S(1)}, u32[]{:S(2)}, u32[]{:S(2)}) collective-permute-start(bf16[272,128]{1,0:T(8,128)(2,1)S(1)} %shard_map.150.refs_4_.refs_0_), channel_id=1, source_target_pairs={{0,16},{8,24},{16,0},{24,8},{1,17},{9,25},{17,1},{25,9},{2,18},{10... | collective-permute-start | bytes 208904 | tf_op jit(solution)/shard_map/ppermute | solution.py:535
  38.2 14.1 %copy-start.1 = (bf16[768,256]{1,0:T(8,128)(2,1)S(1)}, bf16[768,256]{1,0:T(8,128)(2,1)}, u32[]{:S(2)}) copy-start(bf16[768,256]{1,0:T(8,128)(2,1)} %refs_2_.2) | copy-start | bytes 1179652
  38.2 14.1 %all-to-all-start.1 = ((bf16[8,96,128]{2,1,0:T(8,128)(2,1)}), bf16[8,96,128]{2,1,0:T(8,128)(2,1)S(1)}, u32[]{:S(2)}, u32[]{:S(2)}) async-start(bf16[8,96,128]{2,1,0:T(8,128)(2,1)} %shard_map.151), calls=%async_computation.1 | async-start | bytes 393216 | tf_op jit(solution)/shard_map/all_to_all | solution.py:556
  43.1 9.2 %copy-start.8 = (s32[1,128]{1,0:T(1,128)S(1)}, s32[1,128]{1,0:T(1,128)}, u32[]{:S(2)}) copy-start(s32[1,128]{1,0:T(1,128)} %copy-done.7) | copy-start | bytes 1540
  43.1 5.9 %collective-permute-start.12 = (bf16[272,128]{1,0:T(8,128)(2,1)S(1)}, bf16[272,128]{1,0:T(8,128)(2,1)S(1)}, u32[]{:S(2)}, u32[]{:S(2)}) collective-permute-start(bf16[272,128]{1,0:T(8,128)(2,1)S(1)} %shard_map.153.refs_1_), channel_id=1, source_target_pairs={{0,2},{1,3},{2,0},{3,1},{4,6},{5,7},{6,4},{7,5},{8,10},{9,11},{10,... | collective-permute-start | bytes 208904 | tf_op jit(solution)/shard_map/ppermute | solution.py:430
  44.6 5.8 %collective-permute-start.14 = (bf16[272,128]{1,0:T(8,128)(2,1)S(1)}, bf16[272,128]{1,0:T(8,128)(2,1)S(1)}, u32[]{:S(2)}, u32[]{:S(2)}) collective-permute-start(bf16[272,128]{1,0:T(8,128)(2,1)S(1)} %shard_map.153.refs_1_), channel_id=1, source_target_pairs={{0,4},{1,5},{2,6},{3,7},{4,0},{5,1},{6,2},{7,3},{8,12},{9,13},{10,... | collective-permute-start | bytes 208904 | tf_op jit(solution)/shard_map/ppermute | solution.py:430
  45.8 5.6 %collective-permute-start.16 = (bf16[272,128]{1,0:T(8,128)(2,1)S(1)}, bf16[272,128]{1,0:T(8,128)(2,1)S(1)}, u32[]{:S(2)}, u32[]{:S(2)}) collective-permute-start(bf16[272,128]{1,0:T(8,128)(2,1)S(1)} %shard_map.153.refs_1_), channel_id=1, source_target_pairs={{0,6},{1,7},{2,4},{3,5},{4,2},{5,3},{6,0},{7,1},{8,14},{9,15},{10,... | collective-permute-start | bytes 208904 | tf_op jit(solution)/shard_map/ppermute | solution.py:430
  45.8 7.6 %collective-permute-start.11 = (bf16[272,128]{1,0:T(8,128)(2,1)S(1)}, bf16[272,128]{1,0:T(8,128)(2,1)S(1)}, u32[]{:S(2)}, u32[]{:S(2)}) collective-permute-start(bf16[272,128]{1,0:T(8,128)(2,1)S(1)} %shard_map.153.refs_1_), channel_id=1, source_target_pairs={{0,1},{1,0},{2,3},{3,2},{4,5},{5,4},{6,7},{7,6},{8,9},{9,8},{10,11... | collective-permute-start | bytes 208904 | tf_op jit(solution)/shard_map/ppermute | solution.py:430
  49.0 4.4 %collective-permute-start.13 = (bf16[272,128]{1,0:T(8,128)(2,1)S(1)}, bf16[272,128]{1,0:T(8,128)(2,1)S(1)}, u32[]{:S(2)}, u32[]{:S(2)}) collective-permute-start(bf16[272,128]{1,0:T(8,128)(2,1)S(1)} %collective-permute-done.12.refs_3_), channel_id=1, source_target_pairs={{0,1},{1,0},{2,3},{3,2},{4,5},{5,4},{6,7},{7,6},{8,9},{9,8},{10,11... | collective-permute-start | bytes 208904 | tf_op jit(solution)/shard_map/ppermute | solution.py:430
  50.4 3.1 %collective-permute-start.15 = (bf16[272,128]{1,0:T(8,128)(2,1)S(1)}, bf16[272,128]{1,0:T(8,128)(2,1)S(1)}, u32[]{:S(2)}, u32[]{:S(2)}) collective-permute-start(bf16[272,128]{1,0:T(8,128)(2,1)S(1)} %collective-permute-done.14.refs_5_), channel_id=1, source_target_pairs={{0,1},{1,0},{2,3},{3,2},{4,5},{5,4},{6,7},{7,6},{8,9},{9,8},{10,11... | collective-permute-start | bytes 208904 | tf_op jit(solution)/shard_map/ppermute | solution.py:430
  51.4 2.0 %collective-permute-start.17 = (bf16[272,128]{1,0:T(8,128)(2,1)S(1)}, bf16[272,128]{1,0:T(8,128)(2,1)S(1)}, u32[]{:S(2)}, u32[]{:S(2)}) collective-permute-start(bf16[272,128]{1,0:T(8,128)(2,1)S(1)} %collective-permute-done.16.refs_7_), channel_id=1, source_target_pairs={{0,1},{1,0},{2,3},{3,2},{4,5},{5,4},{6,7},{7,6},{8,9},{9,8},{10,11... | collective-permute-start | bytes 208904 | tf_op jit(solution)/shard_map/ppermute | solution.py:430

commit v10 on v9

--- a/solution.py
+++ b/solution.py
@@ -304,7 +304,7 @@
     for i in range(lines):
         store[i] = packed[i * plane : (i + 1) * plane]
     for step in range(lines):
-        sent_out[step][...] = store[lax.rem(line[0] + step, lines)]
+        sent_out[step][...] = store[member(line[0], step)]
 
 
 def filter_grads_kernel(
@@ -352,7 +352,7 @@
             base = k * height
             parts.append(total[base : base + 3 * channels, low:high])
             parts.append(total[base + 3 * channels : base + height, width + low : width + high])
-        owner = lax.rem(line[0] + lines - k, lines)
+        owner = member(line[0], k)
         spot = pl.ds(pl.multiple_of(owner * size, size), size)
         partial_out[spot] = jnp.concatenate(parts, axis=0).astype(bf16)
     tail = pltpu.roll(short[...], line[0] * TAPS, 1)
@@ -385,7 +385,7 @@
     share = plane * channels
     whole = back[...].astype(f32)
     for k in range(lines):
-        owner = lax.rem(line[0] + lines - k, lines)
+        owner = member(line[0], k)
         for s in range(3):
             start = (3 * k + s) * channels
             spot = pl.ds(pl.multiple_of(s * width + owner * share, share), share)
@@ -530,11 +530,11 @@
     )
     height = channels * 4 * (width // LANES)
     if whole:
-        def ahead(value, steps):
-            pairs = [(i, (i + steps) % lines) for i in range(lines)]
+        def across_lines(value, distance):
+            pairs = [(i, i ^ distance) for i in range(lines)]
             return lax.ppermute(value, "seq", pairs)
 
-        met = [sent[0]] + [ahead(sent[k], k) for k in range(1, lines)]
+        met = [sent[0]] + [across_lines(sent[k], k) for k in range(1, lines)]
         size = lines * height + 2 * channels
         partial = call(
             lambda *refs: weights_kernel(channels, scale, lines, *refs),
@@ -552,7 +552,7 @@
             *met,
             partial,
         )
-        partials = [partial] + [ahead(partial, k) for k in range(1, lines)]
+        partials = [partial] + [across_lines(partial, k) for k in range(1, lines)]
         back = lax.all_to_all(moved, "fft", split_axis=0, concat_axis=0, tiled=True)
         grad_features = call(
             lambda *refs: moved_kernel(channels, lines, *refs),

time: 54.9 us -> 55.5 us (1.011)
  the two profiles are of different devices: /device:TPU:9 before, /device:TPU:0 now
where the time goes in v10:
time: 55.5 us; the launch traced here: 55.1 us
  starting transfers between devices  27.7 us (50%)
  Pallas kernels  12.4 us (22%)
  waiting for transfers between devices  12 us (22%)
  local copies, waits for them, and re-layouts  2.27 us (4%)
  between operations  0.83 us (1%)
    pallas_call x9, Pallas kernels, call(): pl.pallas_call(kernel, out_shape=outs, compiler_params=PARAMS, **options)  10 us
    ppermute x6, starting transfers between devices, across_lines(): return lax.ppermute(value, 'seq', pairs)  8.9 us
    ppermute x12, starting transfers between devices, swapped(): return lax.ppermute(value, 'fft', [(i, i ^ distance) for i in range(plane)])  7.94 us
    all_to_all x1, starting transfers between devices, local(): lax.all_to_all(streams, AXES, split_axis=0, concat_axis=0, tiled=True)  7.3 us
    ppermute x12, waiting for transfers between devices, swapped(): return lax.ppermute(value, 'fft', [(i, i ^ distance) for i in range(plane)])  4.89 us
    all_to_all x1, waiting for transfers between devices, local(): lax.all_to_all(streams, AXES, split_axis=0, concat_axis=0, tiled=True)  3.54 us
    ppermute x6, waiting for transfers between devices, across_lines(): return lax.ppermute(value, 'seq', pairs)  3.52 us
    all_to_all x1, starting transfers between devices, local(): back = lax.all_to_all(moved, 'fft', split_axis=0, concat_axis=0, tiled=True)  3.52 us
  transfers between devices with their start and end apart: 20, of which 6 were waited for; matrix products, arithmetic and copies ran while one was open for 0% of the time, Pallas kernels for 15%

profile of v10, /device:TPU:0, one launch (start us, length us, event | category | flops | bytes accessed | tf_op | source)
XLA Modules:
  0.0 55.1 jit_solution(7155936845492653783)
XLA Ops:
  0.6 0.0 copy-start
  0.6 0.0 copy-start.2
  0.7 2.4 %shard_map.145 = (bf16[32,32,128]{2,1,0:T(8,128)(2,1)}, bf16[512,128]{1,0:T(8,128)(2,1)}) custom-call(bf16[256,128]{1,0:T(8,128)(2,1)} %features_at.1, s32[1,128]{1,0:T(1,128)} %refs_4_.1, bf16[256,128]{1,0:T(8,128)(2,1)} %cotangent_at.1, bf16[768,256]{1,0:T(8,128)(2,1)} %refs_2_.2, bf16[256,256]{1,0:T(8,128)(2,1)} %w_out_at.1), custom_call_target="tpu_custom_call" | custom-call | tf_op jit(solution)/shard_map/pallas_call | solution.py:458
  3.1 0.0 copy-start.3
  3.1 0.0 copy-start.4
  3.1 7.3 %all-to-all-start = ((bf16[32,32,128]{2,1,0:T(8,128)(2,1)}), bf16[32,32,128]{2,1,0:T(8,128)(2,1)S(1)}, u32[]{:S(2)}, u32[]{:S(2)}) async-start(bf16[32,32,128]{2,1,0:T(8,128)(2,1)} %get-tuple-element.26), calls=%async_computation | async-start | bytes 524288 | tf_op jit(solution)/shard_map/all_to_all | solution.py:472
  10.4 0.3 collective-permute-start.3
  10.7 1.7 %collective-permute-start.4 = (bf16[512,128]{1,0:T(8,128)(2,1)}, bf16[512,128]{1,0:T(8,128)(2,1)S(1)}, u32[]{:S(2)}, u32[]{:S(2)}) collective-permute-start(bf16[512,128]{1,0:T(8,128)(2,1)} %get-tuple-element.39), channel_id=1, source_target_pairs={{0,2},{1,3},{2,0},{3,1},{4,6},{5,7},{6,4},{7,5},{8,10},{9,11},{10,... | collective-permute-start | bytes 393224 | tf_op jit(solution)/shard_map/ppermute | solution.py:430
  12.4 1.5 %collective-permute-start.5 = (bf16[512,128]{1,0:T(8,128)(2,1)}, bf16[512,128]{1,0:T(8,128)(2,1)S(1)}, u32[]{:S(2)}, u32[]{:S(2)}) collective-permute-start(bf16[512,128]{1,0:T(8,128)(2,1)} %get-tuple-element.39), channel_id=1, source_target_pairs={{0,4},{1,5},{2,6},{3,7},{4,0},{5,1},{6,2},{7,3},{8,12},{9,13},{10,... | collective-permute-start | bytes 393224 | tf_op jit(solution)/shard_map/ppermute | solution.py:430
  13.9 0.3 collective-permute-start.6
  14.2 0.0 copy-done
  14.2 0.1 dynamic-slice_bitcast_fusion
  14.3 0.1 copy.19.refs_1_
  14.4 0.0 copy-done.2
  14.4 0.0 copy-done.3
  14.4 0.0 copy-done.4
  14.4 0.9 %copy-done.5 = f32[8,4096]{1,0:T(8,128)S(1)} copy-done((f32[8,4096]{1,0:T(8,128)S(1)}, f32[8,4096]{1,0:T(8,128)}, u32[]{:S(2)}) %copy-start.5) | copy-done | bytes 131096
  15.3 0.7 %copy-done.6 = s32[1,128]{1,0:T(1,128)S(1)} copy-done((s32[1,128]{1,0:T(1,128)S(1)}, s32[1,128]{1,0:T(1,128)}, u32[]{:S(2)}) %copy-start.6) | copy-done | bytes 536
  16.0 1.0 %shard_map.146 = (f32[256,256]{1,0:T(8,128)S(1)}, f32[256,256]{1,0:T(8,128)S(1)}, bf16[1536,256]{1,0:T(8,128)(2,1)S(1)}, f32[256,256]{1,0:T(8,128)S(1)}, s32[1,128]{1,0:T(1,128)S(1)}) custom-call(f32[8,4096]{1,0:T(8,128)S(1)} %copy-done.4, f32[8,4096]{1,0:T(8,128)S(1)} %copy-done.5, bf16[1536,256]{1,0:T(8,128)(2,1)S(1)} %copy-done.2, ...), custom_call_target="tpu_custom_call" | custom-call | tf_op jit(solution)/shard_map/pallas_call | solution.py:455
  17.0 0.0 copy-start.7
  17.0 0.5 copy-done.7
  17.5 3.5 %all-to-all-done.refs_0_ = bf16[32,32,128]{2,1,0:T(8,128)(2,1)S(1)} async-done(((bf16[32,32,128]{2,1,0:T(8,128)(2,1)}), bf16[32,32,128]{2,1,0:T(8,128)(2,1)S(1)}, u32[]{:S(2)}, u32[]{:S(2)}) %all-to-all-start) | async-done | bytes 262176 | tf_op jit(solution)/shard_map/all_to_all | solution.py:472
  21.1 3.7 %shard_map.147 = (f32[8,128]{1,0:T(8,128)S(1)}, f32[256,256]{1,0:T(8,128)S(1)}, f32[256,256]{1,0:T(8,128)S(1)}, bf16[8,32,128]{2,1,0:T(8,128)(2,1)S(1)}, bf16[8,...) custom-call(bf16[32,32,128]{2,1,0:T(8,128)(2,1)S(1)} %all-to-all-done.refs_0_, ...), custom_call_target="tpu_custom_call" | custom-call | tf_op jit(solution)/shard_map/pallas_call | solution.py:455
  24.8 0.0 collective-permute-done.3.refs_0_
  24.8 0.0 collective-permute-done.4.refs_1_
  24.8 0.0 collective-permute-done.5.refs_2_
  24.8 0.0 collective-permute-done.6.refs_3_
  24.9 0.1 collective-permute-start.7
  24.9 1.0 %collective-permute-start = (bf16[8,32,128]{2,1,0:T(8,128)(2,1)S(1)}, bf16[8,32,128]{2,1,0:T(8,128)(2,1)S(1)}, u32[]{:S(2)}, u32[]{:S(2)}) collective-permute-start(bf16[8,32,128]{2,1,0:T(8,128)(2,1)S(1)} %get-tuple-element.32), channel_id=1, source_target_pairs={{0,8},{8,0},{16,24},{24,16},{1,9},{9,1},{17,25},{25,17},{2,10},{10... | collective-permute-start | bytes 196616 | tf_op jit(solution)/shard_map/ppermute | solution.py:535
  26.0 0.9 %collective-permute-start.1 = (bf16[8,32,128]{2,1,0:T(8,128)(2,1)S(1)}, bf16[8,32,128]{2,1,0:T(8,128)(2,1)S(1)}, u32[]{:S(2)}, u32[]{:S(2)}) collective-permute-start(bf16[8,32,128]{2,1,0:T(8,128)(2,1)S(1)} %get-tuple-element.33), channel_id=1, source_target_pairs={{0,16},{8,24},{16,0},{24,8},{1,17},{9,25},{17,1},{25,9},{2,18},{10... | collective-permute-start | bytes 196616 | tf_op jit(solution)/shard_map/ppermute | solution.py:535
  26.9 2.5 %collective-permute-start.2 = (bf16[8,32,128]{2,1,0:T(8,128)(2,1)S(1)}, bf16[8,32,128]{2,1,0:T(8,128)(2,1)S(1)}, u32[]{:S(2)}, u32[]{:S(2)}) collective-permute-start(bf16[8,32,128]{2,1,0:T(8,128)(2,1)S(1)} %get-tuple-element.34), channel_id=1, source_target_pairs={{0,24},{8,16},{16,8},{24,0},{1,25},{9,17},{17,9},{25,1},{2,26},{10... | collective-permute-start | bytes 196616 | tf_op jit(solution)/shard_map/ppermute | solution.py:535
  29.4 1.8 %shard_map.148 = (f32[8,4096]{1,0:T(8,128)}, f32[8,4096]{1,0:T(8,128)}, f32[8,128]{1,0:T(8,128)S(1)}) custom-call(f32[256,256]{1,0:T(8,128)S(1)} %get-tuple-element.35.refs_0_, f32[256,256]{1,0:T(8,128)S(1)} %get-tuple-element.36.refs_1_, bf16[1536,256]{1,0:T(8,128)(2,1)S(1)} %get-tuple-element.29.refs_4_.refs_2_, ...), custom_call_target="tpu_custom_call" | custom-call | tf_op jit(solution)/shard_map/pallas_call | solution.py:455
  31.2 0.0 collective-permute-done.refs_4_.refs_1_
  31.2 3.2 %collective-permute-done.1.refs_5_.refs_2_ = bf16[8,32,128]{2,1,0:T(8,128)(2,1)S(1)} collective-permute-done((bf16[8,32,128]{2,1,0:T(8,128)(2,1)S(1)}, bf16[8,32,128]{2,1,0:T(8,128)(2,1)S(1)}, u32[]{:S(2)}, u32[]{:S(2)}) %collective-permute-start.1) | collective-permute-done | bytes 65568 | tf_op jit(solution)/shard_map/ppermute | solution.py:535
  34.4 0.0 collective-permute-done.2.refs_6_.refs_3_
  34.4 0.0 collective-permute-done.7.refs_8_
  34.4 0.5 shard_map.150.refs_4_.refs_0_
  34.9 1.4 %collective-permute-start.10 = (bf16[272,128]{1,0:T(8,128)(2,1)S(1)}, bf16[272,128]{1,0:T(8,128)(2,1)S(1)}, u32[]{:S(2)}, u32[]{:S(2)}) collective-permute-start(bf16[272,128]{1,0:T(8,128)(2,1)S(1)} %shard_map.150.refs_4_.refs_0_), channel_id=1, source_target_pairs={{0,24},{8,16},{16,8},{24,0},{1,25},{9,17},{17,9},{25,1},{2,26},{10... | collective-permute-start | bytes 208904 | tf_op jit(solution)/shard_map/ppermute | solution.py:535
  36.3 0.6 %collective-permute-start.8 = (bf16[272,128]{1,0:T(8,128)(2,1)S(1)}, bf16[272,128]{1,0:T(8,128)(2,1)S(1)}, u32[]{:S(2)}, u32[]{:S(2)}) collective-permute-start(bf16[272,128]{1,0:T(8,128)(2,1)S(1)} %shard_map.150.refs_4_.refs_0_), channel_id=1, source_target_pairs={{0,8},{8,0},{16,24},{24,16},{1,9},{9,1},{17,25},{25,17},{2,10},{10... | collective-permute-start | bytes 208904 | tf_op jit(solution)/shard_map/ppermute | solution.py:535
  36.9 2.5 %collective-permute-start.9 = (bf16[272,128]{1,0:T(8,128)(2,1)S(1)}, bf16[272,128]{1,0:T(8,128)(2,1)S(1)}, u32[]{:S(2)}, u32[]{:S(2)}) collective-permute-start(bf16[272,128]{1,0:T(8,128)(2,1)S(1)} %shard_map.150.refs_4_.refs_0_), channel_id=1, source_target_pairs={{0,16},{8,24},{16,0},{24,8},{1,17},{9,25},{17,1},{25,9},{2,18},{10... | collective-permute-start | bytes 208904 | tf_op jit(solution)/shard_map/ppermute | solution.py:535
  39.4 0.7 %shard_map.151 = bf16[8,96,128]{2,1,0:T(8,128)(2,1)} custom-call(bf16[8,32,128]{2,1,0:T(8,128)(2,1)S(1)} %get-tuple-element.31.refs_3_.refs_0_, bf16[8,32,128]{2,1,0:T(8,128)(2,1)S(1)} %collective-permute-done.refs_4_.refs_1_, bf16[8,32,128]{2,1,0:T(8,128)(2,1)S(1)} %collective-permute-done.1.refs_5_.refs_2_, ...), custom_call_target="tpu_custom_call" | custom-call | tf_op jit(solution)/shard_map/pallas_call | solution.py:455
  40.1 3.5 %all-to-all-start.1 = ((bf16[8,96,128]{2,1,0:T(8,128)(2,1)}), bf16[8,96,128]{2,1,0:T(8,128)(2,1)S(1)}, u32[]{:S(2)}, u32[]{:S(2)}) async-start(bf16[8,96,128]{2,1,0:T(8,128)(2,1)} %shard_map.151), calls=%async_computation.1 | async-start | bytes 393216 | tf_op jit(solution)/shard_map/all_to_all | solution.py:556
  43.6 0.0 collective-permute-done.10.refs_3_
  43.6 0.0 collective-permute-done.8.refs_1_
  43.6 0.3 collective-permute-done.9.refs_2_
  44.0 0.0 copy-start.8
  44.0 1.7 %collective-permute-start.12 = (bf16[272,128]{1,0:T(8,128)(2,1)S(1)}, bf16[272,128]{1,0:T(8,128)(2,1)S(1)}, u32[]{:S(2)}, u32[]{:S(2)}) collective-permute-start(bf16[272,128]{1,0:T(8,128)(2,1)S(1)} %shard_map.153.refs_1_), channel_id=1, source_target_pairs={{0,2},{1,3},{2,0},{3,1},{4,6},{5,7},{6,4},{7,5},{8,10},{9,11},{10,... | collective-permute-start | bytes 208904 | tf_op jit(solution)/shard_map/ppermute | solution.py:430
  45.7 1.5 %collective-permute-start.14 = (bf16[272,128]{1,0:T(8,128)(2,1)S(1)}, bf16[272,128]{1,0:T(8,128)(2,1)S(1)}, u32[]{:S(2)}, u32[]{:S(2)}) collective-permute-start(bf16[272,128]{1,0:T(8,128)(2,1)S(1)} %shard_map.153.refs_1_), channel_id=1, source_target_pairs={{0,4},{1,5},{2,6},{3,7},{4,0},{5,1},{6,2},{7,3},{8,12},{9,13},{10,... | collective-permute-start | bytes 208904 | tf_op jit(solution)/shard_map/ppermute | solution.py:430
  47.2 0.4 collective-permute-start.16
  47.5 0.0 collective-permute-start.11
  47.5 3.3 %collective-permute-done.12.refs_3_ = bf16[272,128]{1,0:T(8,128)(2,1)S(1)} collective-permute-done((bf16[272,128]{1,0:T(8,128)(2,1)S(1)}, bf16[272,128]{1,0:T(8,128)(2,1)S(1)}, u32[]{:S(2)}, u32[]{:S(2)}) %collective-permute-start.12) | collective-permute-done | bytes 69664 | tf_op jit(solution)/shard_map/ppermute | solution.py:430
  50.8 0.0 collective-permute-start.13
  50.8 0.0 collective-permute-done.14.refs_5_
  50.8 0.5 collective-permute-start.15
  51.3 1.4 %collective-permute-done.16.refs_7_ = bf16[272,128]{1,0:T(8,128)(2,1)S(1)} collective-permute-done((bf16[272,128]{1,0:T(8,128)(2,1)S(1)}, bf16[272,128]{1,0:T(8,128)(2,1)S(1)}, u32[]{:S(2)}, u32[]{:S(2)}) %collective-permute-start.16) | collective-permute-done | bytes 69664 | tf_op jit(solution)/shard_map/ppermute | solution.py:430
  52.8 0.0 collective-permute-start.17
  52.8 0.0 all-to-all-done.1.refs_1_
  52.8 0.0 copy-done.1
  52.8 1.1 %shard_map.152 = bf16[256,128]{1,0:T(8,128)(2,1)} custom-call(s32[1]{0:T(128)} %bitcast.refs_6_.refs_0_, bf16[8,96,128]{2,1,0:T(8,128)(2,1)S(1)} %all-to-all-done.1.refs_1_, bf16[768,256]{1,0:T(8,128)(2,1)S(1)} %copy-done.1, s32[1,128]{1,0:T(1,128)S(1)} %copy-done.8), custom_call_target="tpu_custom_call" | custom-call | tf_op jit(solution)/shard_map/pallas_call | solution.py:455
  53.9 0.0 collective-permute-done.11.refs_2_
  53.9 0.0 collective-permute-done.13.refs_4_
  53.9 0.0 collective-permute-done.15.refs_6_
  53.9 0.1 collective-permute-done.17.refs_8_
  54.0 1.1 %shard_map.154 = (f32[768,256]{1,0:T(8,128)}, f32[256,256]{1,0:T(8,128)}, f32[3,768]{1,0:T(4,128)}) custom-call(s32[1]{0:T(128)} %bitcast.3.refs_1_.refs_0_, bf16[272,128]{1,0:T(8,128)(2,1)S(1)} %shard_map.153.refs_1_, bf16[272,128]{1,0:T(8,128)(2,1)S(1)} %collective-permute-done.11.refs_2_, bf16[272,128]{1,0:T(8,128)(2,1)S(1)} %collective-permute-done.12.refs_3_, ...), custom_call_target="tpu_custom_call" | custom-call | tf_op jit(solution)/shard_map/pallas_call | solution.py:455
  (7 shorter events, 0.1 us)
Async XLA Ops:
  0.6 13.6 %copy-start = (f32[768,3]{0,1:T(4,128)S(1)}, f32[768,3]{0,1:T(4,128)}, u32[]{:S(2)}) copy-start(f32[768,3]{0,1:T(4,128)} %param.14) | copy-start | bytes 27652
  0.6 13.7 %copy-start.2 = (bf16[1536,256]{1,0:T(8,128)(2,1)S(1)}, bf16[1536,256]{1,0:T(8,128)(2,1)}, u32[]{:S(2)}) copy-start(bf16[1536,256]{1,0:T(8,128)(2,1)} %constant.18.clone.refs_2_) | copy-start | bytes 2359300
  3.1 11.3 %copy-start.3 = (f32[256,256]{1,0:T(8,128)S(1)}, f32[256,256]{1,0:T(8,128)}, u32[]{:S(2)}) copy-start(f32[256,256]{1,0:T(8,128)} %constant.19.clone.refs_3_) | copy-start | bytes 786436
  3.1 11.3 %copy-start.4 = (f32[8,4096]{1,0:T(8,128)S(1)}, f32[8,4096]{1,0:T(8,128)}, u32[]{:S(2)}) copy-start(f32[8,4096]{1,0:T(8,128)} %refs_0_.1) | copy-start | bytes 393220
  3.1 18.0 %all-to-all-start = ((bf16[32,32,128]{2,1,0:T(8,128)(2,1)}), bf16[32,32,128]{2,1,0:T(8,128)(2,1)S(1)}, u32[]{:S(2)}, u32[]{:S(2)}) async-start(bf16[32,32,128]{2,1,0:T(8,128)(2,1)} %get-tuple-element.26), calls=%async_computation | async-start | bytes 524288 | tf_op jit(solution)/shard_map/all_to_all | solution.py:472
  10.4 14.4 %collective-permute-start.3 = (bf16[512,128]{1,0:T(8,128)(2,1)}, bf16[512,128]{1,0:T(8,128)(2,1)S(1)}, u32[]{:S(2)}, u32[]{:S(2)}) collective-permute-start(bf16[512,128]{1,0:T(8,128)(2,1)} %get-tuple-element.39), channel_id=1, source_target_pairs={{0,1},{1,0},{2,3},{3,2},{4,5},{5,4},{6,7},{7,6},{8,9},{9,8},{10,11... | collective-permute-start | bytes 393224 | tf_op jit(solution)/shard_map/ppermute | solution.py:430
  10.7 14.1 %collective-permute-start.4 = (bf16[512,128]{1,0:T(8,128)(2,1)}, bf16[512,128]{1,0:T(8,128)(2,1)S(1)}, u32[]{:S(2)}, u32[]{:S(2)}) collective-permute-start(bf16[512,128]{1,0:T(8,128)(2,1)} %get-tuple-element.39), channel_id=1, source_target_pairs={{0,2},{1,3},{2,0},{3,1},{4,6},{5,7},{6,4},{7,5},{8,10},{9,11},{10,... | collective-permute-start | bytes 393224 | tf_op jit(solution)/shard_map/ppermute | solution.py:430
  12.4 12.4 %collective-permute-start.5 = (bf16[512,128]{1,0:T(8,128)(2,1)}, bf16[512,128]{1,0:T(8,128)(2,1)S(1)}, u32[]{:S(2)}, u32[]{:S(2)}) collective-permute-start(bf16[512,128]{1,0:T(8,128)(2,1)} %get-tuple-element.39), channel_id=1, source_target_pairs={{0,4},{1,5},{2,6},{3,7},{4,0},{5,1},{6,2},{7,3},{8,12},{9,13},{10,... | collective-permute-start | bytes 393224 | tf_op jit(solution)/shard_map/ppermute | solution.py:430
  13.9 10.9 %collective-permute-start.6 = (bf16[512,128]{1,0:T(8,128)(2,1)}, bf16[512,128]{1,0:T(8,128)(2,1)S(1)}, u32[]{:S(2)}, u32[]{:S(2)}) collective-permute-start(bf16[512,128]{1,0:T(8,128)(2,1)} %get-tuple-element.39), channel_id=1, source_target_pairs={{0,6},{1,7},{2,4},{3,5},{4,2},{5,3},{6,0},{7,1},{8,14},{9,15},{10,... | collective-permute-start | bytes 393224 | tf_op jit(solution)/shard_map/ppermute | solution.py:430
  14.4 0.9 %copy-start.5 = (f32[8,4096]{1,0:T(8,128)S(1)}, f32[8,4096]{1,0:T(8,128)}, u32[]{:S(2)}) copy-start(f32[8,4096]{1,0:T(8,128)} %refs_1_.1) | copy-start | bytes 393220
  15.3 0.7 %copy-start.6 = (s32[1,128]{1,0:T(1,128)S(1)}, s32[1,128]{1,0:T(1,128)}, u32[]{:S(2)}) copy-start(s32[1,128]{1,0:T(1,128)} %refs_4_.1) | copy-start | bytes 1540
  17.0 0.5 copy-start.7
  24.9 9.6 %collective-permute-start.7 = (bf16[4,512,128]{2,1,0:T(8,128)(2,1)S(1)}, bf16[4,512,128]{2,1,0:T(8,128)(2,1)S(1)}, u32[]{:S(2)}, u32[]{:S(2)}) collective-permute-start(bf16[4,512,128]{2,1,0:T(8,128)(2,1)S(1)} %shard_map.149.refs_7_), channel_id=1, source_target_pairs={{0,1},{1,0},{2,3},{3,2},{4,5},{5,4},{6,7},{7,6},{8,9},{9,8},{10,11... | collective-permute-start | bytes 1572872 | tf_op jit(solution)/shard_map/ppermute | solution.py:430
  24.9 6.2 %collective-permute-start = (bf16[8,32,128]{2,1,0:T(8,128)(2,1)S(1)}, bf16[8,32,128]{2,1,0:T(8,128)(2,1)S(1)}, u32[]{:S(2)}, u32[]{:S(2)}) collective-permute-start(bf16[8,32,128]{2,1,0:T(8,128)(2,1)S(1)} %get-tuple-element.32), channel_id=1, source_target_pairs={{0,8},{8,0},{16,24},{24,16},{1,9},{9,1},{17,25},{25,17},{2,10},{10... | collective-permute-start | bytes 196616 | tf_op jit(solution)/shard_map/ppermute | solution.py:535
  26.0 8.4 %collective-permute-start.1 = (bf16[8,32,128]{2,1,0:T(8,128)(2,1)S(1)}, bf16[8,32,128]{2,1,0:T(8,128)(2,1)S(1)}, u32[]{:S(2)}, u32[]{:S(2)}) collective-permute-start(bf16[8,32,128]{2,1,0:T(8,128)(2,1)S(1)} %get-tuple-element.33), channel_id=1, source_target_pairs={{0,16},{8,24},{16,0},{24,8},{1,17},{9,25},{17,1},{25,9},{2,18},{10... | collective-permute-start | bytes 196616 | tf_op jit(solution)/shard_map/ppermute | solution.py:535
  26.9 7.5 %collective-permute-start.2 = (bf16[8,32,128]{2,1,0:T(8,128)(2,1)S(1)}, bf16[8,32,128]{2,1,0:T(8,128)(2,1)S(1)}, u32[]{:S(2)}, u32[]{:S(2)}) collective-permute-start(bf16[8,32,128]{2,1,0:T(8,128)(2,1)S(1)} %get-tuple-element.34), channel_id=1, source_target_pairs={{0,24},{8,16},{16,8},{24,0},{1,25},{9,17},{17,9},{25,1},{2,26},{10... | collective-permute-start | bytes 196616 | tf_op jit(solution)/shard_map/ppermute | solution.py:535
  34.9 8.7 %collective-permute-start.10 = (bf16[272,128]{1,0:T(8,128)(2,1)S(1)}, bf16[272,128]{1,0:T(8,128)(2,1)S(1)}, u32[]{:S(2)}, u32[]{:S(2)}) collective-permute-start(bf16[272,128]{1,0:T(8,128)(2,1)S(1)} %shard_map.150.refs_4_.refs_0_), channel_id=1, source_target_pairs={{0,24},{8,16},{16,8},{24,0},{1,25},{9,17},{17,9},{25,1},{2,26},{10... | collective-permute-start | bytes 208904 | tf_op jit(solution)/shard_map/ppermute | solution.py:535
  36.3 7.3 %collective-permute-start.8 = (bf16[272,128]{1,0:T(8,128)(2,1)S(1)}, bf16[272,128]{1,0:T(8,128)(2,1)S(1)}, u32[]{:S(2)}, u32[]{:S(2)}) collective-permute-start(bf16[272,128]{1,0:T(8,128)(2,1)S(1)} %shard_map.150.refs_4_.refs_0_), channel_id=1, source_target_pairs={{0,8},{8,0},{16,24},{24,16},{1,9},{9,1},{17,25},{25,17},{2,10},{10... | collective-permute-start | bytes 208904 | tf_op jit(solution)/shard_map/ppermute | solution.py:535
  36.9 7.0 %collective-permute-start.9 = (bf16[272,128]{1,0:T(8,128)(2,1)S(1)}, bf16[272,128]{1,0:T(8,128)(2,1)S(1)}, u32[]{:S(2)}, u32[]{:S(2)}) collective-permute-start(bf16[272,128]{1,0:T(8,128)(2,1)S(1)} %shard_map.150.refs_4_.refs_0_), channel_id=1, source_target_pairs={{0,16},{8,24},{16,0},{24,8},{1,17},{9,25},{17,1},{25,9},{2,18},{10... | collective-permute-start | bytes 208904 | tf_op jit(solution)/shard_map/ppermute | solution.py:535
  40.1 12.7 %copy-start.1 = (bf16[768,256]{1,0:T(8,128)(2,1)S(1)}, bf16[768,256]{1,0:T(8,128)(2,1)}, u32[]{:S(2)}) copy-start(bf16[768,256]{1,0:T(8,128)(2,1)} %refs_2_.2) | copy-start | bytes 1179652
  40.1 12.7 %all-to-all-start.1 = ((bf16[8,96,128]{2,1,0:T(8,128)(2,1)}), bf16[8,96,128]{2,1,0:T(8,128)(2,1)S(1)}, u32[]{:S(2)}, u32[]{:S(2)}) async-start(bf16[8,96,128]{2,1,0:T(8,128)(2,1)} %shard_map.151), calls=%async_computation.1 | async-start | bytes 393216 | tf_op jit(solution)/shard_map/all_to_all | solution.py:556
  44.0 8.8 %copy-start.8 = (s32[1,128]{1,0:T(1,128)S(1)}, s32[1,128]{1,0:T(1,128)}, u32[]{:S(2)}) copy-start(s32[1,128]{1,0:T(1,128)} %copy-done.7) | copy-start | bytes 1540
  44.0 6.8 %collective-permute-start.12 = (bf16[272,128]{1,0:T(8,128)(2,1)S(1)}, bf16[272,128]{1,0:T(8,128)(2,1)S(1)}, u32[]{:S(2)}, u32[]{:S(2)}) collective-permute-start(bf16[272,128]{1,0:T(8,128)(2,1)S(1)} %shard_map.153.refs_1_), channel_id=1, source_target_pairs={{0,2},{1,3},{2,0},{3,1},{4,6},{5,7},{6,4},{7,5},{8,10},{9,11},{10,... | collective-permute-start | bytes 208904 | tf_op jit(solution)/shard_map/ppermute | solution.py:430
  45.7 5.1 %collective-permute-start.14 = (bf16[272,128]{1,0:T(8,128)(2,1)S(1)}, bf16[272,128]{1,0:T(8,128)(2,1)S(1)}, u32[]{:S(2)}, u32[]{:S(2)}) collective-permute-start(bf16[272,128]{1,0:T(8,128)(2,1)S(1)} %shard_map.153.refs_1_), channel_id=1, source_target_pairs={{0,4},{1,5},{2,6},{3,7},{4,0},{5,1},{6,2},{7,3},{8,12},{9,13},{10,... | collective-permute-start | bytes 208904 | tf_op jit(solution)/shard_map/ppermute | solution.py:430
  47.2 5.6 %collective-permute-start.16 = (bf16[272,128]{1,0:T(8,128)(2,1)S(1)}, bf16[272,128]{1,0:T(8,128)(2,1)S(1)}, u32[]{:S(2)}, u32[]{:S(2)}) collective-permute-start(bf16[272,128]{1,0:T(8,128)(2,1)S(1)} %shard_map.153.refs_1_), channel_id=1, source_target_pairs={{0,6},{1,7},{2,4},{3,5},{4,2},{5,3},{6,0},{7,1},{8,14},{9,15},{10,... | collective-permute-start | bytes 208904 | tf_op jit(solution)/shard_map/ppermute | solution.py:430
  47.5 6.3 %collective-permute-start.11 = (bf16[272,128]{1,0:T(8,128)(2,1)S(1)}, bf16[272,128]{1,0:T(8,128)(2,1)S(1)}, u32[]{:S(2)}, u32[]{:S(2)}) collective-permute-start(bf16[272,128]{1,0:T(8,128)(2,1)S(1)} %shard_map.153.refs_1_), channel_id=1, source_target_pairs={{0,1},{1,0},{2,3},{3,2},{4,5},{5,4},{6,7},{7,6},{8,9},{9,8},{10,11... | collective-permute-start | bytes 208904 | tf_op jit(solution)/shard_map/ppermute | solution.py:430
  50.8 3.1 %collective-permute-start.13 = (bf16[272,128]{1,0:T(8,128)(2,1)S(1)}, bf16[272,128]{1,0:T(8,128)(2,1)S(1)}, u32[]{:S(2)}, u32[]{:S(2)}) collective-permute-start(bf16[272,128]{1,0:T(8,128)(2,1)S(1)} %collective-permute-done.12.refs_3_), channel_id=1, source_target_pairs={{0,1},{1,0},{2,3},{3,2},{4,5},{5,4},{6,7},{7,6},{8,9},{9,8},{10,11... | collective-permute-start | bytes 208904 | tf_op jit(solution)/shard_map/ppermute | solution.py:430
  50.8 3.0 %collective-permute-start.15 = (bf16[272,128]{1,0:T(8,128)(2,1)S(1)}, bf16[272,128]{1,0:T(8,128)(2,1)S(1)}, u32[]{:S(2)}, u32[]{:S(2)}) collective-permute-start(bf16[272,128]{1,0:T(8,128)(2,1)S(1)} %collective-permute-done.14.refs_5_), channel_id=1, source_target_pairs={{0,1},{1,0},{2,3},{3,2},{4,5},{5,4},{6,7},{7,6},{8,9},{9,8},{10,11... | collective-permute-start | bytes 208904 | tf_op jit(solution)/shard_map/ppermute | solution.py:430
  52.8 1.3 %collective-permute-start.17 = (bf16[272,128]{1,0:T(8,128)(2,1)S(1)}, bf16[272,128]{1,0:T(8,128)(2,1)S(1)}, u32[]{:S(2)}, u32[]{:S(2)}) collective-permute-start(bf16[272,128]{1,0:T(8,128)(2,1)S(1)} %collective-permute-done.16.refs_7_), channel_id=1, source_target_pairs={{0,1},{1,0},{2,3},{3,2},{4,5},{5,4},{6,7},{7,6},{8,9},{9,8},{10,11... | collective-permute-start | bytes 208904 | tf_op jit(solution)/shard_map/ppermute | solution.py:430

commit v11 on v9

--- a/solution.py
+++ b/solution.py
@@ -552,7 +552,8 @@
             *met,
             partial,
         )
-        partials = [partial] + [ahead(partial, k) for k in range(1, lines)]
+        pairs = [[(i, i ^ k) for i in range(lines)] for k in range(1, lines)]
+        partials = [partial] + [lax.ppermute(partial, "seq", pair) for pair in pairs]
         back = lax.all_to_all(moved, "fft", split_axis=0, concat_axis=0, tiled=True)
         grad_features = call(
             lambda *refs: moved_kernel(channels, lines, *refs),

time: 54.9 us -> 55.2 us (level)
  the two profiles are of different devices: /device:TPU:9 before, /device:TPU:0 now
where the time goes in v11:
time: 55.2 us; the launch traced here: 54.9 us
  starting transfers between devices  27.1 us (49%)
  Pallas kernels  12.4 us (22%)
  waiting for transfers between devices  12.2 us (22%)
  local copies, waits for them, and re-layouts  2.27 us (4%)
  between operations  0.82 us (1%)
    pallas_call x9, Pallas kernels, call(): pl.pallas_call(kernel, out_shape=outs, compiler_params=PARAMS, **options)  10 us
    ppermute x12, starting transfers between devices, swapped(): return lax.ppermute(value, 'fft', [(i, i ^ distance) for i in range(plane)])  7.94 us
    all_to_all x1, starting transfers between devices, local(): lax.all_to_all(streams, AXES, split_axis=0, concat_axis=0, tiled=True)  7.3 us
    ppermute x3, starting transfers between devices, local(): lax.ppermute(partial, 'seq', pair)  4.45 us
    ppermute x12, waiting for transfers between devices, swapped(): return lax.ppermute(value, 'fft', [(i, i ^ distance) for i in range(plane)])  4.34 us
    ppermute x3, starting transfers between devices, ahead(): return lax.ppermute(value, 'seq', pairs)  3.88 us
    all_to_all x1, waiting for transfers between devices, local(): lax.all_to_all(streams, AXES, split_axis=0, concat_axis=0, tiled=True)  3.54 us
    ppermute x3, waiting for transfers between devices, ahead(): return lax.ppermute(value, 'seq', pairs)  3.54 us
  transfers between devices with their start and end apart: 20, of which 7 were waited for; matrix products, arithmetic and copies ran while one was open for 0% of the time, Pallas kernels for 15%

profile of v11, /device:TPU:0, one launch (start us, length us, event | category | flops | bytes accessed | tf_op | source)
XLA Modules:
  0.0 54.9 jit_solution(16998286699455777751)
XLA Ops:
  0.6 0.0 copy-start
  0.6 0.0 copy-start.2
  0.7 2.4 %shard_map.145 = (bf16[32,32,128]{2,1,0:T(8,128)(2,1)}, bf16[512,128]{1,0:T(8,128)(2,1)}) custom-call(bf16[256,128]{1,0:T(8,128)(2,1)} %features_at.1, s32[1,128]{1,0:T(1,128)} %refs_4_.1, bf16[256,128]{1,0:T(8,128)(2,1)} %cotangent_at.1, bf16[768,256]{1,0:T(8,128)(2,1)} %refs_2_.2, bf16[256,256]{1,0:T(8,128)(2,1)} %w_out_at.1), custom_call_target="tpu_custom_call" | custom-call | tf_op jit(solution)/shard_map/pallas_call | solution.py:458
  3.1 0.0 copy-start.3
  3.1 0.0 copy-start.4
  3.1 7.3 %all-to-all-start = ((bf16[32,32,128]{2,1,0:T(8,128)(2,1)}), bf16[32,32,128]{2,1,0:T(8,128)(2,1)S(1)}, u32[]{:S(2)}, u32[]{:S(2)}) async-start(bf16[32,32,128]{2,1,0:T(8,128)(2,1)} %get-tuple-element.26), calls=%async_computation | async-start | bytes 524288 | tf_op jit(solution)/shard_map/all_to_all | solution.py:472
  10.4 0.3 collective-permute-start.3
  10.7 1.7 %collective-permute-start.4 = (bf16[512,128]{1,0:T(8,128)(2,1)}, bf16[512,128]{1,0:T(8,128)(2,1)S(1)}, u32[]{:S(2)}, u32[]{:S(2)}) collective-permute-start(bf16[512,128]{1,0:T(8,128)(2,1)} %get-tuple-element.39), channel_id=1, source_target_pairs={{0,2},{1,3},{2,0},{3,1},{4,6},{5,7},{6,4},{7,5},{8,10},{9,11},{10,... | collective-permute-start | bytes 393224 | tf_op jit(solution)/shard_map/ppermute | solution.py:430
  12.4 1.5 %collective-permute-start.5 = (bf16[512,128]{1,0:T(8,128)(2,1)}, bf16[512,128]{1,0:T(8,128)(2,1)S(1)}, u32[]{:S(2)}, u32[]{:S(2)}) collective-permute-start(bf16[512,128]{1,0:T(8,128)(2,1)} %get-tuple-element.39), channel_id=1, source_target_pairs={{0,4},{1,5},{2,6},{3,7},{4,0},{5,1},{6,2},{7,3},{8,12},{9,13},{10,... | collective-permute-start | bytes 393224 | tf_op jit(solution)/shard_map/ppermute | solution.py:430
  13.9 0.3 collective-permute-start.6
  14.2 0.0 copy-done
  14.2 0.1 dynamic-slice_bitcast_fusion
  14.3 0.1 copy.19.refs_1_
  14.4 0.0 copy-done.2
  14.4 0.0 copy-done.3
  14.4 0.0 copy-done.4
  14.4 0.9 %copy-done.5 = f32[8,4096]{1,0:T(8,128)S(1)} copy-done((f32[8,4096]{1,0:T(8,128)S(1)}, f32[8,4096]{1,0:T(8,128)}, u32[]{:S(2)}) %copy-start.5) | copy-done | bytes 131096
  15.3 0.7 %copy-done.6 = s32[1,128]{1,0:T(1,128)S(1)} copy-done((s32[1,128]{1,0:T(1,128)S(1)}, s32[1,128]{1,0:T(1,128)}, u32[]{:S(2)}) %copy-start.6) | copy-done | bytes 536
  16.0 1.0 %shard_map.146 = (f32[256,256]{1,0:T(8,128)S(1)}, f32[256,256]{1,0:T(8,128)S(1)}, bf16[1536,256]{1,0:T(8,128)(2,1)S(1)}, f32[256,256]{1,0:T(8,128)S(1)}, s32[1,128]{1,0:T(1,128)S(1)}) custom-call(f32[8,4096]{1,0:T(8,128)S(1)} %copy-done.4, f32[8,4096]{1,0:T(8,128)S(1)} %copy-done.5, bf16[1536,256]{1,0:T(8,128)(2,1)S(1)} %copy-done.2, ...), custom_call_target="tpu_custom_call" | custom-call | tf_op jit(solution)/shard_map/pallas_call | solution.py:455
  17.0 0.0 copy-start.7
  17.0 0.5 copy-done.7
  17.5 3.5 %all-to-all-done.refs_0_ = bf16[32,32,128]{2,1,0:T(8,128)(2,1)S(1)} async-done(((bf16[32,32,128]{2,1,0:T(8,128)(2,1)}), bf16[32,32,128]{2,1,0:T(8,128)(2,1)S(1)}, u32[]{:S(2)}, u32[]{:S(2)}) %all-to-all-start) | async-done | bytes 262176 | tf_op jit(solution)/shard_map/all_to_all | solution.py:472
  21.1 3.7 %shard_map.147 = (f32[8,128]{1,0:T(8,128)S(1)}, f32[256,256]{1,0:T(8,128)S(1)}, f32[256,256]{1,0:T(8,128)S(1)}, bf16[8,32,128]{2,1,0:T(8,128)(2,1)S(1)}, bf16[8,...) custom-call(bf16[32,32,128]{2,1,0:T(8,128)(2,1)S(1)} %all-to-all-done.refs_0_, ...), custom_call_target="tpu_custom_call" | custom-call | tf_op jit(solution)/shard_map/pallas_call | solution.py:455
  24.8 0.0 collective-permute-done.3.refs_0_
  24.8 0.0 collective-permute-done.4.refs_1_
  24.8 0.0 collective-permute-done.5.refs_2_
  24.8 0.0 collective-permute-done.6.refs_3_
  24.8 0.1 collective-permute-start.7
  24.9 1.0 %collective-permute-start = (bf16[8,32,128]{2,1,0:T(8,128)(2,1)S(1)}, bf16[8,32,128]{2,1,0:T(8,128)(2,1)S(1)}, u32[]{:S(2)}, u32[]{:S(2)}) collective-permute-start(bf16[8,32,128]{2,1,0:T(8,128)(2,1)S(1)} %get-tuple-element.32), channel_id=1, source_target_pairs={{0,8},{8,16},{16,24},{24,0},{1,9},{9,17},{17,25},{25,1},{2,10},{10... | collective-permute-start | bytes 196616 | tf_op jit(solution)/shard_map/ppermute | solution.py:535
  26.0 0.9 %collective-permute-start.1 = (bf16[8,32,128]{2,1,0:T(8,128)(2,1)S(1)}, bf16[8,32,128]{2,1,0:T(8,128)(2,1)S(1)}, u32[]{:S(2)}, u32[]{:S(2)}) collective-permute-start(bf16[8,32,128]{2,1,0:T(8,128)(2,1)S(1)} %get-tuple-element.33), channel_id=1, source_target_pairs={{0,16},{8,24},{16,0},{24,8},{1,17},{9,25},{17,1},{25,9},{2,18},{10... | collective-permute-start | bytes 196616 | tf_op jit(solution)/shard_map/ppermute | solution.py:535
  26.9 1.9 %collective-permute-start.2 = (bf16[8,32,128]{2,1,0:T(8,128)(2,1)S(1)}, bf16[8,32,128]{2,1,0:T(8,128)(2,1)S(1)}, u32[]{:S(2)}, u32[]{:S(2)}) collective-permute-start(bf16[8,32,128]{2,1,0:T(8,128)(2,1)S(1)} %get-tuple-element.34), channel_id=1, source_target_pairs={{0,24},{8,0},{16,8},{24,16},{1,25},{9,1},{17,9},{25,17},{2,26},{10... | collective-permute-start | bytes 196616 | tf_op jit(solution)/shard_map/ppermute | solution.py:535
  28.8 1.8 %shard_map.148 = (f32[8,4096]{1,0:T(8,128)}, f32[8,4096]{1,0:T(8,128)}, f32[8,128]{1,0:T(8,128)S(1)}) custom-call(f32[256,256]{1,0:T(8,128)S(1)} %get-tuple-element.35.refs_0_, f32[256,256]{1,0:T(8,128)S(1)} %get-tuple-element.36.refs_1_, bf16[1536,256]{1,0:T(8,128)(2,1)S(1)} %get-tuple-element.29.refs_4_.refs_2_, ...), custom_call_target="tpu_custom_call" | custom-call | tf_op jit(solution)/shard_map/pallas_call | solution.py:455
  30.6 1.2 %collective-permute-done.refs_4_.refs_1_ = bf16[8,32,128]{2,1,0:T(8,128)(2,1)S(1)} collective-permute-done((bf16[8,32,128]{2,1,0:T(8,128)(2,1)S(1)}, bf16[8,32,128]{2,1,0:T(8,128)(2,1)S(1)}, u32[]{:S(2)}, u32[]{:S(2)}) %collective-permute-start) | collective-permute-done | bytes 65568 | tf_op jit(solution)/shard_map/ppermute | solution.py:535
  31.8 2.4 %collective-permute-done.1.refs_5_.refs_2_ = bf16[8,32,128]{2,1,0:T(8,128)(2,1)S(1)} collective-permute-done((bf16[8,32,128]{2,1,0:T(8,128)(2,1)S(1)}, bf16[8,32,128]{2,1,0:T(8,128)(2,1)S(1)}, u32[]{:S(2)}, u32[]{:S(2)}) %collective-permute-start.1) | collective-permute-done | bytes 65568 | tf_op jit(solution)/shard_map/ppermute | solution.py:535
  34.1 0.0 collective-permute-done.2.refs_6_.refs_3_
  34.1 0.0 collective-permute-done.7.refs_8_
  34.1 0.5 shard_map.150.refs_4_.refs_0_
  34.6 2.2 %collective-permute-start.10 = (bf16[272,128]{1,0:T(8,128)(2,1)S(1)}, bf16[272,128]{1,0:T(8,128)(2,1)S(1)}, u32[]{:S(2)}, u32[]{:S(2)}) collective-permute-start(bf16[272,128]{1,0:T(8,128)(2,1)S(1)} %shard_map.150.refs_4_.refs_0_), channel_id=1, source_target_pairs={{0,24},{8,16},{16,8},{24,0},{1,25},{9,17},{17,9},{25,1},{2,26},{10... | collective-permute-start | bytes 208904 | tf_op jit(solution)/shard_map/ppermute | solution.py:556
  36.9 0.0 collective-permute-start.8
  36.9 2.2 %collective-permute-start.9 = (bf16[272,128]{1,0:T(8,128)(2,1)S(1)}, bf16[272,128]{1,0:T(8,128)(2,1)S(1)}, u32[]{:S(2)}, u32[]{:S(2)}) collective-permute-start(bf16[272,128]{1,0:T(8,128)(2,1)S(1)} %shard_map.150.refs_4_.refs_0_), channel_id=1, source_target_pairs={{0,16},{8,24},{16,0},{24,8},{1,17},{9,25},{17,1},{25,9},{2,18},{10... | collective-permute-start | bytes 208904 | tf_op jit(solution)/shard_map/ppermute | solution.py:556
  39.1 0.7 %shard_map.151 = bf16[8,96,128]{2,1,0:T(8,128)(2,1)} custom-call(bf16[8,32,128]{2,1,0:T(8,128)(2,1)S(1)} %get-tuple-element.31.refs_3_.refs_0_, bf16[8,32,128]{2,1,0:T(8,128)(2,1)S(1)} %collective-permute-done.refs_4_.refs_1_, bf16[8,32,128]{2,1,0:T(8,128)(2,1)S(1)} %collective-permute-done.1.refs_5_.refs_2_, ...), custom_call_target="tpu_custom_call" | custom-call | tf_op jit(solution)/shard_map/pallas_call | solution.py:455
  39.8 3.5 %all-to-all-start.1 = ((bf16[8,96,128]{2,1,0:T(8,128)(2,1)}), bf16[8,96,128]{2,1,0:T(8,128)(2,1)S(1)}, u32[]{:S(2)}, u32[]{:S(2)}) async-start(bf16[8,96,128]{2,1,0:T(8,128)(2,1)} %shard_map.151), calls=%async_computation.1 | async-start | bytes 393216 | tf_op jit(solution)/shard_map/all_to_all | solution.py:557
  43.3 0.0 collective-permute-done.10.refs_3_
  43.3 0.0 collective-permute-done.8.refs_1_
  43.4 0.8 %collective-permute-done.9.refs_2_ = bf16[272,128]{1,0:T(8,128)(2,1)S(1)} collective-permute-done((bf16[272,128]{1,0:T(8,128)(2,1)S(1)}, bf16[272,128]{1,0:T(8,128)(2,1)S(1)}, u32[]{:S(2)}, u32[]{:S(2)}) %collective-permute-start.9) | collective-permute-done | bytes 69664 | tf_op jit(solution)/shard_map/ppermute | solution.py:556
  44.2 0.0 copy-start.8
  44.2 1.2 %collective-permute-start.12 = (bf16[272,128]{1,0:T(8,128)(2,1)S(1)}, bf16[272,128]{1,0:T(8,128)(2,1)S(1)}, u32[]{:S(2)}, u32[]{:S(2)}) collective-permute-start(bf16[272,128]{1,0:T(8,128)(2,1)S(1)} %shard_map.153.refs_1_), channel_id=1, source_target_pairs={{0,2},{1,3},{2,0},{3,1},{4,6},{5,7},{6,4},{7,5},{8,10},{9,11},{10,... | collective-permute-start | bytes 208904 | tf_op jit(solution)/shard_map/ppermute | solution.py:430
  45.4 1.5 %collective-permute-start.14 = (bf16[272,128]{1,0:T(8,128)(2,1)S(1)}, bf16[272,128]{1,0:T(8,128)(2,1)S(1)}, u32[]{:S(2)}, u32[]{:S(2)}) collective-permute-start(bf16[272,128]{1,0:T(8,128)(2,1)S(1)} %shard_map.153.refs_1_), channel_id=1, source_target_pairs={{0,4},{1,5},{2,6},{3,7},{4,0},{5,1},{6,2},{7,3},{8,12},{9,13},{10,... | collective-permute-start | bytes 208904 | tf_op jit(solution)/shard_map/ppermute | solution.py:430
  46.9 0.9 %collective-permute-start.16 = (bf16[272,128]{1,0:T(8,128)(2,1)S(1)}, bf16[272,128]{1,0:T(8,128)(2,1)S(1)}, u32[]{:S(2)}, u32[]{:S(2)}) collective-permute-start(bf16[272,128]{1,0:T(8,128)(2,1)S(1)} %shard_map.153.refs_1_), channel_id=1, source_target_pairs={{0,6},{1,7},{2,4},{3,5},{4,2},{5,3},{6,0},{7,1},{8,14},{9,15},{10,... | collective-permute-start | bytes 208904 | tf_op jit(solution)/shard_map/ppermute | solution.py:430
  47.8 0.0 collective-permute-start.11
  47.8 2.8 %collective-permute-done.12.refs_3_ = bf16[272,128]{1,0:T(8,128)(2,1)S(1)} collective-permute-done((bf16[272,128]{1,0:T(8,128)(2,1)S(1)}, bf16[272,128]{1,0:T(8,128)(2,1)S(1)}, u32[]{:S(2)}, u32[]{:S(2)}) %collective-permute-start.12) | collective-permute-done | bytes 69664 | tf_op jit(solution)/shard_map/ppermute | solution.py:430
  50.5 0.0 collective-permute-start.13
  50.5 0.0 collective-permute-done.14.refs_5_
  50.5 0.5 collective-permute-start.15
  51.0 1.4 %collective-permute-done.16.refs_7_ = bf16[272,128]{1,0:T(8,128)(2,1)S(1)} collective-permute-done((bf16[272,128]{1,0:T(8,128)(2,1)S(1)}, bf16[272,128]{1,0:T(8,128)(2,1)S(1)}, u32[]{:S(2)}, u32[]{:S(2)}) %collective-permute-start.16) | collective-permute-done | bytes 69664 | tf_op jit(solution)/shard_map/ppermute | solution.py:430
  52.5 0.0 collective-permute-start.17
  52.5 0.0 all-to-all-done.1.refs_1_
  52.5 0.0 copy-done.1
  52.5 1.1 %shard_map.152 = bf16[256,128]{1,0:T(8,128)(2,1)} custom-call(s32[1]{0:T(128)} %bitcast.refs_6_.refs_0_, bf16[8,96,128]{2,1,0:T(8,128)(2,1)S(1)} %all-to-all-done.1.refs_1_, bf16[768,256]{1,0:T(8,128)(2,1)S(1)} %copy-done.1, s32[1,128]{1,0:T(1,128)S(1)} %copy-done.8), custom_call_target="tpu_custom_call" | custom-call | tf_op jit(solution)/shard_map/pallas_call | solution.py:455
  53.6 0.0 collective-permute-done.11.refs_2_
  53.6 0.0 collective-permute-done.13.refs_4_
  53.6 0.0 collective-permute-done.15.refs_6_
  53.6 0.1 collective-permute-done.17.refs_8_
  53.7 1.1 %shard_map.154 = (f32[768,256]{1,0:T(8,128)}, f32[256,256]{1,0:T(8,128)}, f32[3,768]{1,0:T(4,128)}) custom-call(s32[1]{0:T(128)} %bitcast.3.refs_1_.refs_0_, bf16[272,128]{1,0:T(8,128)(2,1)S(1)} %shard_map.153.refs_1_, bf16[272,128]{1,0:T(8,128)(2,1)S(1)} %collective-permute-done.11.refs_2_, bf16[272,128]{1,0:T(8,128)(2,1)S(1)} %collective-permute-done.12.refs_3_, ...), custom_call_target="tpu_custom_call" | custom-call | tf_op jit(solution)/shard_map/pallas_call | solution.py:455
  (7 shorter events, 0.1 us)
Async XLA Ops:
  0.6 13.6 %copy-start = (f32[768,3]{0,1:T(4,128)S(1)}, f32[768,3]{0,1:T(4,128)}, u32[]{:S(2)}) copy-start(f32[768,3]{0,1:T(4,128)} %param.14) | copy-start | bytes 27652
  0.6 13.7 %copy-start.2 = (bf16[1536,256]{1,0:T(8,128)(2,1)S(1)}, bf16[1536,256]{1,0:T(8,128)(2,1)}, u32[]{:S(2)}) copy-start(bf16[1536,256]{1,0:T(8,128)(2,1)} %constant.18.clone.refs_2_) | copy-start | bytes 2359300
  3.1 11.3 %copy-start.3 = (f32[256,256]{1,0:T(8,128)S(1)}, f32[256,256]{1,0:T(8,128)}, u32[]{:S(2)}) copy-start(f32[256,256]{1,0:T(8,128)} %constant.19.clone.refs_3_) | copy-start | bytes 786436
  3.1 11.3 %copy-start.4 = (f32[8,4096]{1,0:T(8,128)S(1)}, f32[8,4096]{1,0:T(8,128)}, u32[]{:S(2)}) copy-start(f32[8,4096]{1,0:T(8,128)} %refs_0_.1) | copy-start | bytes 393220
  3.1 18.0 %all-to-all-start = ((bf16[32,32,128]{2,1,0:T(8,128)(2,1)}), bf16[32,32,128]{2,1,0:T(8,128)(2,1)S(1)}, u32[]{:S(2)}, u32[]{:S(2)}) async-start(bf16[32,32,128]{2,1,0:T(8,128)(2,1)} %get-tuple-element.26), calls=%async_computation | async-start | bytes 524288 | tf_op jit(solution)/shard_map/all_to_all | solution.py:472
  10.4 14.4 %collective-permute-start.3 = (bf16[512,128]{1,0:T(8,128)(2,1)}, bf16[512,128]{1,0:T(8,128)(2,1)S(1)}, u32[]{:S(2)}, u32[]{:S(2)}) collective-permute-start(bf16[512,128]{1,0:T(8,128)(2,1)} %get-tuple-element.39), channel_id=1, source_target_pairs={{0,1},{1,0},{2,3},{3,2},{4,5},{5,4},{6,7},{7,6},{8,9},{9,8},{10,11... | collective-permute-start | bytes 393224 | tf_op jit(solution)/shard_map/ppermute | solution.py:430
  10.7 14.1 %collective-permute-start.4 = (bf16[512,128]{1,0:T(8,128)(2,1)}, bf16[512,128]{1,0:T(8,128)(2,1)S(1)}, u32[]{:S(2)}, u32[]{:S(2)}) collective-permute-start(bf16[512,128]{1,0:T(8,128)(2,1)} %get-tuple-element.39), channel_id=1, source_target_pairs={{0,2},{1,3},{2,0},{3,1},{4,6},{5,7},{6,4},{7,5},{8,10},{9,11},{10,... | collective-permute-start | bytes 393224 | tf_op jit(solution)/shard_map/ppermute | solution.py:430
  12.4 12.4 %collective-permute-start.5 = (bf16[512,128]{1,0:T(8,128)(2,1)}, bf16[512,128]{1,0:T(8,128)(2,1)S(1)}, u32[]{:S(2)}, u32[]{:S(2)}) collective-permute-start(bf16[512,128]{1,0:T(8,128)(2,1)} %get-tuple-element.39), channel_id=1, source_target_pairs={{0,4},{1,5},{2,6},{3,7},{4,0},{5,1},{6,2},{7,3},{8,12},{9,13},{10,... | collective-permute-start | bytes 393224 | tf_op jit(solution)/shard_map/ppermute | solution.py:430
  13.9 10.9 %collective-permute-start.6 = (bf16[512,128]{1,0:T(8,128)(2,1)}, bf16[512,128]{1,0:T(8,128)(2,1)S(1)}, u32[]{:S(2)}, u32[]{:S(2)}) collective-permute-start(bf16[512,128]{1,0:T(8,128)(2,1)} %get-tuple-element.39), channel_id=1, source_target_pairs={{0,6},{1,7},{2,4},{3,5},{4,2},{5,3},{6,0},{7,1},{8,14},{9,15},{10,... | collective-permute-start | bytes 393224 | tf_op jit(solution)/shard_map/ppermute | solution.py:430
  14.4 0.9 %copy-start.5 = (f32[8,4096]{1,0:T(8,128)S(1)}, f32[8,4096]{1,0:T(8,128)}, u32[]{:S(2)}) copy-start(f32[8,4096]{1,0:T(8,128)} %refs_1_.1) | copy-start | bytes 393220
  15.3 0.7 %copy-start.6 = (s32[1,128]{1,0:T(1,128)S(1)}, s32[1,128]{1,0:T(1,128)}, u32[]{:S(2)}) copy-start(s32[1,128]{1,0:T(1,128)} %refs_4_.1) | copy-start | bytes 1540
  17.0 0.5 copy-start.7
  24.8 9.3 %collective-permute-start.7 = (bf16[4,512,128]{2,1,0:T(8,128)(2,1)S(1)}, bf16[4,512,128]{2,1,0:T(8,128)(2,1)S(1)}, u32[]{:S(2)}, u32[]{:S(2)}) collective-permute-start(bf16[4,512,128]{2,1,0:T(8,128)(2,1)S(1)} %shard_map.149.refs_7_), channel_id=1, source_target_pairs={{0,1},{1,0},{2,3},{3,2},{4,5},{5,4},{6,7},{7,6},{8,9},{9,8},{10,11... | collective-permute-start | bytes 1572872 | tf_op jit(solution)/shard_map/ppermute | solution.py:430
  24.9 6.8 %collective-permute-start = (bf16[8,32,128]{2,1,0:T(8,128)(2,1)S(1)}, bf16[8,32,128]{2,1,0:T(8,128)(2,1)S(1)}, u32[]{:S(2)}, u32[]{:S(2)}) collective-permute-start(bf16[8,32,128]{2,1,0:T(8,128)(2,1)S(1)} %get-tuple-element.32), channel_id=1, source_target_pairs={{0,8},{8,16},{16,24},{24,0},{1,9},{9,17},{17,25},{25,1},{2,10},{10... | collective-permute-start | bytes 196616 | tf_op jit(solution)/shard_map/ppermute | solution.py:535
  26.0 8.2 %collective-permute-start.1 = (bf16[8,32,128]{2,1,0:T(8,128)(2,1)S(1)}, bf16[8,32,128]{2,1,0:T(8,128)(2,1)S(1)}, u32[]{:S(2)}, u32[]{:S(2)}) collective-permute-start(bf16[8,32,128]{2,1,0:T(8,128)(2,1)S(1)} %get-tuple-element.33), channel_id=1, source_target_pairs={{0,16},{8,24},{16,0},{24,8},{1,17},{9,25},{17,1},{25,9},{2,18},{10... | collective-permute-start | bytes 196616 | tf_op jit(solution)/shard_map/ppermute | solution.py:535
  26.9 7.3 %collective-permute-start.2 = (bf16[8,32,128]{2,1,0:T(8,128)(2,1)S(1)}, bf16[8,32,128]{2,1,0:T(8,128)(2,1)S(1)}, u32[]{:S(2)}, u32[]{:S(2)}) collective-permute-start(bf16[8,32,128]{2,1,0:T(8,128)(2,1)S(1)} %get-tuple-element.34), channel_id=1, source_target_pairs={{0,24},{8,0},{16,8},{24,16},{1,25},{9,1},{17,9},{25,17},{2,26},{10... | collective-permute-start | bytes 196616 | tf_op jit(solution)/shard_map/ppermute | solution.py:535
  34.6 8.7 %collective-permute-start.10 = (bf16[272,128]{1,0:T(8,128)(2,1)S(1)}, bf16[272,128]{1,0:T(8,128)(2,1)S(1)}, u32[]{:S(2)}, u32[]{:S(2)}) collective-permute-start(bf16[272,128]{1,0:T(8,128)(2,1)S(1)} %shard_map.150.refs_4_.refs_0_), channel_id=1, source_target_pairs={{0,24},{8,16},{16,8},{24,0},{1,25},{9,17},{17,9},{25,1},{2,26},{10... | collective-permute-start | bytes 208904 | tf_op jit(solution)/shard_map/ppermute | solution.py:556
  36.9 6.5 %collective-permute-start.8 = (bf16[272,128]{1,0:T(8,128)(2,1)S(1)}, bf16[272,128]{1,0:T(8,128)(2,1)S(1)}, u32[]{:S(2)}, u32[]{:S(2)}) collective-permute-start(bf16[272,128]{1,0:T(8,128)(2,1)S(1)} %shard_map.150.refs_4_.refs_0_), channel_id=1, source_target_pairs={{0,8},{8,0},{16,24},{24,16},{1,9},{9,1},{17,25},{25,17},{2,10},{10... | collective-permute-start | bytes 208904 | tf_op jit(solution)/shard_map/ppermute | solution.py:556
  36.9 7.3 %collective-permute-start.9 = (bf16[272,128]{1,0:T(8,128)(2,1)S(1)}, bf16[272,128]{1,0:T(8,128)(2,1)S(1)}, u32[]{:S(2)}, u32[]{:S(2)}) collective-permute-start(bf16[272,128]{1,0:T(8,128)(2,1)S(1)} %shard_map.150.refs_4_.refs_0_), channel_id=1, source_target_pairs={{0,16},{8,24},{16,0},{24,8},{1,17},{9,25},{17,1},{25,9},{2,18},{10... | collective-permute-start | bytes 208904 | tf_op jit(solution)/shard_map/ppermute | solution.py:556
  39.8 12.7 %copy-start.1 = (bf16[768,256]{1,0:T(8,128)(2,1)S(1)}, bf16[768,256]{1,0:T(8,128)(2,1)}, u32[]{:S(2)}) copy-start(bf16[768,256]{1,0:T(8,128)(2,1)} %refs_2_.2) | copy-start | bytes 1179652
  39.8 12.7 %all-to-all-start.1 = ((bf16[8,96,128]{2,1,0:T(8,128)(2,1)}), bf16[8,96,128]{2,1,0:T(8,128)(2,1)S(1)}, u32[]{:S(2)}, u32[]{:S(2)}) async-start(bf16[8,96,128]{2,1,0:T(8,128)(2,1)} %shard_map.151), calls=%async_computation.1 | async-start | bytes 393216 | tf_op jit(solution)/shard_map/all_to_all | solution.py:557
  44.2 8.3 %copy-start.8 = (s32[1,128]{1,0:T(1,128)S(1)}, s32[1,128]{1,0:T(1,128)}, u32[]{:S(2)}) copy-start(s32[1,128]{1,0:T(1,128)} %copy-done.7) | copy-start | bytes 1540
  44.2 6.3 %collective-permute-start.12 = (bf16[272,128]{1,0:T(8,128)(2,1)S(1)}, bf16[272,128]{1,0:T(8,128)(2,1)S(1)}, u32[]{:S(2)}, u32[]{:S(2)}) collective-permute-start(bf16[272,128]{1,0:T(8,128)(2,1)S(1)} %shard_map.153.refs_1_), channel_id=1, source_target_pairs={{0,2},{1,3},{2,0},{3,1},{4,6},{5,7},{6,4},{7,5},{8,10},{9,11},{10,... | collective-permute-start | bytes 208904 | tf_op jit(solution)/shard_map/ppermute | solution.py:430
  45.4 5.1 %collective-permute-start.14 = (bf16[272,128]{1,0:T(8,128)(2,1)S(1)}, bf16[272,128]{1,0:T(8,128)(2,1)S(1)}, u32[]{:S(2)}, u32[]{:S(2)}) collective-permute-start(bf16[272,128]{1,0:T(8,128)(2,1)S(1)} %shard_map.153.refs_1_), channel_id=1, source_target_pairs={{0,4},{1,5},{2,6},{3,7},{4,0},{5,1},{6,2},{7,3},{8,12},{9,13},{10,... | collective-permute-start | bytes 208904 | tf_op jit(solution)/shard_map/ppermute | solution.py:430
  46.9 5.6 %collective-permute-start.16 = (bf16[272,128]{1,0:T(8,128)(2,1)S(1)}, bf16[272,128]{1,0:T(8,128)(2,1)S(1)}, u32[]{:S(2)}, u32[]{:S(2)}) collective-permute-start(bf16[272,128]{1,0:T(8,128)(2,1)S(1)} %shard_map.153.refs_1_), channel_id=1, source_target_pairs={{0,6},{1,7},{2,4},{3,5},{4,2},{5,3},{6,0},{7,1},{8,14},{9,15},{10,... | collective-permute-start | bytes 208904 | tf_op jit(solution)/shard_map/ppermute | solution.py:430
  47.8 5.8 %collective-permute-start.11 = (bf16[272,128]{1,0:T(8,128)(2,1)S(1)}, bf16[272,128]{1,0:T(8,128)(2,1)S(1)}, u32[]{:S(2)}, u32[]{:S(2)}) collective-permute-start(bf16[272,128]{1,0:T(8,128)(2,1)S(1)} %shard_map.153.refs_1_), channel_id=1, source_target_pairs={{0,1},{1,0},{2,3},{3,2},{4,5},{5,4},{6,7},{7,6},{8,9},{9,8},{10,11... | collective-permute-start | bytes 208904 | tf_op jit(solution)/shard_map/ppermute | solution.py:430
  50.5 3.1 %collective-permute-start.13 = (bf16[272,128]{1,0:T(8,128)(2,1)S(1)}, bf16[272,128]{1,0:T(8,128)(2,1)S(1)}, u32[]{:S(2)}, u32[]{:S(2)}) collective-permute-start(bf16[272,128]{1,0:T(8,128)(2,1)S(1)} %collective-permute-done.12.refs_3_), channel_id=1, source_target_pairs={{0,1},{1,0},{2,3},{3,2},{4,5},{5,4},{6,7},{7,6},{8,9},{9,8},{10,11... | collective-permute-start | bytes 208904 | tf_op jit(solution)/shard_map/ppermute | solution.py:430
  50.5 3.1 %collective-permute-start.15 = (bf16[272,128]{1,0:T(8,128)(2,1)S(1)}, bf16[272,128]{1,0:T(8,128)(2,1)S(1)}, u32[]{:S(2)}, u32[]{:S(2)}) collective-permute-start(bf16[272,128]{1,0:T(8,128)(2,1)S(1)} %collective-permute-done.14.refs_5_), channel_id=1, source_target_pairs={{0,1},{1,0},{2,3},{3,2},{4,5},{5,4},{6,7},{7,6},{8,9},{9,8},{10,11... | collective-permute-start | bytes 208904 | tf_op jit(solution)/shard_map/ppermute | solution.py:430
  52.5 1.3 %collective-permute-start.17 = (bf16[272,128]{1,0:T(8,128)(2,1)S(1)}, bf16[272,128]{1,0:T(8,128)(2,1)S(1)}, u32[]{:S(2)}, u32[]{:S(2)}) collective-permute-start(bf16[272,128]{1,0:T(8,128)(2,1)S(1)} %collective-permute-done.16.refs_7_), channel_id=1, source_target_pairs={{0,1},{1,0},{2,3},{3,2},{4,5},{5,4},{6,7},{7,6},{8,9},{9,8},{10,11... | collective-permute-start | bytes 208904 | tf_op jit(solution)/shard_map/ppermute | solution.py:430
